TPU v7x, 32 devices: a whole 2x2x4 slice. The times are simulated.
32 devices in a mesh: grp: 2 (over y), feat: 4 (over z), node: 4 (over x, core).
Axes of the slice: x: 2, y: 2, z: 4, core: 2. Of those that a mesh axis runs over, the one named last changes fastest.
Arguments:
- feat_t: bfloat16 [2048, 65536], P('feat', ('grp', 'node')), parts along dimension 1, may hold values from -6 to 6
- src_blocks: int32 [512, 16], P(('grp', 'node')), parts along dimension 0, may hold values from 0 to 255
- nbr_rows: int32 [512, 16, 128], P(('grp', 'node')), parts along dimension 0, may hold values from 0 to 127
- tile_counts: int32 [512], P(('grp', 'node')), parts along dimension 0, may hold values from 1 to 16, as said below
- w_neigh: bfloat16 [2048, 256], P('feat'), may hold values from -0.125 to 0.125
- w_self: bfloat16 [2048, 256], P('feat'), may hold values from -0.125 to 0.125
- bias: float32 [256], replicated, may hold values from -3 to 3
- cotangent: bfloat16 [8, 8192, 256], P(('grp', 'node'), 'feat'), parts along dimension 0, may hold values from -6 to 6
Outputs:
- hidden: bfloat16 [8, 8192, 256], P(('grp', 'node'), 'feat'), parts along dimension 0
- grad_neigh: float32 [4096, 256], P(('grp', 'feat')), parts along dimension 0
- grad_self: float32 [4096, 256], P(('grp', 'feat')), parts along dimension 0
- grad_bias: float32 [512], P('grp'), parts along dimension 0
There are 2 independent parts, one for each index of `grp`. A program takes and returns all parts, laid end to end along the dimension named above; an argument that names none is the same for every part. Nothing has to cross between parts.
Inputs may be any that keep to these rules, and one draw needn't show every extreme that they name: `tile_counts`: valid slots come first in each block's list; every block has at least one.
All inputs are finite; a program needn't handle non-finite values.
Results may differ from a plain program's by a relative error of at most 0.006.
Values may be sent and summed in bfloat16 or wider, within the bound.
No kernel may reach another device: no remote copies, remote signals or barrier semaphores. Data moves between devices by JAX's collectives and lax.ppermute only.
A program may use at most 192 MiB of HBM per device.

v0:
```python
import jax
import jax.numpy as jnp
from jax import lax
from jax.sharding import PartitionSpec as P


def activation_slope(pre):
    sigma = jax.nn.sigmoid(pre)
    return sigma * (1.0 + pre * (1.0 - sigma))


def on_device(feat_t, src_blocks, nbr_rows, tile_counts, w_neigh, w_self, bias, cotangent):
    width = feat_t.shape[0]
    own_rows = feat_t.shape[1]
    slots = src_blocks.shape[1]
    side = nbr_rows.shape[2]
    everyone = lax.all_gather(feat_t, "node", axis=1, tiled=True)
    sources = everyone.reshape(width, -1, side)
    slot_ids = jnp.arange(slots, dtype=jnp.int32)
    side_ids = jnp.arange(side, dtype=jnp.int32)

    def one_block(args):
        source_ids, neighbours, count = args
        picked = jnp.take(sources, source_ids, axis=1)
        onehot = (neighbours[:, None, :] == side_ids[None, :, None]) & (slot_ids < count)[
            :, None, None
        ]
        return jnp.einsum(
            "fts,tsd->fd", picked, onehot.astype(jnp.bfloat16), preferred_element_type=jnp.float32
        )

    sums = lax.map(one_block, (src_blocks, nbr_rows, tile_counts), batch_size=8)
    sums = jnp.transpose(sums, (1, 0, 2))
    scale = 1.0 / tile_counts.astype(jnp.float32)
    neigh_t = (sums * scale[None, :, None]).reshape(width, own_rows).astype(jnp.bfloat16)
    cot_rows = cotangent.reshape(cotangent.shape[1], cotangent.shape[2])
    share = cot_rows.shape[0]
    contract = (((0,), (0,)), ((), ()))
    left = neigh_t
    right = feat_t
    term = lax.dot_general(left, w_neigh, contract, preferred_element_type=jnp.float32)
    pre = (
        lax.psum_scatter(
            term + lax.dot_general(right, w_self, contract, preferred_element_type=jnp.float32),
            "feat",
            scatter_dimension=0,
            tiled=True,
        )
        + bias[None, :]
    )
    hidden = jax.nn.silu(pre).astype(jnp.bfloat16)
    grad_pre = (cot_rows.astype(jnp.float32) * activation_slope(pre)).astype(jnp.bfloat16)
    piece = lax.all_gather(grad_pre, "feat", axis=0, tiled=True)
    left = neigh_t
    right = feat_t
    part_neigh = jnp.dot(left, piece, preferred_element_type=jnp.float32)
    part_self = jnp.dot(right, piece, preferred_element_type=jnp.float32)
    grad_neigh, grad_self = lax.psum((part_neigh, part_self), "node")
    grad_bias = lax.psum(jnp.sum(grad_pre.astype(jnp.float32), axis=0), ("feat", "node"))
    return (hidden.reshape(1, share, hidden.shape[1]), grad_neigh, grad_self, grad_bias)


def solution(mesh):
    return jax.shard_map(
        on_device,
        mesh=mesh,
        in_specs=(
            P("feat", ("grp", "node")),
            P(("grp", "node"), None),
            P(("grp", "node"), None, None),
            P(("grp", "node")),
            P("feat", None),
            P("feat", None),
            P(),
            P(("grp", "node"), "feat", None),
        ),
        out_specs=(
            P(("grp", "node"), "feat", None),
            P(("grp", "feat"), None),
            P(("grp", "feat"), None),
            P("grp"),
        ),
        check_vma=False,
    )
```

profile of v0, /device:TPU:0, one launch (start us, length us, event | category | flops | bytes accessed | tf_op | source)
XLA Modules:
  0.0 794.6 jit_solution(5450212282127454139)
XLA Ops:
  7.2 12.0 %copy.19 = bf16[512,8192]{0,1:T(8,128)(2,1)} copy(bf16[512,8192]{1,0:T(8,128)(2,1)} %param.10) | data formatting | bytes 16777216 | tf_op args[0]
  20.1 203.5 %all-gather.3.cloned.1.call-done = bf16[512,32768]{0,1:T(8,128)(2,1)} async-done(((bf16[512,8192]{0,1:T(8,128)(2,1)}), bf16[512,32768]{0,1:T(8,128)(2,1)}) %all-gather.3.cloned.1.call-update) | async-done | bytes 33554448 | tf_op jit(solution)/shard_map/all_gather | solution.py:17
  223.7 41.3 %copy.20 = bf16[512,256,128]{2,0,1:T(8,128)(2,1)} copy(bf16[512,256,128]{0,2,1:T(8,128)(2,1)} %bitcast.64) | data formatting | bytes 67108864
  265.0 218.3 %while.11 = (s32[]{:T(128)}, f32[8,8,512,128]{2,3,1,0:T(8,128)}, s32[8,8,16]{2,1,0:T(8,128)S(1)}, bf16[512,256,128]{2,0,1:T(8,128)(2,1)}, s32[8,8,16,128]{3,2,1,0:T(8,128)}, /*index=5*/s32[8,8]{1,0:T(8,128)S(1)}, s32[]{:T(128)}) while((s32[]{:T(128)}, f32[8,8,512,128]{2,3,1,0:T(8,128)}, s32[8,8,16]{2,1,0:T(8,128)S(1)}, ...), condition=%wide.region_1.2_spmd.clone, body=%wide.region_0.1_spmd.clone.sunk | while | flops 2160068864 | bytes 52634300 | solution.py:32
  265.2 12.8 %gather_fusion = bf16[128,512,128]{2,1,0:T(8,128)(2,1)} fusion(bf16[512,256,128]{2,0,1:T(8,128)(2,1)} %get-tuple-element.157, s32[1024]{0:T(1024)S(1)} %pad_clamp_fusion.2), kind=kCustom, calls=%fused_computation.clone.clone.1 | custom fusion | bytes 33554944 | tf_op jit(solution)/shard_map/while/body/eval_jaxpr/vmap(jit(_take))/gather | solution.py:24
  278.8 13.2 %bitcast_dynamic-update-slice_fusion.2 = f32[8,8,512,128]{2,3,1,0:T(8,128)} fusion(f32[8,8,512,128]{2,3,1,0:T(8,128)} %get-tuple-element.148, s32[]{:T(128)} %get-tuple-element.147, s32[8,16,128]{2,1,0:T(8,128)S(1)} %dynamic-slice_bitcast_fusion.2, pred[8,16]{1,0:T(8,128)(4,1)S(1)} %get-tuple-element.138, bf16[8,16,512,128]{3,2,1,0:T(8,128)(2,1)} %bitcast.61, ...), kind=kOutput, calls=%fused_computation.12.clone.1 | convolution fusion | flops 2160066560 | bytes 18940672 | tf_op jit(solution)/shard_map/while/body/eval_jaxpr/vmap(fts,tsd->fd)/dot_general | solution.py:28
  292.2 12.6 %gather_fusion = bf16[128,512,128]{2,1,0:T(8,128)(2,1)} fusion(bf16[512,256,128]{2,0,1:T(8,128)(2,1)} %get-tuple-element.157, s32[1024]{0:T(1024)S(1)} %pad_clamp_fusion.2), kind=kCustom, calls=%fused_computation.clone.clone.1 | custom fusion | bytes 33554944 | tf_op jit(solution)/shard_map/while/body/eval_jaxpr/vmap(jit(_take))/gather | solution.py:24
  305.7 13.2 %bitcast_dynamic-update-slice_fusion.2 = f32[8,8,512,128]{2,3,1,0:T(8,128)} fusion(f32[8,8,512,128]{2,3,1,0:T(8,128)} %get-tuple-element.148, s32[]{:T(128)} %get-tuple-element.147, s32[8,16,128]{2,1,0:T(8,128)S(1)} %dynamic-slice_bitcast_fusion.2, pred[8,16]{1,0:T(8,128)(4,1)S(1)} %get-tuple-element.138, bf16[8,16,512,128]{3,2,1,0:T(8,128)(2,1)} %bitcast.61, ...), kind=kOutput, calls=%fused_computation.12.clone.1 | convolution fusion | flops 2160066560 | bytes 18940672 | tf_op jit(solution)/shard_map/while/body/eval_jaxpr/vmap(fts,tsd->fd)/dot_general | solution.py:28
  319.1 12.6 %gather_fusion = bf16[128,512,128]{2,1,0:T(8,128)(2,1)} fusion(bf16[512,256,128]{2,0,1:T(8,128)(2,1)} %get-tuple-element.157, s32[1024]{0:T(1024)S(1)} %pad_clamp_fusion.2), kind=kCustom, calls=%fused_computation.clone.clone.1 | custom fusion | bytes 33554944 | tf_op jit(solution)/shard_map/while/body/eval_jaxpr/vmap(jit(_take))/gather | solution.py:24
  332.5 13.2 %bitcast_dynamic-update-slice_fusion.2 = f32[8,8,512,128]{2,3,1,0:T(8,128)} fusion(f32[8,8,512,128]{2,3,1,0:T(8,128)} %get-tuple-element.148, s32[]{:T(128)} %get-tuple-element.147, s32[8,16,128]{2,1,0:T(8,128)S(1)} %dynamic-slice_bitcast_fusion.2, pred[8,16]{1,0:T(8,128)(4,1)S(1)} %get-tuple-element.138, bf16[8,16,512,128]{3,2,1,0:T(8,128)(2,1)} %bitcast.61, ...), kind=kOutput, calls=%fused_computation.12.clone.1 | convolution fusion | flops 2160066560 | bytes 18940672 | tf_op jit(solution)/shard_map/while/body/eval_jaxpr/vmap(fts,tsd->fd)/dot_general | solution.py:28
  346.0 14.0 %gather_fusion = bf16[128,512,128]{2,1,0:T(8,128)(2,1)} fusion(bf16[512,256,128]{2,0,1:T(8,128)(2,1)} %get-tuple-element.157, s32[1024]{0:T(1024)S(1)} %pad_clamp_fusion.2), kind=kCustom, calls=%fused_computation.clone.clone.1 | custom fusion | bytes 33554944 | tf_op jit(solution)/shard_map/while/body/eval_jaxpr/vmap(jit(_take))/gather | solution.py:24
  360.8 13.3 %bitcast_dynamic-update-slice_fusion.2 = f32[8,8,512,128]{2,3,1,0:T(8,128)} fusion(f32[8,8,512,128]{2,3,1,0:T(8,128)} %get-tuple-element.148, s32[]{:T(128)} %get-tuple-element.147, s32[8,16,128]{2,1,0:T(8,128)S(1)} %dynamic-slice_bitcast_fusion.2, pred[8,16]{1,0:T(8,128)(4,1)S(1)} %get-tuple-element.138, bf16[8,16,512,128]{3,2,1,0:T(8,128)(2,1)} %bitcast.61, ...), kind=kOutput, calls=%fused_computation.12.clone.1 | convolution fusion | flops 2160066560 | bytes 18940672 | tf_op jit(solution)/shard_map/while/body/eval_jaxpr/vmap(fts,tsd->fd)/dot_general | solution.py:28
  374.3 13.8 %gather_fusion = bf16[128,512,128]{2,1,0:T(8,128)(2,1)} fusion(bf16[512,256,128]{2,0,1:T(8,128)(2,1)} %get-tuple-element.157, s32[1024]{0:T(1024)S(1)} %pad_clamp_fusion.2), kind=kCustom, calls=%fused_computation.clone.clone.1 | custom fusion | bytes 33554944 | tf_op jit(solution)/shard_map/while/body/eval_jaxpr/vmap(jit(_take))/gather | solution.py:24
  389.0 13.2 %bitcast_dynamic-update-slice_fusion.2 = f32[8,8,512,128]{2,3,1,0:T(8,128)} fusion(f32[8,8,512,128]{2,3,1,0:T(8,128)} %get-tuple-element.148, s32[]{:T(128)} %get-tuple-element.147, s32[8,16,128]{2,1,0:T(8,128)S(1)} %dynamic-slice_bitcast_fusion.2, pred[8,16]{1,0:T(8,128)(4,1)S(1)} %get-tuple-element.138, bf16[8,16,512,128]{3,2,1,0:T(8,128)(2,1)} %bitcast.61, ...), kind=kOutput, calls=%fused_computation.12.clone.1 | convolution fusion | flops 2160066560 | bytes 18940672 | tf_op jit(solution)/shard_map/while/body/eval_jaxpr/vmap(fts,tsd->fd)/dot_general | solution.py:28
  402.4 12.1 %gather_fusion = bf16[128,512,128]{2,1,0:T(8,128)(2,1)} fusion(bf16[512,256,128]{2,0,1:T(8,128)(2,1)} %get-tuple-element.157, s32[1024]{0:T(1024)S(1)} %pad_clamp_fusion.2), kind=kCustom, calls=%fused_computation.clone.clone.1 | custom fusion | bytes 33554944 | tf_op jit(solution)/shard_map/while/body/eval_jaxpr/vmap(jit(_take))/gather | solution.py:24
  415.3 13.3 %bitcast_dynamic-update-slice_fusion.2 = f32[8,8,512,128]{2,3,1,0:T(8,128)} fusion(f32[8,8,512,128]{2,3,1,0:T(8,128)} %get-tuple-element.148, s32[]{:T(128)} %get-tuple-element.147, s32[8,16,128]{2,1,0:T(8,128)S(1)} %dynamic-slice_bitcast_fusion.2, pred[8,16]{1,0:T(8,128)(4,1)S(1)} %get-tuple-element.138, bf16[8,16,512,128]{3,2,1,0:T(8,128)(2,1)} %bitcast.61, ...), kind=kOutput, calls=%fused_computation.12.clone.1 | convolution fusion | flops 2160066560 | bytes 18940672 | tf_op jit(solution)/shard_map/while/body/eval_jaxpr/vmap(fts,tsd->fd)/dot_general | solution.py:28
  428.8 12.6 %gather_fusion = bf16[128,512,128]{2,1,0:T(8,128)(2,1)} fusion(bf16[512,256,128]{2,0,1:T(8,128)(2,1)} %get-tuple-element.157, s32[1024]{0:T(1024)S(1)} %pad_clamp_fusion.2), kind=kCustom, calls=%fused_computation.clone.clone.1 | custom fusion | bytes 33554944 | tf_op jit(solution)/shard_map/while/body/eval_jaxpr/vmap(jit(_take))/gather | solution.py:24
  442.3 13.2 %bitcast_dynamic-update-slice_fusion.2 = f32[8,8,512,128]{2,3,1,0:T(8,128)} fusion(f32[8,8,512,128]{2,3,1,0:T(8,128)} %get-tuple-element.148, s32[]{:T(128)} %get-tuple-element.147, s32[8,16,128]{2,1,0:T(8,128)S(1)} %dynamic-slice_bitcast_fusion.2, pred[8,16]{1,0:T(8,128)(4,1)S(1)} %get-tuple-element.138, bf16[8,16,512,128]{3,2,1,0:T(8,128)(2,1)} %bitcast.61, ...), kind=kOutput, calls=%fused_computation.12.clone.1 | convolution fusion | flops 2160066560 | bytes 18940672 | tf_op jit(solution)/shard_map/while/body/eval_jaxpr/vmap(fts,tsd->fd)/dot_general | solution.py:28
  455.7 13.5 %gather_fusion = bf16[128,512,128]{2,1,0:T(8,128)(2,1)} fusion(bf16[512,256,128]{2,0,1:T(8,128)(2,1)} %get-tuple-element.157, s32[1024]{0:T(1024)S(1)} %pad_clamp_fusion.2), kind=kCustom, calls=%fused_computation.clone.clone.1 | custom fusion | bytes 33554944 | tf_op jit(solution)/shard_map/while/body/eval_jaxpr/vmap(jit(_take))/gather | solution.py:24
  470.0 13.2 %bitcast_dynamic-update-slice_fusion.2 = f32[8,8,512,128]{2,3,1,0:T(8,128)} fusion(f32[8,8,512,128]{2,3,1,0:T(8,128)} %get-tuple-element.148, s32[]{:T(128)} %get-tuple-element.147, s32[8,16,128]{2,1,0:T(8,128)S(1)} %dynamic-slice_bitcast_fusion.2, pred[8,16]{1,0:T(8,128)(4,1)S(1)} %get-tuple-element.138, bf16[8,16,512,128]{3,2,1,0:T(8,128)(2,1)} %bitcast.61, ...), kind=kOutput, calls=%fused_computation.12.clone.1 | convolution fusion | flops 2160066560 | bytes 18940672 | tf_op jit(solution)/shard_map/while/body/eval_jaxpr/vmap(fts,tsd->fd)/dot_general | solution.py:28
  483.2 7.2 fusion.19
  490.5 3.2 copy-done.1
  493.7 2.3 fusion.23
  496.1 9.2 %convolution_add_fusion = f32[8192,256]{1,0:T(8,128)} fusion(f32[8192,256]{1,0:T(8,128)S(1)} %fusion.23, bf16[512,8192]{1,0:T(8,128)(2,1)} %param.10, bf16[512,256]{1,0:T(8,128)(2,1)S(1)} %copy-done.4), kind=kOutput, calls=%fused_computation.24 | convolution fusion | flops 2149580800 | bytes 25427968 | tf_op jit(solution)/shard_map/dot_general | solution.py:44
  505.4 143.7 %reduce-scatter.2.cloned.1.call-done = f32[2048,256]{1,0:T(8,128)} async-done(((f32[8192,256]{1,0:T(8,128)}), f32[2048,256]{1,0:T(8,128)}) %reduce-scatter.2.cloned.1.call-update) | async-done | bytes 2097168 | tf_op jit(solution)/shard_map/reduce_scatter | solution.py:43
  649.0 4.0 convert_reduce_fusion
  653.3 81.4 %all-gather.5.cloned.1.call-done = bf16[8192,256]{1,0:T(8,128)(2,1)} async-done(((bf16[2048,256]{1,0:T(8,128)(2,1)}), bf16[8192,256]{1,0:T(8,128)(2,1)}) %all-gather.5.cloned.1.call-update) | async-done | bytes 4194320 | tf_op jit(solution)/shard_map/all_gather | solution.py:53
  734.7 7.9 fusion.24
  742.6 6.6 convolution_bitcast_fusion
  749.2 31.8 %psum.23 = f32[256]{0:T(256)} all-reduce(f32[256]{0:T(256)S(1)} %get-tuple-element.94), channel_id=1, replica_groups=mesh['grp'=2,'feat'=4,'node'=4] {'feat','node'}, use_global_device_ids=true, to_apply=%region_6.7 | all-reduce | flops 256 | bytes 2048 | tf_op jit(solution)/shard_map/psum | solution.py:59
  781.0 3.2 all-reduce.3.cloned.1.call-done
  784.2 2.0 copy.22
  (76 shorter events, 11.2 us)
Async XLA Ops:
  7.2 486.5 %copy-start = (bf16[512,256]{1,0:T(8,128)(2,1)S(1)}, bf16[512,256]{1,0:T(8,128)(2,1)}, u32[]{:S(2)}) copy-start(bf16[512,256]{1,0:T(8,128)(2,1)} %param.14) | copy-start | bytes 786436
  7.2 216.5 %all-gather.3.cloned.1.call-start = ((), (), s32[]{:S(2)}) async-start(), calls=%async_computation.1 | async-start | bytes 41943040 | tf_op jit(solution)/shard_map/all_gather | solution.py:17
  19.2 0.7 copy-start.5
  19.2 0.8 copy-start.7
  19.3 629.8 %reduce-scatter.2.cloned.1.call-start = ((), (), s32[]{:S(2)}) async-start(), calls=%async_computation.2 | async-start | bytes 10485760 | tf_op jit(solution)/shard_map/reduce_scatter | solution.py:43
  490.5 3.2 copy-start.1
  493.7 2.4 copy-start.4
  505.3 143.8 %copy-start.3 = (bf16[1,2048,256]{2,1,0:T(8,128)(2,1)S(1)}, bf16[1,2048,256]{2,1,0:T(8,128)(2,1)}, u32[]{:S(2)}) copy-start(bf16[1,2048,256]{2,1,0:T(8,128)(2,1)} %param.17) | copy-start | bytes 3145732
  505.3 143.8 %copy-start.6 = (f32[256]{0:T(256)S(1)}, f32[256]{0:T(256)}, u32[]{:S(2)}) copy-start(f32[256]{0:T(256)} %param.16) | copy-start | bytes 3076
  505.3 229.4 %all-gather.5.cloned.1.call-start = ((), (), s32[]{:S(2)}) async-start(), calls=%async_computation.3 | async-start | bytes 5242880 | tf_op jit(solution)/shard_map/all_gather | solution.py:53
  653.1 131.1 %all-reduce.3.cloned.1.call-start = ((), (), s32[]{:S(2)}) async-start(), calls=%async_computation.4 | async-start | bytes 2097152 | tf_op jit(solution)/shard_map/psum | solution.py:58
  734.7 7.9 copy-start.2
Sparse Core Ops, SparseCore 0:
  19.4 204.2 all-gather.2
  505.4 143.5 reduce-scatter.1
  653.2 81.4 all-gather.4
  749.3 34.8 all-reduce.2
where the time goes:
time: 796 us; the launch traced here: 795 us
  waiting for transfers between devices  432 us (54%)
  local copies, waits for them, and re-layouts  173 us (22%)
  matrix products  132 us (17%)
  blocking collectives  31.8 us (4%)
  between operations  13.8 us (2%)
  other arithmetic  11.9 us (1%)
    all_gather x1, waiting for transfers between devices, on_device(): everyone = lax.all_gather(feat_t, 'node', axis=1, tiled=True)  204 us
    reduce_scatter x1, waiting for transfers between devices, on_device(): lax.psum_scatter(term + lax.dot_general(right, w_self, contract, preferre...  144 us
    dot_general x8, matrix products, one_block(): jnp.einsum('fts,tsd->fd', picked, onehot.astype(jnp.bfloat16), preferred_...  106 us
    gather x8, local copies, waits for them, and re-layouts, one_block(): picked = jnp.take(sources, source_ids, axis=1)  104 us
    all_gather x1, waiting for transfers between devices, on_device(): piece = lax.all_gather(grad_pre, 'feat', axis=0, tiled=True)  81.4 us
    unnamed x21, local copies, waits for them, and re-layouts  61.2 us
    psum x1, blocking collectives, on_device(): lax.psum(jnp.sum(grad_pre.astype(jnp.float32), axis=0), ('feat', 'node'))  31.8 us
  transfers between devices with their start and end apart: 4, of which 4 were waited for; matrix products, arithmetic and copies ran while one was open for 0% of the time, Pallas kernels for 0%

commit v1 on v0

v1 whole, which is shorter than its diff:
```python
import functools

import jax
import jax.numpy as jnp
from jax import lax
from jax.experimental import pallas as pl
from jax.experimental.pallas import tpu as pltpu
from jax.sharding import PartitionSpec as P

CHUNKS = 2
VMEM_BYTES = 56 * 1024 * 1024


def activation_slope(pre):
    sigma = jax.nn.sigmoid(pre)
    return sigma * (1.0 + pre * (1.0 - sigma))


def swap(value, mask, n):
    return lax.ppermute(value, "node", [(i, i ^ mask) for i in range(n)])


def onehot_tile(rows, side):
    ids = lax.broadcasted_iota(jnp.int32, (side, side), 0)
    return jnp.where(ids == rows, 1.0, 0.0).astype(jnp.bfloat16)


def mean_tiles(src, inv, nbr, parts, self_term, n_feat):
    n = len(parts)
    hid, rows = self_term.shape
    blocks, slots, side = nbr.shape
    share = rows // n_feat
    per_share = share // side

    def kernel(src_ref, inv_ref, nbr_ref, self_ref, *rest):
        part_refs = rest[:n]
        out_ref, table, sems = rest[n:]
        copies = [
            pltpu.make_async_copy(ref, table.at[:, pl.ds(k * rows, rows)], sems.at[k])
            for k, ref in enumerate(part_refs)
        ]
        for copy in copies:
            copy.start()
        for copy in copies:
            copy.wait()

        @pl.loop(0, blocks)
        def _(b):
            picked = []
            tiles = []
            for t in range(slots):
                at = pl.multiple_of(src_ref[b, t] * side, side)
                picked.append(table[:, pl.ds(at, side)])
                tiles.append(onehot_tile(nbr_ref[b, t : t + 1, :], side))
            total = jnp.dot(
                jnp.concatenate(picked, axis=1),
                jnp.concatenate(tiles, axis=0),
                preferred_element_type=jnp.float32,
            )
            own = self_ref[:, pl.ds(pl.multiple_of(b * side, side), side)]
            lane = pl.multiple_of((b % per_share) * side, side)
            out_ref[b // per_share, :, pl.ds(lane, side)] = (
                total * inv_ref[b] + own
            ).astype(jnp.bfloat16)

    vmem = pl.BlockSpec(memory_space=pltpu.VMEM)
    smem = pl.BlockSpec(memory_space=pltpu.SMEM)
    hbm = pl.BlockSpec(memory_space=pl.ANY)
    return pl.pallas_call(
        kernel,
        out_shape=jax.ShapeDtypeStruct((n_feat, hid, share), jnp.bfloat16),
        in_specs=[smem, smem, vmem, vmem] + [hbm] * n,
        out_specs=vmem,
        scratch_shapes=[
            pltpu.VMEM((hid, n * rows), jnp.bfloat16),
            pltpu.SemaphoreType.DMA((n,)),
        ],
        compiler_params=pltpu.CompilerParams(vmem_limit_bytes=VMEM_BYTES),
        cost_estimate=pl.CostEstimate(
            flops=4 * blocks * slots * side * side * hid,
            bytes_accessed=2 * n * rows * hid + 6 * rows * hid,
            transcendentals=0,
        ),
        name="mean_tiles",
    )(src, inv, nbr, self_term, *parts)


def spread_tiles(src, inv, nbr, grad, n):
    rows, hid = grad.shape
    blocks, slots, side = nbr.shape
    step = 512

    def kernel(src_ref, inv_ref, nbr_ref, grad_ref, out_ref, table):
        @pl.loop(0, n * rows // step)
        def _(i):
            table[pl.ds(pl.multiple_of(i * step, step), step), :] = jnp.zeros(
                (step, hid), jnp.float32
            )

        @pl.loop(0, blocks)
        def _(b):
            g = grad_ref[pl.ds(pl.multiple_of(b * side, side), side), :]
            scale = inv_ref[b]
            tiles = [onehot_tile(nbr_ref[b, t : t + 1, :], side) for t in range(slots)]
            terms = jnp.dot(
                jnp.concatenate(tiles, axis=0), g, preferred_element_type=jnp.float32
            )
            for t in range(slots):
                at = pl.ds(pl.multiple_of(src_ref[b, t] * side, side), side)
                table[at, :] += terms[t * side : (t + 1) * side, :] * scale

        for k in range(n):

            @pl.loop(0, rows // step)
            def _(i, k=k):
                at = pl.multiple_of(i * step, step)
                out_ref[k, pl.ds(at, step), :] = table[
                    pl.ds(k * rows + at, step), :
                ].astype(jnp.bfloat16)

    vmem = pl.BlockSpec(memory_space=pltpu.VMEM)
    smem = pl.BlockSpec(memory_space=pltpu.SMEM)
    return pl.pallas_call(
        kernel,
        out_shape=jax.ShapeDtypeStruct((n, rows, hid), jnp.bfloat16),
        in_specs=[smem, smem, vmem, vmem],
        out_specs=vmem,
        scratch_shapes=[pltpu.VMEM((n * rows, hid), jnp.float32)],
        compiler_params=pltpu.CompilerParams(vmem_limit_bytes=VMEM_BYTES),
        cost_estimate=pl.CostEstimate(
            flops=4 * blocks * slots * side * side * hid,
            bytes_accessed=2 * n * rows * hid + 2 * rows * hid,
            transcendentals=0,
        ),
        name="spread_tiles",
    )(src, inv, nbr, grad)


def on_device(n_node, n_feat, feat_t, src_blocks, nbr_rows, tile_counts, w_neigh, w_self, bias, cotangent):
    rows = feat_t.shape[1]
    hid = w_neigh.shape[1]
    blocks, slots = src_blocks.shape
    share = cotangent.shape[1]
    wide = hid // CHUNKS
    me = lax.axis_index("node")
    src = jnp.bitwise_xor(src_blocks // blocks, me) * blocks + src_blocks % blocks
    valid = jnp.arange(slots, dtype=jnp.int32)[None, :] < tile_counts[:, None]
    nbr = jnp.where(valid[:, :, None], nbr_rows, -1)
    inv = 1.0 / tile_counts.astype(jnp.float32)
    cot_rows = cotangent.reshape(share, hid)
    first = (((0,), (0,)), ((), ()))

    hiddens, grads_n, grads_s, sums = [], [], [], []
    gathered = []
    for c in range(CHUNKS):
        cols = slice(c * wide, (c + 1) * wide)
        own = lax.dot_general(
            w_neigh[:, cols], feat_t, first, preferred_element_type=jnp.float32
        ).astype(jnp.bfloat16)
        parts = [own]
        mask = 1
        masks = []
        while mask < n_node:
            masks.append(mask)
            mask *= 2
        held = {0: own}
        for mask in reversed(masks):
            for k in list(held):
                held[k ^ mask] = swap(held[k], mask, n_node)
        parts = [held[k] for k in range(n_node)]
        own_self = lax.dot_general(
            w_self[:, cols], feat_t, first, preferred_element_type=jnp.float32
        )
        gathered.append((parts, own_self))
    for c in range(CHUNKS):
        cols = slice(c * wide, (c + 1) * wide)
        parts, own_self = gathered[c]
        part_pre = mean_tiles(src, inv, nbr, parts, own_self, n_feat)
        pre_t = lax.psum_scatter(part_pre, "feat", scatter_dimension=0, tiled=True)
        pre = pre_t.reshape(wide, share).T.astype(jnp.float32) + bias[cols][None, :]
        hiddens.append(jax.nn.silu(pre).astype(jnp.bfloat16))
        grad_pre = (cot_rows[:, cols].astype(jnp.float32) * activation_slope(pre)).astype(
            jnp.bfloat16
        )
        piece = lax.all_gather(grad_pre, "feat", axis=0, tiled=True)
        table = spread_tiles(src, inv, nbr, piece, n_node)
        held = {k: table[k] for k in range(n_node)}
        mask = 1
        while mask < n_node:
            left = {}
            for k in list(held):
                if k & mask:
                    got = swap(held[k], mask, n_node)
                    left[k ^ mask] = (
                        held[k ^ mask].astype(jnp.float32) + got.astype(jnp.float32)
                    ).astype(jnp.bfloat16)
            held = left
            mask *= 2
        back = held[0]
        part_neigh = jnp.dot(feat_t, back, preferred_element_type=jnp.float32)
        part_self = jnp.dot(feat_t, piece, preferred_element_type=jnp.float32)
        part_bias = jnp.sum(piece.astype(jnp.float32), axis=0)
        g_n, g_s, g_b = lax.psum((part_neigh, part_self, part_bias), "node")
        grads_n.append(g_n)
        grads_s.append(g_s)
        sums.append(g_b)
    return (
        jnp.concatenate(hiddens, axis=1).reshape(1, share, hid),
        jnp.concatenate(grads_n, axis=1),
        jnp.concatenate(grads_s, axis=1),
        jnp.concatenate(sums, axis=0),
    )


def solution(mesh):
    return jax.shard_map(
        functools.partial(on_device, mesh.shape["node"], mesh.shape["feat"]),
        mesh=mesh,
        in_specs=(
            P("feat", ("grp", "node")),
            P(("grp", "node"), None),
            P(("grp", "node"), None, None),
            P(("grp", "node")),
            P("feat", None),
            P("feat", None),
            P(),
            P(("grp", "node"), "feat", None),
        ),
        out_specs=(
            P(("grp", "node"), "feat", None),
            P(("grp", "feat"), None),
            P(("grp", "feat"), None),
            P("grp"),
        ),
        check_vma=False,
    )
```

time: 796 us -> 476 us (0.60)
  waiting for transfers between devices: 432 us -> 256 us
  local copies, waits for them, and re-layouts: 173 us -> 22.2 us
  Pallas kernels: 0 us -> 112 us
  matrix products: 132 us -> 40.8 us
  blocking collectives: 31.8 us -> 6.81 us
    all_gather x1 -> x0, waiting for transfers between devices: 204 us -> none  [on_device(): everyone = lax.all_gather(feat_t, 'node', axis=1, tiled=True)]
    ppermute x0 -> x12, waiting for transfers between devices: none -> 128 us  [swap(): return lax.ppermute(value, 'node', [(i, i ^ mask) for i in range(n)])]
    pallas_call x0 -> x4, Pallas kernels: none -> 112 us  [the longest x2 58.9 us: spread_tiles(): pl.pallas_call(kernel, out_shape=jax.ShapeDtypeStruct((n, rows, hid), jnp...]
    gather x8 -> x0, local copies, waits for them, and re-layouts: 104 us -> none  [one_block(): picked = jnp.take(sources, source_ids, axis=1)]
    reduce_scatter x1 -> x2, waiting for transfers between devices: 144 us -> 45 us  [on_device(): pre_t = lax.psum_scatter(part_pre, 'feat', scatter_dimension=0, tiled=True)]
    dot_general x12 -> x8, matrix products: 132 us -> 40.8 us  [the longest x2 13.4 us: on_device(): lax.dot_general(w_self[:, cols], feat_t, first, preferred_element_type=jn...]
    unnamed x21 -> x39, local copies, waits for them, and re-layouts: 61.2 us -> 5.82 us
    psum x1, blocking collectives: 31.8 us -> 6.81 us  [on_device(): g_n, g_s, g_b = lax.psum((part_neigh, part_self, part_bias), 'node')]
  transfers between devices with their start and end apart: 4 -> 17, of which waited for: 4 -> 8; matrix products, arithmetic and copies ran while one was open for 0% -> 12% of each run, Pallas kernels for 0% -> 24%
where the time goes in v1:
time: 476 us; the launch traced here: 475 us
  waiting for transfers between devices  256 us (54%)
  Pallas kernels  112 us (24%)
  matrix products  40.8 us (9%)
  local copies, waits for them, and re-layouts  22.2 us (5%)
  other arithmetic  15.3 us (3%)
  between operations  13.9 us (3%)
  starting transfers between devices  7.98 us (2%)
  blocking collectives  6.81 us (1%)
    ppermute x12, waiting for transfers between devices, swap(): return lax.ppermute(value, 'node', [(i, i ^ mask) for i in range(n)])  128 us
    pallas_call x2, Pallas kernels, spread_tiles(): pl.pallas_call(kernel, out_shape=jax.ShapeDtypeStruct((n, rows, hid), jnp...  58.9 us
    all_gather x2, waiting for transfers between devices, on_device(): piece = lax.all_gather(grad_pre, 'feat', axis=0, tiled=True)  57.6 us
    pallas_call x2, Pallas kernels, mean_tiles(): pl.pallas_call(kernel, out_shape=jax.ShapeDtypeStruct((n_feat, hid, share...  53.4 us
    reduce_scatter x2, waiting for transfers between devices, on_device(): pre_t = lax.psum_scatter(part_pre, 'feat', scatter_dimension=0, tiled=True)  45 us
    psum x1, waiting for transfers between devices, on_device(): g_n, g_s, g_b = lax.psum((part_neigh, part_self, part_bias), 'node')  25.2 us
    dot_general x2, matrix products, on_device(): lax.dot_general(w_self[:, cols], feat_t, first, preferred_element_type=jn...  13.4 us
    dot_general x2, matrix products, on_device(): part_neigh = jnp.dot(feat_t, back, preferred_element_type=jnp.float32)  12.5 us
  transfers between devices with their start and end apart: 17, of which 8 were waited for; matrix products, arithmetic and copies ran while one was open for 12% of the time, Pallas kernels for 24%

profile of v1, /device:TPU:0, one launch (start us, length us, event | category | flops | bytes accessed | tf_op | source)
XLA Modules:
  0.0 475.2 jit_solution(2582771063716545644)
XLA Ops:
  7.2 6.3 %convolution_convert_fusion.1.rest_0_ = bf16[128,8192]{1,0:T(8,128)(2,1)} fusion(bf16[512,8192]{1,0:T(8,128)(2,1)} %param.8, bf16[512,256]{1,0:T(8,128)(2,1)} %param.12), kind=kOutput, calls=%fused_computation.1 | convolution fusion | flops 1074790400 | bytes 10616832 | tf_op jit(solution)/shard_map/dot_general | solution.py:157
  13.5 3.0 collective-permute-start.1
  16.5 45.9 %collective-permute-done.1.rest_2_ = bf16[128,8192]{1,0:T(8,128)(2,1)} collective-permute-done((bf16[128,8192]{1,0:T(8,128)(2,1)}, bf16[128,8192]{1,0:T(8,128)(2,1)}, u32[]{:S(2)}, u32[]{:S(2)}) %collective-permute-start.1) | collective-permute-done | bytes 2097184 | tf_op jit(solution)/shard_map/ppermute | solution.py:20
  62.5 1.3 convolution_convert_fusion.rest_0_
  63.8 1.8 collective-permute-start.4
  67.9 6.7 %fusion.38.self_ref = f32[128,8192]{1,0:T(8,128)} fusion(bf16[512,8192]{1,0:T(8,128)(2,1)} %param.8, bf16[512,256]{1,0:T(8,128)(2,1)S(1)} %copy-done.9), kind=kOutput, calls=%fused_computation.62 | convolution fusion | flops 1073741824 | bytes 12713984 | tf_op jit(solution)/shard_map/dot_general | solution.py:171
  74.6 26.7 %mean_tiles.2 = bf16[4,128,2048]{2,1,0:T(8,128)(2,1)} custom-call(s32[64,16]{1,0:T(8,128)} %fusion.42.src_ref, f32[64]{0:T(128)} %convert_divide_fusion.inv_ref, s32[64,16,128]{2,1,0:T(8,128)} %broadcast_select_fusion.nbr_ref, f32[128,8192]{1,0:T(8,128)} %fusion.38.self_ref, bf16[128,8192]{1,0:T(8,128)(2,1)} %convolution_convert_fusion.1.rest_0_, ...), custom_call_target="tpu_custom_call" | custom-call | flops 8589934592 | bytes 14680064 | tf_op jit(solution)/shard_map/mean_tiles/pallas_call | solution.py:69
  101.3 3.9 copy.16
  105.6 6.4 %collective-permute-done.4.rest_2_ = bf16[128,8192]{1,0:T(8,128)(2,1)} collective-permute-done((bf16[128,8192]{1,0:T(8,128)(2,1)S(1)}, bf16[128,8192]{1,0:T(8,128)(2,1)}, u32[]{:S(2)}, u32[]{:S(2)}) %collective-permute-start.4) | collective-permute-done | bytes 2097184 | tf_op jit(solution)/shard_map/ppermute | solution.py:20
  112.0 6.7 %fusion.35.self_ref = f32[128,8192]{1,0:T(8,128)} fusion(bf16[512,8192]{1,0:T(8,128)(2,1)} %param.8, bf16[512,256]{1,0:T(8,128)(2,1)S(1)} %copy-done.9), kind=kOutput, calls=%fused_computation.59 | convolution fusion | flops 1073741824 | bytes 12713984 | tf_op jit(solution)/shard_map/dot_general | solution.py:171
  118.7 1.3 copy-done.14
  121.3 26.7 %mean_tiles.3 = bf16[4,128,2048]{2,1,0:T(8,128)(2,1)} custom-call(s32[64,16]{1,0:T(8,128)} %fusion.42.src_ref, f32[64]{0:T(128)} %convert_divide_fusion.inv_ref, s32[64,16,128]{2,1,0:T(8,128)} %broadcast_select_fusion.nbr_ref, f32[128,8192]{1,0:T(8,128)} %fusion.35.self_ref, bf16[128,8192]{1,0:T(8,128)(2,1)} %copy-done.5, bf16[128,8192]{1,0:T(8,128)(2,1)} %copy-done.14, ...), custom_call_target="tpu_custom_call" | custom-call | flops 8589934592 | bytes 14680064 | tf_op jit(solution)/shard_map/mean_tiles/pallas_call | solution.py:69
  148.1 3.9 copy.17
  152.7 45.0 %reduce-scatter.5.cloned.1.call-done = bf16[1,128,2048]{1,2,0:T(8,128)(2,1)} async-done(((bf16[4,128,2048]{1,2,0:T(8,128)(2,1)}), bf16[1,128,2048]{1,2,0:T(8,128)(2,1)}) %reduce-scatter.5.cloned.1.call-update) | async-done | bytes 524304 | tf_op jit(solution)/shard_map/reduce_scatter | solution.py:179
  197.7 3.2 fusion.33
  201.5 44.8 %all-gather.5.cloned.1.call-done.grad_ref = bf16[8192,128]{1,0:T(8,128)(2,1)} async-done(((bf16[2048,128]{1,0:T(8,128)(2,1)}), bf16[8192,128]{1,0:T(8,128)(2,1)}) %all-gather.5.cloned.1.call-update) | async-done | bytes 2097168 | tf_op jit(solution)/shard_map/all_gather | solution.py:185
  246.3 29.3 %spread_tiles.3 = bf16[4,8192,128]{2,1,0:T(8,128)(2,1)} custom-call(s32[64,16]{1,0:T(8,128)} %fusion.42.src_ref, f32[64]{0:T(128)} %convert_divide_fusion.inv_ref, s32[64,16,128]{2,1,0:T(8,128)} %broadcast_select_fusion.nbr_ref, bf16[8192,128]{1,0:T(8,128)(2,1)} %all-gather.5.cloned.1.call-done.grad_ref), custom_call_target="tpu_custom_call" | custom-call | flops 8589934592 | bytes 10485760 | tf_op jit(solution)/shard_map/spread_tiles/pallas_call | solution.py:123
  275.6 4.5 slice_bitcast_fusion.2
  280.2 12.8 %all-gather.3.cloned.1.call-done.grad_ref = bf16[8192,128]{1,0:T(8,128)(2,1)} async-done(((bf16[2048,128]{1,0:T(8,128)(2,1)}), bf16[8192,128]{1,0:T(8,128)(2,1)}) %all-gather.3.cloned.1.call-update) | async-done | bytes 2097168 | tf_op jit(solution)/shard_map/all_gather | solution.py:185
  293.0 29.5 %spread_tiles.2 = bf16[4,8192,128]{2,1,0:T(8,128)(2,1)} custom-call(s32[64,16]{1,0:T(8,128)} %fusion.42.src_ref, f32[64]{0:T(128)} %convert_divide_fusion.inv_ref, s32[64,16,128]{2,1,0:T(8,128)} %broadcast_select_fusion.nbr_ref, bf16[8192,128]{1,0:T(8,128)(2,1)} %all-gather.3.cloned.1.call-done.grad_ref), custom_call_target="tpu_custom_call" | custom-call | flops 8589934592 | bytes 10485760 | tf_op jit(solution)/shard_map/spread_tiles/pallas_call | solution.py:123
  322.5 4.0 slice_bitcast_fusion.7
  328.2 2.9 fusion
  331.1 1.5 collective-permute-start.11
  332.6 1.9 fusion.2
  335.1 3.6 convolution_bitcast_fusion
  338.8 3.6 convolution_bitcast_fusion.1
  342.4 37.3 %collective-permute-done.11 = bf16[8192,128]{1,0:T(8,128)(2,1)} collective-permute-done((bf16[8192,128]{1,0:T(8,128)(2,1)S(1)}, bf16[8192,128]{1,0:T(8,128)(2,1)}, u32[]{:S(2)}, u32[]{:S(2)}) %collective-permute-start.11) | collective-permute-done | bytes 2097184 | tf_op jit(solution)/shard_map/ppermute | solution.py:20
  379.7 6.6 %fusion.8 = f32[512,128]{0,1:T(8,128)} fusion(bf16[512,8192]{1,0:T(8,128)(2,1)S(1)} %bitcast.120, bf16[8192,128]{1,0:T(8,128)(2,1)} %collective-permute-done.11, bf16[8192,128]{1,0:T(8,128)(2,1)} %collective-permute-done.9, bf16[4,8192,128]{2,1,0:T(8,128)(2,1)} %spread_tiles.3), kind=kOutput, calls=%fused_computation.24 | convolution fusion | flops 1082130432 | bytes 14942208 | tf_op jit(solution)/shard_map/dot_general | solution.py:200
  386.3 37.9 %collective-permute-done.8 = bf16[8192,128]{1,0:T(8,128)(2,1)} collective-permute-done((bf16[8192,128]{1,0:T(8,128)(2,1)}, bf16[8192,128]{1,0:T(8,128)(2,1)}, u32[]{:S(2)}, u32[]{:S(2)}) %collective-permute-start.8) | collective-permute-done | bytes 2097184 | tf_op jit(solution)/shard_map/ppermute | solution.py:20
  424.2 5.9 %fusion.9 = f32[512,128]{0,1:T(8,128)} fusion(bf16[512,8192]{1,0:T(8,128)(2,1)S(1)} %bitcast.120, bf16[8192,128]{1,0:T(8,128)(2,1)} %collective-permute-done.8, bf16[8192,128]{1,0:T(8,128)(2,1)} %collective-permute-done.6, bf16[4,8192,128]{2,1,0:T(8,128)(2,1)S(1)} %copy-done.1), kind=kOutput, calls=%fused_computation.25 | convolution fusion | flops 1082130432 | bytes 14942208 | tf_op jit(solution)/shard_map/dot_general | solution.py:200
  432.8 6.8 %all-reduce = (f32[128]{0:T(128)S(1)}, f32[128]{0:T(128)S(1)}) all-reduce(f32[128]{0:T(128)S(1)} %convert_reduce_fusion, f32[128]{0:T(128)S(1)} %convert_reduce_fusion.1), channel_id=1, replica_groups=mesh['grp'=2,'feat'=4,'node'=4] {'node'}, use_global_device_ids=true, to_apply=%region_9.10 | all-reduce | flops 256 | bytes 2048 | tf_op jit(solution)/shard_map/psum | solution.py:203
  440.2 25.2 %all-reduce.4.cloned.1.call-done = (f32[512,128]{0,1:T(8,128)}, f32[512,128]{0,1:T(8,128)}, f32[512,128]{0,1:T(8,128)}, f32[512,128]{0,1:T(8,128)}) async-done(((f32[512,128]{0,1:T(8,128)}, f32[512,128]{0,1:T(8,128)}, f32[512,128]{0,1:T(8,128)}, f32[512,128]{0,1:T(8,128)}), (f32[512,128]{0,1:T(8,128)}, f32[512,128]{0,1:T(8,128)}, f32[512,128]{0,1:T(8,128)}, ...) | async-done | bytes 1048592 | tf_op jit(solution)/shard_map/psum | solution.py:203
  (77 shorter events, 14.1 us)
Async XLA Ops:
  7.2 55.3 %copy-start.10 = (bf16[512,256]{1,0:T(8,128)(2,1)S(1)}, bf16[512,256]{1,0:T(8,128)(2,1)}, u32[]{:S(2)}) copy-start(bf16[512,256]{1,0:T(8,128)(2,1)} %param.12) | copy-start | bytes 786436
  7.2 145.5 %reduce-scatter.3.cloned.1.call-start = ((), (), s32[]{:S(2)}) async-start(), calls=%async_computation.2 | async-start | bytes 2621440 | tf_op jit(solution)/shard_map/reduce_scatter | solution.py:179
  7.2 55.3 %copy-start = (bf16[512,8192]{1,0:T(8,128)(2,1)S(1)}, bf16[512,8192]{1,0:T(8,128)(2,1)}, u32[]{:S(2)}) copy-start(bf16[512,8192]{1,0:T(8,128)(2,1)} %param.8) | copy-start | bytes 25165828
  13.5 52.1 %copy-start.11 = (s32[64,16]{0,1:T(8,128)S(1)}, s32[64,16]{0,1:T(8,128)}, u32[]{:S(2)}) copy-start(s32[64,16]{0,1:T(8,128)} %param.9) | copy-start | bytes 12292
  13.5 52.2 %copy-start.13 = (s32[64]{0:T(128)S(1)}, s32[64]{0:T(128)}, u32[]{:S(2)}) copy-start(s32[64]{0:T(128)} %param.11) | copy-start | bytes 772
  13.5 53.4 %copy-start.8 = (s32[64,16,128]{2,1,0:T(8,128)S(1)}, s32[64,16,128]{2,1,0:T(8,128)}, u32[]{:S(2)}) copy-start(s32[64,16,128]{2,1,0:T(8,128)} %param.10) | copy-start | bytes 1572868
  13.5 54.4 %copy-start.9 = (bf16[512,256]{1,0:T(8,128)(2,1)S(1)}, bf16[512,256]{1,0:T(8,128)(2,1)}, u32[]{:S(2)}) copy-start(bf16[512,256]{1,0:T(8,128)(2,1)} %param.13) | copy-start | bytes 786436
  13.5 49.0 %collective-permute-start.1 = (bf16[128,8192]{1,0:T(8,128)(2,1)}, bf16[128,8192]{1,0:T(8,128)(2,1)}, u32[]{:S(2)}, u32[]{:S(2)}) collective-permute-start(bf16[128,8192]{1,0:T(8,128)(2,1)} %convolution_convert_fusion.1.rest_0_), channel_id=1, source_target_pairs={{0,2},{1,3},{2,0},{3,1},{4,6},{5,7},{6,4},{7,5},{8,10},{9,11},{10,... | collective-permute-start | bytes 6291464 | tf_op jit(solution)/shard_map/ppermute | solution.py:20
  16.5 58.1 %collective-permute-start = (bf16[128,8192]{1,0:T(8,128)(2,1)}, bf16[128,8192]{1,0:T(8,128)(2,1)}, u32[]{:S(2)}, u32[]{:S(2)}) collective-permute-start(bf16[128,8192]{1,0:T(8,128)(2,1)} %convolution_convert_fusion.1.rest_0_), channel_id=1, source_target_pairs={{0,1},{1,0},{2,3},{3,2},{4,5},{5,4},{6,7},{7,6},{8,9},{9,8},{10,11... | collective-permute-start | bytes 6291464 | tf_op jit(solution)/shard_map/ppermute | solution.py:20
  62.5 12.2 %collective-permute-start.2 = (bf16[128,8192]{1,0:T(8,128)(2,1)}, bf16[128,8192]{1,0:T(8,128)(2,1)}, u32[]{:S(2)}, u32[]{:S(2)}) collective-permute-start(bf16[128,8192]{1,0:T(8,128)(2,1)} %collective-permute-done.1.rest_2_), channel_id=1, source_target_pairs={{0,1},{1,0},{2,3},{3,2},{4,5},{5,4},{6,7},{7,6},{8,9},{9,8},{10,11... | collective-permute-start | bytes 6291464 | tf_op jit(solution)/shard_map/ppermute | solution.py:20
  63.8 41.5 %copy-start.5 = (bf16[128,8192]{1,0:T(8,128)(2,1)}, bf16[128,8192]{1,0:T(8,128)(2,1)S(1)}, u32[]{:S(2)}) copy-start(bf16[128,8192]{1,0:T(8,128)(2,1)S(1)} %convolution_convert_fusion.rest_0_) | copy-start | bytes 6291460
  63.8 48.2 %collective-permute-start.4 = (bf16[128,8192]{1,0:T(8,128)(2,1)S(1)}, bf16[128,8192]{1,0:T(8,128)(2,1)}, u32[]{:S(2)}, u32[]{:S(2)}) collective-permute-start(bf16[128,8192]{1,0:T(8,128)(2,1)S(1)} %convolution_convert_fusion.rest_0_), channel_id=1, source_target_pairs={{0,2},{1,3},{2,0},{3,1},{4,6},{5,7},{6,4},{7,5},{8,10},{9,11},{10,... | collective-permute-start | bytes 6291464 | tf_op jit(solution)/shard_map/ppermute | solution.py:20
  105.3 92.4 %reduce-scatter.5.cloned.1.call-start = ((), (), s32[]{:S(2)}) async-start(), calls=%async_computation.3 | async-start | bytes 2621440 | tf_op jit(solution)/shard_map/reduce_scatter | solution.py:179
  105.3 13.4 %collective-permute-start.3 = (bf16[128,8192]{1,0:T(8,128)(2,1)S(1)}, bf16[128,8192]{1,0:T(8,128)(2,1)S(1)}, u32[]{:S(2)}, u32[]{:S(2)}) collective-permute-start(bf16[128,8192]{1,0:T(8,128)(2,1)S(1)} %convolution_convert_fusion.rest_0_), channel_id=1, source_target_pairs={{0,1},{1,0},{2,3},{3,2},{4,5},{5,4},{6,7},{7,6},{8,9},{9,8},{10,11... | collective-permute-start | bytes 6291464 | tf_op jit(solution)/shard_map/ppermute | solution.py:20
  112.0 6.7 %collective-permute-start.5 = (bf16[128,8192]{1,0:T(8,128)(2,1)}, bf16[128,8192]{1,0:T(8,128)(2,1)S(1)}, u32[]{:S(2)}, u32[]{:S(2)}) collective-permute-start(bf16[128,8192]{1,0:T(8,128)(2,1)} %collective-permute-done.4.rest_2_), channel_id=1, source_target_pairs={{0,1},{1,0},{2,3},{3,2},{4,5},{5,4},{6,7},{7,6},{8,9},{9,8},{10,11... | collective-permute-start | bytes 6291464 | tf_op jit(solution)/shard_map/ppermute | solution.py:20
  152.0 45.7 %copy-start.7 = (bf16[1,2048,256]{2,1,0:T(8,128)(2,1)S(1)}, bf16[1,2048,256]{2,1,0:T(8,128)(2,1)}, u32[]{:S(2)}) copy-start(bf16[1,2048,256]{2,1,0:T(8,128)(2,1)} %param.15) | copy-start | bytes 3145732
  152.0 94.3 %all-gather.5.cloned.1.call-start = ((), (), s32[]{:S(2)}) async-start(), calls=%async_computation.5 | async-start | bytes 2621440 | tf_op jit(solution)/shard_map/all_gather | solution.py:185
  200.9 92.1 %all-gather.3.cloned.1.call-start = ((), (), s32[]{:S(2)}) async-start(), calls=%async_computation.4 | async-start | bytes 2621440 | tf_op jit(solution)/shard_map/all_gather | solution.py:185
  201.5 263.9 %all-reduce.4.cloned.1.call-start = ((), (), s32[]{:S(2)}) async-start(), calls=%async_computation.6 | async-start | bytes 2097152 | tf_op jit(solution)/shard_map/psum | solution.py:203
  280.1 48.1 %collective-permute-start.10 = (bf16[8192,128]{1,0:T(8,128)(2,1)}, bf16[8192,128]{1,0:T(8,128)(2,1)S(1)}, u32[]{:S(2)}, u32[]{:S(2)}) collective-permute-start(bf16[8192,128]{1,0:T(8,128)(2,1)} %get-tuple-element.17), channel_id=1, source_target_pairs={{0,1},{1,0},{2,3},{3,2},{4,5},{5,4},{6,7},{7,6},{8,9},{9,8},{10,11... | collective-permute-start | bytes 6291464 | tf_op jit(solution)/shard_map/ppermute | solution.py:20
  322.5 5.1 %copy-start.6 = (bf16[8192,128]{1,0:T(8,128)(2,1)S(1)}, bf16[8192,128]{1,0:T(8,128)(2,1)}, u32[]{:S(2)}) copy-start(bf16[8192,128]{1,0:T(8,128)(2,1)} %get-tuple-element.16) | copy-start | bytes 6291460
  322.5 12.6 %slice-start = ((s8[8388608]{0:T(1024)(128)(4,1)}), s8[4194304]{0:T(1024)(128)(4,1)S(1)}, s32[]{:S(2)}) async-start(s8[8388608]{0:T(1024)(128)(4,1)} %bitcast.119), calls=%async_computation.7 | async-start | bytes 8388608
  326.5 6.1 %collective-permute-start.7 = (bf16[8192,128]{1,0:T(8,128)(2,1)S(1)}, bf16[8192,128]{1,0:T(8,128)(2,1)S(1)}, u32[]{:S(2)}, u32[]{:S(2)}) collective-permute-start(bf16[8192,128]{1,0:T(8,128)(2,1)S(1)} %get-tuple-element.15), channel_id=1, source_target_pairs={{0,1},{1,0},{2,3},{3,2},{4,5},{5,4},{6,7},{7,6},{8,9},{9,8},{10,11... | collective-permute-start | bytes 6291464 | tf_op jit(solution)/shard_map/ppermute | solution.py:20
  326.5 6.1 %copy-start.1 = (bf16[4,8192,128]{2,1,0:T(8,128)(2,1)S(1)}, bf16[4,8192,128]{2,1,0:T(8,128)(2,1)}, u32[]{:S(2)}) copy-start(bf16[4,8192,128]{2,1,0:T(8,128)(2,1)} %spread_tiles.2) | copy-start | bytes 25165828
  327.6 14.8 %collective-permute-start.9 = (bf16[8192,128]{1,0:T(8,128)(2,1)S(1)}, bf16[8192,128]{1,0:T(8,128)(2,1)}, u32[]{:S(2)}, u32[]{:S(2)}) collective-permute-start(bf16[8192,128]{1,0:T(8,128)(2,1)S(1)} %copy-done.6), channel_id=1, source_target_pairs={{0,1},{1,0},{2,3},{3,2},{4,5},{5,4},{6,7},{7,6},{8,9},{9,8},{10,11... | collective-permute-start | bytes 6291464 | tf_op jit(solution)/shard_map/ppermute | solution.py:20
  328.1 7.0 %slice-start.1 = ((s8[8388608]{0:T(1024)(128)(4,1)}), s8[4194304]{0:T(1024)(128)(4,1)S(1)}, s32[]{:S(2)}) async-start(s8[8388608]{0:T(1024)(128)(4,1)} %bitcast.119), calls=%async_computation.8 | async-start | bytes 8388608
  328.1 58.2 %collective-permute-start.6 = (bf16[8192,128]{1,0:T(8,128)(2,1)}, bf16[8192,128]{1,0:T(8,128)(2,1)}, u32[]{:S(2)}, u32[]{:S(2)}) collective-permute-start(bf16[8192,128]{1,0:T(8,128)(2,1)} %get-tuple-element.14), channel_id=1, source_target_pairs={{0,1},{1,0},{2,3},{3,2},{4,5},{5,4},{6,7},{7,6},{8,9},{9,8},{10,11... | collective-permute-start | bytes 6291464 | tf_op jit(solution)/shard_map/ppermute | solution.py:20
  331.1 4.0 copy-start.2
  331.1 48.6 %collective-permute-start.11 = (bf16[8192,128]{1,0:T(8,128)(2,1)S(1)}, bf16[8192,128]{1,0:T(8,128)(2,1)}, u32[]{:S(2)}, u32[]{:S(2)}) collective-permute-start(bf16[8192,128]{1,0:T(8,128)(2,1)S(1)} %fusion), channel_id=1, source_target_pairs={{0,2},{1,3},{2,0},{3,1},{4,6},{5,7},{6,4},{7,5},{8,10},{9,11},{10,... | collective-permute-start | bytes 6291464 | tf_op jit(solution)/shard_map/ppermute | solution.py:20
  334.5 4.3 copy-start.3
  334.5 89.7 %collective-permute-start.8 = (bf16[8192,128]{1,0:T(8,128)(2,1)}, bf16[8192,128]{1,0:T(8,128)(2,1)}, u32[]{:S(2)}, u32[]{:S(2)}) collective-permute-start(bf16[8192,128]{1,0:T(8,128)(2,1)} %fusion.2), channel_id=1, source_target_pairs={{0,2},{1,3},{2,0},{3,1},{4,6},{5,7},{6,4},{7,5},{8,10},{9,11},{10,... | collective-permute-start | bytes 6291464 | tf_op jit(solution)/shard_map/ppermute | solution.py:20
  430.1 1.6 copy-start.4
  (3 other events, 3.3 us)
Sparse Core Ops, SparseCore 0:
  105.4 44.2 reduce-scatter.2
  152.1 45.4 reduce-scatter.4
  201.0 45.2 all-gather.4
  248.3 44.6 all-gather.2
  430.3 35.1 all-reduce.3

commit v2 on v1

v2 whole, which is shorter than its diff:
```python
import functools

import jax
import jax.numpy as jnp
from jax import lax
from jax.experimental import pallas as pl
from jax.experimental.pallas import tpu as pltpu
from jax.sharding import PartitionSpec as P

CHUNKS = 2
VMEM_BYTES = 56 * 1024 * 1024
HBM = pl.BlockSpec(memory_space=pl.ANY)
VMEM = pl.BlockSpec(memory_space=pltpu.VMEM)
SMEM = pl.BlockSpec(memory_space=pltpu.SMEM)
PARAMS = pltpu.CompilerParams(vmem_limit_bytes=VMEM_BYTES)


def cost(flops, moved):
    return pl.CostEstimate(flops=flops, bytes_accessed=moved, transcendentals=0)


def swap(value, mask, n):
    return lax.ppermute(value, "node", [(i, i ^ mask) for i in range(n)])


def masks_of(n):
    assert n & (n - 1) == 0
    return [1 << i for i in range(n.bit_length() - 1)]


def sum_over_node(value, n):
    for mask in masks_of(n):
        value = value + swap(value, mask, n)
    return value


def onehot_tile(row, ids):
    side = ids.shape[0]
    some = jnp.broadcast_to(row.astype(jnp.float32), (16, side)).astype(jnp.bfloat16)
    rows = jnp.concatenate([some] * (side // 16), axis=0)
    return jnp.where(ids == rows, jnp.bfloat16(1.0), jnp.bfloat16(0.0))


def side_ids(side):
    return lax.broadcasted_iota(jnp.int32, (side, side), 0).astype(jnp.float32).astype(jnp.bfloat16)


def project(feat_t, weights_t, n):
    width, rows = feat_t.shape
    wide = weights_t.shape[0] // (2 * n)
    step = min(1024, rows)

    def kernel(feat_ref, w_ref, *outs):
        for c in range(2 * n):
            outs[c][...] = jnp.dot(
                w_ref[c * wide : (c + 1) * wide, :],
                feat_ref[...],
                preferred_element_type=jnp.float32,
            ).astype(outs[c].dtype)

    return pl.pallas_call(
        kernel,
        grid=(rows // step,),
        in_specs=[
            pl.BlockSpec((width, step), lambda i: (0, i)),
            pl.BlockSpec(weights_t.shape, lambda i: (0, 0)),
        ],
        out_specs=[pl.BlockSpec((wide, step), lambda i: (0, i))] * (2 * n),
        out_shape=[jax.ShapeDtypeStruct((wide, rows), jnp.bfloat16)] * n
        + [jax.ShapeDtypeStruct((wide, rows), jnp.float32)] * n,
        compiler_params=PARAMS,
        cost_estimate=cost(
            2 * width * rows * weights_t.shape[0], 2 * width * rows + 6 * n * wide * rows
        ),
        name="project",
    )(feat_t, weights_t)


def mean_tiles(src, inv, nbr, parts, self_term):
    n = len(parts)
    wide, rows = self_term.shape
    blocks, slots, side = nbr.shape

    def kernel(src_ref, inv_ref, nbr_ref, self_ref, *rest):
        part_refs = rest[:n]
        out_ref, table, sems = rest[n:]
        copies = [
            pltpu.make_async_copy(ref, table.at[:, pl.ds(k * rows, rows)], sems.at[k])
            for k, ref in enumerate(part_refs)
        ]
        for copy in copies:
            copy.start()
        for copy in copies:
            copy.wait()
        ids = side_ids(side)

        @pl.loop(0, blocks)
        def _(b):
            picked = []
            tiles = []
            for t in range(slots):
                at = pl.multiple_of(src_ref[b, t] * side, side)
                picked.append(table[:, pl.ds(at, side)])
                tiles.append(onehot_tile(nbr_ref[b, t : t + 1, :], ids))
            total = jnp.dot(
                jnp.concatenate(picked, axis=1),
                jnp.concatenate(tiles, axis=0),
                preferred_element_type=jnp.float32,
            )
            at = pl.ds(pl.multiple_of(b * side, side), side)
            pre_t = total * inv_ref[b] + self_ref[:, at]
            out_ref[at, :] = pre_t.T.astype(jnp.bfloat16)

    return pl.pallas_call(
        kernel,
        out_shape=jax.ShapeDtypeStruct((rows, wide), jnp.bfloat16),
        in_specs=[SMEM, SMEM, VMEM, VMEM] + [HBM] * n,
        out_specs=VMEM,
        scratch_shapes=[
            pltpu.VMEM((wide, n * rows), jnp.bfloat16),
            pltpu.SemaphoreType.DMA((n,)),
        ],
        compiler_params=PARAMS,
        cost_estimate=cost(
            8 * blocks * slots * side * side * wide, 2 * n * rows * wide + 6 * rows * wide
        ),
        name="mean_tiles",
    )(src, inv, nbr, self_term, *parts)


def activate(pre, bias, cot, hidden, c):
    share, wide = pre.shape
    hid = cot.shape[1]
    chunk = pl.BlockSpec((share, wide), lambda i: (0, c))
    whole = pl.BlockSpec((share, wide), lambda i: (0, 0))
    held = [] if hidden is None else [hidden]

    def kernel(pre_ref, bias_ref, cot_ref, *rest):
        hidden_ref, grad_ref = rest[-2:]
        value = pre_ref[...].astype(jnp.float32) + bias_ref[...]
        sigma = jax.nn.sigmoid(value)
        hidden_ref[...] = (value * sigma).astype(jnp.bfloat16)
        slope = sigma * (1.0 + value * (1.0 - sigma))
        grad_ref[...] = (cot_ref[...].astype(jnp.float32) * slope).astype(jnp.bfloat16)

    return pl.pallas_call(
        kernel,
        grid=(1,),
        in_specs=[whole, pl.BlockSpec((1, wide), lambda i: (0, c)), chunk] + [HBM] * len(held),
        out_specs=[chunk, whole],
        out_shape=[
            jax.ShapeDtypeStruct((share, hid), jnp.bfloat16),
            jax.ShapeDtypeStruct((share, wide), jnp.bfloat16),
        ],
        input_output_aliases={3: 0} if held else {},
        compiler_params=PARAMS,
        cost_estimate=cost(20 * share * wide, 8 * share * wide),
        name="activate",
    )(pre, bias, cot, *held)


def spread_tiles(src, inv, nbr, grad, n):
    rows, wide = grad.shape
    blocks, slots, side = nbr.shape
    step = 512

    def kernel(src_ref, inv_ref, nbr_ref, grad_ref, *rest):
        outs, table = rest[:n], rest[n]
        ids = side_ids(side)

        @pl.loop(0, n * rows // step)
        def _(i):
            table[pl.ds(pl.multiple_of(i * step, step), step), :] = jnp.zeros(
                (step, wide), jnp.float32
            )

        @pl.loop(0, blocks)
        def _(b):
            g = grad_ref[pl.ds(pl.multiple_of(b * side, side), side), :]
            scale = inv_ref[b]
            tiles = [onehot_tile(nbr_ref[b, t : t + 1, :], ids) for t in range(slots)]
            terms = jnp.dot(
                jnp.concatenate(tiles, axis=0), g, preferred_element_type=jnp.float32
            )
            for t in range(slots):
                at = pl.ds(pl.multiple_of(src_ref[b, t] * side, side), side)
                table[at, :] += terms[t * side : (t + 1) * side, :] * scale

        for k in range(n):

            @pl.loop(0, rows // step)
            def _(i, k=k):
                at = pl.multiple_of(i * step, step)
                outs[k][pl.ds(at, step), :] = table[pl.ds(k * rows + at, step), :].astype(
                    jnp.bfloat16
                )

    return pl.pallas_call(
        kernel,
        out_shape=[jax.ShapeDtypeStruct((rows, wide), jnp.bfloat16)] * n,
        in_specs=[SMEM, SMEM, VMEM, VMEM],
        out_specs=[VMEM] * n,
        scratch_shapes=[pltpu.VMEM((n * rows, wide), jnp.float32)],
        compiler_params=PARAMS,
        cost_estimate=cost(
            8 * blocks * slots * side * side * wide, 2 * n * rows * wide + 2 * rows * wide
        ),
        name="spread_tiles",
    )(src, inv, nbr, grad)


def weight_grad(feat_t, grad, with_sum):
    width, rows = feat_t.shape
    wide = grad.shape[1]
    step = min(1024, rows)
    extra = 8 if with_sum else 0

    def kernel(feat_ref, grad_ref, out_ref):
        @pl.when(pl.program_id(0) == 0)
        def _():
            out_ref[...] = jnp.zeros_like(out_ref)

        out_ref[:width, :] += jnp.dot(
            feat_ref[...], grad_ref[...], preferred_element_type=jnp.float32
        )
        if with_sum:
            out_ref[width : width + 1, :] += jnp.sum(
                grad_ref[...].astype(jnp.float32), axis=0, keepdims=True
            )

    return pl.pallas_call(
        kernel,
        grid=(rows // step,),
        in_specs=[
            pl.BlockSpec((width, step), lambda i: (0, i)),
            pl.BlockSpec((step, wide), lambda i: (i, 0)),
        ],
        out_specs=pl.BlockSpec((width + extra, wide), lambda i: (0, 0)),
        out_shape=jax.ShapeDtypeStruct((width + extra, wide), jnp.float32),
        compiler_params=PARAMS,
        cost_estimate=cost(2 * width * rows * wide, 2 * rows * (width + wide)),
        name="weight_grad",
    )(feat_t, grad)


def on_device(n_node, n_feat, feat_t, src_blocks, nbr_rows, tile_counts, w_neigh, w_self, bias, cotangent):
    width, rows = feat_t.shape
    hid = w_neigh.shape[1]
    blocks, slots = src_blocks.shape
    share = cotangent.shape[1]
    me = lax.axis_index("node")
    src = jnp.bitwise_xor(src_blocks // blocks, me) * blocks + src_blocks % blocks
    valid = jnp.arange(slots, dtype=jnp.int32)[None, :] < tile_counts[:, None]
    nbr = jnp.where(valid[:, :, None], nbr_rows, -1)
    inv = 1.0 / tile_counts.astype(jnp.float32)
    cot_rows = cotangent.reshape(share, hid)
    bias_row = bias[None, :]

    weights_t = jnp.concatenate([w_neigh.T, w_self.T], axis=0)
    projected = project(feat_t, weights_t, CHUNKS)

    gathered = []
    for c in range(CHUNKS):
        held = {0: projected[c]}
        for mask in reversed(masks_of(n_node)):
            for k in list(held):
                held[k ^ mask] = swap(held[k], mask, n_node)
        gathered.append([held[k] for k in range(n_node)])

    hidden = None
    pieces = []
    for c in range(CHUNKS):
        part_pre = mean_tiles(src, inv, nbr, gathered[c], projected[CHUNKS + c])
        pre = lax.psum_scatter(part_pre, "feat", scatter_dimension=0, tiled=True)
        hidden, grad_pre = activate(pre, bias_row, cot_rows, hidden, c)
        pieces.append(lax.all_gather(grad_pre, "feat", axis=0, tiled=True))

    grads_n, grads_s, sums = [], [], []
    for c in range(CHUNKS):
        held = dict(enumerate(spread_tiles(src, inv, nbr, pieces[c], n_node)))
        for mask in masks_of(n_node):
            left = {}
            for k in held:
                if k & mask:
                    got = swap(held[k], mask, n_node)
                    left[k ^ mask] = (
                        held[k ^ mask].astype(jnp.float32) + got.astype(jnp.float32)
                    ).astype(jnp.bfloat16)
            held = left
        grads_n.append(sum_over_node(weight_grad(feat_t, held[0], False), n_node))
        both = sum_over_node(weight_grad(feat_t, pieces[c], True), n_node)
        grads_s.append(both[:width])
        sums.append(both[width])
    return (
        hidden.reshape(1, share, hid),
        jnp.concatenate(grads_n, axis=1),
        jnp.concatenate(grads_s, axis=1),
        jnp.concatenate(sums, axis=0),
    )


def solution(mesh):
    return jax.shard_map(
        functools.partial(on_device, mesh.shape["node"], mesh.shape["feat"]),
        mesh=mesh,
        in_specs=(
            P("feat", ("grp", "node")),
            P(("grp", "node"), None),
            P(("grp", "node"), None, None),
            P(("grp", "node")),
            P("feat", None),
            P("feat", None),
            P(),
            P(("grp", "node"), "feat", None),
        ),
        out_specs=(
            P(("grp", "node"), "feat", None),
            P(("grp", "feat"), None),
            P(("grp", "feat"), None),
            P("grp"),
        ),
        check_vma=False,
    )
```

time: 476 us -> 475 us (level)
  Pallas kernels: 112 us -> 173 us
  matrix products: 40.8 us -> 0 us
  local copies, waits for them, and re-layouts: 22.2 us -> 5.16 us
  blocking collectives: 6.81 us -> 0 us
  starting transfers between devices: 7.98 us -> 13.5 us
    pallas_call x4 -> x11, Pallas kernels: 112 us -> 173 us  [the longest x2 63.2 us: mean_tiles(): pl.pallas_call(kernel, out_shape=jax.ShapeDtypeStruct((rows, wide), jnp.b...]
    dot_general x8 -> x0, matrix products: 40.8 us -> none  [the longest x2 13.4 us: on_device(): lax.dot_general(w_self[:, cols], feat_t, first, preferred_element_type=jn...]
    ppermute x12 -> x20, waiting for transfers between devices: 128 us -> 160 us  [swap(): return lax.ppermute(value, 'node', [(i, i ^ mask) for i in range(n)])]
    psum x1 -> x0, waiting for transfers between devices: 25.2 us -> none  [on_device(): g_n, g_s, g_b = lax.psum((part_neigh, part_self, part_bias), 'node')]
    squeeze x2, local copies, waits for them, and re-layouts: 8.53 us -> 0.01 us  [on_device(): sums.append(both[width])]
    pallas_call x2 -> x0, local copies, waits for them, and re-layouts: 7.85 us -> none  [mean_tiles(): pl.pallas_call(kernel, out_shape=jax.ShapeDtypeStruct((n_feat, hid, share...]
    psum x1 -> x0, blocking collectives: 6.81 us -> none  [on_device(): g_n, g_s, g_b = lax.psum((part_neigh, part_self, part_bias), 'node')]
    ppermute x12 -> x20, starting transfers between devices: 7.77 us -> 13.3 us  [swap(): return lax.ppermute(value, 'node', [(i, i ^ mask) for i in range(n)])]
  transfers between devices with their start and end apart: 17 -> 24, of which waited for: 8 -> 12; matrix products, arithmetic and copies ran while one was open for 12% -> 2% of each run, Pallas kernels for 24% -> 33%
where the time goes in v2:
time: 475 us; the launch traced here: 474 us
  waiting for transfers between devices  256 us (54%)
  Pallas kernels  173 us (36%)
  between operations  14 us (3%)
  starting transfers between devices  13.5 us (3%)
  other arithmetic  12.6 us (3%)
  local copies, waits for them, and re-layouts  5.16 us (1%)
    ppermute x20, waiting for transfers between devices, swap(): return lax.ppermute(value, 'node', [(i, i ^ mask) for i in range(n)])  160 us
    pallas_call x2, Pallas kernels, mean_tiles(): pl.pallas_call(kernel, out_shape=jax.ShapeDtypeStruct((rows, wide), jnp.b...  63.2 us
    pallas_call x2, Pallas kernels, spread_tiles(): pl.pallas_call(kernel, out_shape=[jax.ShapeDtypeStruct((rows, wide), jnp....  59.1 us
    all_gather x2, waiting for transfers between devices, on_device(): pieces.append(lax.all_gather(grad_pre, 'feat', axis=0, tiled=True))  53 us
    reduce_scatter x2, waiting for transfers between devices, on_device(): pre = lax.psum_scatter(part_pre, 'feat', scatter_dimension=0, tiled=True)  42.9 us
    pallas_call x4, Pallas kernels, weight_grad(): pl.pallas_call(kernel, grid=(rows // step,), in_specs=[pl.BlockSpec((widt...  33.7 us
    ppermute x20, starting transfers between devices, swap(): return lax.ppermute(value, 'node', [(i, i ^ mask) for i in range(n)])  13.3 us
    pallas_call x1, Pallas kernels, project(): pl.pallas_call(kernel, grid=(rows // step,), in_specs=[pl.BlockSpec((widt...  11.7 us
  transfers between devices with their start and end apart: 24, of which 12 were waited for; matrix products, arithmetic and copies ran while one was open for 2% of the time, Pallas kernels for 33%

profile of v2, /device:TPU:0, one launch (start us, length us, event | category | flops | bytes accessed | tf_op | source)
XLA Modules:
  0.0 474.1 jit_solution(3144211740922260436)
XLA Ops:
  8.3 1.1 copy.18
  10.2 11.7 %project.1 = (bf16[128,8192]{1,0:T(8,128)(2,1)}, bf16[128,8192]{1,0:T(8,128)(2,1)}, f32[128,8192]{1,0:T(8,128)}, f32[128,8192]{1,0:T(8,128)}) custom-call(bf16[512,8192]{1,0:T(8,128)(2,1)} %feat_ref.9, bf16[512,512]{1,0:T(8,128)(2,1)} %pad_maximum_fusion.w_ref), custom_call_target="tpu_custom_call" | custom-call | flops 4294967296 | bytes 20971520 | tf_op jit(solution)/shard_map/project/pallas_call | solution.py:61
  21.9 2.9 collective-permute-start.4
  24.9 45.8 %collective-permute-done.4.rest_2_ = bf16[128,8192]{1,0:T(8,128)(2,1)S(1)} collective-permute-done((bf16[128,8192]{1,0:T(8,128)(2,1)}, bf16[128,8192]{1,0:T(8,128)(2,1)S(1)}, u32[]{:S(2)}, u32[]{:S(2)}) %collective-permute-start.4) | collective-permute-done | bytes 2097184 | tf_op jit(solution)/shard_map/ppermute | solution.py:23
  70.7 1.7 collective-permute-start.1
  75.0 31.6 %mean_tiles.3 = bf16[8192,128]{1,0:T(8,128)(2,1)} custom-call(s32[64,16]{1,0:T(8,128)} %fusion.2.src_ref, f32[64]{0:T(128)} %convert_divide_fusion.inv_ref, s32[64,16,128]{2,1,0:T(8,128)} %broadcast_select_fusion.nbr_ref, f32[128,8192]{1,0:T(8,128)} %get-tuple-element.22.self_ref, bf16[128,8192]{1,0:T(8,128)(2,1)} %get-tuple-element.23.rest_0_, ...), custom_call_target="tpu_custom_call" | custom-call | flops 17179869184 | bytes 14680064 | tf_op jit(solution)/shard_map/mean_tiles/pallas_call | solution.py:114
  106.7 1.5 copy-done.11
  108.3 10.7 %collective-permute-done.1.rest_2_ = bf16[128,8192]{1,0:T(8,128)(2,1)} collective-permute-done((bf16[128,8192]{1,0:T(8,128)(2,1)}, bf16[128,8192]{1,0:T(8,128)(2,1)}, u32[]{:S(2)}, u32[]{:S(2)}) %collective-permute-start.1) | collective-permute-done | bytes 2097184 | tf_op jit(solution)/shard_map/ppermute | solution.py:23
  119.1 4.4 collective-permute-done.2.rest_3_
  123.5 1.3 copy-done.14
  124.8 31.6 %mean_tiles.2 = bf16[8192,128]{1,0:T(8,128)(2,1)} custom-call(s32[64,16]{1,0:T(8,128)} %fusion.2.src_ref, f32[64]{0:T(128)} %convert_divide_fusion.inv_ref, s32[64,16,128]{2,1,0:T(8,128)} %broadcast_select_fusion.nbr_ref, f32[128,8192]{1,0:T(8,128)} %get-tuple-element.20.self_ref, bf16[128,8192]{1,0:T(8,128)(2,1)} %get-tuple-element.21.rest_0_, ...), custom_call_target="tpu_custom_call" | custom-call | flops 17179869184 | bytes 14680064 | tf_op jit(solution)/shard_map/mean_tiles/pallas_call | solution.py:114
  156.5 2.5 activate.2
  159.0 42.9 %reduce-scatter.3.cloned.1.call-done.pre_ref = bf16[2048,128]{1,0:T(8,128)(2,1)} async-done(((bf16[8192,128]{1,0:T(8,128)(2,1)}), bf16[2048,128]{1,0:T(8,128)(2,1)}) %reduce-scatter.3.cloned.1.call-update) | async-done | bytes 524304 | tf_op jit(solution)/shard_map/reduce_scatter | solution.py:274
  201.9 2.5 activate.3
  205.0 44.8 %all-gather.5.cloned.1.call-done.grad_ref = bf16[8192,128]{1,0:T(8,128)(2,1)} async-done(((bf16[2048,128]{1,0:T(8,128)(2,1)}), bf16[8192,128]{1,0:T(8,128)(2,1)}) %all-gather.5.cloned.1.call-update) | async-done | bytes 2097168 | tf_op jit(solution)/shard_map/all_gather | solution.py:276
  249.8 29.6 %spread_tiles.3 = (bf16[8192,128]{1,0:T(8,128)(2,1)}, bf16[8192,128]{1,0:T(8,128)(2,1)}, bf16[8192,128]{1,0:T(8,128)(2,1)}, bf16[8192,128]{1,0:T(8,128)(2,1)}) custom-call(s32[64,16]{1,0:T(8,128)} %fusion.2.src_ref, f32[64]{0:T(128)} %convert_divide_fusion.inv_ref, s32[64,16,128]{2,1,0:T(8,128)} %broadcast_select_fusion.nbr_ref, ...), custom_call_target="tpu_custom_call" | custom-call | flops 17179869184 | bytes 10485760 | tf_op jit(solution)/shard_map/spread_tiles/pallas_call | solution.py:198
  279.4 8.4 %weight_grad.7 = f32[520,128]{1,0:T(8,128)} custom-call(bf16[512,8192]{1,0:T(8,128)(2,1)} %feat_ref.9, bf16[8192,128]{1,0:T(8,128)(2,1)} %all-gather.5.cloned.1.call-done.grad_ref), custom_call_target="tpu_custom_call" | custom-call | flops 1073741824 | bytes 10485760 | tf_op jit(solution)/shard_map/weight_grad/pallas_call | solution.py:231
  288.3 8.2 %all-gather.3.cloned.1.call-done.grad_ref = bf16[8192,128]{1,0:T(8,128)(2,1)} async-done(((bf16[2048,128]{1,0:T(8,128)(2,1)}), bf16[8192,128]{1,0:T(8,128)(2,1)}) %all-gather.3.cloned.1.call-update) | async-done | bytes 2097168 | tf_op jit(solution)/shard_map/all_gather | solution.py:276
  296.5 29.5 %spread_tiles.2 = (bf16[8192,128]{1,0:T(8,128)(2,1)}, bf16[8192,128]{1,0:T(8,128)(2,1)}, bf16[8192,128]{1,0:T(8,128)(2,1)}, bf16[8192,128]{1,0:T(8,128)(2,1)}) custom-call(s32[64,16]{1,0:T(8,128)} %fusion.2.src_ref, f32[64]{0:T(128)} %convert_divide_fusion.inv_ref, s32[64,16,128]{2,1,0:T(8,128)} %broadcast_select_fusion.nbr_ref, ...), custom_call_target="tpu_custom_call" | custom-call | flops 17179869184 | bytes 10485760 | tf_op jit(solution)/shard_map/spread_tiles/pallas_call | solution.py:198
  326.0 8.5 %weight_grad.6 = f32[520,128]{1,0:T(8,128)} custom-call(bf16[512,8192]{1,0:T(8,128)(2,1)} %feat_ref.9, bf16[8192,128]{1,0:T(8,128)(2,1)} %all-gather.3.cloned.1.call-done.grad_ref), custom_call_target="tpu_custom_call" | custom-call | flops 1073741824 | bytes 10485760 | tf_op jit(solution)/shard_map/weight_grad/pallas_call | solution.py:231
  335.6 1.5 collective-permute-start.13
  337.9 1.5 collective-permute-start.17
  340.7 43.4 %collective-permute-done.13 = bf16[8192,128]{1,0:T(8,128)(2,1)S(1)} collective-permute-done((bf16[8192,128]{1,0:T(8,128)(2,1)S(1)}, bf16[8192,128]{1,0:T(8,128)(2,1)S(1)}, u32[]{:S(2)}, u32[]{:S(2)}) %collective-permute-start.13) | collective-permute-done | bytes 2097184 | tf_op jit(solution)/shard_map/ppermute | solution.py:23
  384.1 2.2 add_convert_fusion.grad_ref
  386.3 8.5 %weight_grad.5 = f32[512,128]{1,0:T(8,128)} custom-call(bf16[512,8192]{1,0:T(8,128)(2,1)} %feat_ref.9, bf16[8192,128]{1,0:T(8,128)(2,1)} %add_convert_fusion.grad_ref), custom_call_target="tpu_custom_call" | custom-call | flops 1073741824 | bytes 10485760 | tf_op jit(solution)/shard_map/weight_grad/pallas_call | solution.py:231
  394.8 45.2 %collective-permute-done.8 = bf16[8192,128]{1,0:T(8,128)(2,1)} collective-permute-done((bf16[8192,128]{1,0:T(8,128)(2,1)S(1)}, bf16[8192,128]{1,0:T(8,128)(2,1)}, u32[]{:S(2)}, u32[]{:S(2)}) %collective-permute-start.8) | collective-permute-done | bytes 2097184 | tf_op jit(solution)/shard_map/ppermute | solution.py:23
  440.0 3.8 add_convert_fusion.3.grad_ref
  443.8 8.4 %weight_grad.4 = f32[512,128]{1,0:T(8,128)} custom-call(bf16[512,8192]{1,0:T(8,128)(2,1)} %feat_ref.9, bf16[8192,128]{1,0:T(8,128)(2,1)} %add_convert_fusion.3.grad_ref), custom_call_target="tpu_custom_call" | custom-call | flops 1073741824 | bytes 10485760 | tf_op jit(solution)/shard_map/weight_grad/pallas_call | solution.py:231
  452.3 1.5 collective-permute-start.15
  453.9 1.5 collective-permute-start.10
  456.9 4.6 collective-permute-done.15
  461.5 5.2 %collective-permute-done.10 = f32[512,128]{1,0:T(8,128)S(1)} collective-permute-done((f32[512,128]{1,0:T(8,128)S(1)}, f32[512,128]{1,0:T(8,128)S(1)}, u32[]{:S(2)}, u32[]{:S(2)}) %collective-permute-start.10) | collective-permute-done | bytes 262176 | tf_op jit(solution)/shard_map/ppermute | solution.py:23
  (88 shorter events, 11.6 us)
Async XLA Ops:
  7.2 149.3 %reduce-scatter.5.cloned.1.call-start = ((), (), s32[]{:S(2)}) async-start(), calls=%async_computation.3 | async-start | bytes 2621440 | tf_op jit(solution)/shard_map/reduce_scatter | solution.py:274
  10.2 62.2 %copy-start.9 = (s32[64,16]{0,1:T(8,128)S(1)}, s32[64,16]{0,1:T(8,128)}, u32[]{:S(2)}) copy-start(s32[64,16]{0,1:T(8,128)} %param.9) | copy-start | bytes 12292
  10.2 62.3 %copy-start.10 = (s32[64]{0:T(128)S(1)}, s32[64]{0:T(128)}, u32[]{:S(2)}) copy-start(s32[64]{0:T(128)} %param.11) | copy-start | bytes 772
  10.2 63.6 %copy-start.8 = (s32[64,16,128]{2,1,0:T(8,128)S(1)}, s32[64,16,128]{2,1,0:T(8,128)}, u32[]{:S(2)}) copy-start(s32[64,16,128]{2,1,0:T(8,128)} %param.10) | copy-start | bytes 1572868
  21.9 48.8 %collective-permute-start.4 = (bf16[128,8192]{1,0:T(8,128)(2,1)}, bf16[128,8192]{1,0:T(8,128)(2,1)S(1)}, u32[]{:S(2)}, u32[]{:S(2)}) collective-permute-start(bf16[128,8192]{1,0:T(8,128)(2,1)} %get-tuple-element.23.rest_0_), channel_id=1, source_target_pairs={{0,2},{1,3},{2,0},{3,1},{4,6},{5,7},{6,4},{7,5},{8,10},{9,11},{10,... | collective-permute-start | bytes 6291464 | tf_op jit(solution)/shard_map/ppermute | solution.py:23
  24.9 49.9 %collective-permute-start.3 = (bf16[128,8192]{1,0:T(8,128)(2,1)}, bf16[128,8192]{1,0:T(8,128)(2,1)}, u32[]{:S(2)}, u32[]{:S(2)}) collective-permute-start(bf16[128,8192]{1,0:T(8,128)(2,1)} %get-tuple-element.23.rest_0_), channel_id=1, source_target_pairs={{0,1},{1,0},{2,3},{3,2},{4,5},{5,4},{6,7},{7,6},{8,9},{9,8},{10,11... | collective-permute-start | bytes 6291464 | tf_op jit(solution)/shard_map/ppermute | solution.py:23
  70.7 4.3 collective-permute-start.5
  70.7 48.4 %collective-permute-start.1 = (bf16[128,8192]{1,0:T(8,128)(2,1)}, bf16[128,8192]{1,0:T(8,128)(2,1)}, u32[]{:S(2)}, u32[]{:S(2)}) collective-permute-start(bf16[128,8192]{1,0:T(8,128)(2,1)} %get-tuple-element.21.rest_0_), channel_id=1, source_target_pairs={{0,2},{1,3},{2,0},{3,1},{4,6},{5,7},{6,4},{7,5},{8,10},{9,11},{10,... | collective-permute-start | bytes 6291464 | tf_op jit(solution)/shard_map/ppermute | solution.py:23
  106.7 95.2 %reduce-scatter.3.cloned.1.call-start = ((), (), s32[]{:S(2)}) async-start(), calls=%async_computation.2 | async-start | bytes 2621440 | tf_op jit(solution)/shard_map/reduce_scatter | solution.py:274
  108.2 10.9 %collective-permute-start = (bf16[128,8192]{1,0:T(8,128)(2,1)S(1)}, bf16[128,8192]{1,0:T(8,128)(2,1)S(1)}, u32[]{:S(2)}, u32[]{:S(2)}) collective-permute-start(bf16[128,8192]{1,0:T(8,128)(2,1)S(1)} %copy-done.11), channel_id=1, source_target_pairs={{0,1},{1,0},{2,3},{3,2},{4,5},{5,4},{6,7},{7,6},{8,9},{9,8},{10,11... | collective-permute-start | bytes 6291464 | tf_op jit(solution)/shard_map/ppermute | solution.py:23
  119.1 4.4 collective-permute-start.2
  156.4 93.4 %all-gather.5.cloned.1.call-start = ((), (), s32[]{:S(2)}) async-start(), calls=%async_computation.5 | async-start | bytes 2621440 | tf_op jit(solution)/shard_map/all_gather | solution.py:276
  204.4 92.1 %all-gather.3.cloned.1.call-start = ((), (), s32[]{:S(2)}) async-start(), calls=%async_computation.4 | async-start | bytes 2621440 | tf_op jit(solution)/shard_map/all_gather | solution.py:276
  279.4 55.6 %collective-permute-start.12 = (bf16[8192,128]{1,0:T(8,128)(2,1)}, bf16[8192,128]{1,0:T(8,128)(2,1)S(1)}, u32[]{:S(2)}, u32[]{:S(2)}) collective-permute-start(bf16[8192,128]{1,0:T(8,128)(2,1)} %get-tuple-element.35), channel_id=1, source_target_pairs={{0,1},{1,0},{2,3},{3,2},{4,5},{5,4},{6,7},{7,6},{8,9},{9,8},{10,11... | collective-permute-start | bytes 6291464 | tf_op jit(solution)/shard_map/ppermute | solution.py:23
  287.8 49.3 %collective-permute-start.18 = (f32[520,128]{1,0:T(8,128)}, f32[520,128]{1,0:T(8,128)S(1)}, u32[]{:S(2)}, u32[]{:S(2)}) collective-permute-start(f32[520,128]{1,0:T(8,128)} %weight_grad.7), channel_id=1, source_target_pairs={{0,1},{1,0},{2,3},{3,2},{4,5},{5,4},{6,7},{7,6},{8,9},{9,8},{10,11... | collective-permute-start | bytes 798728 | tf_op jit(solution)/shard_map/ppermute | solution.py:23
  326.0 9.0 %copy-start.1 = (bf16[8192,128]{1,0:T(8,128)(2,1)S(1)}, bf16[8192,128]{1,0:T(8,128)(2,1)}, u32[]{:S(2)}) copy-start(bf16[8192,128]{1,0:T(8,128)(2,1)} %get-tuple-element.34) | copy-start | bytes 6291460
  326.0 11.9 %collective-permute-start.7 = (bf16[8192,128]{1,0:T(8,128)(2,1)}, bf16[8192,128]{1,0:T(8,128)(2,1)S(1)}, u32[]{:S(2)}, u32[]{:S(2)}) collective-permute-start(bf16[8192,128]{1,0:T(8,128)(2,1)} %get-tuple-element.30), channel_id=1, source_target_pairs={{0,1},{1,0},{2,3},{3,2},{4,5},{5,4},{6,7},{7,6},{8,9},{9,8},{10,11... | collective-permute-start | bytes 6291464 | tf_op jit(solution)/shard_map/ppermute | solution.py:23
  334.5 2.7 collective-permute-start.16
  334.9 5.1 %collective-permute-start.11 = (bf16[8192,128]{1,0:T(8,128)(2,1)}, bf16[8192,128]{1,0:T(8,128)(2,1)S(1)}, u32[]{:S(2)}, u32[]{:S(2)}) collective-permute-start(bf16[8192,128]{1,0:T(8,128)(2,1)} %get-tuple-element.33), channel_id=1, source_target_pairs={{0,1},{1,0},{2,3},{3,2},{4,5},{5,4},{6,7},{7,6},{8,9},{9,8},{10,11... | collective-permute-start | bytes 6291464 | tf_op jit(solution)/shard_map/ppermute | solution.py:23
  335.0 4.4 copy-start
  335.6 48.5 %collective-permute-start.13 = (bf16[8192,128]{1,0:T(8,128)(2,1)S(1)}, bf16[8192,128]{1,0:T(8,128)(2,1)S(1)}, u32[]{:S(2)}, u32[]{:S(2)}) collective-permute-start(bf16[8192,128]{1,0:T(8,128)(2,1)S(1)} %add_convert_fusion.1), channel_id=1, source_target_pairs={{0,2},{1,3},{2,0},{3,1},{4,6},{5,7},{6,4},{7,5},{8,10},{9,11},{10,... | collective-permute-start | bytes 6291464 | tf_op jit(solution)/shard_map/ppermute | solution.py:23
  337.1 57.6 %collective-permute-start.6 = (bf16[8192,128]{1,0:T(8,128)(2,1)}, bf16[8192,128]{1,0:T(8,128)(2,1)S(1)}, u32[]{:S(2)}, u32[]{:S(2)}) collective-permute-start(bf16[8192,128]{1,0:T(8,128)(2,1)} %get-tuple-element.28), channel_id=1, source_target_pairs={{0,1},{1,0},{2,3},{3,2},{4,5},{5,4},{6,7},{7,6},{8,9},{9,8},{10,11... | collective-permute-start | bytes 6291464 | tf_op jit(solution)/shard_map/ppermute | solution.py:23
  337.2 114.9 %collective-permute-start.19 = (f32[520,128]{1,0:T(8,128)S(1)}, f32[520,128]{1,0:T(8,128)S(1)}, u32[]{:S(2)}, u32[]{:S(2)}) collective-permute-start(f32[520,128]{1,0:T(8,128)S(1)} %add.70), channel_id=1, source_target_pairs={{0,2},{1,3},{2,0},{3,1},{4,6},{5,7},{6,4},{7,5},{8,10},{9,11},{10,... | collective-permute-start | bytes 798728 | tf_op jit(solution)/shard_map/ppermute | solution.py:23
  337.9 114.3 %collective-permute-start.17 = (f32[520,128]{1,0:T(8,128)S(1)}, f32[520,128]{1,0:T(8,128)S(1)}, u32[]{:S(2)}, u32[]{:S(2)}) collective-permute-start(f32[520,128]{1,0:T(8,128)S(1)} %add.68), channel_id=1, source_target_pairs={{0,2},{1,3},{2,0},{3,1},{4,6},{5,7},{6,4},{7,5},{8,10},{9,11},{10,... | collective-permute-start | bytes 798728 | tf_op jit(solution)/shard_map/ppermute | solution.py:23
  339.5 44.7 %copy-start.2 = (bf16[8192,128]{1,0:T(8,128)(2,1)S(1)}, bf16[8192,128]{1,0:T(8,128)(2,1)}, u32[]{:S(2)}) copy-start(bf16[8192,128]{1,0:T(8,128)(2,1)} %get-tuple-element.32) | copy-start | bytes 6291460
  340.0 100.0 %collective-permute-start.8 = (bf16[8192,128]{1,0:T(8,128)(2,1)S(1)}, bf16[8192,128]{1,0:T(8,128)(2,1)}, u32[]{:S(2)}, u32[]{:S(2)}) collective-permute-start(bf16[8192,128]{1,0:T(8,128)(2,1)S(1)} %add_convert_fusion.4), channel_id=1, source_target_pairs={{0,2},{1,3},{2,0},{3,1},{4,6},{5,7},{6,4},{7,5},{8,10},{9,11},{10,... | collective-permute-start | bytes 6291464 | tf_op jit(solution)/shard_map/ppermute | solution.py:23
  386.3 53.7 %copy-start.3 = (bf16[8192,128]{1,0:T(8,128)(2,1)S(1)}, bf16[8192,128]{1,0:T(8,128)(2,1)}, u32[]{:S(2)}) copy-start(bf16[8192,128]{1,0:T(8,128)(2,1)} %get-tuple-element.27) | copy-start | bytes 6291460
  394.8 57.5 %collective-permute-start.14 = (f32[512,128]{1,0:T(8,128)}, f32[512,128]{1,0:T(8,128)S(1)}, u32[]{:S(2)}, u32[]{:S(2)}) collective-permute-start(f32[512,128]{1,0:T(8,128)} %weight_grad.5), channel_id=1, source_target_pairs={{0,1},{1,0},{2,3},{3,2},{4,5},{5,4},{6,7},{7,6},{8,9},{9,8},{10,11... | collective-permute-start | bytes 786440 | tf_op jit(solution)/shard_map/ppermute | solution.py:23
  443.8 8.5 %copy-start.6 = (f32[512,128]{1,0:T(8,128)S(1)}, f32[512,128]{1,0:T(8,128)}, u32[]{:S(2)}) copy-start(f32[512,128]{1,0:T(8,128)} %weight_grad.5) | copy-start | bytes 786436
  452.1 1.7 collective-permute-start.9
  452.3 9.2 %collective-permute-start.15 = (f32[512,128]{1,0:T(8,128)S(1)}, f32[512,128]{1,0:T(8,128)S(1)}, u32[]{:S(2)}, u32[]{:S(2)}) collective-permute-start(f32[512,128]{1,0:T(8,128)S(1)} %add.66), channel_id=1, source_target_pairs={{0,2},{1,3},{2,0},{3,1},{4,6},{5,7},{6,4},{7,5},{8,10},{9,11},{10,... | collective-permute-start | bytes 786440 | tf_op jit(solution)/shard_map/ppermute | solution.py:23
  453.9 12.8 %collective-permute-start.10 = (f32[512,128]{1,0:T(8,128)S(1)}, f32[512,128]{1,0:T(8,128)S(1)}, u32[]{:S(2)}, u32[]{:S(2)}) collective-permute-start(f32[512,128]{1,0:T(8,128)S(1)} %add.61), channel_id=1, source_target_pairs={{0,2},{1,3},{2,0},{3,1},{4,6},{5,7},{6,4},{7,5},{8,10},{9,11},{10,... | collective-permute-start | bytes 786440 | tf_op jit(solution)/shard_map/ppermute | solution.py:23
  (7 other events, 18.3 us)
Sparse Core Ops, SparseCore 0:
  106.8 45.3 reduce-scatter.4
  156.5 45.3 reduce-scatter.2
  204.5 45.2 all-gather.4
  251.8 44.6 all-gather.2

commit v3 on v2

v3 whole, which is shorter than its diff:
```python
import functools

import jax
import jax.numpy as jnp
from jax import lax
from jax.experimental import pallas as pl
from jax.experimental.pallas import tpu as pltpu
from jax.sharding import PartitionSpec as P

CHUNKS = 2
MIB = 1024 * 1024
HBM = pl.BlockSpec(memory_space=pl.ANY)
VMEM = pl.BlockSpec(memory_space=pltpu.VMEM)
SMEM = pl.BlockSpec(memory_space=pltpu.SMEM)
PARAMS = pltpu.CompilerParams(vmem_limit_bytes=24 * MIB)


def cost(flops, moved):
    return pl.CostEstimate(flops=flops, bytes_accessed=moved, transcendentals=0)


def swap(value, mask, n):
    return lax.ppermute(value, "node", [(i, i ^ mask) for i in range(n)])


def masks_of(n):
    assert n & (n - 1) == 0
    return [1 << i for i in range(n.bit_length() - 1)]


def sum_over_node(value, n):
    for mask in masks_of(n):
        value = value + swap(value, mask, n)
    return value


def total_of(values):
    if len(values) == 1:
        return values[0]
    return sum(v.astype(jnp.float32) for v in values).astype(jnp.bfloat16)


def onehot_tile(row, ids):
    side = ids.shape[0]
    some = jnp.broadcast_to(row.astype(jnp.float32), (16, side)).astype(jnp.bfloat16)
    rows = jnp.concatenate([some] * (side // 16), axis=0)
    return jnp.where(ids == rows, jnp.bfloat16(1.0), jnp.bfloat16(0.0))


def side_ids(side):
    return lax.broadcasted_iota(jnp.int32, (side, side), 0).astype(jnp.float32).astype(jnp.bfloat16)


def project(feat_t, weights_t, n):
    width, rows = feat_t.shape
    wide = weights_t.shape[0] // (2 * n)
    step = min(1024, rows)

    def kernel(feat_ref, w_ref, *outs):
        value = jnp.dot(w_ref[...], feat_ref[...], preferred_element_type=jnp.float32)
        for c in range(2 * n):
            outs[c][...] = value[c * wide : (c + 1) * wide, :].astype(outs[c].dtype)

    return pl.pallas_call(
        kernel,
        grid=(rows // step,),
        in_specs=[
            pl.BlockSpec((width, step), lambda i: (0, i)),
            pl.BlockSpec(weights_t.shape, lambda i: (0, 0)),
        ],
        out_specs=[pl.BlockSpec((wide, step), lambda i: (0, i))] * (2 * n),
        out_shape=[jax.ShapeDtypeStruct((wide, rows), jnp.bfloat16)] * n
        + [jax.ShapeDtypeStruct((wide, rows), jnp.float32)] * n,
        compiler_params=PARAMS,
        cost_estimate=cost(
            2 * width * rows * weights_t.shape[0], 2 * width * rows + 6 * n * wide * rows
        ),
        name="project",
    )(feat_t, weights_t)


def mean_tiles(order, src, inv, nbr, parts, self_term, n_feat):
    n = len(parts)
    wide, rows = self_term.shape
    blocks, slots, side = nbr.shape
    share = rows // n_feat
    per_share = blocks // n_feat

    def kernel(order_ref, src_ref, inv_ref, nbr_ref, self_hbm, *rest):
        part_refs = rest[:n]
        out_hbm, table, self_ref, ready, sems, out_sems = rest[n:]
        copies = [
            pltpu.make_async_copy(ref, table.at[:, pl.ds(k * rows, rows)], sems.at[k])
            for k, ref in enumerate(part_refs)
        ]
        copies.append(pltpu.make_async_copy(self_hbm, self_ref, sems.at[n]))
        for copy in copies:
            copy.start()
        for copy in copies:
            copy.wait()
        ids = side_ids(side)

        def out_copy(s):
            at = pl.ds(pl.multiple_of(s * share, share), share)
            return pltpu.make_async_copy(ready.at[at, :], out_hbm.at[at, :], out_sems.at[s])

        @pl.loop(0, n_feat)
        def _(s):
            first = lax.rem(order_ref[0] + s, n_feat) * per_share

            @pl.loop(0, per_share, unroll=2)
            def _(i):
                b = first + i
                picked = []
                tiles = []
                for t in range(slots):
                    at = pl.multiple_of(src_ref[b, t] * side, side)
                    picked.append(table[:, pl.ds(at, side)])
                    tiles.append(onehot_tile(nbr_ref[b, t : t + 1, :], ids))
                total = jnp.dot(
                    jnp.concatenate(picked, axis=1),
                    jnp.concatenate(tiles, axis=0),
                    preferred_element_type=jnp.float32,
                )
                own = self_ref[:, pl.ds(pl.multiple_of(b * side, side), side)]
                pre_t = total * inv_ref[b] + own
                at = pl.multiple_of((s * per_share + i) * side, side)
                ready[pl.ds(at, side), :] = pre_t.T.astype(jnp.bfloat16)

            out_copy(s).start()

        @pl.loop(0, n_feat)
        def _(s):
            out_copy(s).wait()

    return pl.pallas_call(
        kernel,
        out_shape=jax.ShapeDtypeStruct((rows, wide), jnp.bfloat16),
        in_specs=[SMEM, SMEM, SMEM, VMEM, HBM] + [HBM] * n,
        out_specs=HBM,
        scratch_shapes=[
            pltpu.VMEM((wide, n * rows), jnp.bfloat16),
            pltpu.VMEM((wide, rows), jnp.float32),
            pltpu.VMEM((rows, wide), jnp.bfloat16),
            pltpu.SemaphoreType.DMA((n + 1,)),
            pltpu.SemaphoreType.DMA((n_feat,)),
        ],
        compiler_params=pltpu.CompilerParams(vmem_limit_bytes=24 * MIB),
        cost_estimate=cost(
            8 * blocks * slots * side * side * wide, 2 * n * rows * wide + 6 * rows * wide
        ),
        name="mean_tiles",
    )(order, src, inv, nbr, self_term, *parts)


def activate(shares, bias, cot, hidden, c, after):
    share, wide = shares[0].shape
    hid = cot.shape[1]
    chunk = pl.BlockSpec((share, wide), lambda i: (0, c))
    whole = pl.BlockSpec((share, wide), lambda i: (0, 0))
    held = [] if hidden is None else [hidden]
    n = len(shares)

    def kernel(bias_ref, cot_ref, *rest):
        hidden_ref, grad_ref = rest[-2:]
        value = bias_ref[...]
        for ref in rest[:n]:
            value = value + ref[...].astype(jnp.float32)
        sigma = jax.nn.sigmoid(value)
        hidden_ref[...] = (value * sigma).astype(jnp.bfloat16)
        slope = sigma * (1.0 + value * (1.0 - sigma))
        grad_ref[...] = (cot_ref[...].astype(jnp.float32) * slope).astype(jnp.bfloat16)

    return pl.pallas_call(
        kernel,
        grid=(1,),
        in_specs=[pl.BlockSpec((1, wide), lambda i: (0, c)), chunk] + [whole] * n + [HBM] * len(held + after),
        out_specs=[chunk, whole],
        out_shape=[
            jax.ShapeDtypeStruct((share, hid), jnp.bfloat16),
            jax.ShapeDtypeStruct((share, wide), jnp.bfloat16),
        ],
        input_output_aliases={2 + n: 0} if held else {},
        compiler_params=pltpu.CompilerParams(vmem_limit_bytes=24 * MIB),
        cost_estimate=cost(20 * share * wide, (6 + 2 * n) * share * wide),
        name="activate",
    )(bias, cot, *shares, *held, *after)


def spread_tiles(order, src, inv, nbr, pieces, n, after):
    wide = pieces[0].shape[1]
    share = pieces[0].shape[0]
    m = len(pieces)
    rows = m * share
    blocks, slots, side = nbr.shape
    step = 512
    assert slots % 2 == 0

    def kernel(order_ref, src_ref, inv_ref, nbr_ref, *rest):
        outs = rest[m + len(after) : m + len(after) + n + 1]
        table, grad_ref, ready, sems, out_sems = rest[m + len(after) + n + 1 :]
        loads = []
        for s in range(m):
            at = pl.multiple_of(lax.rem(order_ref[0] + s, m) * share, share)
            loads.append(
                pltpu.make_async_copy(rest[s], grad_ref.at[pl.ds(at, share), :], sems.at[s])
            )
        for load in loads:
            load.start()
        ids = side_ids(side)

        @pl.loop(0, n * rows // step)
        def _(i):
            table[pl.ds(pl.multiple_of(i * step, step), step), :] = jnp.zeros(
                (step, wide), jnp.float32
            )

        for load in loads:
            load.wait()
        copies = [pltpu.make_async_copy(grad_ref, outs[n], out_sems.at[n])]
        copies[0].start()

        @pl.loop(0, blocks, unroll=2)
        def _(b):
            g = grad_ref[pl.ds(pl.multiple_of(b * side, side), side), :]
            scale = inv_ref[b]
            tiles = [onehot_tile(nbr_ref[b, t : t + 1, :], ids) for t in range(slots)]
            terms = jnp.dot(
                jnp.concatenate(tiles, axis=0), g, preferred_element_type=jnp.float32
            )
            for t in range(0, slots, 2):
                one, two = src_ref[b, t], src_ref[b, t + 1]
                same = jnp.where(one == two, scale, 0.0)
                at_one = pl.ds(pl.multiple_of(one * side, side), side)
                at_two = pl.ds(pl.multiple_of(two * side, side), side)
                term_one = terms[t * side : (t + 1) * side, :]
                term_two = terms[(t + 1) * side : (t + 2) * side, :]
                new_one = table[at_one, :] + (term_one * scale + term_two * same)
                new_two = table[at_two, :] + (term_two * scale + term_one * same)
                table[at_one, :] = new_one
                table[at_two, :] = new_two

        for k in reversed(range(n)):

            @pl.loop(0, rows // step)
            def _(i, k=k):
                at = pl.multiple_of(i * step, step)
                ready[k, pl.ds(at, step), :] = table[pl.ds(k * rows + at, step), :].astype(
                    jnp.bfloat16
                )

            copies.append(pltpu.make_async_copy(ready.at[k], outs[k], out_sems.at[k]))
            copies[-1].start()
        for copy in copies:
            copy.wait()

    return pl.pallas_call(
        kernel,
        out_shape=[jax.ShapeDtypeStruct((rows, wide), jnp.bfloat16)] * (n + 1),
        in_specs=[SMEM, SMEM, SMEM, VMEM] + [HBM] * (m + len(after)),
        out_specs=[HBM] * (n + 1),
        scratch_shapes=[
            pltpu.VMEM((n * rows, wide), jnp.float32),
            pltpu.VMEM((rows, wide), jnp.bfloat16),
            pltpu.VMEM((n, rows, wide), jnp.bfloat16),
            pltpu.SemaphoreType.DMA((m,)),
            pltpu.SemaphoreType.DMA((n + 1,)),
        ],
        compiler_params=pltpu.CompilerParams(vmem_limit_bytes=40 * MIB),
        cost_estimate=cost(
            8 * blocks * slots * side * side * wide, 2 * n * rows * wide + 2 * rows * wide
        ),
        name="spread_tiles",
    )(order, src, inv, nbr, *pieces, *after)


def weight_grad(feat_t, grads, with_sum):
    width, rows = feat_t.shape
    wide = grads[0].shape[1]
    step = min(2048, rows)
    extra = 8 if with_sum else 0

    def kernel(feat_ref, *rest):
        out_ref = rest[-1]

        @pl.when(pl.program_id(0) == 0)
        def _():
            out_ref[...] = jnp.zeros_like(out_ref)

        value = rest[0][...]
        if len(grads) > 1:
            value = sum(ref[...].astype(jnp.float32) for ref in rest[:-1]).astype(jnp.bfloat16)
        out_ref[:width, :] += jnp.dot(feat_ref[...], value, preferred_element_type=jnp.float32)
        if with_sum:
            out_ref[width : width + 1, :] += jnp.sum(
                value.astype(jnp.float32), axis=0, keepdims=True
            )

    return pl.pallas_call(
        kernel,
        grid=(rows // step,),
        in_specs=[pl.BlockSpec((width, step), lambda i: (0, i))]
        + [pl.BlockSpec((step, wide), lambda i: (i, 0))] * len(grads),
        out_specs=pl.BlockSpec((width + extra, wide), lambda i: (0, 0)),
        out_shape=jax.ShapeDtypeStruct((width + extra, wide), jnp.float32),
        compiler_params=pltpu.CompilerParams(vmem_limit_bytes=16 * MIB),
        cost_estimate=cost(2 * width * rows * wide, 2 * rows * (width + wide)),
        name="weight_grad",
    )(feat_t, *grads)


def reduce_shares(part, n, direct):
    share = part.shape[0] // n
    if not direct:
        return [lax.psum_scatter(part, "feat", scatter_dimension=0, tiled=True)]
    got = [part[:share]]
    for s in range(1, n):
        got.append(
            lax.ppermute(
                part[s * share : (s + 1) * share], "feat", [(i, (i + s) % n) for i in range(n)]
            )
        )
    return got


def gather_shares(value, n, direct):
    if not direct:
        return [lax.all_gather(value, "feat", axis=0, tiled=True)]
    got = [value]
    for s in range(1, n):
        got.append(lax.ppermute(value, "feat", [((i + s) % n, i) for i in range(n)]))
    return got


def on_device(n_node, n_feat, feat_t, src_blocks, nbr_rows, tile_counts, w_neigh, w_self, bias, cotangent):
    width, rows = feat_t.shape
    hid = w_neigh.shape[1]
    blocks, slots = src_blocks.shape
    share = cotangent.shape[1]
    me = lax.axis_index("node")
    src = jnp.bitwise_xor(src_blocks // blocks, me) * blocks + src_blocks % blocks
    valid = jnp.arange(slots, dtype=jnp.int32)[None, :] < tile_counts[:, None]
    nbr = jnp.where(valid[:, :, None], nbr_rows, -1)
    inv = 1.0 / tile_counts.astype(jnp.float32)
    cot_rows = cotangent.reshape(share, hid)
    bias_row = bias[None, :]

    weights_t = jnp.concatenate([w_neigh.T, w_self.T], axis=0)
    projected = project(feat_t, weights_t, CHUNKS)

    gathered = []
    for c in range(CHUNKS):
        held = {0: projected[c]}
        for mask in reversed(masks_of(n_node)):
            for k in list(held):
                held[k ^ mask] = swap(held[k], mask, n_node)
        gathered.append([held[k] for k in range(n_node)])

    direct = n_feat <= 4
    order = jnp.reshape(lax.axis_index("feat") if direct else 0, (1,)).astype(jnp.int32)
    part_pres = [
        mean_tiles(order, src, inv, nbr, gathered[c], projected[CHUNKS + c], n_feat)
        for c in range(CHUNKS)
    ]
    hidden = None
    grad_pres, pieces = [], []
    for c in range(CHUNKS):
        shares = reduce_shares(part_pres[c], n_feat, direct)
        hidden, grad_pre = activate(
            shares, bias_row, cot_rows, hidden, c, part_pres[c + 1 : c + 2]
        )
        grad_pres.append(grad_pre)
        pieces.append(gather_shares(grad_pre, n_feat, direct and c == CHUNKS - 1))

    grads_n, grads_s, sums = [], [], []
    after = [grad_pres[-1]]
    for c in range(CHUNKS):
        *tables, piece = spread_tiles(order, src, inv, nbr, pieces[c], n_node, after)
        held = {k: [v] for k, v in enumerate(tables)}
        for mask in masks_of(n_node):
            left = {}
            for k in reversed(list(held)):
                if k & mask:
                    mine = held[k ^ mask]
                    left[k ^ mask] = mine + [swap(total_of(held[k]), mask, n_node)]
            held = left
            if mask == 1:
                after = [total_of(v) for k, v in held.items() if k]
                held = {k: [total_of(v)] if k else v for k, v in held.items()}
        grads_n.append(sum_over_node(weight_grad(feat_t, held[0], False), n_node))
        both = sum_over_node(weight_grad(feat_t, [piece], True), n_node)
        grads_s.append(both[:width])
        sums.append(both[width])
    return (
        hidden.reshape(1, share, hid),
        jnp.concatenate(grads_n, axis=1),
        jnp.concatenate(grads_s, axis=1),
        jnp.concatenate(sums, axis=0),
    )


def solution(mesh):
    return jax.shard_map(
        functools.partial(on_device, mesh.shape["node"], mesh.shape["feat"]),
        mesh=mesh,
        in_specs=(
            P("feat", ("grp", "node")),
            P(("grp", "node"), None),
            P(("grp", "node"), None, None),
            P(("grp", "node")),
            P("feat", None),
            P("feat", None),
            P(),
            P(("grp", "node"), "feat", None),
        ),
        out_specs=(
            P(("grp", "node"), "feat", None),
            P(("grp", "feat"), None),
            P(("grp", "feat"), None),
            P("grp"),
        ),
        check_vma=False,
    )
```

time: 475 us -> 502 us (1.057); the launches traced: 474 us -> 493 us
  Pallas kernels: 173 us -> 113 us
  waiting for transfers between devices: 256 us -> 310 us
  local copies, waits for them, and re-layouts: 5.16 us -> 21.2 us
  starting transfers between devices: 13.5 us -> 26.6 us
  other arithmetic: 12.6 us -> 7.05 us
    ppermute x0 -> x9, waiting for transfers between devices: none -> 129 us  [the longest x6 97.1 us: reduce_shares(): lax.ppermute(part[s * share:(s + 1) * share], 'feat', [(i, (i + s) % n) f...]
    all_gather x2 -> x1, waiting for transfers between devices: 53 us -> 0.94 us  [gather_shares(): return [lax.all_gather(value, 'feat', axis=0, tiled=True)]]
    reduce_scatter x2 -> x0, waiting for transfers between devices: 42.9 us -> none  [on_device(): pre = lax.psum_scatter(part_pre, 'feat', scatter_dimension=0, tiled=True)]
    pallas_call x2, Pallas kernels: 63.2 us -> 41.9 us  [mean_tiles(): pl.pallas_call(kernel, out_shape=jax.ShapeDtypeStruct((rows, wide), jnp.b...]
    ppermute x20, waiting for transfers between devices: 160 us -> 181 us  [swap(): return lax.ppermute(value, 'node', [(i, i ^ mask) for i in range(n)])]
    pallas_call x4, Pallas kernels: 33.7 us -> 14.2 us  [weight_grad(): pl.pallas_call(kernel, grid=(rows // step,), in_specs=[pl.BlockSpec((widt...]
    unnamed x33 -> x51, local copies, waits for them, and re-layouts: 5.12 us -> 20.9 us
    ppermute x0 -> x9, starting transfers between devices: none -> 14.4 us  [the longest x6 9.81 us: reduce_shares(): lax.ppermute(part[s * share:(s + 1) * share], 'feat', [(i, (i + s) % n) f...]
  transfers between devices with their start and end apart: 24 -> 30, of which waited for: 12 -> 16; matrix products, arithmetic and copies ran while one was open for 2% -> 1% of each run, Pallas kernels for 33% -> 12%
where the time goes in v3:
time: 502 us; the launch traced here: 493 us
  waiting for transfers between devices  310 us (62%)
  Pallas kernels  113 us (23%)
  starting transfers between devices  26.6 us (5%)
  local copies, waits for them, and re-layouts  21.2 us (4%)
  between operations  14.4 us (3%)
  other arithmetic  7.05 us (1%)
    ppermute x20, waiting for transfers between devices, swap(): return lax.ppermute(value, 'node', [(i, i ^ mask) for i in range(n)])  181 us
    ppermute x6, waiting for transfers between devices, reduce_shares(): lax.ppermute(part[s * share:(s + 1) * share], 'feat', [(i, (i + s) % n) f...  97.1 us
    pallas_call x2, Pallas kernels, spread_tiles(): pl.pallas_call(kernel, out_shape=[jax.ShapeDtypeStruct((rows, wide), jnp....  46.6 us
    pallas_call x2, Pallas kernels, mean_tiles(): pl.pallas_call(kernel, out_shape=jax.ShapeDtypeStruct((rows, wide), jnp.b...  41.9 us
    ppermute x3, waiting for transfers between devices, gather_shares(): lax.ppermute(value, 'feat', [((i + s) % n, i) for i in range(n)])  31.7 us
    unnamed x51, local copies, waits for them, and re-layouts  20.9 us
    pallas_call x4, Pallas kernels, weight_grad(): pl.pallas_call(kernel, grid=(rows // step,), in_specs=[pl.BlockSpec((widt...  14.2 us
    ppermute x20, starting transfers between devices, swap(): return lax.ppermute(value, 'node', [(i, i ^ mask) for i in range(n)])  12.2 us
  transfers between devices with their start and end apart: 30, of which 16 were waited for; matrix products, arithmetic and copies ran while one was open for 1% of the time, Pallas kernels for 12%

profile of v3, /device:TPU:0, one launch (start us, length us, event | category | flops | bytes accessed | tf_op | source)
XLA Modules:
  0.0 493.0 jit_solution(14495969835272988121)
XLA Ops:
  9.5 3.4 copy-done
  12.8 7.5 %project.1 = (bf16[128,8192]{1,0:T(8,128)(2,1)}, bf16[128,8192]{1,0:T(8,128)(2,1)S(1)}, f32[128,8192]{1,0:T(8,128)S(1)}, f32[128,8192]{1,0:T(8,128)S(1)}) custom-call(bf16[512,8192]{1,0:T(8,128)(2,1)S(1)} %copy-done, bf16[512,512]{1,0:T(8,128)(2,1)S(1)} %pad_maximum_fusion.w_ref), custom_call_target="tpu_custom_call" | custom-call | flops 4294967296 | bytes 20971520 | tf_op jit(solution)/shard_map/project/pallas_call | solution.py:64
  20.3 2.0 copy-done.15
  22.3 2.0 copy-done.17
  24.3 2.9 collective-permute-start.7
  27.3 46.7 %collective-permute-done.7.rest_2_ = bf16[128,8192]{1,0:T(8,128)(2,1)} collective-permute-done((bf16[128,8192]{1,0:T(8,128)(2,1)}, bf16[128,8192]{1,0:T(8,128)(2,1)}, u32[]{:S(2)}, u32[]{:S(2)}) %collective-permute-start.7) | collective-permute-done | bytes 2097184 | tf_op jit(solution)/shard_map/ppermute | solution.py:23
  75.0 43.1 %collective-permute-done.1.rest_2_ = bf16[128,8192]{1,0:T(8,128)(2,1)} collective-permute-done((bf16[128,8192]{1,0:T(8,128)(2,1)S(1)}, bf16[128,8192]{1,0:T(8,128)(2,1)}, u32[]{:S(2)}, u32[]{:S(2)}) %collective-permute-start.1) | collective-permute-done | bytes 2097184 | tf_op jit(solution)/shard_map/ppermute | solution.py:23
  118.2 2.2 copy-done.18
  120.3 21.5 %mean_tiles.3 = bf16[8192,128]{1,0:T(8,128)(2,1)S(1)} custom-call(s32[1]{0:T(128)} %bitcast.2.order_ref, s32[64,16]{1,0:T(8,128)S(1)} %fusion.2.src_ref, f32[64]{0:T(128)S(1)} %convert_divide_fusion.inv_ref, s32[64,16,128]{2,1,0:T(8,128)S(1)} %broadcast_select_fusion.nbr_ref, f32[128,8192]{1,0:T(8,128)S(1)} %copy-done.18, ...), custom_call_target="tpu_custom_call" | custom-call | flops 17179869184 | bytes 14680064 | tf_op jit(solution)/shard_map/mean_tiles/pallas_call | solution.py:136
  142.0 3.9 collective-permute-start.11
  148.6 20.4 %mean_tiles.2.rest_4_ = bf16[8192,128]{1,0:T(8,128)(2,1)S(1)} custom-call(s32[1]{0:T(128)} %bitcast.2.order_ref, s32[64,16]{1,0:T(8,128)S(1)} %fusion.2.src_ref, f32[64]{0:T(128)S(1)} %convert_divide_fusion.inv_ref, s32[64,16,128]{2,1,0:T(8,128)S(1)} %broadcast_select_fusion.nbr_ref, f32[128,8192]{1,0:T(8,128)S(1)} %copy-done.16, ...), custom_call_target="tpu_custom_call" | custom-call | flops 17179869184 | bytes 14680064 | tf_op jit(solution)/shard_map/mean_tiles/pallas_call | solution.py:136
  169.0 22.4 %collective-permute-done.10.rest_2_ = bf16[2048,128]{1,0:T(8,128)(2,1)S(1)} collective-permute-done((bf16[2048,128]{1,0:T(8,128)(2,1)S(1)}, bf16[2048,128]{1,0:T(8,128)(2,1)S(1)}, u32[]{:S(2)}, u32[]{:S(2)}) %collective-permute-start.10) | collective-permute-done | bytes 524320 | tf_op jit(solution)/shard_map/ppermute | solution.py:319
  194.0 2.9 collective-permute-start.4
  198.8 15.5 %collective-permute-done.5.rest_3_ = bf16[2048,128]{1,0:T(8,128)(2,1)S(1)} collective-permute-done((bf16[2048,128]{1,0:T(8,128)(2,1)S(1)}, bf16[2048,128]{1,0:T(8,128)(2,1)S(1)}, u32[]{:S(2)}, u32[]{:S(2)}) %collective-permute-start.5) | collective-permute-done | bytes 524320 | tf_op jit(solution)/shard_map/ppermute | solution.py:319
  214.3 59.2 %collective-permute-done.4.rest_2_ = bf16[2048,128]{1,0:T(8,128)(2,1)S(1)} collective-permute-done((bf16[2048,128]{1,0:T(8,128)(2,1)S(1)}, bf16[2048,128]{1,0:T(8,128)(2,1)S(1)}, u32[]{:S(2)}, u32[]{:S(2)}) %collective-permute-start.4) | collective-permute-done | bytes 524320 | tf_op jit(solution)/shard_map/ppermute | solution.py:319
  278.7 23.3 %spread_tiles.2 = (bf16[8192,128]{1,0:T(8,128)(2,1)S(1)}, bf16[8192,128]{1,0:T(8,128)(2,1)S(1)}, bf16[8192,128]{1,0:T(8,128)(2,1)S(1)}, bf16[8192,128]{1,0:T(8,128)(2,1)S(1)}, bf16[8192,128]{1,0:T(8,128)(2,1)S(1)}) custom-call(s32[1]{0:T(128)} %bitcast.2.order_ref, s32[64,16]{1,0:T(8,128)S(1)} %fusion.2.src_ref, f32[64]{0:T(128)S(1)} %convert_divide_fusion.inv_ref, ...), custom_call_target="tpu_custom_call" | custom-call | flops 17179869184 | bytes 10485760 | tf_op jit(solution)/shard_map/spread_tiles/pallas_call | solution.py:257
  305.1 2.9 collective-permute-start.17
  309.9 10.2 %collective-permute-done.19.rest_3_ = bf16[2048,128]{1,0:T(8,128)(2,1)S(1)} collective-permute-done((bf16[2048,128]{1,0:T(8,128)(2,1)S(1)}, bf16[2048,128]{1,0:T(8,128)(2,1)S(1)}, u32[]{:S(2)}, u32[]{:S(2)}) %collective-permute-start.19) | collective-permute-done | bytes 524320 | tf_op jit(solution)/shard_map/ppermute | solution.py:331
  320.0 21.5 %collective-permute-done.18.rest_2_ = bf16[2048,128]{1,0:T(8,128)(2,1)S(1)} collective-permute-done((bf16[2048,128]{1,0:T(8,128)(2,1)S(1)}, bf16[2048,128]{1,0:T(8,128)(2,1)S(1)}, u32[]{:S(2)}, u32[]{:S(2)}) %collective-permute-start.18) | collective-permute-done | bytes 524320 | tf_op jit(solution)/shard_map/ppermute | solution.py:331
  341.5 23.3 %spread_tiles.3 = (bf16[8192,128]{1,0:T(8,128)(2,1)S(1)}, bf16[8192,128]{1,0:T(8,128)(2,1)S(1)}, bf16[8192,128]{1,0:T(8,128)(2,1)S(1)}, bf16[8192,128]{1,0:T(8,128)(2,1)S(1)}, bf16[8192,128]{1,0:T(8,128)(2,1)S(1)}) custom-call(s32[1]{0:T(128)} %bitcast.2.order_ref, s32[64,16]{1,0:T(8,128)S(1)} %fusion.2.src_ref, f32[64]{0:T(128)S(1)} %convert_divide_fusion.inv_ref, ...), custom_call_target="tpu_custom_call" | custom-call | flops 17179869184 | bytes 10485760 | tf_op jit(solution)/shard_map/spread_tiles/pallas_call | solution.py:257
  369.6 5.1 %collective-permute-done.21 = bf16[8192,128]{1,0:T(8,128)(2,1)S(1)} collective-permute-done((bf16[8192,128]{1,0:T(8,128)(2,1)S(1)}, bf16[8192,128]{1,0:T(8,128)(2,1)S(1)}, u32[]{:S(2)}, u32[]{:S(2)}) %collective-permute-start.21) | collective-permute-done | bytes 2097184 | tf_op jit(solution)/shard_map/ppermute | solution.py:23
  374.7 2.3 add_convert_fusion
  378.6 3.5 weight_grad.6
  382.2 3.5 weight_grad.7
  389.7 27.1 %collective-permute-done.14.rest_2_ = bf16[8192,128]{1,0:T(8,128)(2,1)S(1)} collective-permute-done((bf16[8192,128]{1,0:T(8,128)(2,1)}, bf16[8192,128]{1,0:T(8,128)(2,1)S(1)}, u32[]{:S(2)}, u32[]{:S(2)}) %collective-permute-start.14) | collective-permute-done | bytes 2097184 | tf_op jit(solution)/shard_map/ppermute | solution.py:23
  416.8 3.6 weight_grad.4
  420.5 41.3 %collective-permute-done.22.rest_2_ = bf16[8192,128]{1,0:T(8,128)(2,1)S(1)} collective-permute-done((bf16[8192,128]{1,0:T(8,128)(2,1)S(1)}, bf16[8192,128]{1,0:T(8,128)(2,1)S(1)}, u32[]{:S(2)}, u32[]{:S(2)}) %collective-permute-start.22) | collective-permute-done | bytes 2097184 | tf_op jit(solution)/shard_map/ppermute | solution.py:23
  461.7 3.6 weight_grad.5
  465.4 2.0 collective-permute-done.26
  467.5 4.7 collective-permute-done.28
  475.9 5.7 %collective-permute-done.16 = f32[512,128]{1,0:T(8,128)S(1)} collective-permute-done((f32[512,128]{1,0:T(8,128)S(1)}, f32[512,128]{1,0:T(8,128)S(1)}, u32[]{:S(2)}, u32[]{:S(2)}) %collective-permute-start.16) | collective-permute-done | bytes 262176 | tf_op jit(solution)/shard_map/ppermute | solution.py:23
  481.6 3.7 collective-permute-done.24
  (116 shorter events, 35.7 us)
Async XLA Ops:
  7.2 268.9 %all-gather.2.cloned.1.call-start = ((), (), s32[]{:S(2)}) async-start(), calls=%async_computation | async-start | bytes 2621440 | tf_op jit(solution)/shard_map/all_gather | solution.py:328
  24.3 117.5 %copy-start.12 = (bf16[128,8192]{1,0:T(8,128)(2,1)}, bf16[128,8192]{1,0:T(8,128)(2,1)S(1)}, u32[]{:S(2)}) copy-start(bf16[128,8192]{1,0:T(8,128)(2,1)S(1)} %get-tuple-element.23.rest_0_) | copy-start | bytes 6291460
  24.3 49.7 %collective-permute-start.7 = (bf16[128,8192]{1,0:T(8,128)(2,1)}, bf16[128,8192]{1,0:T(8,128)(2,1)}, u32[]{:S(2)}, u32[]{:S(2)}) collective-permute-start(bf16[128,8192]{1,0:T(8,128)(2,1)} %get-tuple-element.25.rest_0_), channel_id=1, source_target_pairs={{0,2},{1,3},{2,0},{3,1},{4,6},{5,7},{6,4},{7,5},{8,10},{9,11},{10,... | collective-permute-start | bytes 6291464 | tf_op jit(solution)/shard_map/ppermute | solution.py:23
  27.3 90.9 %collective-permute-start.1 = (bf16[128,8192]{1,0:T(8,128)(2,1)S(1)}, bf16[128,8192]{1,0:T(8,128)(2,1)}, u32[]{:S(2)}, u32[]{:S(2)}) collective-permute-start(bf16[128,8192]{1,0:T(8,128)(2,1)S(1)} %get-tuple-element.23.rest_0_), channel_id=1, source_target_pairs={{0,2},{1,3},{2,0},{3,1},{4,6},{5,7},{6,4},{7,5},{8,10},{9,11},{10,... | collective-permute-start | bytes 6291464 | tf_op jit(solution)/shard_map/ppermute | solution.py:23
  27.3 90.9 %collective-permute-start.6 = (bf16[128,8192]{1,0:T(8,128)(2,1)}, bf16[128,8192]{1,0:T(8,128)(2,1)}, u32[]{:S(2)}, u32[]{:S(2)}) collective-permute-start(bf16[128,8192]{1,0:T(8,128)(2,1)} %get-tuple-element.25.rest_0_), channel_id=1, source_target_pairs={{0,1},{1,0},{2,3},{3,2},{4,5},{5,4},{6,7},{7,6},{8,9},{9,8},{10,11... | collective-permute-start | bytes 6291464 | tf_op jit(solution)/shard_map/ppermute | solution.py:23
  74.0 44.1 %collective-permute-start.8 = (bf16[128,8192]{1,0:T(8,128)(2,1)}, bf16[128,8192]{1,0:T(8,128)(2,1)}, u32[]{:S(2)}, u32[]{:S(2)}) collective-permute-start(bf16[128,8192]{1,0:T(8,128)(2,1)} %collective-permute-done.7.rest_2_), channel_id=1, source_target_pairs={{0,1},{1,0},{2,3},{3,2},{4,5},{5,4},{6,7},{7,6},{8,9},{9,8},{10,11... | collective-permute-start | bytes 6291464 | tf_op jit(solution)/shard_map/ppermute | solution.py:23
  74.0 72.9 %collective-permute-start = (bf16[128,8192]{1,0:T(8,128)(2,1)S(1)}, bf16[128,8192]{1,0:T(8,128)(2,1)}, u32[]{:S(2)}, u32[]{:S(2)}) collective-permute-start(bf16[128,8192]{1,0:T(8,128)(2,1)S(1)} %get-tuple-element.23.rest_0_), channel_id=1, source_target_pairs={{0,1},{1,0},{2,3},{3,2},{4,5},{5,4},{6,7},{7,6},{8,9},{9,8},{10,11... | collective-permute-start | bytes 6291464 | tf_op jit(solution)/shard_map/ppermute | solution.py:23
  75.0 72.0 %copy-start.7 = (s32[64,16,128]{2,1,0:T(8,128)}, s32[64,16,128]{2,1,0:T(8,128)S(1)}, u32[]{:S(2)}) copy-start(s32[64,16,128]{2,1,0:T(8,128)S(1)} %broadcast_select_fusion.nbr_ref) | copy-start | bytes 1572868
  118.1 28.8 %collective-permute-start.2 = (bf16[128,8192]{1,0:T(8,128)(2,1)}, bf16[128,8192]{1,0:T(8,128)(2,1)S(1)}, u32[]{:S(2)}, u32[]{:S(2)}) collective-permute-start(bf16[128,8192]{1,0:T(8,128)(2,1)} %collective-permute-done.1.rest_2_), channel_id=1, source_target_pairs={{0,1},{1,0},{2,3},{3,2},{4,5},{5,4},{6,7},{7,6},{8,9},{9,8},{10,11... | collective-permute-start | bytes 6291464 | tf_op jit(solution)/shard_map/ppermute | solution.py:23
  142.0 27.0 %collective-permute-start.11 = (bf16[2048,128]{1,0:T(8,128)(2,1)S(1)}, bf16[2048,128]{1,0:T(8,128)(2,1)S(1)}, u32[]{:S(2)}, u32[]{:S(2)}) collective-permute-start(bf16[2048,128]{1,0:T(8,128)(2,1)S(1)} %get-tuple-element.40), channel_id=1, source_target_pairs={{0,12},{4,0},{8,4},{12,8},{1,13},{5,1},{9,5},{13,9},{2,14},{6,2},{... | collective-permute-start | bytes 1572872 | tf_op jit(solution)/shard_map/ppermute | solution.py:319
  145.9 45.5 %collective-permute-start.10 = (bf16[2048,128]{1,0:T(8,128)(2,1)S(1)}, bf16[2048,128]{1,0:T(8,128)(2,1)S(1)}, u32[]{:S(2)}, u32[]{:S(2)}) collective-permute-start(bf16[2048,128]{1,0:T(8,128)(2,1)S(1)} %get-tuple-element.41), channel_id=1, source_target_pairs={{0,8},{4,12},{8,0},{12,4},{1,9},{5,13},{9,1},{13,5},{2,10},{6,14},... | collective-permute-start | bytes 1572872 | tf_op jit(solution)/shard_map/ppermute | solution.py:319
  145.9 45.5 %collective-permute-start.9 = (bf16[2048,128]{1,0:T(8,128)(2,1)S(1)}, bf16[2048,128]{1,0:T(8,128)(2,1)S(1)}, u32[]{:S(2)}, u32[]{:S(2)}) collective-permute-start(bf16[2048,128]{1,0:T(8,128)(2,1)S(1)} %get-tuple-element.42), channel_id=1, source_target_pairs={{0,4},{4,8},{8,12},{12,0},{1,5},{5,9},{9,13},{13,1},{2,6},{6,10},{... | collective-permute-start | bytes 1572872 | tf_op jit(solution)/shard_map/ppermute | solution.py:319
  193.9 20.4 %collective-permute-start.5 = (bf16[2048,128]{1,0:T(8,128)(2,1)S(1)}, bf16[2048,128]{1,0:T(8,128)(2,1)S(1)}, u32[]{:S(2)}, u32[]{:S(2)}) collective-permute-start(bf16[2048,128]{1,0:T(8,128)(2,1)S(1)} %get-tuple-element.44), channel_id=1, source_target_pairs={{0,12},{4,0},{8,4},{12,8},{1,13},{5,1},{9,5},{13,9},{2,14},{6,2},{... | collective-permute-start | bytes 1572872 | tf_op jit(solution)/shard_map/ppermute | solution.py:319
  194.0 79.5 %collective-permute-start.4 = (bf16[2048,128]{1,0:T(8,128)(2,1)S(1)}, bf16[2048,128]{1,0:T(8,128)(2,1)S(1)}, u32[]{:S(2)}, u32[]{:S(2)}) collective-permute-start(bf16[2048,128]{1,0:T(8,128)(2,1)S(1)} %get-tuple-element.45), channel_id=1, source_target_pairs={{0,8},{4,12},{8,0},{12,4},{1,9},{5,13},{9,1},{13,5},{2,10},{6,14},... | collective-permute-start | bytes 1572872 | tf_op jit(solution)/shard_map/ppermute | solution.py:319
  196.9 76.7 %collective-permute-start.3 = (bf16[2048,128]{1,0:T(8,128)(2,1)S(1)}, bf16[2048,128]{1,0:T(8,128)(2,1)S(1)}, u32[]{:S(2)}, u32[]{:S(2)}) collective-permute-start(bf16[2048,128]{1,0:T(8,128)(2,1)S(1)} %get-tuple-element.46), channel_id=1, source_target_pairs={{0,4},{4,8},{8,12},{12,0},{1,5},{5,9},{9,13},{13,1},{2,6},{6,10},{... | collective-permute-start | bytes 1572872 | tf_op jit(solution)/shard_map/ppermute | solution.py:319
  303.3 4.6 collective-permute-start.13
  303.4 16.7 %collective-permute-start.19 = (bf16[2048,128]{1,0:T(8,128)(2,1)S(1)}, bf16[2048,128]{1,0:T(8,128)(2,1)S(1)}, u32[]{:S(2)}, u32[]{:S(2)}) collective-permute-start(bf16[2048,128]{1,0:T(8,128)(2,1)S(1)} %get-tuple-element.29.rest_1_.rest_0_), channel_id=1, source_target_pairs={{12,0},{0,4},{4,8},{8,12},{13,1},{1,5},{5,9},{9,13},{14,2},{2,6},{... | collective-permute-start | bytes 1572872 | tf_op jit(solution)/shard_map/ppermute | solution.py:331
  303.4 38.2 %collective-permute-start.18 = (bf16[2048,128]{1,0:T(8,128)(2,1)S(1)}, bf16[2048,128]{1,0:T(8,128)(2,1)S(1)}, u32[]{:S(2)}, u32[]{:S(2)}) collective-permute-start(bf16[2048,128]{1,0:T(8,128)(2,1)S(1)} %get-tuple-element.29.rest_1_.rest_0_), channel_id=1, source_target_pairs={{8,0},{12,4},{0,8},{4,12},{9,1},{13,5},{1,9},{5,13},{10,2},{14,6},... | collective-permute-start | bytes 1572872 | tf_op jit(solution)/shard_map/ppermute | solution.py:331
  305.1 36.5 %collective-permute-start.17 = (bf16[2048,128]{1,0:T(8,128)(2,1)S(1)}, bf16[2048,128]{1,0:T(8,128)(2,1)S(1)}, u32[]{:S(2)}, u32[]{:S(2)}) collective-permute-start(bf16[2048,128]{1,0:T(8,128)(2,1)S(1)} %get-tuple-element.29.rest_1_.rest_0_), channel_id=1, source_target_pairs={{4,0},{8,4},{12,8},{0,12},{5,1},{9,5},{13,9},{1,13},{6,2},{10,6},{... | collective-permute-start | bytes 1572872 | tf_op jit(solution)/shard_map/ppermute | solution.py:331
  367.6 7.1 %collective-permute-start.21 = (bf16[8192,128]{1,0:T(8,128)(2,1)S(1)}, bf16[8192,128]{1,0:T(8,128)(2,1)S(1)}, u32[]{:S(2)}, u32[]{:S(2)}) collective-permute-start(bf16[8192,128]{1,0:T(8,128)(2,1)S(1)} %get-tuple-element.37), channel_id=1, source_target_pairs={{0,1},{1,0},{2,3},{3,2},{4,5},{5,4},{6,7},{7,6},{8,9},{9,8},{10,11... | collective-permute-start | bytes 6291464 | tf_op jit(solution)/shard_map/ppermute | solution.py:23
  367.6 20.5 %collective-permute-start.12 = (bf16[8192,128]{1,0:T(8,128)(2,1)}, bf16[8192,128]{1,0:T(8,128)(2,1)S(1)}, u32[]{:S(2)}, u32[]{:S(2)}) collective-permute-start(bf16[8192,128]{1,0:T(8,128)(2,1)} %copy-done.11), channel_id=1, source_target_pairs={{0,1},{1,0},{2,3},{3,2},{4,5},{5,4},{6,7},{7,6},{8,9},{9,8},{10,11... | collective-permute-start | bytes 6291464 | tf_op jit(solution)/shard_map/ppermute | solution.py:23
  368.1 48.7 %collective-permute-start.14 = (bf16[8192,128]{1,0:T(8,128)(2,1)}, bf16[8192,128]{1,0:T(8,128)(2,1)S(1)}, u32[]{:S(2)}, u32[]{:S(2)}) collective-permute-start(bf16[8192,128]{1,0:T(8,128)(2,1)} %add_convert_fusion.1.rest_4_), channel_id=1, source_target_pairs={{0,2},{1,3},{2,0},{3,1},{4,6},{5,7},{6,4},{7,5},{8,10},{9,11},{10,... | collective-permute-start | bytes 6291464 | tf_op jit(solution)/shard_map/ppermute | solution.py:23
  369.6 50.8 %collective-permute-start.20 = (bf16[8192,128]{1,0:T(8,128)(2,1)S(1)}, bf16[8192,128]{1,0:T(8,128)(2,1)S(1)}, u32[]{:S(2)}, u32[]{:S(2)}) collective-permute-start(bf16[8192,128]{1,0:T(8,128)(2,1)S(1)} %get-tuple-element.35), channel_id=1, source_target_pairs={{0,1},{1,0},{2,3},{3,2},{4,5},{5,4},{6,7},{7,6},{8,9},{9,8},{10,11... | collective-permute-start | bytes 6291464 | tf_op jit(solution)/shard_map/ppermute | solution.py:23
  377.0 84.7 %collective-permute-start.22 = (bf16[8192,128]{1,0:T(8,128)(2,1)S(1)}, bf16[8192,128]{1,0:T(8,128)(2,1)S(1)}, u32[]{:S(2)}, u32[]{:S(2)}) collective-permute-start(bf16[8192,128]{1,0:T(8,128)(2,1)S(1)} %add_convert_fusion), channel_id=1, source_target_pairs={{0,2},{1,3},{2,0},{3,1},{4,6},{5,7},{6,4},{7,5},{8,10},{9,11},{10,... | collective-permute-start | bytes 6291464 | tf_op jit(solution)/shard_map/ppermute | solution.py:23
  382.2 3.6 collective-permute-start.25
  385.8 1.7 collective-permute-start.27
  387.5 79.9 %collective-permute-start.26 = (f32[520,128]{1,0:T(8,128)S(1)}, f32[520,128]{1,0:T(8,128)S(1)}, u32[]{:S(2)}, u32[]{:S(2)}) collective-permute-start(f32[520,128]{1,0:T(8,128)S(1)} %add.49), channel_id=1, source_target_pairs={{0,2},{1,3},{2,0},{3,1},{4,6},{5,7},{6,4},{7,5},{8,10},{9,11},{10,... | collective-permute-start | bytes 798728 | tf_op jit(solution)/shard_map/ppermute | solution.py:23
  388.1 84.1 %collective-permute-start.28 = (f32[520,128]{1,0:T(8,128)S(1)}, f32[520,128]{1,0:T(8,128)S(1)}, u32[]{:S(2)}, u32[]{:S(2)}) collective-permute-start(f32[520,128]{1,0:T(8,128)S(1)} %add.51), channel_id=1, source_target_pairs={{0,2},{1,3},{2,0},{3,1},{4,6},{5,7},{6,4},{7,5},{8,10},{9,11},{10,... | collective-permute-start | bytes 798728 | tf_op jit(solution)/shard_map/ppermute | solution.py:23
  420.4 51.9 %collective-permute-start.15 = (f32[512,128]{1,0:T(8,128)S(1)}, f32[512,128]{1,0:T(8,128)S(1)}, u32[]{:S(2)}, u32[]{:S(2)}) collective-permute-start(f32[512,128]{1,0:T(8,128)S(1)} %weight_grad.4), channel_id=1, source_target_pairs={{0,1},{1,0},{2,3},{3,2},{4,5},{5,4},{6,7},{7,6},{8,9},{9,8},{10,11... | collective-permute-start | bytes 786440 | tf_op jit(solution)/shard_map/ppermute | solution.py:23
  465.3 8.6 %collective-permute-start.23 = (f32[512,128]{1,0:T(8,128)S(1)}, f32[512,128]{1,0:T(8,128)S(1)}, u32[]{:S(2)}, u32[]{:S(2)}) collective-permute-start(f32[512,128]{1,0:T(8,128)S(1)} %weight_grad.5), channel_id=1, source_target_pairs={{0,1},{1,0},{2,3},{3,2},{4,5},{5,4},{6,7},{7,6},{8,9},{9,8},{10,11... | collective-permute-start | bytes 786440 | tf_op jit(solution)/shard_map/ppermute | solution.py:23
  472.3 9.3 %collective-permute-start.16 = (f32[512,128]{1,0:T(8,128)S(1)}, f32[512,128]{1,0:T(8,128)S(1)}, u32[]{:S(2)}, u32[]{:S(2)}) collective-permute-start(f32[512,128]{1,0:T(8,128)S(1)} %add.44), channel_id=1, source_target_pairs={{0,2},{1,3},{2,0},{3,1},{4,6},{5,7},{6,4},{7,5},{8,10},{9,11},{10,... | collective-permute-start | bytes 786440 | tf_op jit(solution)/shard_map/ppermute | solution.py:23
  473.9 11.4 %collective-permute-start.24 = (f32[512,128]{1,0:T(8,128)S(1)}, f32[512,128]{1,0:T(8,128)S(1)}, u32[]{:S(2)}, u32[]{:S(2)}) collective-permute-start(f32[512,128]{1,0:T(8,128)S(1)} %add.47), channel_id=1, source_target_pairs={{0,2},{1,3},{2,0},{3,1},{4,6},{5,7},{6,4},{7,5},{8,10},{9,11},{10,... | collective-permute-start | bytes 786440 | tf_op jit(solution)/shard_map/ppermute | solution.py:23
  (22 other events, 448.2 us)
Sparse Core Ops, SparseCore 0:
  193.9 82.1 all-gather.1

commit v4 on v3

--- a/solution.py
+++ b/solution.py
@@ -8,6 +8,7 @@
 from jax.sharding import PartitionSpec as P
 
 CHUNKS = 2
+NEAR_PIECES = 4
 MIB = 1024 * 1024
 HBM = pl.BlockSpec(memory_space=pl.ANY)
 VMEM = pl.BlockSpec(memory_space=pltpu.VMEM)
@@ -348,24 +349,28 @@
     weights_t = jnp.concatenate([w_neigh.T, w_self.T], axis=0)
     projected = project(feat_t, weights_t, CHUNKS)
 
-    gathered = []
+    direct = False
+    order = jnp.reshape(lax.axis_index("feat") if direct else 0, (1,)).astype(jnp.int32)
+    part_pres = []
     for c in range(CHUNKS):
         held = {0: projected[c]}
         for mask in reversed(masks_of(n_node)):
             for k in list(held):
-                held[k ^ mask] = swap(held[k], mask, n_node)
-        gathered.append([held[k] for k in range(n_node)])
-
-    direct = n_feat <= 4
-    order = jnp.reshape(lax.axis_index("feat") if direct else 0, (1,)).astype(jnp.int32)
-    part_pres = [
-        mean_tiles(order, src, inv, nbr, gathered[c], projected[CHUNKS + c], n_feat)
-        for c in range(CHUNKS)
-    ]
+                value = held[k]
+                if k and part_pres:
+                    value, _ = lax.optimization_barrier((value, part_pres[-1]))
+                held[k ^ mask] = swap(value, mask, n_node)
+        gathered = [held[k] for k in range(n_node)]
+        part_pres.append(
+            mean_tiles(order, src, inv, nbr, gathered, projected[CHUNKS + c], n_feat)
+        )
     hidden = None
     grad_pres, pieces = [], []
     for c in range(CHUNKS):
-        shares = reduce_shares(part_pres[c], n_feat, direct)
+        part_pre = part_pres[c]
+        if pieces:
+            part_pre, pieces[-1][-1] = lax.optimization_barrier((part_pre, pieces[-1][-1]))
+        shares = reduce_shares(part_pre, n_feat, direct)
         hidden, grad_pre = activate(
             shares, bias_row, cot_rows, hidden, c, part_pres[c + 1 : c + 2]
         )
@@ -373,7 +378,9 @@
         pieces.append(gather_shares(grad_pre, n_feat, direct and c == CHUNKS - 1))
 
     grads_n, grads_s, sums = [], [], []
-    after = [grad_pres[-1]]
+    after = []
+    arrived = None
+    sent = []
     for c in range(CHUNKS):
         *tables, piece = spread_tiles(order, src, inv, nbr, pieces[c], n_node, after)
         held = {k: [v] for k, v in enumerate(tables)}
@@ -382,15 +389,26 @@
             for k in reversed(list(held)):
                 if k & mask:
                     mine = held[k ^ mask]
-                    left[k ^ mask] = mine + [swap(total_of(held[k]), mask, n_node)]
+                    theirs = total_of(held[k])
+                    if arrived is not None and mask == 1 and k != mask:
+                        theirs, arrived = lax.optimization_barrier((theirs, arrived))
+                        sent[c - 1][-1] = arrived
+                    cut = rows // (NEAR_PIECES if mask == 1 and k != mask else 1)
+                    got = [
+                        swap(theirs[at : at + cut], mask, n_node) for at in range(0, rows, cut)
+                    ]
+                    left[k ^ mask] = mine + [got[0] if len(got) == 1 else jnp.concatenate(got)]
             held = left
             if mask == 1:
                 after = [total_of(v) for k, v in held.items() if k]
                 held = {k: [total_of(v)] if k else v for k, v in held.items()}
-        grads_n.append(sum_over_node(weight_grad(feat_t, held[0], False), n_node))
+        arrived = held[0][-1]
+        sent.append(held[0])
         both = sum_over_node(weight_grad(feat_t, [piece], True), n_node)
         grads_s.append(both[:width])
         sums.append(both[width])
+    for terms in sent:
+        grads_n.append(sum_over_node(weight_grad(feat_t, terms, False), n_node))
     return (
         hidden.reshape(1, share, hid),
         jnp.concatenate(grads_n, axis=1),

time: 502 us -> 404 us (0.80); the launches traced: 493 us -> 404 us
  waiting for transfers between devices: 310 us -> 219 us
  local copies, waits for them, and re-layouts: 21.2 us -> 33.8 us
  starting transfers between devices: 26.6 us -> 16.2 us
    ppermute x9 -> x0, waiting for transfers between devices: 129 us -> none  [the longest x6 97.1 us: reduce_shares(): lax.ppermute(part[s * share:(s + 1) * share], 'feat', [(i, (i + s) % n) f...]
    all_gather x1 -> x2, waiting for transfers between devices: 0.94 us -> 83.5 us  [gather_shares(): return [lax.all_gather(value, 'feat', axis=0, tiled=True)]]
    ppermute x20 -> x26, waiting for transfers between devices: 181 us -> 122 us  [swap(): return lax.ppermute(value, 'node', [(i, i ^ mask) for i in range(n)])]
    ppermute x9 -> x0, starting transfers between devices: 14.4 us -> none  [the longest x6 9.81 us: reduce_shares(): lax.ppermute(part[s * share:(s + 1) * share], 'feat', [(i, (i + s) % n) f...]
    reduce_scatter x0 -> x2, waiting for transfers between devices: none -> 13.5 us  [reduce_shares(): return [lax.psum_scatter(part, 'feat', scatter_dimension=0, tiled=True)]]
    unnamed x51 -> x59, local copies, waits for them, and re-layouts: 20.9 us -> 31.9 us
    ppermute x20 -> x26, starting transfers between devices: 12.2 us -> 15.9 us  [swap(): return lax.ppermute(value, 'node', [(i, i ^ mask) for i in range(n)])]
  transfers between devices with their start and end apart: 30 -> 30, of which waited for: 16 -> 21; matrix products, arithmetic and copies ran while one was open for 1% -> 2% of each run, Pallas kernels for 12% -> 26%
where the time goes in v4:
time: 404 us
  waiting for transfers between devices  219 us (54%)
  Pallas kernels  115 us (28%)
  local copies, waits for them, and re-layouts  33.8 us (8%)
  starting transfers between devices  16.2 us (4%)
  between operations  14.1 us (3%)
  other arithmetic  5.23 us (1%)
    ppermute x26, waiting for transfers between devices, swap(): return lax.ppermute(value, 'node', [(i, i ^ mask) for i in range(n)])  122 us
    all_gather x2, waiting for transfers between devices, gather_shares(): return [lax.all_gather(value, 'feat', axis=0, tiled=True)]  83.5 us
    pallas_call x2, Pallas kernels, spread_tiles(): pl.pallas_call(kernel, out_shape=[jax.ShapeDtypeStruct((rows, wide), jnp....  46.6 us
    pallas_call x2, Pallas kernels, mean_tiles(): pl.pallas_call(kernel, out_shape=jax.ShapeDtypeStruct((rows, wide), jnp.b...  42.7 us
    unnamed x59, local copies, waits for them, and re-layouts  31.9 us
    ppermute x26, starting transfers between devices, swap(): return lax.ppermute(value, 'node', [(i, i ^ mask) for i in range(n)])  15.9 us
    pallas_call x4, Pallas kernels, weight_grad(): pl.pallas_call(kernel, grid=(rows // step,), in_specs=[pl.BlockSpec((widt...  15.5 us
    reduce_scatter x2, waiting for transfers between devices, reduce_shares(): return [lax.psum_scatter(part, 'feat', scatter_dimension=0, tiled=True)]  13.5 us
  transfers between devices with their start and end apart: 30, of which 21 were waited for; matrix products, arithmetic and copies ran while one was open for 2% of the time, Pallas kernels for 26%

profile of v4, /device:TPU:0, one launch (start us, length us, event | category | flops | bytes accessed | tf_op | source)
XLA Modules:
  0.0 403.7 jit_solution(11289695039496364261)
XLA Ops:
  9.5 3.4 copy-done
  12.8 7.5 %project.1 = (bf16[128,8192]{1,0:T(8,128)(2,1)}, bf16[128,8192]{1,0:T(8,128)(2,1)S(1)}, f32[128,8192]{1,0:T(8,128)S(1)}, f32[128,8192]{1,0:T(8,128)S(1)}) custom-call(bf16[512,8192]{1,0:T(8,128)(2,1)S(1)} %copy-done, bf16[512,512]{1,0:T(8,128)(2,1)S(1)} %pad_maximum_fusion.w_ref), custom_call_target="tpu_custom_call" | custom-call | flops 4294967296 | bytes 20971520 | tf_op jit(solution)/shard_map/project/pallas_call | solution.py:65
  20.3 2.0 copy-done.21
  22.3 2.0 copy-done.23
  24.3 2.9 collective-permute-start.3
  27.3 45.9 %collective-permute-done.3.rest_2_ = bf16[128,8192]{1,0:T(8,128)(2,1)} collective-permute-done((bf16[128,8192]{1,0:T(8,128)(2,1)}, bf16[128,8192]{1,0:T(8,128)(2,1)}, u32[]{:S(2)}, u32[]{:S(2)}) %collective-permute-start.3) | collective-permute-done | bytes 2097184 | tf_op jit(solution)/shard_map/ppermute | solution.py:24
  73.2 1.7 collective-permute-start.1
  75.4 2.3 collective-permute-done.4.rest_3_
  77.7 2.2 copy-done.24
  79.9 22.1 %mean_tiles.2 = bf16[8192,128]{1,0:T(8,128)(2,1)} custom-call(s32[1]{0:T(128)} %constant.29.clone.1.order_ref, s32[64,16]{1,0:T(8,128)S(1)} %fusion.2.src_ref, f32[64]{0:T(128)S(1)} %convert_divide_fusion.inv_ref, s32[64,16,128]{2,1,0:T(8,128)S(1)} %broadcast_select_fusion.nbr_ref, f32[128,8192]{1,0:T(8,128)S(1)} %copy-done.24, ...), custom_call_target="tpu_custom_call" | custom-call | flops 17179869184 | bytes 14680064 | tf_op jit(solution)/shard_map/mean_tiles/pallas_call | solution.py:137
  102.4 19.0 %collective-permute-done.1.rest_2_ = bf16[128,8192]{1,0:T(8,128)(2,1)} collective-permute-done((bf16[128,8192]{1,0:T(8,128)(2,1)S(1)}, bf16[128,8192]{1,0:T(8,128)(2,1)}, u32[]{:S(2)}, u32[]{:S(2)}) %collective-permute-start.1) | collective-permute-done | bytes 2097184 | tf_op jit(solution)/shard_map/ppermute | solution.py:24
  121.4 4.4 %collective-permute-done.5.rest_3_ = bf16[128,8192]{1,0:T(8,128)(2,1)S(1)} collective-permute-done((bf16[128,8192]{1,0:T(8,128)(2,1)}, bf16[128,8192]{1,0:T(8,128)(2,1)S(1)}, u32[]{:S(2)}, u32[]{:S(2)}) %collective-permute-start.5) | collective-permute-done | bytes 2097184 | tf_op jit(solution)/shard_map/ppermute | solution.py:24
  127.3 2.2 copy-done.22
  129.5 20.6 %mean_tiles.3.rest_1_ = bf16[8192,128]{1,0:T(8,128)(2,1)} custom-call(s32[1]{0:T(128)} %constant.29.clone.1.order_ref, s32[64,16]{1,0:T(8,128)S(1)} %fusion.2.src_ref, f32[64]{0:T(128)S(1)} %convert_divide_fusion.inv_ref, s32[64,16,128]{2,1,0:T(8,128)S(1)} %broadcast_select_fusion.nbr_ref, f32[128,8192]{1,0:T(8,128)S(1)} %copy-done.22, ...), custom_call_target="tpu_custom_call" | custom-call | flops 17179869184 | bytes 14680064 | tf_op jit(solution)/shard_map/mean_tiles/pallas_call | solution.py:137
  151.2 1.7 activate.2
  153.0 47.5 %all-gather.3.cloned.1.call-done.rest_0_ = bf16[8192,128]{1,0:T(8,128)(2,1)} async-done(((bf16[2048,128]{1,0:T(8,128)(2,1)}), bf16[8192,128]{1,0:T(8,128)(2,1)}) %all-gather.3.cloned.1.call-update) | async-done | bytes 2097168 | tf_op jit(solution)/shard_map/all_gather | solution.py:329
  203.4 23.3 %spread_tiles.2 = (bf16[8192,128]{1,0:T(8,128)(2,1)S(1)}, bf16[8192,128]{1,0:T(8,128)(2,1)S(1)}, bf16[8192,128]{1,0:T(8,128)(2,1)S(1)}, bf16[8192,128]{1,0:T(8,128)(2,1)S(1)}, bf16[8192,128]{1,0:T(8,128)(2,1)S(1)}) custom-call(s32[1]{0:T(128)} %constant.29.clone.1.order_ref, s32[64,16]{1,0:T(8,128)S(1)} %fusion.2.src_ref, f32[64]{0:T(128)S(1)} %convert_divide_fusion.inv_ref, ...), custom_call_target="tpu_custom_call" | custom-call | flops 17179869184 | bytes 10485760 | tf_op jit(solution)/shard_map/spread_tiles/pallas_call | solution.py:258
  232.1 13.5 %reduce-scatter.5.cloned.1.call-done.rest_0_ = bf16[2048,128]{1,0:T(8,128)(2,1)} async-done(((bf16[8192,128]{1,0:T(8,128)(2,1)}), bf16[2048,128]{1,0:T(8,128)(2,1)}) %reduce-scatter.5.cloned.1.call-update) | async-done | bytes 524304 | tf_op jit(solution)/shard_map/reduce_scatter | solution.py:316
  248.6 1.8 fusion.8
  254.7 1.9 add_convert_fusion.1.rest_1_
  258.0 36.0 %all-gather.5.cloned.1.call-done.rest_0_ = bf16[8192,128]{1,0:T(8,128)(2,1)} async-done(((bf16[2048,128]{1,0:T(8,128)(2,1)}), bf16[8192,128]{1,0:T(8,128)(2,1)}) %all-gather.5.cloned.1.call-update) | async-done | bytes 2097168 | tf_op jit(solution)/shard_map/all_gather | solution.py:329
  295.6 23.3 %spread_tiles.3 = (bf16[8192,128]{1,0:T(8,128)(2,1)S(1)}, bf16[8192,128]{1,0:T(8,128)(2,1)S(1)}, bf16[8192,128]{1,0:T(8,128)(2,1)S(1)}, bf16[8192,128]{1,0:T(8,128)(2,1)S(1)}, bf16[8192,128]{1,0:T(8,128)(2,1)S(1)}) custom-call(s32[1]{0:T(128)} %constant.29.clone.1.order_ref, s32[64,16]{1,0:T(8,128)S(1)} %fusion.2.src_ref, f32[64]{0:T(128)S(1)} %convert_divide_fusion.inv_ref, ...), custom_call_target="tpu_custom_call" | custom-call | flops 17179869184 | bytes 10485760 | tf_op jit(solution)/shard_map/spread_tiles/pallas_call | solution.py:258
  325.4 3.4 copy-done.1
  328.7 3.5 weight_grad.6
  332.4 3.5 weight_grad.7
  336.5 4.8 %weight_grad.4 = f32[512,128]{1,0:T(8,128)S(1)} custom-call(bf16[512,8192]{1,0:T(8,128)(2,1)S(1)} %copy-done.1, bf16[8192,128]{1,0:T(8,128)(2,1)S(1)} %get-tuple-element.37.rest_0_, bf16[8192,128]{1,0:T(8,128)(2,1)S(1)} %collective-permute-done.6.rest_1_, bf16[8192,128]{1,0:T(8,128)(2,1)} %collective-permute-done.11.rest_2_), custom_call_target="tpu_custom_call" | custom-call | flops 1073741824 | bytes 10485760 | tf_op jit(solution)/shard_map/weight_grad/pallas_call | solution.py:300
  345.1 27.3 %collective-permute-done.19.rest_2_ = bf16[8192,128]{1,0:T(8,128)(2,1)S(1)} collective-permute-done((bf16[8192,128]{1,0:T(8,128)(2,1)S(1)}, bf16[8192,128]{1,0:T(8,128)(2,1)S(1)}, u32[]{:S(2)}, u32[]{:S(2)}) %collective-permute-start.19) | collective-permute-done | bytes 2097184 | tf_op jit(solution)/shard_map/ppermute | solution.py:24
  372.4 3.6 weight_grad.5
  376.1 2.0 collective-permute-done.23
  378.2 5.5 %collective-permute-done.13 = f32[512,128]{1,0:T(8,128)S(1)} collective-permute-done((f32[512,128]{1,0:T(8,128)S(1)}, f32[512,128]{1,0:T(8,128)S(1)}, u32[]{:S(2)}, u32[]{:S(2)}) %collective-permute-start.13) | collective-permute-done | bytes 262176 | tf_op jit(solution)/shard_map/ppermute | solution.py:24
  383.7 4.9 %collective-permute-done.25 = f32[520,128]{1,0:T(8,128)S(1)} collective-permute-done((f32[520,128]{1,0:T(8,128)S(1)}, f32[520,128]{1,0:T(8,128)S(1)}, u32[]{:S(2)}, u32[]{:S(2)}) %collective-permute-start.25) | collective-permute-done | bytes 266272 | tf_op jit(solution)/shard_map/ppermute | solution.py:24
  391.6 4.6 %collective-permute-done.21 = f32[512,128]{1,0:T(8,128)S(1)} collective-permute-done((f32[512,128]{1,0:T(8,128)S(1)}, f32[512,128]{1,0:T(8,128)S(1)}, u32[]{:S(2)}, u32[]{:S(2)}) %collective-permute-start.21) | collective-permute-done | bytes 262176 | tf_op jit(solution)/shard_map/ppermute | solution.py:24
  (126 shorter events, 39.2 us)
Async XLA Ops:
  7.2 143.0 %reduce-scatter.3.cloned.1.call-start = ((), (), s32[]{:S(2)}) async-start(), calls=%async_computation.2 | async-start | bytes 2621440 | tf_op jit(solution)/shard_map/reduce_scatter | solution.py:316
  12.8 62.3 %copy-start.25 = (s32[64,16,128]{2,1,0:T(8,128)S(1)}, s32[64,16,128]{2,1,0:T(8,128)}, u32[]{:S(2)}) copy-start(s32[64,16,128]{2,1,0:T(8,128)} %param.10) | copy-start | bytes 1572868
  24.3 77.8 %copy-start.17 = (bf16[128,8192]{1,0:T(8,128)(2,1)}, bf16[128,8192]{1,0:T(8,128)(2,1)S(1)}, u32[]{:S(2)}) copy-start(bf16[128,8192]{1,0:T(8,128)(2,1)S(1)} %get-tuple-element.28.rest_0_) | copy-start | bytes 6291460
  24.3 48.9 %collective-permute-start.3 = (bf16[128,8192]{1,0:T(8,128)(2,1)}, bf16[128,8192]{1,0:T(8,128)(2,1)}, u32[]{:S(2)}, u32[]{:S(2)}) collective-permute-start(bf16[128,8192]{1,0:T(8,128)(2,1)} %get-tuple-element.30.rest_0_), channel_id=1, source_target_pairs={{0,2},{1,3},{2,0},{3,1},{4,6},{5,7},{6,4},{7,5},{8,10},{9,11},{10,... | collective-permute-start | bytes 6291464 | tf_op jit(solution)/shard_map/ppermute | solution.py:24
  27.3 48.1 %collective-permute-start.2 = (bf16[128,8192]{1,0:T(8,128)(2,1)}, bf16[128,8192]{1,0:T(8,128)(2,1)}, u32[]{:S(2)}, u32[]{:S(2)}) collective-permute-start(bf16[128,8192]{1,0:T(8,128)(2,1)} %get-tuple-element.30.rest_0_), channel_id=1, source_target_pairs={{0,1},{1,0},{2,3},{3,2},{4,5},{5,4},{6,7},{7,6},{8,9},{9,8},{10,11... | collective-permute-start | bytes 6291464 | tf_op jit(solution)/shard_map/ppermute | solution.py:24
  73.2 4.5 %collective-permute-start.4 = (bf16[128,8192]{1,0:T(8,128)(2,1)}, bf16[128,8192]{1,0:T(8,128)(2,1)}, u32[]{:S(2)}, u32[]{:S(2)}) collective-permute-start(bf16[128,8192]{1,0:T(8,128)(2,1)} %collective-permute-done.3.rest_2_), channel_id=1, source_target_pairs={{0,1},{1,0},{2,3},{3,2},{4,5},{5,4},{6,7},{7,6},{8,9},{9,8},{10,11... | collective-permute-start | bytes 6291464 | tf_op jit(solution)/shard_map/ppermute | solution.py:24
  73.2 48.1 %collective-permute-start.1 = (bf16[128,8192]{1,0:T(8,128)(2,1)S(1)}, bf16[128,8192]{1,0:T(8,128)(2,1)}, u32[]{:S(2)}, u32[]{:S(2)}) collective-permute-start(bf16[128,8192]{1,0:T(8,128)(2,1)S(1)} %get-tuple-element.28.rest_0_), channel_id=1, source_target_pairs={{0,2},{1,3},{2,0},{3,1},{4,6},{5,7},{6,4},{7,5},{8,10},{9,11},{10,... | collective-permute-start | bytes 6291464 | tf_op jit(solution)/shard_map/ppermute | solution.py:24
  102.1 98.4 %all-gather.3.cloned.1.call-start = ((), (), s32[]{:S(2)}) async-start(), calls=%async_computation.3 | async-start | bytes 2621440 | tf_op jit(solution)/shard_map/all_gather | solution.py:329
  102.1 19.2 %collective-permute-start = (bf16[128,8192]{1,0:T(8,128)(2,1)S(1)}, bf16[128,8192]{1,0:T(8,128)(2,1)S(1)}, u32[]{:S(2)}, u32[]{:S(2)}) collective-permute-start(bf16[128,8192]{1,0:T(8,128)(2,1)S(1)} %get-tuple-element.28.rest_0_), channel_id=1, source_target_pairs={{0,1},{1,0},{2,3},{3,2},{4,5},{5,4},{6,7},{7,6},{8,9},{9,8},{10,11... | collective-permute-start | bytes 6291464 | tf_op jit(solution)/shard_map/ppermute | solution.py:24
  121.3 4.4 %collective-permute-start.5 = (bf16[128,8192]{1,0:T(8,128)(2,1)}, bf16[128,8192]{1,0:T(8,128)(2,1)S(1)}, u32[]{:S(2)}, u32[]{:S(2)}) collective-permute-start(bf16[128,8192]{1,0:T(8,128)(2,1)} %collective-permute-done.1.rest_2_), channel_id=1, source_target_pairs={{0,1},{1,0},{2,3},{3,2},{4,5},{5,4},{6,7},{7,6},{8,9},{9,8},{10,11... | collective-permute-start | bytes 6291464 | tf_op jit(solution)/shard_map/ppermute | solution.py:24
  152.9 92.6 %reduce-scatter.5.cloned.1.call-start = ((), (), s32[]{:S(2)}) async-start(), calls=%async_computation.4 | async-start | bytes 2621440 | tf_op jit(solution)/shard_map/reduce_scatter | solution.py:316
  200.5 93.5 %all-gather.5.cloned.1.call-start = ((), (), s32[]{:S(2)}) async-start(), calls=%async_computation.5 | async-start | bytes 2621440 | tf_op jit(solution)/shard_map/all_gather | solution.py:329
  250.4 2.0 collective-permute-start.10
  250.5 2.6 collective-permute-start.7
  251.0 2.9 collective-permute-start.8
  251.1 3.6 collective-permute-start.9
  256.5 62.4 %collective-permute-start.11 = (bf16[8192,128]{1,0:T(8,128)(2,1)}, bf16[8192,128]{1,0:T(8,128)(2,1)}, u32[]{:S(2)}, u32[]{:S(2)}) collective-permute-start(bf16[8192,128]{1,0:T(8,128)(2,1)} %add_convert_fusion.1.rest_1_), channel_id=1, source_target_pairs={{0,2},{1,3},{2,0},{3,1},{4,6},{5,7},{6,4},{7,5},{8,10},{9,11},{10,... | collective-permute-start | bytes 6291464 | tf_op jit(solution)/shard_map/ppermute | solution.py:24
  319.1 2.0 collective-permute-start.15
  319.1 2.6 collective-permute-start.16
  319.6 2.9 collective-permute-start.17
  319.7 3.6 collective-permute-start.18
  320.5 16.0 %collective-permute-start.6 = (bf16[8192,128]{1,0:T(8,128)(2,1)S(1)}, bf16[8192,128]{1,0:T(8,128)(2,1)S(1)}, u32[]{:S(2)}, u32[]{:S(2)}) collective-permute-start(bf16[8192,128]{1,0:T(8,128)(2,1)S(1)} %copy-done.16), channel_id=1, source_target_pairs={{0,1},{1,0},{2,3},{3,2},{4,5},{5,4},{6,7},{7,6},{8,9},{9,8},{10,11... | collective-permute-start | bytes 6291464 | tf_op jit(solution)/shard_map/ppermute | solution.py:24
  321.0 24.1 %collective-permute-start.14 = (bf16[8192,128]{1,0:T(8,128)(2,1)S(1)}, bf16[8192,128]{1,0:T(8,128)(2,1)S(1)}, u32[]{:S(2)}, u32[]{:S(2)}) collective-permute-start(bf16[8192,128]{1,0:T(8,128)(2,1)S(1)} %get-tuple-element.45), channel_id=1, source_target_pairs={{0,1},{1,0},{2,3},{3,2},{4,5},{5,4},{6,7},{7,6},{8,9},{9,8},{10,11... | collective-permute-start | bytes 6291464 | tf_op jit(solution)/shard_map/ppermute | solution.py:24
  323.8 48.5 %collective-permute-start.19 = (bf16[8192,128]{1,0:T(8,128)(2,1)S(1)}, bf16[8192,128]{1,0:T(8,128)(2,1)S(1)}, u32[]{:S(2)}, u32[]{:S(2)}) collective-permute-start(bf16[8192,128]{1,0:T(8,128)(2,1)S(1)} %add_convert_fusion), channel_id=1, source_target_pairs={{0,2},{1,3},{2,0},{3,1},{4,6},{5,7},{6,4},{7,5},{8,10},{9,11},{10,... | collective-permute-start | bytes 6291464 | tf_op jit(solution)/shard_map/ppermute | solution.py:24
  332.3 9.1 %collective-permute-start.22 = (f32[520,128]{1,0:T(8,128)S(1)}, f32[520,128]{1,0:T(8,128)S(1)}, u32[]{:S(2)}, u32[]{:S(2)}) collective-permute-start(f32[520,128]{1,0:T(8,128)S(1)} %weight_grad.6), channel_id=1, source_target_pairs={{0,1},{1,0},{2,3},{3,2},{4,5},{5,4},{6,7},{7,6},{8,9},{9,8},{10,11... | collective-permute-start | bytes 798728 | tf_op jit(solution)/shard_map/ppermute | solution.py:24
  335.9 8.1 %collective-permute-start.24 = (f32[520,128]{1,0:T(8,128)S(1)}, f32[520,128]{1,0:T(8,128)S(1)}, u32[]{:S(2)}, u32[]{:S(2)}) collective-permute-start(f32[520,128]{1,0:T(8,128)S(1)} %weight_grad.7), channel_id=1, source_target_pairs={{0,1},{1,0},{2,3},{3,2},{4,5},{5,4},{6,7},{7,6},{8,9},{9,8},{10,11... | collective-permute-start | bytes 798728 | tf_op jit(solution)/shard_map/ppermute | solution.py:24
  341.3 1.6 collective-permute-start.12
  341.4 36.7 %collective-permute-start.23 = (f32[520,128]{1,0:T(8,128)S(1)}, f32[520,128]{1,0:T(8,128)S(1)}, u32[]{:S(2)}, u32[]{:S(2)}) collective-permute-start(f32[520,128]{1,0:T(8,128)S(1)} %add.53), channel_id=1, source_target_pairs={{0,2},{1,3},{2,0},{3,1},{4,6},{5,7},{6,4},{7,5},{8,10},{9,11},{10,... | collective-permute-start | bytes 798728 | tf_op jit(solution)/shard_map/ppermute | solution.py:24
  342.9 40.8 %collective-permute-start.13 = (f32[512,128]{1,0:T(8,128)S(1)}, f32[512,128]{1,0:T(8,128)S(1)}, u32[]{:S(2)}, u32[]{:S(2)}) collective-permute-start(f32[512,128]{1,0:T(8,128)S(1)} %add.48), channel_id=1, source_target_pairs={{0,2},{1,3},{2,0},{3,1},{4,6},{5,7},{6,4},{7,5},{8,10},{9,11},{10,... | collective-permute-start | bytes 786440 | tf_op jit(solution)/shard_map/ppermute | solution.py:24
  344.0 44.6 %collective-permute-start.25 = (f32[520,128]{1,0:T(8,128)S(1)}, f32[520,128]{1,0:T(8,128)S(1)}, u32[]{:S(2)}, u32[]{:S(2)}) collective-permute-start(f32[520,128]{1,0:T(8,128)S(1)} %add.55), channel_id=1, source_target_pairs={{0,2},{1,3},{2,0},{3,1},{4,6},{5,7},{6,4},{7,5},{8,10},{9,11},{10,... | collective-permute-start | bytes 798728 | tf_op jit(solution)/shard_map/ppermute | solution.py:24
  376.0 12.7 %collective-permute-start.20 = (f32[512,128]{1,0:T(8,128)S(1)}, f32[512,128]{1,0:T(8,128)S(1)}, u32[]{:S(2)}, u32[]{:S(2)}) collective-permute-start(f32[512,128]{1,0:T(8,128)S(1)} %weight_grad.5), channel_id=1, source_target_pairs={{0,1},{1,0},{2,3},{3,2},{4,5},{5,4},{6,7},{7,6},{8,9},{9,8},{10,11... | collective-permute-start | bytes 786440 | tf_op jit(solution)/shard_map/ppermute | solution.py:24
  388.7 7.6 %collective-permute-start.21 = (f32[512,128]{1,0:T(8,128)S(1)}, f32[512,128]{1,0:T(8,128)S(1)}, u32[]{:S(2)}, u32[]{:S(2)}) collective-permute-start(f32[512,128]{1,0:T(8,128)S(1)} %add.51), channel_id=1, source_target_pairs={{0,2},{1,3},{2,0},{3,1},{4,6},{5,7},{6,4},{7,5},{8,10},{9,11},{10,... | collective-permute-start | bytes 786440 | tf_op jit(solution)/shard_map/ppermute | solution.py:24
  (26 other events, 294.2 us)
Sparse Core Ops, SparseCore 0:
  102.2 45.3 reduce-scatter.2
  153.1 47.4 all-gather.2
  202.9 42.5 reduce-scatter.4
  248.7 45.2 all-gather.4

commit v5 on v4

--- a/solution.py
+++ b/solution.py
@@ -9,6 +9,7 @@
 
 CHUNKS = 2
 NEAR_PIECES = 4
+RING_CUTS = 2
 MIB = 1024 * 1024
 HBM = pl.BlockSpec(memory_space=pl.ANY)
 VMEM = pl.BlockSpec(memory_space=pltpu.VMEM)
@@ -52,53 +53,57 @@
     return lax.broadcasted_iota(jnp.int32, (side, side), 0).astype(jnp.float32).astype(jnp.bfloat16)
 
 
-def project(feat_t, weights_t, n):
+def project(feat_t, weight, n, dtype, after):
     width, rows = feat_t.shape
-    wide = weights_t.shape[0] // (2 * n)
+    hid = weight.shape[1]
+    wide = hid // n
     step = min(1024, rows)
 
-    def kernel(feat_ref, w_ref, *outs):
-        value = jnp.dot(w_ref[...], feat_ref[...], preferred_element_type=jnp.float32)
-        for c in range(2 * n):
-            outs[c][...] = value[c * wide : (c + 1) * wide, :].astype(outs[c].dtype)
+    def kernel(feat_ref, w_ref, *rest):
+        outs, turned = rest[len(after) : len(after) + n], rest[-1]
+
+        @pl.when(pl.program_id(0) == 0)
+        def _():
+            turned[...] = w_ref[...].astype(jnp.float32).T.astype(jnp.bfloat16)
+
+        value = jnp.dot(turned[...], feat_ref[...], preferred_element_type=jnp.float32)
+        for c in range(n):
+            outs[c][...] = value[c * wide : (c + 1) * wide, :].astype(dtype)
 
     return pl.pallas_call(
         kernel,
         grid=(rows // step,),
         in_specs=[
             pl.BlockSpec((width, step), lambda i: (0, i)),
-            pl.BlockSpec(weights_t.shape, lambda i: (0, 0)),
-        ],
-        out_specs=[pl.BlockSpec((wide, step), lambda i: (0, i))] * (2 * n),
-        out_shape=[jax.ShapeDtypeStruct((wide, rows), jnp.bfloat16)] * n
-        + [jax.ShapeDtypeStruct((wide, rows), jnp.float32)] * n,
-        compiler_params=PARAMS,
-        cost_estimate=cost(
-            2 * width * rows * weights_t.shape[0], 2 * width * rows + 6 * n * wide * rows
-        ),
+            pl.BlockSpec(weight.shape, lambda i: (0, 0)),
+        ]
+        + [HBM] * len(after),
+        out_specs=[pl.BlockSpec((wide, step), lambda i: (0, i))] * n,
+        out_shape=[jax.ShapeDtypeStruct((wide, rows), dtype)] * n,
+        scratch_shapes=[pltpu.VMEM((hid, width), jnp.bfloat16)],
+        compiler_params=pltpu.CompilerParams(vmem_limit_bytes=24 * MIB),
+        cost_estimate=cost(2 * width * rows * hid, 2 * width * rows + 4 * hid * rows),
         name="project",
-    )(feat_t, weights_t)
-
-
-def mean_tiles(order, src, inv, nbr, parts, self_term, n_feat):
+    )(feat_t, weight, *after)
+
+
+def mean_tiles(src, inv, nbr, parts, self_term, n_feat):
     n = len(parts)
     wide, rows = self_term.shape
     blocks, slots, side = nbr.shape
     share = rows // n_feat
     per_share = blocks // n_feat
 
-    def kernel(order_ref, src_ref, inv_ref, nbr_ref, self_hbm, *rest):
+    def kernel(src_ref, inv_ref, nbr_ref, self_ref, *rest):
         part_refs = rest[:n]
-        out_hbm, table, self_ref, ready, sems, out_sems = rest[n:]
-        copies = [
-            pltpu.make_async_copy(ref, table.at[:, pl.ds(k * rows, rows)], sems.at[k])
-            for k, ref in enumerate(part_refs)
-        ]
-        copies.append(pltpu.make_async_copy(self_hbm, self_ref, sems.at[n]))
-        for copy in copies:
-            copy.start()
-        for copy in copies:
-            copy.wait()
+        out_hbm, table, ready, out_sems = rest[n:]
+        for k, ref in enumerate(part_refs):
+
+            @pl.loop(0, rows // side, unroll=4)
+            def _(i, k=k, ref=ref):
+                at = pl.multiple_of(i * side, side)
+                table[:, pl.ds(k * rows + at, side)] = ref[:, pl.ds(at, side)]
+
         ids = side_ids(side)
 
         def out_copy(s):
@@ -107,11 +112,9 @@
 
         @pl.loop(0, n_feat)
         def _(s):
-            first = lax.rem(order_ref[0] + s, n_feat) * per_share
-
             @pl.loop(0, per_share, unroll=2)
             def _(i):
-                b = first + i
+                b = s * per_share + i
                 picked = []
                 tiles = []
                 for t in range(slots):
@@ -125,7 +128,7 @@
                 )
                 own = self_ref[:, pl.ds(pl.multiple_of(b * side, side), side)]
                 pre_t = total * inv_ref[b] + own
-                at = pl.multiple_of((s * per_share + i) * side, side)
+                at = pl.multiple_of(b * side, side)
                 ready[pl.ds(at, side), :] = pre_t.T.astype(jnp.bfloat16)
 
             out_copy(s).start()
@@ -137,21 +140,19 @@
     return pl.pallas_call(
         kernel,
         out_shape=jax.ShapeDtypeStruct((rows, wide), jnp.bfloat16),
-        in_specs=[SMEM, SMEM, SMEM, VMEM, HBM] + [HBM] * n,
+        in_specs=[SMEM, SMEM, VMEM, VMEM] + [VMEM] * n,
         out_specs=HBM,
         scratch_shapes=[
             pltpu.VMEM((wide, n * rows), jnp.bfloat16),
-            pltpu.VMEM((wide, rows), jnp.float32),
             pltpu.VMEM((rows, wide), jnp.bfloat16),
-            pltpu.SemaphoreType.DMA((n + 1,)),
             pltpu.SemaphoreType.DMA((n_feat,)),
         ],
-        compiler_params=pltpu.CompilerParams(vmem_limit_bytes=24 * MIB),
+        compiler_params=pltpu.CompilerParams(vmem_limit_bytes=32 * MIB),
         cost_estimate=cost(
             8 * blocks * slots * side * side * wide, 2 * n * rows * wide + 6 * rows * wide
         ),
         name="mean_tiles",
-    )(order, src, inv, nbr, self_term, *parts)
+    )(src, inv, nbr, self_term, *parts)
 
 
 def activate(shares, bias, cot, hidden, c, after):
@@ -189,10 +190,11 @@
 
 
 def spread_tiles(order, src, inv, nbr, pieces, n, after):
-    wide = pieces[0].shape[1]
-    share = pieces[0].shape[0]
-    m = len(pieces)
-    rows = m * share
+    cut, wide = pieces[0][0].shape
+    shares, cuts = len(pieces), len(pieces[0])
+    m = shares * cuts
+    rows = m * cut
+    pieces = [piece for share in pieces for piece in share]
     blocks, slots, side = nbr.shape
     step = 512
     assert slots % 2 == 0
@@ -202,10 +204,9 @@
         table, grad_ref, ready, sems, out_sems = rest[m + len(after) + n + 1 :]
         loads = []
         for s in range(m):
-            at = pl.multiple_of(lax.rem(order_ref[0] + s, m) * share, share)
-            loads.append(
-                pltpu.make_async_copy(rest[s], grad_ref.at[pl.ds(at, share), :], sems.at[s])
-            )
+            at = lax.rem(order_ref[0] + s // cuts, shares) * (cuts * cut) + s % cuts * cut
+            place = pl.ds(pl.multiple_of(at, cut), cut)
+            loads.append(pltpu.make_async_copy(rest[s], grad_ref.at[place, :], sems.at[s]))
         for load in loads:
             load.start()
         ids = side_ids(side)
@@ -310,27 +311,16 @@
     )(feat_t, *grads)
 
 
-def reduce_shares(part, n, direct):
-    share = part.shape[0] // n
-    if not direct:
-        return [lax.psum_scatter(part, "feat", scatter_dimension=0, tiled=True)]
-    got = [part[:share]]
-    for s in range(1, n):
-        got.append(
-            lax.ppermute(
-                part[s * share : (s + 1) * share], "feat", [(i, (i + s) % n) for i in range(n)]
-            )
+def gather_shares(value, n, ring):
+    if not ring:
+        return [[lax.all_gather(value, "feat", axis=0, tiled=True)]]
+    cut = value.shape[0] // RING_CUTS
+    steps = [[value[h * cut : (h + 1) * cut] for h in range(RING_CUTS)]]
+    for _ in range(n - 1):
+        steps.append(
+            [lax.ppermute(v, "feat", [(i, (i - 1) % n) for i in range(n)]) for v in steps[-1]]
         )
-    return got
-
-
-def gather_shares(value, n, direct):
-    if not direct:
-        return [lax.all_gather(value, "feat", axis=0, tiled=True)]
-    got = [value]
-    for s in range(1, n):
-        got.append(lax.ppermute(value, "feat", [((i + s) % n, i) for i in range(n)]))
-    return got
+    return steps
 
 
 def on_device(n_node, n_feat, feat_t, src_blocks, nbr_rows, tile_counts, w_neigh, w_self, bias, cotangent):
@@ -346,43 +336,51 @@
     cot_rows = cotangent.reshape(share, hid)
     bias_row = bias[None, :]
 
-    weights_t = jnp.concatenate([w_neigh.T, w_self.T], axis=0)
-    projected = project(feat_t, weights_t, CHUNKS)
-
-    direct = False
-    order = jnp.reshape(lax.axis_index("feat") if direct else 0, (1,)).astype(jnp.int32)
+    projected = project(feat_t, w_neigh, CHUNKS, jnp.bfloat16, [])
+    own_terms = project(feat_t, w_self, CHUNKS, jnp.float32, projected[:1])
+
+    ring = n_feat <= 4
+    feat_index = jnp.reshape(lax.axis_index("feat"), (1,)).astype(jnp.int32)
+    in_place = jnp.zeros((1,), jnp.int32)
     part_pres = []
     for c in range(CHUNKS):
         held = {0: projected[c]}
         for mask in reversed(masks_of(n_node)):
             for k in list(held):
                 value = held[k]
-                if k and part_pres:
-                    value, _ = lax.optimization_barrier((value, part_pres[-1]))
+                if k:
+                    behind = part_pres[-1] if part_pres else own_terms[0]
+                    value, _ = lax.optimization_barrier((value, behind))
                 held[k ^ mask] = swap(value, mask, n_node)
         gathered = [held[k] for k in range(n_node)]
         part_pres.append(
-            mean_tiles(order, src, inv, nbr, gathered, projected[CHUNKS + c], n_feat)
+            mean_tiles(src, inv, nbr, gathered, own_terms[c], n_feat)
         )
     hidden = None
     grad_pres, pieces = [], []
     for c in range(CHUNKS):
         part_pre = part_pres[c]
-        if pieces:
-            part_pre, pieces[-1][-1] = lax.optimization_barrier((part_pre, pieces[-1][-1]))
-        shares = reduce_shares(part_pre, n_feat, direct)
+        shares = [lax.psum_scatter(part_pre, "feat", scatter_dimension=0, tiled=True)]
         hidden, grad_pre = activate(
             shares, bias_row, cot_rows, hidden, c, part_pres[c + 1 : c + 2]
         )
         grad_pres.append(grad_pre)
-        pieces.append(gather_shares(grad_pre, n_feat, direct and c == CHUNKS - 1))
+        pieces.append(gather_shares(grad_pre, n_feat, ring))
 
     grads_n, grads_s, sums = [], [], []
-    after = []
+    after = [grad_pres[-1]]
     arrived = None
     sent = []
     for c in range(CHUNKS):
-        *tables, piece = spread_tiles(order, src, inv, nbr, pieces[c], n_node, after)
+        *tables, piece = spread_tiles(
+            feat_index if len(pieces[c]) > 1 else in_place,
+            src,
+            inv,
+            nbr,
+            pieces[c],
+            n_node,
+            after,
+        )
         held = {k: [v] for k, v in enumerate(tables)}
         for mask in masks_of(n_node):
             left = {}

time: 404 us -> 412 us (1.020)
  starting transfers between devices: 16.2 us -> 48.3 us
  waiting for transfers between devices: 219 us -> 196 us
  local copies, waits for them, and re-layouts: 33.8 us -> 23.5 us
  Pallas kernels: 115 us -> 122 us
    all_gather x2 -> x0, waiting for transfers between devices: 83.5 us -> none  [gather_shares(): return [lax.all_gather(value, 'feat', axis=0, tiled=True)]]
    ppermute x0 -> x12, waiting for transfers between devices: none -> 61.1 us  [gather_shares(): lax.ppermute(v, 'feat', [(i, (i - 1) % n) for i in range(n)])]
    ppermute x0 -> x12, starting transfers between devices: none -> 32.7 us  [gather_shares(): lax.ppermute(v, 'feat', [(i, (i - 1) % n) for i in range(n)])]
    unnamed x59 -> x65, local copies, waits for them, and re-layouts: 31.9 us -> 23.1 us
    pallas_call x1 -> x2, Pallas kernels: 7.48 us -> 10.5 us  [project(): pl.pallas_call(kernel, grid=(rows // step,), in_specs=[pl.BlockSpec((widt...]
  transfers between devices with their start and end apart: 30 -> 40, of which waited for: 21 -> 26; matrix products, arithmetic and copies ran while one was open for 2% -> 2% of each run, Pallas kernels for 26% -> 23%
where the time goes in v5:
time: 412 us; the launch traced here: 411 us
  waiting for transfers between devices  196 us (48%)
  Pallas kernels  122 us (30%)
  starting transfers between devices  48.3 us (12%)
  local copies, waits for them, and re-layouts  23.5 us (6%)
  between operations  14.5 us (4%)
  other arithmetic  6.96 us (2%)
    ppermute x26, waiting for transfers between devices, swap(): return lax.ppermute(value, 'node', [(i, i ^ mask) for i in range(n)])  118 us
    ppermute x12, waiting for transfers between devices, gather_shares(): lax.ppermute(v, 'feat', [(i, (i - 1) % n) for i in range(n)])  61.1 us
    pallas_call x2, Pallas kernels, spread_tiles(): pl.pallas_call(kernel, out_shape=[jax.ShapeDtypeStruct((rows, wide), jnp....  46.7 us
    pallas_call x2, Pallas kernels, mean_tiles(): pl.pallas_call(kernel, out_shape=jax.ShapeDtypeStruct((rows, wide), jnp.b...  46.6 us
    ppermute x12, starting transfers between devices, gather_shares(): lax.ppermute(v, 'feat', [(i, (i - 1) % n) for i in range(n)])  32.7 us
    unnamed x65, local copies, waits for them, and re-layouts  23.1 us
    reduce_scatter x2, waiting for transfers between devices, on_device(): lax.psum_scatter(part_pre, 'feat', scatter_dimension=0, tiled=True)  16.9 us
    pallas_call x4, Pallas kernels, weight_grad(): pl.pallas_call(kernel, grid=(rows // step,), in_specs=[pl.BlockSpec((widt...  15.5 us
  transfers between devices with their start and end apart: 40, of which 26 were waited for; matrix products, arithmetic and copies ran while one was open for 2% of the time, Pallas kernels for 23%

profile of v5, /device:TPU:0, one launch (start us, length us, event | category | flops | bytes accessed | tf_op | source)
XLA Modules:
  0.0 411.1 jit_solution(578415977220279726)
XLA Ops:
  11.5 5.7 %project.2 = (bf16[128,8192]{1,0:T(8,128)(2,1)S(1)}, bf16[128,8192]{1,0:T(8,128)(2,1)}) custom-call(bf16[512,8192]{1,0:T(8,128)(2,1)S(1)} %copy-done, bf16[512,256]{1,0:T(8,128)(2,1)S(1)} %copy-done.7), custom_call_target="tpu_custom_call" | custom-call | flops 2147483648 | bytes 16777216 | tf_op jit(solution)/shard_map/project/pallas_call | solution.py:73
  20.2 4.8 %project.3 = (f32[128,8192]{1,0:T(8,128)S(1)}, f32[128,8192]{1,0:T(8,128)S(1)}) custom-call(bf16[512,8192]{1,0:T(8,128)(2,1)S(1)} %copy-done, bf16[512,256]{1,0:T(8,128)(2,1)S(1)} %copy-done.10, bf16[128,8192]{1,0:T(8,128)(2,1)S(1)} %get-tuple-element.26.rest_0_), custom_call_target="tpu_custom_call" | custom-call | flops 2147483648 | bytes 16777216 | tf_op jit(solution)/shard_map/project/pallas_call | solution.py:73
  29.0 36.9 %collective-permute-done.3.rest_2_ = bf16[128,8192]{1,0:T(8,128)(2,1)} collective-permute-done((bf16[128,8192]{1,0:T(8,128)(2,1)S(1)}, bf16[128,8192]{1,0:T(8,128)(2,1)}, u32[]{:S(2)}, u32[]{:S(2)}) %collective-permute-start.3) | collective-permute-done | bytes 2097184 | tf_op jit(solution)/shard_map/ppermute | solution.py:25
  72.6 23.6 %mean_tiles.2 = bf16[8192,128]{1,0:T(8,128)(2,1)} custom-call(s32[64,16]{1,0:T(8,128)S(1)} %fusion.2.src_ref, f32[64]{0:T(128)S(1)} %convert_divide_fusion.inv_ref, s32[64,16,128]{2,1,0:T(8,128)S(1)} %broadcast_select_fusion.nbr_ref, f32[128,8192]{1,0:T(8,128)S(1)} %copy-done.15, bf16[128,8192]{1,0:T(8,128)(2,1)S(1)} %get-tuple-element.26.rest_0_, ...), custom_call_target="tpu_custom_call" | custom-call | flops 17179869184 | bytes 14680064 | tf_op jit(solution)/shard_map/mean_tiles/pallas_call | solution.py:140
  96.5 17.8 %collective-permute-done.1.rest_2_ = bf16[128,8192]{1,0:T(8,128)(2,1)} collective-permute-done((bf16[128,8192]{1,0:T(8,128)(2,1)}, bf16[128,8192]{1,0:T(8,128)(2,1)}, u32[]{:S(2)}, u32[]{:S(2)}) %collective-permute-start.1) | collective-permute-done | bytes 2097184 | tf_op jit(solution)/shard_map/ppermute | solution.py:25
  114.3 4.4 %collective-permute-done.5.rest_3_ = bf16[128,8192]{1,0:T(8,128)(2,1)S(1)} collective-permute-done((bf16[128,8192]{1,0:T(8,128)(2,1)}, bf16[128,8192]{1,0:T(8,128)(2,1)S(1)}, u32[]{:S(2)}, u32[]{:S(2)}) %collective-permute-start.5) | collective-permute-done | bytes 2097184 | tf_op jit(solution)/shard_map/ppermute | solution.py:25
  120.9 23.0 %mean_tiles.3.rest_1_ = bf16[8192,128]{1,0:T(8,128)(2,1)} custom-call(s32[64,16]{1,0:T(8,128)S(1)} %fusion.2.src_ref, f32[64]{0:T(128)S(1)} %convert_divide_fusion.inv_ref, s32[64,16,128]{2,1,0:T(8,128)S(1)} %broadcast_select_fusion.nbr_ref, f32[128,8192]{1,0:T(8,128)S(1)} %copy-done.13, bf16[128,8192]{1,0:T(8,128)(2,1)} %get-tuple-element.28.rest_0_, ...), custom_call_target="tpu_custom_call" | custom-call | flops 17179869184 | bytes 14680064 | tf_op jit(solution)/shard_map/mean_tiles/pallas_call | solution.py:140
  147.4 3.9 collective-permute-start.6
  151.7 11.5 %collective-permute-done.6.rest_2_ = bf16[1024,128]{1,0:T(8,128)(2,1)S(1)} collective-permute-done((bf16[1024,128]{1,0:T(8,128)(2,1)S(1)}, bf16[1024,128]{1,0:T(8,128)(2,1)S(1)}, u32[]{:S(2)}, u32[]{:S(2)}) %collective-permute-start.6) | collective-permute-done | bytes 262176 | tf_op jit(solution)/shard_map/ppermute | solution.py:321
  163.2 4.3 %collective-permute-start.8 = (bf16[1024,128]{1,0:T(8,128)(2,1)S(1)}, bf16[1024,128]{1,0:T(8,128)(2,1)S(1)}, u32[]{:S(2)}, u32[]{:S(2)}) collective-permute-start(bf16[1024,128]{1,0:T(8,128)(2,1)S(1)} %collective-permute-done.6.rest_2_), channel_id=1, source_target_pairs={{0,12},{4,0},{8,4},{12,8},{1,13},{5,1},{9,5},{13,9},{2,14},{6,2},{... | collective-permute-start | bytes 786440 | tf_op jit(solution)/shard_map/ppermute | solution.py:321
  167.5 9.0 %collective-permute-done.7.rest_3_ = bf16[1024,128]{1,0:T(8,128)(2,1)S(1)} collective-permute-done((bf16[1024,128]{1,0:T(8,128)(2,1)S(1)}, bf16[1024,128]{1,0:T(8,128)(2,1)S(1)}, u32[]{:S(2)}, u32[]{:S(2)}) %collective-permute-start.7) | collective-permute-done | bytes 262176 | tf_op jit(solution)/shard_map/ppermute | solution.py:321
  178.7 12.8 %collective-permute-done.8.rest_4_ = bf16[1024,128]{1,0:T(8,128)(2,1)S(1)} collective-permute-done((bf16[1024,128]{1,0:T(8,128)(2,1)S(1)}, bf16[1024,128]{1,0:T(8,128)(2,1)S(1)}, u32[]{:S(2)}, u32[]{:S(2)}) %collective-permute-start.8) | collective-permute-done | bytes 262176 | tf_op jit(solution)/shard_map/ppermute | solution.py:321
  191.5 11.2 %collective-permute-done.9.rest_5_ = bf16[1024,128]{1,0:T(8,128)(2,1)S(1)} collective-permute-done((bf16[1024,128]{1,0:T(8,128)(2,1)S(1)}, bf16[1024,128]{1,0:T(8,128)(2,1)S(1)}, u32[]{:S(2)}, u32[]{:S(2)}) %collective-permute-start.9) | collective-permute-done | bytes 262176 | tf_op jit(solution)/shard_map/ppermute | solution.py:321
  202.7 16.8 %reduce-scatter.3.cloned.1.call-done.rest_0_ = bf16[2048,128]{1,0:T(8,128)(2,1)} async-done(((bf16[8192,128]{1,0:T(8,128)(2,1)}), bf16[2048,128]{1,0:T(8,128)(2,1)}) %reduce-scatter.3.cloned.1.call-update) | async-done | bytes 524304 | tf_op jit(solution)/shard_map/reduce_scatter | solution.py:363
  226.7 23.3 %spread_tiles.2 = (bf16[8192,128]{1,0:T(8,128)(2,1)S(1)}, bf16[8192,128]{1,0:T(8,128)(2,1)S(1)}, bf16[8192,128]{1,0:T(8,128)(2,1)S(1)}, bf16[8192,128]{1,0:T(8,128)(2,1)S(1)}, bf16[8192,128]{1,0:T(8,128)(2,1)S(1)}) custom-call(s32[1]{0:T(128)} %bitcast.3.order_ref, s32[64,16]{1,0:T(8,128)S(1)} %fusion.2.src_ref, f32[64]{0:T(128)S(1)} %convert_divide_fusion.inv_ref, ...), custom_call_target="tpu_custom_call" | custom-call | flops 17179869184 | bytes 10485760 | tf_op jit(solution)/shard_map/spread_tiles/pallas_call | solution.py:259
  252.1 4.7 %collective-permute-start.13 = (bf16[1024,128]{1,0:T(8,128)(2,1)S(1)}, bf16[1024,128]{1,0:T(8,128)(2,1)S(1)}, u32[]{:S(2)}, u32[]{:S(2)}) collective-permute-start(bf16[1024,128]{1,0:T(8,128)(2,1)S(1)} %get-tuple-element.59.rest_0_), channel_id=1, source_target_pairs={{0,12},{4,0},{8,4},{12,8},{1,13},{5,1},{9,5},{13,9},{2,14},{6,2},{... | collective-permute-start | bytes 786440 | tf_op jit(solution)/shard_map/ppermute | solution.py:321
  257.8 4.4 %collective-permute-done.13.rest_2_ = bf16[1024,128]{1,0:T(8,128)(2,1)S(1)} collective-permute-done((bf16[1024,128]{1,0:T(8,128)(2,1)S(1)}, bf16[1024,128]{1,0:T(8,128)(2,1)S(1)}, u32[]{:S(2)}, u32[]{:S(2)}) %collective-permute-start.13) | collective-permute-done | bytes 262176 | tf_op jit(solution)/shard_map/ppermute | solution.py:321
  262.2 4.3 %collective-permute-start.14 = (bf16[1024,128]{1,0:T(8,128)(2,1)S(1)}, bf16[1024,128]{1,0:T(8,128)(2,1)S(1)}, u32[]{:S(2)}, u32[]{:S(2)}) collective-permute-start(bf16[1024,128]{1,0:T(8,128)(2,1)S(1)} %get-tuple-element.58.rest_1_), channel_id=1, source_target_pairs={{0,12},{4,0},{8,4},{12,8},{1,13},{5,1},{9,5},{13,9},{2,14},{6,2},{... | collective-permute-start | bytes 786440 | tf_op jit(solution)/shard_map/ppermute | solution.py:321
  266.4 4.5 %collective-permute-done.14.rest_3_ = bf16[1024,128]{1,0:T(8,128)(2,1)S(1)} collective-permute-done((bf16[1024,128]{1,0:T(8,128)(2,1)S(1)}, bf16[1024,128]{1,0:T(8,128)(2,1)S(1)}, u32[]{:S(2)}, u32[]{:S(2)}) %collective-permute-start.14) | collective-permute-done | bytes 262176 | tf_op jit(solution)/shard_map/ppermute | solution.py:321
  270.9 4.3 %collective-permute-start.15 = (bf16[1024,128]{1,0:T(8,128)(2,1)S(1)}, bf16[1024,128]{1,0:T(8,128)(2,1)S(1)}, u32[]{:S(2)}, u32[]{:S(2)}) collective-permute-start(bf16[1024,128]{1,0:T(8,128)(2,1)S(1)} %collective-permute-done.13.rest_2_), channel_id=1, source_target_pairs={{0,12},{4,0},{8,4},{12,8},{1,13},{5,1},{9,5},{13,9},{2,14},{6,2},{... | collective-permute-start | bytes 786440 | tf_op jit(solution)/shard_map/ppermute | solution.py:321
  282.0 4.3 %collective-permute-start.17 = (bf16[1024,128]{1,0:T(8,128)(2,1)S(1)}, bf16[1024,128]{1,0:T(8,128)(2,1)S(1)}, u32[]{:S(2)}, u32[]{:S(2)}) collective-permute-start(bf16[1024,128]{1,0:T(8,128)(2,1)S(1)} %collective-permute-done.15.rest_4_), channel_id=1, source_target_pairs={{0,12},{4,0},{8,4},{12,8},{1,13},{5,1},{9,5},{13,9},{2,14},{6,2},{... | collective-permute-start | bytes 786440 | tf_op jit(solution)/shard_map/ppermute | solution.py:321
  287.6 4.3 %collective-permute-start.18 = (bf16[1024,128]{1,0:T(8,128)(2,1)S(1)}, bf16[1024,128]{1,0:T(8,128)(2,1)S(1)}, u32[]{:S(2)}, u32[]{:S(2)}) collective-permute-start(bf16[1024,128]{1,0:T(8,128)(2,1)S(1)} %collective-permute-done.16.rest_5_), channel_id=1, source_target_pairs={{0,12},{4,0},{8,4},{12,8},{1,13},{5,1},{9,5},{13,9},{2,14},{6,2},{... | collective-permute-start | bytes 786440 | tf_op jit(solution)/shard_map/ppermute | solution.py:321
  295.8 23.4 %spread_tiles.3 = (bf16[8192,128]{1,0:T(8,128)(2,1)S(1)}, bf16[8192,128]{1,0:T(8,128)(2,1)S(1)}, bf16[8192,128]{1,0:T(8,128)(2,1)S(1)}, bf16[8192,128]{1,0:T(8,128)(2,1)S(1)}, bf16[8192,128]{1,0:T(8,128)(2,1)S(1)}) custom-call(s32[1]{0:T(128)} %bitcast.3.order_ref, s32[64,16]{1,0:T(8,128)S(1)} %fusion.2.src_ref, f32[64]{0:T(128)S(1)} %convert_divide_fusion.inv_ref, ...), custom_call_target="tpu_custom_call" | custom-call | flops 17179869184 | bytes 10485760 | tf_op jit(solution)/shard_map/spread_tiles/pallas_call | solution.py:259
  319.2 4.4 %collective-permute-done.23.rest_2_ = bf16[8192,128]{1,0:T(8,128)(2,1)} collective-permute-done((bf16[8192,128]{1,0:T(8,128)(2,1)}, bf16[8192,128]{1,0:T(8,128)(2,1)}, u32[]{:S(2)}, u32[]{:S(2)}) %collective-permute-start.23) | collective-permute-done | bytes 2097184 | tf_op jit(solution)/shard_map/ppermute | solution.py:25
  332.8 3.5 weight_grad.6
  336.4 3.5 weight_grad.7
  342.8 4.8 %weight_grad.4 = f32[512,128]{1,0:T(8,128)S(1)} custom-call(bf16[512,8192]{1,0:T(8,128)(2,1)S(1)} %bitcast.9, bf16[8192,128]{1,0:T(8,128)(2,1)S(1)} %get-tuple-element.36.rest_0_, bf16[8192,128]{1,0:T(8,128)(2,1)S(1)} %collective-permute-done.12.rest_1_, bf16[8192,128]{1,0:T(8,128)(2,1)} %collective-permute-done.23.rest_2_), custom_call_target="tpu_custom_call" | custom-call | flops 1073741824 | bytes 10485760 | tf_op jit(solution)/shard_map/weight_grad/pallas_call | solution.py:301
  347.7 31.8 %collective-permute-done.31.rest_2_ = bf16[8192,128]{1,0:T(8,128)(2,1)S(1)} collective-permute-done((bf16[8192,128]{1,0:T(8,128)(2,1)S(1)}, bf16[8192,128]{1,0:T(8,128)(2,1)S(1)}, u32[]{:S(2)}, u32[]{:S(2)}) %collective-permute-start.31) | collective-permute-done | bytes 2097184 | tf_op jit(solution)/shard_map/ppermute | solution.py:25
  379.5 3.6 weight_grad.5
  385.3 4.8 %collective-permute-done.37 = f32[520,128]{1,0:T(8,128)S(1)} collective-permute-done((f32[520,128]{1,0:T(8,128)S(1)}, f32[520,128]{1,0:T(8,128)S(1)}, u32[]{:S(2)}, u32[]{:S(2)}) %collective-permute-start.37) | collective-permute-done | bytes 266272 | tf_op jit(solution)/shard_map/ppermute | solution.py:25
  393.8 5.7 %collective-permute-done.25 = f32[512,128]{1,0:T(8,128)S(1)} collective-permute-done((f32[512,128]{1,0:T(8,128)S(1)}, f32[512,128]{1,0:T(8,128)S(1)}, u32[]{:S(2)}, u32[]{:S(2)}) %collective-permute-start.25) | collective-permute-done | bytes 262176 | tf_op jit(solution)/shard_map/ppermute | solution.py:25
  399.6 3.9 collective-permute-done.33
  (153 shorter events, 67.5 us)
Async XLA Ops:
  7.2 136.7 %reduce-scatter.5.cloned.1.call-start = ((), (), s32[]{:S(2)}) async-start(), calls=%async_computation.3 | async-start | bytes 2621440 | tf_op jit(solution)/shard_map/reduce_scatter | solution.py:363
  17.3 48.7 %collective-permute-start.3 = (bf16[128,8192]{1,0:T(8,128)(2,1)S(1)}, bf16[128,8192]{1,0:T(8,128)(2,1)}, u32[]{:S(2)}, u32[]{:S(2)}) collective-permute-start(bf16[128,8192]{1,0:T(8,128)(2,1)S(1)} %get-tuple-element.26.rest_0_), channel_id=1, source_target_pairs={{0,2},{1,3},{2,0},{3,1},{4,6},{5,7},{6,4},{7,5},{8,10},{9,11},{10,... | collective-permute-start | bytes 6291464 | tf_op jit(solution)/shard_map/ppermute | solution.py:25
  20.2 47.9 %collective-permute-start.2 = (bf16[128,8192]{1,0:T(8,128)(2,1)S(1)}, bf16[128,8192]{1,0:T(8,128)(2,1)}, u32[]{:S(2)}, u32[]{:S(2)}) collective-permute-start(bf16[128,8192]{1,0:T(8,128)(2,1)S(1)} %get-tuple-element.26.rest_0_), channel_id=1, source_target_pairs={{0,1},{1,0},{2,3},{3,2},{4,5},{5,4},{6,7},{7,6},{8,9},{9,8},{10,11... | collective-permute-start | bytes 6291464 | tf_op jit(solution)/shard_map/ppermute | solution.py:25
  65.9 48.4 %collective-permute-start.1 = (bf16[128,8192]{1,0:T(8,128)(2,1)}, bf16[128,8192]{1,0:T(8,128)(2,1)}, u32[]{:S(2)}, u32[]{:S(2)}) collective-permute-start(bf16[128,8192]{1,0:T(8,128)(2,1)} %get-tuple-element.28.rest_0_), channel_id=1, source_target_pairs={{0,2},{1,3},{2,0},{3,1},{4,6},{5,7},{6,4},{7,5},{8,10},{9,11},{10,... | collective-permute-start | bytes 6291464 | tf_op jit(solution)/shard_map/ppermute | solution.py:25
  96.2 123.3 %reduce-scatter.3.cloned.1.call-start = ((), (), s32[]{:S(2)}) async-start(), calls=%async_computation.2 | async-start | bytes 2621440 | tf_op jit(solution)/shard_map/reduce_scatter | solution.py:363
  96.3 18.0 %collective-permute-start = (bf16[128,8192]{1,0:T(8,128)(2,1)}, bf16[128,8192]{1,0:T(8,128)(2,1)S(1)}, u32[]{:S(2)}, u32[]{:S(2)}) collective-permute-start(bf16[128,8192]{1,0:T(8,128)(2,1)} %get-tuple-element.28.rest_0_), channel_id=1, source_target_pairs={{0,1},{1,0},{2,3},{3,2},{4,5},{5,4},{6,7},{7,6},{8,9},{9,8},{10,11... | collective-permute-start | bytes 6291464 | tf_op jit(solution)/shard_map/ppermute | solution.py:25
  147.4 15.8 %collective-permute-start.6 = (bf16[1024,128]{1,0:T(8,128)(2,1)S(1)}, bf16[1024,128]{1,0:T(8,128)(2,1)S(1)}, u32[]{:S(2)}, u32[]{:S(2)}) collective-permute-start(bf16[1024,128]{1,0:T(8,128)(2,1)S(1)} %get-tuple-element.57.rest_0_), channel_id=1, source_target_pairs={{0,12},{4,0},{8,4},{12,8},{1,13},{5,1},{9,5},{13,9},{2,14},{6,2},{... | collective-permute-start | bytes 786440 | tf_op jit(solution)/shard_map/ppermute | solution.py:321
  151.3 25.2 %collective-permute-start.7 = (bf16[1024,128]{1,0:T(8,128)(2,1)S(1)}, bf16[1024,128]{1,0:T(8,128)(2,1)S(1)}, u32[]{:S(2)}, u32[]{:S(2)}) collective-permute-start(bf16[1024,128]{1,0:T(8,128)(2,1)S(1)} %get-tuple-element.56.rest_1_), channel_id=1, source_target_pairs={{0,12},{4,0},{8,4},{12,8},{1,13},{5,1},{9,5},{13,9},{2,14},{6,2},{... | collective-permute-start | bytes 786440 | tf_op jit(solution)/shard_map/ppermute | solution.py:321
  163.2 28.3 %collective-permute-start.8 = (bf16[1024,128]{1,0:T(8,128)(2,1)S(1)}, bf16[1024,128]{1,0:T(8,128)(2,1)S(1)}, u32[]{:S(2)}, u32[]{:S(2)}) collective-permute-start(bf16[1024,128]{1,0:T(8,128)(2,1)S(1)} %collective-permute-done.6.rest_2_), channel_id=1, source_target_pairs={{0,12},{4,0},{8,4},{12,8},{1,13},{5,1},{9,5},{13,9},{2,14},{6,2},{... | collective-permute-start | bytes 786440 | tf_op jit(solution)/shard_map/ppermute | solution.py:321
  176.5 26.2 %collective-permute-start.9 = (bf16[1024,128]{1,0:T(8,128)(2,1)S(1)}, bf16[1024,128]{1,0:T(8,128)(2,1)S(1)}, u32[]{:S(2)}, u32[]{:S(2)}) collective-permute-start(bf16[1024,128]{1,0:T(8,128)(2,1)S(1)} %collective-permute-done.7.rest_3_), channel_id=1, source_target_pairs={{0,12},{4,0},{8,4},{12,8},{1,13},{5,1},{9,5},{13,9},{2,14},{6,2},{... | collective-permute-start | bytes 786440 | tf_op jit(solution)/shard_map/ppermute | solution.py:321
  191.5 30.4 %collective-permute-start.10 = (bf16[1024,128]{1,0:T(8,128)(2,1)S(1)}, bf16[1024,128]{1,0:T(8,128)(2,1)}, u32[]{:S(2)}, u32[]{:S(2)}) collective-permute-start(bf16[1024,128]{1,0:T(8,128)(2,1)S(1)} %collective-permute-done.8.rest_4_), channel_id=1, source_target_pairs={{0,12},{4,0},{8,4},{12,8},{1,13},{5,1},{9,5},{13,9},{2,14},{6,2},{... | collective-permute-start | bytes 786440 | tf_op jit(solution)/shard_map/ppermute | solution.py:321
  202.7 19.2 %collective-permute-start.11 = (bf16[1024,128]{1,0:T(8,128)(2,1)S(1)}, bf16[1024,128]{1,0:T(8,128)(2,1)}, u32[]{:S(2)}, u32[]{:S(2)}) collective-permute-start(bf16[1024,128]{1,0:T(8,128)(2,1)S(1)} %collective-permute-done.9.rest_5_), channel_id=1, source_target_pairs={{0,12},{4,0},{8,4},{12,8},{1,13},{5,1},{9,5},{13,9},{2,14},{6,2},{... | collective-permute-start | bytes 786440 | tf_op jit(solution)/shard_map/ppermute | solution.py:321
  252.1 10.1 %collective-permute-start.13 = (bf16[1024,128]{1,0:T(8,128)(2,1)S(1)}, bf16[1024,128]{1,0:T(8,128)(2,1)S(1)}, u32[]{:S(2)}, u32[]{:S(2)}) collective-permute-start(bf16[1024,128]{1,0:T(8,128)(2,1)S(1)} %get-tuple-element.59.rest_0_), channel_id=1, source_target_pairs={{0,12},{4,0},{8,4},{12,8},{1,13},{5,1},{9,5},{13,9},{2,14},{6,2},{... | collective-permute-start | bytes 786440 | tf_op jit(solution)/shard_map/ppermute | solution.py:321
  256.8 18.4 %collective-permute-start.19 = (bf16[2048,128]{1,0:T(8,128)(2,1)S(1)}, bf16[2048,128]{1,0:T(8,128)(2,1)S(1)}, u32[]{:S(2)}, u32[]{:S(2)}) collective-permute-start(bf16[2048,128]{1,0:T(8,128)(2,1)S(1)} %get-tuple-element.52), channel_id=1, source_target_pairs={{0,1},{1,0},{2,3},{3,2},{4,5},{5,4},{6,7},{7,6},{8,9},{9,8},{10,11... | collective-permute-start | bytes 1572872 | tf_op jit(solution)/shard_map/ppermute | solution.py:25
  256.8 18.5 %collective-permute-start.20 = (bf16[2048,128]{1,0:T(8,128)(2,1)S(1)}, bf16[2048,128]{1,0:T(8,128)(2,1)S(1)}, u32[]{:S(2)}, u32[]{:S(2)}) collective-permute-start(bf16[2048,128]{1,0:T(8,128)(2,1)S(1)} %get-tuple-element.55), channel_id=1, source_target_pairs={{0,1},{1,0},{2,3},{3,2},{4,5},{5,4},{6,7},{7,6},{8,9},{9,8},{10,11... | collective-permute-start | bytes 1572872 | tf_op jit(solution)/shard_map/ppermute | solution.py:25
  257.3 18.0 %collective-permute-start.21 = (bf16[2048,128]{1,0:T(8,128)(2,1)S(1)}, bf16[2048,128]{1,0:T(8,128)(2,1)S(1)}, u32[]{:S(2)}, u32[]{:S(2)}) collective-permute-start(bf16[2048,128]{1,0:T(8,128)(2,1)S(1)} %get-tuple-element.54), channel_id=1, source_target_pairs={{0,1},{1,0},{2,3},{3,2},{4,5},{5,4},{6,7},{7,6},{8,9},{9,8},{10,11... | collective-permute-start | bytes 1572872 | tf_op jit(solution)/shard_map/ppermute | solution.py:25
  257.3 18.0 %collective-permute-start.22 = (bf16[2048,128]{1,0:T(8,128)(2,1)S(1)}, bf16[2048,128]{1,0:T(8,128)(2,1)S(1)}, u32[]{:S(2)}, u32[]{:S(2)}) collective-permute-start(bf16[2048,128]{1,0:T(8,128)(2,1)S(1)} %get-tuple-element.53), channel_id=1, source_target_pairs={{0,1},{1,0},{2,3},{3,2},{4,5},{5,4},{6,7},{7,6},{8,9},{9,8},{10,11... | collective-permute-start | bytes 1572872 | tf_op jit(solution)/shard_map/ppermute | solution.py:25
  262.2 8.8 %collective-permute-start.14 = (bf16[1024,128]{1,0:T(8,128)(2,1)S(1)}, bf16[1024,128]{1,0:T(8,128)(2,1)S(1)}, u32[]{:S(2)}, u32[]{:S(2)}) collective-permute-start(bf16[1024,128]{1,0:T(8,128)(2,1)S(1)} %get-tuple-element.58.rest_1_), channel_id=1, source_target_pairs={{0,12},{4,0},{8,4},{12,8},{1,13},{5,1},{9,5},{13,9},{2,14},{6,2},{... | collective-permute-start | bytes 786440 | tf_op jit(solution)/shard_map/ppermute | solution.py:321
  270.9 11.0 %collective-permute-start.15 = (bf16[1024,128]{1,0:T(8,128)(2,1)S(1)}, bf16[1024,128]{1,0:T(8,128)(2,1)S(1)}, u32[]{:S(2)}, u32[]{:S(2)}) collective-permute-start(bf16[1024,128]{1,0:T(8,128)(2,1)S(1)} %collective-permute-done.13.rest_2_), channel_id=1, source_target_pairs={{0,12},{4,0},{8,4},{12,8},{1,13},{5,1},{9,5},{13,9},{2,14},{6,2},{... | collective-permute-start | bytes 786440 | tf_op jit(solution)/shard_map/ppermute | solution.py:321
  275.2 12.4 %collective-permute-start.16 = (bf16[1024,128]{1,0:T(8,128)(2,1)S(1)}, bf16[1024,128]{1,0:T(8,128)(2,1)S(1)}, u32[]{:S(2)}, u32[]{:S(2)}) collective-permute-start(bf16[1024,128]{1,0:T(8,128)(2,1)S(1)} %collective-permute-done.14.rest_3_), channel_id=1, source_target_pairs={{0,12},{4,0},{8,4},{12,8},{1,13},{5,1},{9,5},{13,9},{2,14},{6,2},{... | collective-permute-start | bytes 786440 | tf_op jit(solution)/shard_map/ppermute | solution.py:321
  277.1 46.4 %collective-permute-start.23 = (bf16[8192,128]{1,0:T(8,128)(2,1)}, bf16[8192,128]{1,0:T(8,128)(2,1)}, u32[]{:S(2)}, u32[]{:S(2)}) collective-permute-start(bf16[8192,128]{1,0:T(8,128)(2,1)} %add_convert_fusion.1.rest_8_), channel_id=1, source_target_pairs={{0,2},{1,3},{2,0},{3,1},{4,6},{5,7},{6,4},{7,5},{8,10},{9,11},{10,... | collective-permute-start | bytes 6291464 | tf_op jit(solution)/shard_map/ppermute | solution.py:25
  282.0 10.8 %collective-permute-start.17 = (bf16[1024,128]{1,0:T(8,128)(2,1)S(1)}, bf16[1024,128]{1,0:T(8,128)(2,1)S(1)}, u32[]{:S(2)}, u32[]{:S(2)}) collective-permute-start(bf16[1024,128]{1,0:T(8,128)(2,1)S(1)} %collective-permute-done.15.rest_4_), channel_id=1, source_target_pairs={{0,12},{4,0},{8,4},{12,8},{1,13},{5,1},{9,5},{13,9},{2,14},{6,2},{... | collective-permute-start | bytes 786440 | tf_op jit(solution)/shard_map/ppermute | solution.py:321
  287.6 8.2 %collective-permute-start.18 = (bf16[1024,128]{1,0:T(8,128)(2,1)S(1)}, bf16[1024,128]{1,0:T(8,128)(2,1)S(1)}, u32[]{:S(2)}, u32[]{:S(2)}) collective-permute-start(bf16[1024,128]{1,0:T(8,128)(2,1)S(1)} %collective-permute-done.16.rest_5_), channel_id=1, source_target_pairs={{0,12},{4,0},{8,4},{12,8},{1,13},{5,1},{9,5},{13,9},{2,14},{6,2},{... | collective-permute-start | bytes 786440 | tf_op jit(solution)/shard_map/ppermute | solution.py:321
  325.1 17.6 %collective-permute-start.12 = (bf16[8192,128]{1,0:T(8,128)(2,1)S(1)}, bf16[8192,128]{1,0:T(8,128)(2,1)S(1)}, u32[]{:S(2)}, u32[]{:S(2)}) collective-permute-start(bf16[8192,128]{1,0:T(8,128)(2,1)S(1)} %copy-done.17), channel_id=1, source_target_pairs={{0,1},{1,0},{2,3},{3,2},{4,5},{5,4},{6,7},{7,6},{8,9},{9,8},{10,11... | collective-permute-start | bytes 6291464 | tf_op jit(solution)/shard_map/ppermute | solution.py:25
  325.7 22.0 %collective-permute-start.26 = (bf16[8192,128]{1,0:T(8,128)(2,1)}, bf16[8192,128]{1,0:T(8,128)(2,1)S(1)}, u32[]{:S(2)}, u32[]{:S(2)}) collective-permute-start(bf16[8192,128]{1,0:T(8,128)(2,1)} %copy-done.18), channel_id=1, source_target_pairs={{0,1},{1,0},{2,3},{3,2},{4,5},{5,4},{6,7},{7,6},{8,9},{9,8},{10,11... | collective-permute-start | bytes 6291464 | tf_op jit(solution)/shard_map/ppermute | solution.py:25
  331.0 48.5 %collective-permute-start.31 = (bf16[8192,128]{1,0:T(8,128)(2,1)S(1)}, bf16[8192,128]{1,0:T(8,128)(2,1)S(1)}, u32[]{:S(2)}, u32[]{:S(2)}) collective-permute-start(bf16[8192,128]{1,0:T(8,128)(2,1)S(1)} %add_convert_fusion), channel_id=1, source_target_pairs={{0,2},{1,3},{2,0},{3,1},{4,6},{5,7},{6,4},{7,5},{8,10},{9,11},{10,... | collective-permute-start | bytes 6291464 | tf_op jit(solution)/shard_map/ppermute | solution.py:25
  340.6 44.7 %collective-permute-start.35 = (f32[520,128]{1,0:T(8,128)S(1)}, f32[520,128]{1,0:T(8,128)S(1)}, u32[]{:S(2)}, u32[]{:S(2)}) collective-permute-start(f32[520,128]{1,0:T(8,128)S(1)} %add.53), channel_id=1, source_target_pairs={{0,2},{1,3},{2,0},{3,1},{4,6},{5,7},{6,4},{7,5},{8,10},{9,11},{10,... | collective-permute-start | bytes 798728 | tf_op jit(solution)/shard_map/ppermute | solution.py:25
  341.7 48.4 %collective-permute-start.37 = (f32[520,128]{1,0:T(8,128)S(1)}, f32[520,128]{1,0:T(8,128)S(1)}, u32[]{:S(2)}, u32[]{:S(2)}) collective-permute-start(f32[520,128]{1,0:T(8,128)S(1)} %add.55), channel_id=1, source_target_pairs={{0,2},{1,3},{2,0},{3,1},{4,6},{5,7},{6,4},{7,5},{8,10},{9,11},{10,... | collective-permute-start | bytes 798728 | tf_op jit(solution)/shard_map/ppermute | solution.py:25
  347.6 42.6 %collective-permute-start.24 = (f32[512,128]{1,0:T(8,128)S(1)}, f32[512,128]{1,0:T(8,128)S(1)}, u32[]{:S(2)}, u32[]{:S(2)}) collective-permute-start(f32[512,128]{1,0:T(8,128)S(1)} %weight_grad.4), channel_id=1, source_target_pairs={{0,1},{1,0},{2,3},{3,2},{4,5},{5,4},{6,7},{7,6},{8,9},{9,8},{10,11... | collective-permute-start | bytes 786440 | tf_op jit(solution)/shard_map/ppermute | solution.py:25
  383.2 8.9 %collective-permute-start.32 = (f32[512,128]{1,0:T(8,128)S(1)}, f32[512,128]{1,0:T(8,128)S(1)}, u32[]{:S(2)}, u32[]{:S(2)}) collective-permute-start(f32[512,128]{1,0:T(8,128)S(1)} %weight_grad.5), channel_id=1, source_target_pairs={{0,1},{1,0},{2,3},{3,2},{4,5},{5,4},{6,7},{7,6},{8,9},{9,8},{10,11... | collective-permute-start | bytes 786440 | tf_op jit(solution)/shard_map/ppermute | solution.py:25
  390.2 9.3 %collective-permute-start.25 = (f32[512,128]{1,0:T(8,128)S(1)}, f32[512,128]{1,0:T(8,128)S(1)}, u32[]{:S(2)}, u32[]{:S(2)}) collective-permute-start(f32[512,128]{1,0:T(8,128)S(1)} %add.48), channel_id=1, source_target_pairs={{0,2},{1,3},{2,0},{3,1},{4,6},{5,7},{6,4},{7,5},{8,10},{9,11},{10,... | collective-permute-start | bytes 786440 | tf_op jit(solution)/shard_map/ppermute | solution.py:25
  392.1 11.4 %collective-permute-start.33 = (f32[512,128]{1,0:T(8,128)S(1)}, f32[512,128]{1,0:T(8,128)S(1)}, u32[]{:S(2)}, u32[]{:S(2)}) collective-permute-start(f32[512,128]{1,0:T(8,128)S(1)} %add.51), channel_id=1, source_target_pairs={{0,2},{1,3},{2,0},{3,1},{4,6},{5,7},{6,4},{7,5},{8,10},{9,11},{10,... | collective-permute-start | bytes 786440 | tf_op jit(solution)/shard_map/ppermute | solution.py:25
  (40 other events, 568.4 us)
Sparse Core Ops, SparseCore 0:
  96.4 45.3 reduce-scatter.4
  144.1 75.3 reduce-scatter.2

commit v6 on v5

--- a/solution.py
+++ b/solution.py
@@ -30,10 +30,17 @@
     return [1 << i for i in range(n.bit_length() - 1)]
 
 
-def sum_over_node(value, n):
-    for mask in masks_of(n):
-        value = value + swap(value, mask, n)
-    return value
+def sum_over_node(keep, send, low, n):
+    near, *far = masks_of(n)
+    total = keep + swap(send, near, n)
+    for mask in far:
+        total = total + swap(total, mask, n)
+    other = swap(total, near, n)
+    return jnp.where(
+        low[0] == 0,
+        jnp.concatenate([total, other], axis=0),
+        jnp.concatenate([other, total], axis=0),
+    )
 
 
 def total_of(values):
@@ -94,16 +101,18 @@
     share = rows // n_feat
     per_share = blocks // n_feat
 
-    def kernel(src_ref, inv_ref, nbr_ref, self_ref, *rest):
+    def kernel(src_ref, inv_ref, nbr_ref, self_hbm, *rest):
         part_refs = rest[:n]
-        out_hbm, table, ready, out_sems = rest[n:]
-        for k, ref in enumerate(part_refs):
-
-            @pl.loop(0, rows // side, unroll=4)
-            def _(i, k=k, ref=ref):
-                at = pl.multiple_of(i * side, side)
-                table[:, pl.ds(k * rows + at, side)] = ref[:, pl.ds(at, side)]
-
+        out_hbm, table, self_ref, ready, sems, out_sems = rest[n:]
+        copies = [
+            pltpu.make_async_copy(ref, table.at[:, pl.ds(k * rows, rows)], sems.at[k])
+            for k, ref in enumerate(part_refs)
+        ]
+        copies.append(pltpu.make_async_copy(self_hbm, self_ref, sems.at[n]))
+        for copy in copies:
+            copy.start()
+        for copy in copies:
+            copy.wait()
         ids = side_ids(side)
 
         def out_copy(s):
@@ -140,14 +149,16 @@
     return pl.pallas_call(
         kernel,
         out_shape=jax.ShapeDtypeStruct((rows, wide), jnp.bfloat16),
-        in_specs=[SMEM, SMEM, VMEM, VMEM] + [VMEM] * n,
+        in_specs=[SMEM, SMEM, VMEM, HBM] + [HBM] * n,
         out_specs=HBM,
         scratch_shapes=[
             pltpu.VMEM((wide, n * rows), jnp.bfloat16),
+            pltpu.VMEM((wide, rows), jnp.float32),
             pltpu.VMEM((rows, wide), jnp.bfloat16),
+            pltpu.SemaphoreType.DMA((n + 1,)),
             pltpu.SemaphoreType.DMA((n_feat,)),
         ],
-        compiler_params=pltpu.CompilerParams(vmem_limit_bytes=32 * MIB),
+        compiler_params=pltpu.CompilerParams(vmem_limit_bytes=56 * MIB),
         cost_estimate=cost(
             8 * blocks * slots * side * side * wide, 2 * n * rows * wide + 6 * rows * wide
         ),
@@ -276,39 +287,47 @@
     )(order, src, inv, nbr, *pieces, *after)
 
 
-def weight_grad(feat_t, grads, with_sum):
+def weight_grad(low, feat_t, grads, with_sum):
     width, rows = feat_t.shape
     wide = grads[0].shape[1]
     step = min(2048, rows)
-    extra = 8 if with_sum else 0
-
-    def kernel(feat_ref, *rest):
-        out_ref = rest[-1]
+    tall = width + (16 if with_sum else 0)
+    half = tall // 2
+
+    def kernel(low_ref, feat_ref, *rest):
+        keep_ref, send_ref, total = rest[-3:]
 
         @pl.when(pl.program_id(0) == 0)
         def _():
-            out_ref[...] = jnp.zeros_like(out_ref)
+            total[...] = jnp.zeros_like(total)
 
         value = rest[0][...]
         if len(grads) > 1:
-            value = sum(ref[...].astype(jnp.float32) for ref in rest[:-1]).astype(jnp.bfloat16)
-        out_ref[:width, :] += jnp.dot(feat_ref[...], value, preferred_element_type=jnp.float32)
+            value = sum(ref[...].astype(jnp.float32) for ref in rest[:-3]).astype(jnp.bfloat16)
+        total[:width, :] += jnp.dot(feat_ref[...], value, preferred_element_type=jnp.float32)
         if with_sum:
-            out_ref[width : width + 1, :] += jnp.sum(
+            total[width : width + 1, :] += jnp.sum(
                 value.astype(jnp.float32), axis=0, keepdims=True
             )
+
+        @pl.when(pl.program_id(0) == rows // step - 1)
+        def _():
+            low = low_ref[0]
+            keep_ref[...] = total[pl.ds(pl.multiple_of(low * half, 8), half), :]
+            send_ref[...] = total[pl.ds(pl.multiple_of((1 - low) * half, 8), half), :]
 
     return pl.pallas_call(
         kernel,
         grid=(rows // step,),
-        in_specs=[pl.BlockSpec((width, step), lambda i: (0, i))]
+        in_specs=[SMEM, pl.BlockSpec((width, step), lambda i: (0, i))]
         + [pl.BlockSpec((step, wide), lambda i: (i, 0))] * len(grads),
-        out_specs=pl.BlockSpec((width + extra, wide), lambda i: (0, 0)),
-        out_shape=jax.ShapeDtypeStruct((width + extra, wide), jnp.float32),
+        out_specs=[pl.BlockSpec((half, wide), lambda i: (0, 0))] * 2,
+        out_shape=[jax.ShapeDtypeStruct((half, wide), jnp.float32)] * 2,
+        scratch_shapes=[pltpu.VMEM((tall, wide), jnp.float32)],
         compiler_params=pltpu.CompilerParams(vmem_limit_bytes=16 * MIB),
         cost_estimate=cost(2 * width * rows * wide, 2 * rows * (width + wide)),
         name="weight_grad",
-    )(feat_t, *grads)
+    )(low, feat_t, *grads)
 
 
 def gather_shares(value, n, ring):
@@ -342,6 +361,7 @@
     ring = n_feat <= 4
     feat_index = jnp.reshape(lax.axis_index("feat"), (1,)).astype(jnp.int32)
     in_place = jnp.zeros((1,), jnp.int32)
+    low = jnp.reshape(jnp.bitwise_and(me, 1), (1,)).astype(jnp.int32)
     part_pres = []
     for c in range(CHUNKS):
         held = {0: projected[c]}
@@ -360,15 +380,19 @@
     grad_pres, pieces = [], []
     for c in range(CHUNKS):
         part_pre = part_pres[c]
+        if pieces:
+            steps = pieces[-1]
+            near_end = steps[max(len(steps) - 2, 0)]
+            part_pre, near_end[-1] = lax.optimization_barrier((part_pre, near_end[-1]))
         shares = [lax.psum_scatter(part_pre, "feat", scatter_dimension=0, tiled=True)]
         hidden, grad_pre = activate(
             shares, bias_row, cot_rows, hidden, c, part_pres[c + 1 : c + 2]
         )
         grad_pres.append(grad_pre)
-        pieces.append(gather_shares(grad_pre, n_feat, ring))
+        pieces.append(gather_shares(grad_pre, n_feat, ring and c < CHUNKS - 1))
 
     grads_n, grads_s, sums = [], [], []
-    after = [grad_pres[-1]]
+    after = []
     arrived = None
     sent = []
     for c in range(CHUNKS):
@@ -402,11 +426,12 @@
                 held = {k: [total_of(v)] if k else v for k, v in held.items()}
         arrived = held[0][-1]
         sent.append(held[0])
-        both = sum_over_node(weight_grad(feat_t, [piece], True), n_node)
+        both = sum_over_node(*weight_grad(low, feat_t, [piece], True), low, n_node)
+        after = after + [both]
         grads_s.append(both[:width])
         sums.append(both[width])
     for terms in sent:
-        grads_n.append(sum_over_node(weight_grad(feat_t, terms, False), n_node))
+        grads_n.append(sum_over_node(*weight_grad(low, feat_t, terms, False), low, n_node))
     return (
         hidden.reshape(1, share, hid),
         jnp.concatenate(grads_n, axis=1),

time: 412 us -> 443 us (1.075)
  local copies, waits for them, and re-layouts: 23.5 us -> 45.2 us
  waiting for transfers between devices: 196 us -> 212 us
  starting transfers between devices: 48.3 us -> 36.5 us
  other arithmetic: 6.96 us -> 13.2 us
    ppermute x26 -> x30, waiting for transfers between devices: 118 us -> 157 us  [swap(): return lax.ppermute(value, 'node', [(i, i ^ mask) for i in range(n)])]
    unnamed x65 -> x93, local copies, waits for them, and re-layouts: 23.1 us -> 42 us
    reduce_scatter x2, waiting for transfers between devices: 16.9 us -> 0.02 us  [on_device(): lax.psum_scatter(part_pre, 'feat', scatter_dimension=0, tiled=True)]
    ppermute x12 -> x6, starting transfers between devices: 32.7 us -> 18.5 us  [gather_shares(): lax.ppermute(v, 'feat', [(i, (i - 1) % n) for i in range(n)])]
    ppermute x12 -> x6, waiting for transfers between devices: 61.1 us -> 54.7 us  [gather_shares(): lax.ppermute(v, 'feat', [(i, (i - 1) % n) for i in range(n)])]
    ppermute x26 -> x30, starting transfers between devices: 15.5 us -> 17.9 us  [swap(): return lax.ppermute(value, 'node', [(i, i ^ mask) for i in range(n)])]
  transfers between devices with their start and end apart: 40 -> 39, of which waited for: 26 -> 21; matrix products, arithmetic and copies ran while one was open for 2% -> 3% of each run, Pallas kernels for 23% -> 26%
where the time goes in v6:
time: 443 us; the launch traced here: 442 us
  waiting for transfers between devices  212 us (48%)
  Pallas kernels  121 us (27%)
  local copies, waits for them, and re-layouts  45.2 us (10%)
  starting transfers between devices  36.5 us (8%)
  between operations  14.2 us (3%)
  other arithmetic  13.2 us (3%)
    ppermute x30, waiting for transfers between devices, swap(): return lax.ppermute(value, 'node', [(i, i ^ mask) for i in range(n)])  157 us
    ppermute x6, waiting for transfers between devices, gather_shares(): lax.ppermute(v, 'feat', [(i, (i - 1) % n) for i in range(n)])  54.7 us
    pallas_call x2, Pallas kernels, mean_tiles(): pl.pallas_call(kernel, out_shape=jax.ShapeDtypeStruct((rows, wide), jnp.b...  47.1 us
    pallas_call x2, Pallas kernels, spread_tiles(): pl.pallas_call(kernel, out_shape=[jax.ShapeDtypeStruct((rows, wide), jnp....  46.8 us
    unnamed x93, local copies, waits for them, and re-layouts  42 us
    ppermute x6, starting transfers between devices, gather_shares(): lax.ppermute(v, 'feat', [(i, (i - 1) % n) for i in range(n)])  18.5 us
    ppermute x30, starting transfers between devices, swap(): return lax.ppermute(value, 'node', [(i, i ^ mask) for i in range(n)])  17.9 us
    pallas_call x4, Pallas kernels, weight_grad(): pl.pallas_call(kernel, grid=(rows // step,), in_specs=[SMEM, pl.BlockSpec...  14.3 us
  transfers between devices with their start and end apart: 39, of which 21 were waited for; matrix products, arithmetic and copies ran while one was open for 3% of the time, Pallas kernels for 26%

profile of v6, /device:TPU:0, one launch (start us, length us, event | category | flops | bytes accessed | tf_op | source)
XLA Modules:
  0.0 442.3 jit_solution(15398607315717883329)
XLA Ops:
  7.2 3.4 copy-done
  11.5 5.7 %project.2 = (bf16[128,8192]{1,0:T(8,128)(2,1)S(1)}, bf16[128,8192]{1,0:T(8,128)(2,1)}) custom-call(bf16[512,8192]{1,0:T(8,128)(2,1)S(1)} %copy-done, bf16[512,256]{1,0:T(8,128)(2,1)S(1)} %copy-done.17), custom_call_target="tpu_custom_call" | custom-call | flops 2147483648 | bytes 16777216 | tf_op jit(solution)/shard_map/project/pallas_call | solution.py:80
  17.3 3.0 collective-permute-start.3
  20.3 4.8 %project.3 = (f32[128,8192]{1,0:T(8,128)S(1)}, f32[128,8192]{1,0:T(8,128)S(1)}) custom-call(bf16[512,8192]{1,0:T(8,128)(2,1)S(1)} %copy-done, bf16[512,256]{1,0:T(8,128)(2,1)S(1)} %copy-done.20, bf16[128,8192]{1,0:T(8,128)(2,1)S(1)} %get-tuple-element.36.rest_0_), custom_call_target="tpu_custom_call" | custom-call | flops 2147483648 | bytes 16777216 | tf_op jit(solution)/shard_map/project/pallas_call | solution.py:80
  29.1 36.9 %collective-permute-done.3.rest_2_ = bf16[128,8192]{1,0:T(8,128)(2,1)} collective-permute-done((bf16[128,8192]{1,0:T(8,128)(2,1)S(1)}, bf16[128,8192]{1,0:T(8,128)(2,1)}, u32[]{:S(2)}, u32[]{:S(2)}) %collective-permute-start.3) | collective-permute-done | bytes 2097184 | tf_op jit(solution)/shard_map/ppermute | solution.py:25
  70.5 23.4 %mean_tiles.2 = bf16[8192,128]{1,0:T(8,128)(2,1)} custom-call(s32[64,16]{1,0:T(8,128)} %fusion.2.src_ref, f32[64]{0:T(128)} %convert_divide_fusion.inv_ref, s32[64,16,128]{2,1,0:T(8,128)} %broadcast_select_fusion.nbr_ref, f32[128,8192]{1,0:T(8,128)} %copy-done.24, bf16[128,8192]{1,0:T(8,128)(2,1)} %copy-done.10, ...), custom_call_target="tpu_custom_call" | custom-call | flops 17179869184 | bytes 14680064 | tf_op jit(solution)/shard_map/mean_tiles/pallas_call | solution.py:149
  94.3 20.1 %collective-permute-done.1.rest_2_ = bf16[128,8192]{1,0:T(8,128)(2,1)} collective-permute-done((bf16[128,8192]{1,0:T(8,128)(2,1)}, bf16[128,8192]{1,0:T(8,128)(2,1)}, u32[]{:S(2)}, u32[]{:S(2)}) %collective-permute-start.1) | collective-permute-done | bytes 2097184 | tf_op jit(solution)/shard_map/ppermute | solution.py:25
  114.4 4.4 collective-permute-done.5.rest_3_
  120.1 23.7 %mean_tiles.3.rest_1_ = bf16[8192,128]{1,0:T(8,128)(2,1)} custom-call(s32[64,16]{1,0:T(8,128)} %fusion.2.src_ref, f32[64]{0:T(128)} %convert_divide_fusion.inv_ref, s32[64,16,128]{2,1,0:T(8,128)} %broadcast_select_fusion.nbr_ref, f32[128,8192]{1,0:T(8,128)} %copy-done.23, bf16[128,8192]{1,0:T(8,128)(2,1)} %get-tuple-element.38.rest_0_, ...), custom_call_target="tpu_custom_call" | custom-call | flops 17179869184 | bytes 14680064 | tf_op jit(solution)/shard_map/mean_tiles/pallas_call | solution.py:149
  147.7 3.9 collective-permute-start.6
  151.6 5.9 %collective-permute-done.6.rest_3_ = bf16[1024,128]{1,0:T(8,128)(2,1)S(1)} collective-permute-done((bf16[1024,128]{1,0:T(8,128)(2,1)S(1)}, bf16[1024,128]{1,0:T(8,128)(2,1)S(1)}, u32[]{:S(2)}, u32[]{:S(2)}) %collective-permute-start.6) | collective-permute-done | bytes 262176 | tf_op jit(solution)/shard_map/ppermute | solution.py:340
  157.5 4.3 collective-permute-start.7
  161.8 5.1 %collective-permute-done.7.rest_5_ = bf16[1024,128]{1,0:T(8,128)(2,1)S(1)} collective-permute-done((bf16[1024,128]{1,0:T(8,128)(2,1)S(1)}, bf16[1024,128]{1,0:T(8,128)(2,1)S(1)}, u32[]{:S(2)}, u32[]{:S(2)}) %collective-permute-start.7) | collective-permute-done | bytes 262176 | tf_op jit(solution)/shard_map/ppermute | solution.py:340
  166.9 4.3 collective-permute-start.8
  171.2 5.4 %collective-permute-done.8.rest_2_ = bf16[1024,128]{1,0:T(8,128)(2,1)S(1)} collective-permute-done((bf16[1024,128]{1,0:T(8,128)(2,1)S(1)}, bf16[1024,128]{1,0:T(8,128)(2,1)S(1)}, u32[]{:S(2)}, u32[]{:S(2)}) %collective-permute-start.8) | collective-permute-done | bytes 262176 | tf_op jit(solution)/shard_map/ppermute | solution.py:340
  176.6 4.3 collective-permute-start.9
  181.6 12.7 %collective-permute-done.9.rest_4_ = bf16[1024,128]{1,0:T(8,128)(2,1)S(1)} collective-permute-done((bf16[1024,128]{1,0:T(8,128)(2,1)S(1)}, bf16[1024,128]{1,0:T(8,128)(2,1)S(1)}, u32[]{:S(2)}, u32[]{:S(2)}) %collective-permute-start.9) | collective-permute-done | bytes 262176 | tf_op jit(solution)/shard_map/ppermute | solution.py:340
  196.8 15.7 %collective-permute-done.10.rest_6_ = bf16[1024,128]{1,0:T(8,128)(2,1)S(1)} collective-permute-done((bf16[1024,128]{1,0:T(8,128)(2,1)S(1)}, bf16[1024,128]{1,0:T(8,128)(2,1)S(1)}, u32[]{:S(2)}, u32[]{:S(2)}) %collective-permute-start.10) | collective-permute-done | bytes 262176 | tf_op jit(solution)/shard_map/ppermute | solution.py:340
  213.1 10.0 %collective-permute-done.11.rest_7_ = bf16[1024,128]{1,0:T(8,128)(2,1)S(1)} collective-permute-done((bf16[1024,128]{1,0:T(8,128)(2,1)S(1)}, bf16[1024,128]{1,0:T(8,128)(2,1)S(1)}, u32[]{:S(2)}, u32[]{:S(2)}) %collective-permute-start.11) | collective-permute-done | bytes 262176 | tf_op jit(solution)/shard_map/ppermute | solution.py:340
  231.5 23.6 %spread_tiles.2 = (bf16[8192,128]{1,0:T(8,128)(2,1)S(1)}, bf16[8192,128]{1,0:T(8,128)(2,1)S(1)}, bf16[8192,128]{1,0:T(8,128)(2,1)S(1)}, bf16[8192,128]{1,0:T(8,128)(2,1)S(1)}, bf16[8192,128]{1,0:T(8,128)(2,1)S(1)}) custom-call(s32[1]{0:T(128)} %bitcast.4.order_ref, s32[64,16]{1,0:T(8,128)S(1)} %copy-done.21, f32[64]{0:T(128)S(1)} %copy-done.40, ...), custom_call_target="tpu_custom_call" | custom-call | flops 17179869184 | bytes 10485760 | tf_op jit(solution)/shard_map/spread_tiles/pallas_call | solution.py:270
  263.6 2.9 fusion.8
  267.5 3.8 copy-done.1
  273.0 3.6 weight_grad.4
  276.7 7.9 %add_convert_fusion.1.rest_1_ = bf16[8192,128]{1,0:T(8,128)(2,1)} fusion(bf16[8192,128]{1,0:T(8,128)(2,1)S(1)} %get-tuple-element.50, bf16[2048,128]{1,0:T(8,128)(2,1)} %collective-permute-done.16, bf16[2048,128]{1,0:T(8,128)(2,1)} %collective-permute-done.15, bf16[2048,128]{1,0:T(8,128)(2,1)S(1)} %collective-permute-done.14, ...), kind=kLoop, calls=%fused_computation.1 | loop fusion | flops 11534336 | bytes 6291456 | tf_op jit(solution)/shard_map/convert_element_type | solution.py:49
  287.1 49.3 %collective-permute-done.18 = f32[264,128]{1,0:T(8,128)S(1)} collective-permute-done((f32[264,128]{1,0:T(8,128)S(1)}, f32[264,128]{1,0:T(8,128)S(1)}, u32[]{:S(2)}, u32[]{:S(2)}) %collective-permute-start.18) | collective-permute-done | bytes 135200 | tf_op jit(solution)/shard_map/ppermute | solution.py:25
  340.6 23.3 %spread_tiles.3 = (bf16[8192,128]{1,0:T(8,128)(2,1)S(1)}, bf16[8192,128]{1,0:T(8,128)(2,1)S(1)}, bf16[8192,128]{1,0:T(8,128)(2,1)S(1)}, bf16[8192,128]{1,0:T(8,128)(2,1)S(1)}, bf16[8192,128]{1,0:T(8,128)(2,1)S(1)}) custom-call(s32[1]{0:T(128)} %constant.42.clone.1.order_ref, s32[64,16]{1,0:T(8,128)S(1)} %copy-done.21, f32[64]{0:T(128)S(1)} %copy-done.40, ...), custom_call_target="tpu_custom_call" | custom-call | flops 17179869184 | bytes 10485760 | tf_op jit(solution)/shard_map/spread_tiles/pallas_call | solution.py:270
  371.3 3.4 copy-done.2
  374.7 3.6 weight_grad.5
  378.5 3.6 weight_grad.7
  385.4 34.8 %collective-permute-done.22 = f32[256,128]{1,0:T(8,128)S(1)} collective-permute-done((f32[256,128]{1,0:T(8,128)S(1)}, f32[256,128]{1,0:T(8,128)S(1)}, u32[]{:S(2)}, u32[]{:S(2)}) %collective-permute-start.22) | collective-permute-done | bytes 131104 | tf_op jit(solution)/shard_map/ppermute | solution.py:25
  422.4 3.6 weight_grad.6
  429.4 4.0 collective-permute-done.31
  (183 shorter events, 64.0 us)
Async XLA Ops:
  7.2 136.6 %reduce-scatter.3.cloned.1.call-start = ((), (), s32[]{:S(2)}) async-start(), calls=%async_computation.2 | async-start | bytes 2621440 | tf_op jit(solution)/shard_map/reduce_scatter | solution.py:387
  17.3 48.7 %collective-permute-start.3 = (bf16[128,8192]{1,0:T(8,128)(2,1)S(1)}, bf16[128,8192]{1,0:T(8,128)(2,1)}, u32[]{:S(2)}, u32[]{:S(2)}) collective-permute-start(bf16[128,8192]{1,0:T(8,128)(2,1)S(1)} %get-tuple-element.36.rest_0_), channel_id=1, source_target_pairs={{0,2},{1,3},{2,0},{3,1},{4,6},{5,7},{6,4},{7,5},{8,10},{9,11},{10,... | collective-permute-start | bytes 6291464 | tf_op jit(solution)/shard_map/ppermute | solution.py:25
  20.3 49.8 %collective-permute-start.2 = (bf16[128,8192]{1,0:T(8,128)(2,1)S(1)}, bf16[128,8192]{1,0:T(8,128)(2,1)}, u32[]{:S(2)}, u32[]{:S(2)}) collective-permute-start(bf16[128,8192]{1,0:T(8,128)(2,1)S(1)} %get-tuple-element.36.rest_0_), channel_id=1, source_target_pairs={{0,1},{1,0},{2,3},{3,2},{4,5},{5,4},{6,7},{7,6},{8,9},{9,8},{10,11... | collective-permute-start | bytes 6291464 | tf_op jit(solution)/shard_map/ppermute | solution.py:25
  66.0 4.5 %collective-permute-start.4 = (bf16[128,8192]{1,0:T(8,128)(2,1)}, bf16[128,8192]{1,0:T(8,128)(2,1)}, u32[]{:S(2)}, u32[]{:S(2)}) collective-permute-start(bf16[128,8192]{1,0:T(8,128)(2,1)} %collective-permute-done.3.rest_2_), channel_id=1, source_target_pairs={{0,1},{1,0},{2,3},{3,2},{4,5},{5,4},{6,7},{7,6},{8,9},{9,8},{10,11... | collective-permute-start | bytes 6291464 | tf_op jit(solution)/shard_map/ppermute | solution.py:25
  66.0 48.4 %collective-permute-start.1 = (bf16[128,8192]{1,0:T(8,128)(2,1)}, bf16[128,8192]{1,0:T(8,128)(2,1)}, u32[]{:S(2)}, u32[]{:S(2)}) collective-permute-start(bf16[128,8192]{1,0:T(8,128)(2,1)} %get-tuple-element.38.rest_0_), channel_id=1, source_target_pairs={{0,2},{1,3},{2,0},{3,1},{4,6},{5,7},{6,4},{7,5},{8,10},{9,11},{10,... | collective-permute-start | bytes 6291464 | tf_op jit(solution)/shard_map/ppermute | solution.py:25
  94.0 166.5 %reduce-scatter.5.cloned.1.call-start = ((), (), s32[]{:S(2)}) async-start(), calls=%async_computation.3 | async-start | bytes 2621440 | tf_op jit(solution)/shard_map/reduce_scatter | solution.py:387
  94.0 20.4 %collective-permute-start = (bf16[128,8192]{1,0:T(8,128)(2,1)}, bf16[128,8192]{1,0:T(8,128)(2,1)S(1)}, u32[]{:S(2)}, u32[]{:S(2)}) collective-permute-start(bf16[128,8192]{1,0:T(8,128)(2,1)} %get-tuple-element.38.rest_0_), channel_id=1, source_target_pairs={{0,1},{1,0},{2,3},{3,2},{4,5},{5,4},{6,7},{7,6},{8,9},{9,8},{10,11... | collective-permute-start | bytes 6291464 | tf_op jit(solution)/shard_map/ppermute | solution.py:25
  114.4 4.4 collective-permute-start.5
  147.7 9.8 %collective-permute-start.6 = (bf16[1024,128]{1,0:T(8,128)(2,1)S(1)}, bf16[1024,128]{1,0:T(8,128)(2,1)S(1)}, u32[]{:S(2)}, u32[]{:S(2)}) collective-permute-start(bf16[1024,128]{1,0:T(8,128)(2,1)S(1)} %get-tuple-element.77.rest_1_), channel_id=1, source_target_pairs={{0,12},{4,0},{8,4},{12,8},{1,13},{5,1},{9,5},{13,9},{2,14},{6,2},{... | collective-permute-start | bytes 786440 | tf_op jit(solution)/shard_map/ppermute | solution.py:340
  157.5 9.3 %collective-permute-start.7 = (bf16[1024,128]{1,0:T(8,128)(2,1)S(1)}, bf16[1024,128]{1,0:T(8,128)(2,1)S(1)}, u32[]{:S(2)}, u32[]{:S(2)}) collective-permute-start(bf16[1024,128]{1,0:T(8,128)(2,1)S(1)} %collective-permute-done.6.rest_3_), channel_id=1, source_target_pairs={{0,12},{4,0},{8,4},{12,8},{1,13},{5,1},{9,5},{13,9},{2,14},{6,2},{... | collective-permute-start | bytes 786440 | tf_op jit(solution)/shard_map/ppermute | solution.py:340
  166.9 171.0 %all-gather.2.cloned.1.call-start = ((), (), s32[]{:S(2)}) async-start(), calls=%async_computation.4 | async-start | bytes 2621440 | tf_op jit(solution)/shard_map/all_gather | solution.py:335
  166.9 9.7 %collective-permute-start.8 = (bf16[1024,128]{1,0:T(8,128)(2,1)S(1)}, bf16[1024,128]{1,0:T(8,128)(2,1)S(1)}, u32[]{:S(2)}, u32[]{:S(2)}) collective-permute-start(bf16[1024,128]{1,0:T(8,128)(2,1)S(1)} %get-tuple-element.76.rest_0_), channel_id=1, source_target_pairs={{0,12},{4,0},{8,4},{12,8},{1,13},{5,1},{9,5},{13,9},{2,14},{6,2},{... | collective-permute-start | bytes 786440 | tf_op jit(solution)/shard_map/ppermute | solution.py:340
  176.6 17.7 %collective-permute-start.9 = (bf16[1024,128]{1,0:T(8,128)(2,1)S(1)}, bf16[1024,128]{1,0:T(8,128)(2,1)S(1)}, u32[]{:S(2)}, u32[]{:S(2)}) collective-permute-start(bf16[1024,128]{1,0:T(8,128)(2,1)S(1)} %collective-permute-done.8.rest_2_), channel_id=1, source_target_pairs={{0,12},{4,0},{8,4},{12,8},{1,13},{5,1},{9,5},{13,9},{2,14},{6,2},{... | collective-permute-start | bytes 786440 | tf_op jit(solution)/shard_map/ppermute | solution.py:340
  194.4 18.0 %collective-permute-start.10 = (bf16[1024,128]{1,0:T(8,128)(2,1)S(1)}, bf16[1024,128]{1,0:T(8,128)(2,1)S(1)}, u32[]{:S(2)}, u32[]{:S(2)}) collective-permute-start(bf16[1024,128]{1,0:T(8,128)(2,1)S(1)} %collective-permute-done.9.rest_4_), channel_id=1, source_target_pairs={{0,12},{4,0},{8,4},{12,8},{1,13},{5,1},{9,5},{13,9},{2,14},{6,2},{... | collective-permute-start | bytes 786440 | tf_op jit(solution)/shard_map/ppermute | solution.py:340
  196.7 26.3 %collective-permute-start.11 = (bf16[1024,128]{1,0:T(8,128)(2,1)S(1)}, bf16[1024,128]{1,0:T(8,128)(2,1)S(1)}, u32[]{:S(2)}, u32[]{:S(2)}) collective-permute-start(bf16[1024,128]{1,0:T(8,128)(2,1)S(1)} %collective-permute-done.7.rest_5_), channel_id=1, source_target_pairs={{0,12},{4,0},{8,4},{12,8},{1,13},{5,1},{9,5},{13,9},{2,14},{6,2},{... | collective-permute-start | bytes 786440 | tf_op jit(solution)/shard_map/ppermute | solution.py:340
  266.5 10.1 %collective-permute-start.13 = (bf16[2048,128]{1,0:T(8,128)(2,1)}, bf16[2048,128]{1,0:T(8,128)(2,1)S(1)}, u32[]{:S(2)}, u32[]{:S(2)}) collective-permute-start(bf16[2048,128]{1,0:T(8,128)(2,1)} %get-tuple-element.72), channel_id=1, source_target_pairs={{0,1},{1,0},{2,3},{3,2},{4,5},{5,4},{6,7},{7,6},{8,9},{9,8},{10,11... | collective-permute-start | bytes 1572872 | tf_op jit(solution)/shard_map/ppermute | solution.py:25
  266.5 10.1 %collective-permute-start.14 = (bf16[2048,128]{1,0:T(8,128)(2,1)}, bf16[2048,128]{1,0:T(8,128)(2,1)S(1)}, u32[]{:S(2)}, u32[]{:S(2)}) collective-permute-start(bf16[2048,128]{1,0:T(8,128)(2,1)} %get-tuple-element.75), channel_id=1, source_target_pairs={{0,1},{1,0},{2,3},{3,2},{4,5},{5,4},{6,7},{7,6},{8,9},{9,8},{10,11... | collective-permute-start | bytes 1572872 | tf_op jit(solution)/shard_map/ppermute | solution.py:25
  267.0 9.6 %collective-permute-start.15 = (bf16[2048,128]{1,0:T(8,128)(2,1)}, bf16[2048,128]{1,0:T(8,128)(2,1)}, u32[]{:S(2)}, u32[]{:S(2)}) collective-permute-start(bf16[2048,128]{1,0:T(8,128)(2,1)} %get-tuple-element.74), channel_id=1, source_target_pairs={{0,1},{1,0},{2,3},{3,2},{4,5},{5,4},{6,7},{7,6},{8,9},{9,8},{10,11... | collective-permute-start | bytes 1572872 | tf_op jit(solution)/shard_map/ppermute | solution.py:25
  267.0 9.6 %collective-permute-start.16 = (bf16[2048,128]{1,0:T(8,128)(2,1)}, bf16[2048,128]{1,0:T(8,128)(2,1)}, u32[]{:S(2)}, u32[]{:S(2)}) collective-permute-start(bf16[2048,128]{1,0:T(8,128)(2,1)} %get-tuple-element.73), channel_id=1, source_target_pairs={{0,1},{1,0},{2,3},{3,2},{4,5},{5,4},{6,7},{7,6},{8,9},{9,8},{10,11... | collective-permute-start | bytes 1572872 | tf_op jit(solution)/shard_map/ppermute | solution.py:25
  276.5 10.5 %collective-permute-start.17 = (f32[264,128]{1,0:T(8,128)S(1)}, f32[264,128]{1,0:T(8,128)S(1)}, u32[]{:S(2)}, u32[]{:S(2)}) collective-permute-start(f32[264,128]{1,0:T(8,128)S(1)} %get-tuple-element.54), channel_id=1, source_target_pairs={{0,1},{1,0},{2,3},{3,2},{4,5},{5,4},{6,7},{7,6},{8,9},{9,8},{10,11... | collective-permute-start | bytes 405512 | tf_op jit(solution)/shard_map/ppermute | solution.py:25
  284.6 79.4 %collective-permute-start.20 = (bf16[8192,128]{1,0:T(8,128)(2,1)}, bf16[8192,128]{1,0:T(8,128)(2,1)S(1)}, u32[]{:S(2)}, u32[]{:S(2)}) collective-permute-start(bf16[8192,128]{1,0:T(8,128)(2,1)} %add_convert_fusion.1.rest_1_), channel_id=1, source_target_pairs={{0,2},{1,3},{2,0},{3,1},{4,6},{5,7},{6,4},{7,5},{8,10},{9,11},{10,... | collective-permute-start | bytes 6291464 | tf_op jit(solution)/shard_map/ppermute | solution.py:25
  287.0 49.4 %collective-permute-start.18 = (f32[264,128]{1,0:T(8,128)S(1)}, f32[264,128]{1,0:T(8,128)S(1)}, u32[]{:S(2)}, u32[]{:S(2)}) collective-permute-start(f32[264,128]{1,0:T(8,128)S(1)} %add.48), channel_id=1, source_target_pairs={{0,2},{1,3},{2,0},{3,1},{4,6},{5,7},{6,4},{7,5},{8,10},{9,11},{10,... | collective-permute-start | bytes 405512 | tf_op jit(solution)/shard_map/ppermute | solution.py:25
  364.8 3.5 collective-permute-start.28
  365.5 5.8 %collective-permute-start.12 = (bf16[8192,128]{1,0:T(8,128)(2,1)S(1)}, bf16[8192,128]{1,0:T(8,128)(2,1)S(1)}, u32[]{:S(2)}, u32[]{:S(2)}) collective-permute-start(bf16[8192,128]{1,0:T(8,128)(2,1)S(1)} %copy-done.26), channel_id=1, source_target_pairs={{0,1},{1,0},{2,3},{3,2},{4,5},{5,4},{6,7},{7,6},{8,9},{9,8},{10,11... | collective-permute-start | bytes 6291464 | tf_op jit(solution)/shard_map/ppermute | solution.py:25
  366.0 56.4 %collective-permute-start.24 = (bf16[8192,128]{1,0:T(8,128)(2,1)S(1)}, bf16[8192,128]{1,0:T(8,128)(2,1)S(1)}, u32[]{:S(2)}, u32[]{:S(2)}) collective-permute-start(bf16[8192,128]{1,0:T(8,128)(2,1)S(1)} %get-tuple-element.60), channel_id=1, source_target_pairs={{0,1},{1,0},{2,3},{3,2},{4,5},{5,4},{6,7},{7,6},{8,9},{9,8},{10,11... | collective-permute-start | bytes 6291464 | tf_op jit(solution)/shard_map/ppermute | solution.py:25
  368.8 53.6 %collective-permute-start.29 = (bf16[8192,128]{1,0:T(8,128)(2,1)S(1)}, bf16[8192,128]{1,0:T(8,128)(2,1)S(1)}, u32[]{:S(2)}, u32[]{:S(2)}) collective-permute-start(bf16[8192,128]{1,0:T(8,128)(2,1)S(1)} %add_convert_fusion), channel_id=1, source_target_pairs={{0,2},{1,3},{2,0},{3,1},{4,6},{5,7},{6,4},{7,5},{8,10},{9,11},{10,... | collective-permute-start | bytes 6291464 | tf_op jit(solution)/shard_map/ppermute | solution.py:25
  378.3 4.2 collective-permute-start.21
  382.5 37.7 %collective-permute-start.22 = (f32[256,128]{1,0:T(8,128)S(1)}, f32[256,128]{1,0:T(8,128)S(1)}, u32[]{:S(2)}, u32[]{:S(2)}) collective-permute-start(f32[256,128]{1,0:T(8,128)S(1)} %add.50), channel_id=1, source_target_pairs={{0,2},{1,3},{2,0},{3,1},{4,6},{5,7},{6,4},{7,5},{8,10},{9,11},{10,... | collective-permute-start | bytes 393224 | tf_op jit(solution)/shard_map/ppermute | solution.py:25
  384.4 37.9 %collective-permute-start.34 = (f32[264,128]{1,0:T(8,128)S(1)}, f32[264,128]{1,0:T(8,128)S(1)}, u32[]{:S(2)}, u32[]{:S(2)}) collective-permute-start(f32[264,128]{1,0:T(8,128)S(1)} %add.55), channel_id=1, source_target_pairs={{0,2},{1,3},{2,0},{3,1},{4,6},{5,7},{6,4},{7,5},{8,10},{9,11},{10,... | collective-permute-start | bytes 405512 | tf_op jit(solution)/shard_map/ppermute | solution.py:25
  420.2 6.4 %collective-permute-start.23 = (f32[256,128]{1,0:T(8,128)S(1)}, f32[256,128]{1,0:T(8,128)S(1)}, u32[]{:S(2)}, u32[]{:S(2)}) collective-permute-start(f32[256,128]{1,0:T(8,128)S(1)} %add.51), channel_id=1, source_target_pairs={{0,1},{1,0},{2,3},{3,2},{4,5},{5,4},{6,7},{7,6},{8,9},{9,8},{10,11... | collective-permute-start | bytes 393224 | tf_op jit(solution)/shard_map/ppermute | solution.py:25
  422.3 4.3 collective-permute-start.35
  427.6 5.8 %collective-permute-start.31 = (f32[256,128]{1,0:T(8,128)S(1)}, f32[256,128]{1,0:T(8,128)S(1)}, u32[]{:S(2)}, u32[]{:S(2)}) collective-permute-start(f32[256,128]{1,0:T(8,128)S(1)} %add.53), channel_id=1, source_target_pairs={{0,2},{1,3},{2,0},{3,1},{4,6},{5,7},{6,4},{7,5},{8,10},{9,11},{10,... | collective-permute-start | bytes 393224 | tf_op jit(solution)/shard_map/ppermute | solution.py:25
  (54 other events, 721.2 us)
Sparse Core Ops, SparseCore 0:
  94.1 45.3 reduce-scatter.2
  167.0 61.3 reduce-scatter.4
  263.7 44.2 all-gather.1

commit v7 on v6

--- a/solution.py
+++ b/solution.py
@@ -9,7 +9,6 @@
 
 CHUNKS = 2
 NEAR_PIECES = 4
-RING_CUTS = 2
 MIB = 1024 * 1024
 HBM = pl.BlockSpec(memory_space=pl.ANY)
 VMEM = pl.BlockSpec(memory_space=pltpu.VMEM)
@@ -166,19 +165,16 @@
     )(src, inv, nbr, self_term, *parts)
 
 
-def activate(shares, bias, cot, hidden, c, after):
-    share, wide = shares[0].shape
+def activate(pre, bias, cot, hidden, c):
+    share, wide = pre.shape
     hid = cot.shape[1]
     chunk = pl.BlockSpec((share, wide), lambda i: (0, c))
     whole = pl.BlockSpec((share, wide), lambda i: (0, 0))
     held = [] if hidden is None else [hidden]
-    n = len(shares)
-
-    def kernel(bias_ref, cot_ref, *rest):
+
+    def kernel(bias_ref, cot_ref, pre_ref, *rest):
         hidden_ref, grad_ref = rest[-2:]
-        value = bias_ref[...]
-        for ref in rest[:n]:
-            value = value + ref[...].astype(jnp.float32)
+        value = pre_ref[...].astype(jnp.float32) + bias_ref[...]
         sigma = jax.nn.sigmoid(value)
         hidden_ref[...] = (value * sigma).astype(jnp.bfloat16)
         slope = sigma * (1.0 + value * (1.0 - sigma))
@@ -187,39 +183,30 @@
     return pl.pallas_call(
         kernel,
         grid=(1,),
-        in_specs=[pl.BlockSpec((1, wide), lambda i: (0, c)), chunk] + [whole] * n + [HBM] * len(held + after),
+        in_specs=[pl.BlockSpec((1, wide), lambda i: (0, c)), chunk, whole] + [HBM] * len(held),
         out_specs=[chunk, whole],
         out_shape=[
             jax.ShapeDtypeStruct((share, hid), jnp.bfloat16),
             jax.ShapeDtypeStruct((share, wide), jnp.bfloat16),
         ],
-        input_output_aliases={2 + n: 0} if held else {},
+        input_output_aliases={3: 0} if held else {},
         compiler_params=pltpu.CompilerParams(vmem_limit_bytes=24 * MIB),
-        cost_estimate=cost(20 * share * wide, (6 + 2 * n) * share * wide),
+        cost_estimate=cost(20 * share * wide, 8 * share * wide),
         name="activate",
-    )(bias, cot, *shares, *held, *after)
-
-
-def spread_tiles(order, src, inv, nbr, pieces, n, after):
-    cut, wide = pieces[0][0].shape
-    shares, cuts = len(pieces), len(pieces[0])
-    m = shares * cuts
-    rows = m * cut
-    pieces = [piece for share in pieces for piece in share]
+    )(bias, cot, pre, *held)
+
+
+def spread_tiles(src, inv, nbr, grad, n, after):
+    rows, wide = grad.shape
     blocks, slots, side = nbr.shape
     step = 512
     assert slots % 2 == 0
 
-    def kernel(order_ref, src_ref, inv_ref, nbr_ref, *rest):
-        outs = rest[m + len(after) : m + len(after) + n + 1]
-        table, grad_ref, ready, sems, out_sems = rest[m + len(after) + n + 1 :]
-        loads = []
-        for s in range(m):
-            at = lax.rem(order_ref[0] + s // cuts, shares) * (cuts * cut) + s % cuts * cut
-            place = pl.ds(pl.multiple_of(at, cut), cut)
-            loads.append(pltpu.make_async_copy(rest[s], grad_ref.at[place, :], sems.at[s]))
-        for load in loads:
-            load.start()
+    def kernel(src_ref, inv_ref, nbr_ref, grad_hbm, *rest):
+        outs = rest[len(after) : len(after) + n]
+        table, grad_ref, ready, sem, out_sems = rest[len(after) + n :]
+        load = pltpu.make_async_copy(grad_hbm, grad_ref, sem)
+        load.start()
         ids = side_ids(side)
 
         @pl.loop(0, n * rows // step)
@@ -228,10 +215,7 @@
                 (step, wide), jnp.float32
             )
 
-        for load in loads:
-            load.wait()
-        copies = [pltpu.make_async_copy(grad_ref, outs[n], out_sems.at[n])]
-        copies[0].start()
+        load.wait()
 
         @pl.loop(0, blocks, unroll=2)
         def _(b):
@@ -253,6 +237,7 @@
                 table[at_one, :] = new_one
                 table[at_two, :] = new_two
 
+        copies = []
         for k in reversed(range(n)):
 
             @pl.loop(0, rows // step)
@@ -269,22 +254,22 @@
 
     return pl.pallas_call(
         kernel,
-        out_shape=[jax.ShapeDtypeStruct((rows, wide), jnp.bfloat16)] * (n + 1),
-        in_specs=[SMEM, SMEM, SMEM, VMEM] + [HBM] * (m + len(after)),
-        out_specs=[HBM] * (n + 1),
+        out_shape=[jax.ShapeDtypeStruct((rows, wide), jnp.bfloat16)] * n,
+        in_specs=[SMEM, SMEM, VMEM, HBM] + [HBM] * len(after),
+        out_specs=[HBM] * n,
         scratch_shapes=[
             pltpu.VMEM((n * rows, wide), jnp.float32),
             pltpu.VMEM((rows, wide), jnp.bfloat16),
             pltpu.VMEM((n, rows, wide), jnp.bfloat16),
-            pltpu.SemaphoreType.DMA((m,)),
-            pltpu.SemaphoreType.DMA((n + 1,)),
+            pltpu.SemaphoreType.DMA,
+            pltpu.SemaphoreType.DMA((n,)),
         ],
         compiler_params=pltpu.CompilerParams(vmem_limit_bytes=40 * MIB),
         cost_estimate=cost(
             8 * blocks * slots * side * side * wide, 2 * n * rows * wide + 2 * rows * wide
         ),
         name="spread_tiles",
-    )(order, src, inv, nbr, *pieces, *after)
+    )(src, inv, nbr, grad, *after)
 
 
 def weight_grad(low, feat_t, grads, with_sum):
@@ -330,18 +315,6 @@
     )(low, feat_t, *grads)
 
 
-def gather_shares(value, n, ring):
-    if not ring:
-        return [[lax.all_gather(value, "feat", axis=0, tiled=True)]]
-    cut = value.shape[0] // RING_CUTS
-    steps = [[value[h * cut : (h + 1) * cut] for h in range(RING_CUTS)]]
-    for _ in range(n - 1):
-        steps.append(
-            [lax.ppermute(v, "feat", [(i, (i - 1) % n) for i in range(n)]) for v in steps[-1]]
-        )
-    return steps
-
-
 def on_device(n_node, n_feat, feat_t, src_blocks, nbr_rows, tile_counts, w_neigh, w_self, bias, cotangent):
     width, rows = feat_t.shape
     hid = w_neigh.shape[1]
@@ -358,11 +331,9 @@
     projected = project(feat_t, w_neigh, CHUNKS, jnp.bfloat16, [])
     own_terms = project(feat_t, w_self, CHUNKS, jnp.float32, projected[:1])
 
-    ring = n_feat <= 4
-    feat_index = jnp.reshape(lax.axis_index("feat"), (1,)).astype(jnp.int32)
-    in_place = jnp.zeros((1,), jnp.int32)
     low = jnp.reshape(jnp.bitwise_and(me, 1), (1,)).astype(jnp.int32)
-    part_pres = []
+    hidden = None
+    part_pres, pieces = [], []
     for c in range(CHUNKS):
         held = {0: projected[c]}
         for mask in reversed(masks_of(n_node)):
@@ -373,38 +344,23 @@
                     value, _ = lax.optimization_barrier((value, behind))
                 held[k ^ mask] = swap(value, mask, n_node)
         gathered = [held[k] for k in range(n_node)]
-        part_pres.append(
-            mean_tiles(src, inv, nbr, gathered, own_terms[c], n_feat)
-        )
-    hidden = None
-    grad_pres, pieces = [], []
-    for c in range(CHUNKS):
-        part_pre = part_pres[c]
+        own_term = own_terms[c]
         if pieces:
-            steps = pieces[-1]
-            near_end = steps[max(len(steps) - 2, 0)]
-            part_pre, near_end[-1] = lax.optimization_barrier((part_pre, near_end[-1]))
-        shares = [lax.psum_scatter(part_pre, "feat", scatter_dimension=0, tiled=True)]
-        hidden, grad_pre = activate(
-            shares, bias_row, cot_rows, hidden, c, part_pres[c + 1 : c + 2]
-        )
-        grad_pres.append(grad_pre)
-        pieces.append(gather_shares(grad_pre, n_feat, ring and c < CHUNKS - 1))
+            own_term, _ = lax.optimization_barrier((own_term, grad_pre))
+        part_pre = mean_tiles(src, inv, nbr, gathered, own_term, n_feat)
+        part_pres.append(part_pre)
+        if pieces:
+            part_pre, pieces[-1] = lax.optimization_barrier((part_pre, pieces[-1]))
+        pre = lax.psum_scatter(part_pre, "feat", scatter_dimension=0, tiled=True)
+        hidden, grad_pre = activate(pre, bias_row, cot_rows, hidden, c)
+        pieces.append(lax.all_gather(grad_pre, "feat", axis=0, tiled=True))
 
     grads_n, grads_s, sums = [], [], []
     after = []
     arrived = None
     sent = []
     for c in range(CHUNKS):
-        *tables, piece = spread_tiles(
-            feat_index if len(pieces[c]) > 1 else in_place,
-            src,
-            inv,
-            nbr,
-            pieces[c],
-            n_node,
-            after,
-        )
+        tables = spread_tiles(src, inv, nbr, pieces[c], n_node, after)
         held = {k: [v] for k, v in enumerate(tables)}
         for mask in masks_of(n_node):
             left = {}
@@ -426,8 +382,7 @@
                 held = {k: [total_of(v)] if k else v for k, v in held.items()}
         arrived = held[0][-1]
         sent.append(held[0])
-        both = sum_over_node(*weight_grad(low, feat_t, [piece], True), low, n_node)
-        after = after + [both]
+        both = sum_over_node(*weight_grad(low, feat_t, [pieces[c]], True), low, n_node)
         grads_s.append(both[:width])
         sums.append(both[width])
     for terms in sent:

time: 443 us -> 410 us (0.926)
  starting transfers between devices: 36.5 us -> 16.6 us
  local copies, waits for them, and re-layouts: 45.2 us -> 30.8 us
  other arithmetic: 13.2 us -> 8.57 us
    all_gather x1 -> x2, waiting for transfers between devices: 0.02 us -> 58.6 us  [on_device(): pieces.append(lax.all_gather(grad_pre, 'feat', axis=0, tiled=True))]
    ppermute x6 -> x0, waiting for transfers between devices: 54.7 us -> none  [gather_shares(): lax.ppermute(v, 'feat', [(i, (i - 1) % n) for i in range(n)])]
    ppermute x6 -> x0, starting transfers between devices: 18.5 us -> none  [gather_shares(): lax.ppermute(v, 'feat', [(i, (i - 1) % n) for i in range(n)])]
    ppermute x30, waiting for transfers between devices: 157 us -> 140 us  [swap(): return lax.ppermute(value, 'node', [(i, i ^ mask) for i in range(n)])]
    reduce_scatter x2, waiting for transfers between devices: 0.02 us -> 15.6 us  [on_device(): pre = lax.psum_scatter(part_pre, 'feat', scatter_dimension=0, tiled=True)]
    unnamed x93 -> x61, local copies, waits for them, and re-layouts: 42 us -> 28.9 us
    convert_element_type x2, other arithmetic: 8.44 us -> 3.85 us  [total_of(): return sum((v.astype(jnp.float32) for v in values)).astype(jnp.bfloat16)]
  transfers between devices with their start and end apart: 39 -> 34, of which waited for: 21 -> 21; matrix products, arithmetic and copies ran while one was open for 3% -> 2% of each run, Pallas kernels for 26% -> 23%
where the time goes in v7:
time: 410 us; the launch traced here: 409 us
  waiting for transfers between devices  214 us (52%)
  Pallas kernels  125 us (30%)
  local copies, waits for them, and re-layouts  30.8 us (8%)
  starting transfers between devices  16.6 us (4%)
  between operations  14.2 us (3%)
  other arithmetic  8.57 us (2%)
    ppermute x30, waiting for transfers between devices, swap(): return lax.ppermute(value, 'node', [(i, i ^ mask) for i in range(n)])  140 us
    all_gather x2, waiting for transfers between devices, on_device(): pieces.append(lax.all_gather(grad_pre, 'feat', axis=0, tiled=True))  58.6 us
    pallas_call x2, Pallas kernels, spread_tiles(): pl.pallas_call(kernel, out_shape=[jax.ShapeDtypeStruct((rows, wide), jnp....  47.7 us
    pallas_call x2, Pallas kernels, mean_tiles(): pl.pallas_call(kernel, out_shape=jax.ShapeDtypeStruct((rows, wide), jnp.b...  47.1 us
    unnamed x61, local copies, waits for them, and re-layouts  28.9 us
    pallas_call x4, Pallas kernels, weight_grad(): pl.pallas_call(kernel, grid=(rows // step,), in_specs=[SMEM, pl.BlockSpec...  17.7 us
    ppermute x30, starting transfers between devices, swap(): return lax.ppermute(value, 'node', [(i, i ^ mask) for i in range(n)])  16.2 us
    reduce_scatter x2, waiting for transfers between devices, on_device(): pre = lax.psum_scatter(part_pre, 'feat', scatter_dimension=0, tiled=True)  15.6 us
  transfers between devices with their start and end apart: 34, of which 21 were waited for; matrix products, arithmetic and copies ran while one was open for 2% of the time, Pallas kernels for 23%

profile of v7, /device:TPU:0, one launch (start us, length us, event | category | flops | bytes accessed | tf_op | source)
XLA Modules:
  0.0 409.0 jit_solution(2640036208095674168)
XLA Ops:
  7.2 3.4 copy-done
  11.5 4.5 %project.2 = (bf16[128,8192]{1,0:T(8,128)(2,1)S(1)}, bf16[128,8192]{1,0:T(8,128)(2,1)S(1)}) custom-call(bf16[512,8192]{1,0:T(8,128)(2,1)S(1)} %copy-done, bf16[512,256]{1,0:T(8,128)(2,1)S(1)} %copy-done.17), custom_call_target="tpu_custom_call" | custom-call | flops 2147483648 | bytes 16777216 | tf_op jit(solution)/shard_map/project/pallas_call | solution.py:79
  17.4 3.0 collective-permute-start.1
  20.4 4.8 %project.3 = (f32[128,8192]{1,0:T(8,128)S(1)}, f32[128,8192]{1,0:T(8,128)S(1)}) custom-call(bf16[512,8192]{1,0:T(8,128)(2,1)S(1)} %copy-done, bf16[512,256]{1,0:T(8,128)(2,1)S(1)} %copy-done.18, bf16[128,8192]{1,0:T(8,128)(2,1)S(1)} %get-tuple-element.35.rest_0_), custom_call_target="tpu_custom_call" | custom-call | flops 2147483648 | bytes 16777216 | tf_op jit(solution)/shard_map/project/pallas_call | solution.py:79
  25.2 2.0 copy-done.21
  27.2 2.0 copy-done.22
  29.2 36.9 %collective-permute-done.1.rest_2_ = bf16[128,8192]{1,0:T(8,128)(2,1)} collective-permute-done((bf16[128,8192]{1,0:T(8,128)(2,1)S(1)}, bf16[128,8192]{1,0:T(8,128)(2,1)}, u32[]{:S(2)}, u32[]{:S(2)}) %collective-permute-start.1) | collective-permute-done | bytes 2097184 | tf_op jit(solution)/shard_map/ppermute | solution.py:24
  68.5 2.2 collective-permute-done.2.rest_3_
  70.6 23.6 %mean_tiles.2 = bf16[8192,128]{1,0:T(8,128)(2,1)} custom-call(s32[64,16]{1,0:T(8,128)} %fusion.2.src_ref, f32[64]{0:T(128)} %convert_divide_fusion.inv_ref, s32[64,16,128]{2,1,0:T(8,128)} %broadcast_select_fusion.nbr_ref, f32[128,8192]{1,0:T(8,128)} %copy-done.22, bf16[128,8192]{1,0:T(8,128)(2,1)} %copy-done.11, ...), custom_call_target="tpu_custom_call" | custom-call | flops 17179869184 | bytes 14680064 | tf_op jit(solution)/shard_map/mean_tiles/pallas_call | solution.py:148
  94.4 1.8 collective-permute-start.4
  96.2 46.1 %collective-permute-done.4.rest_2_ = bf16[128,8192]{1,0:T(8,128)(2,1)} collective-permute-done((bf16[128,8192]{1,0:T(8,128)(2,1)S(1)}, bf16[128,8192]{1,0:T(8,128)(2,1)}, u32[]{:S(2)}, u32[]{:S(2)}) %collective-permute-start.4) | collective-permute-done | bytes 2097184 | tf_op jit(solution)/shard_map/ppermute | solution.py:24
  143.3 1.7 activate.2
  145.1 1.6 collective-permute-done.5.rest_3_
  146.7 23.5 %mean_tiles.3 = bf16[8192,128]{1,0:T(8,128)(2,1)} custom-call(s32[64,16]{1,0:T(8,128)} %fusion.2.src_ref, f32[64]{0:T(128)} %convert_divide_fusion.inv_ref, s32[64,16,128]{2,1,0:T(8,128)} %broadcast_select_fusion.nbr_ref, f32[128,8192]{1,0:T(8,128)} %copy-done.21, bf16[128,8192]{1,0:T(8,128)(2,1)} %copy-done.23, ...), custom_call_target="tpu_custom_call" | custom-call | flops 17179869184 | bytes 14680064 | tf_op jit(solution)/shard_map/mean_tiles/pallas_call | solution.py:148
  170.2 22.5 %all-gather.3.cloned.1.call-done.grad_hbm.rest_0_ = bf16[8192,128]{1,0:T(8,128)(2,1)} async-done(((bf16[2048,128]{1,0:T(8,128)(2,1)}), bf16[8192,128]{1,0:T(8,128)(2,1)}) %all-gather.3.cloned.1.call-update) | async-done | bytes 2097168 | tf_op jit(solution)/shard_map/all_gather | solution.py:356
  195.6 23.8 %spread_tiles.2 = (bf16[8192,128]{1,0:T(8,128)(2,1)S(1)}, bf16[8192,128]{1,0:T(8,128)(2,1)}, bf16[8192,128]{1,0:T(8,128)(2,1)S(1)}, bf16[8192,128]{1,0:T(8,128)(2,1)S(1)}) custom-call(s32[64,16]{1,0:T(8,128)S(1)} %copy-done.19, f32[64]{0:T(128)S(1)} %copy-done.25, s32[64,16,128]{2,1,0:T(8,128)S(1)} %copy-done.13, bf16[8192,128]{1,0:T(8,128)(2,1)S(1)} %copy-done.5), custom_call_target="tpu_custom_call" | custom-call | flops 17179869184 | bytes 10485760 | tf_op jit(solution)/shard_map/spread_tiles/pallas_call | solution.py:255
  222.2 15.6 %reduce-scatter.5.cloned.1.call-done.pre_ref = bf16[2048,128]{1,0:T(8,128)(2,1)} async-done(((bf16[8192,128]{1,0:T(8,128)(2,1)}), bf16[2048,128]{1,0:T(8,128)(2,1)}) %reduce-scatter.5.cloned.1.call-update) | async-done | bytes 524304 | tf_op jit(solution)/shard_map/reduce_scatter | solution.py:354
  240.9 1.7 fusion.8
  246.7 2.0 add_convert_fusion.1.rest_0_
  250.2 36.1 %all-gather.5.cloned.1.call-done.grad_hbm.rest_0_ = bf16[8192,128]{1,0:T(8,128)(2,1)} async-done(((bf16[2048,128]{1,0:T(8,128)(2,1)}), bf16[8192,128]{1,0:T(8,128)(2,1)}) %all-gather.5.cloned.1.call-update) | async-done | bytes 2097168 | tf_op jit(solution)/shard_map/all_gather | solution.py:356
  288.9 23.8 %spread_tiles.3 = (bf16[8192,128]{1,0:T(8,128)(2,1)S(1)}, bf16[8192,128]{1,0:T(8,128)(2,1)}, bf16[8192,128]{1,0:T(8,128)(2,1)S(1)}, bf16[8192,128]{1,0:T(8,128)(2,1)S(1)}) custom-call(s32[64,16]{1,0:T(8,128)S(1)} %copy-done.19, f32[64]{0:T(128)S(1)} %copy-done.25, s32[64,16,128]{2,1,0:T(8,128)S(1)} %copy-done.14, bf16[8192,128]{1,0:T(8,128)(2,1)S(1)} %copy-done.7, ...), custom_call_target="tpu_custom_call" | custom-call | flops 17179869184 | bytes 10485760 | tf_op jit(solution)/shard_map/spread_tiles/pallas_call | solution.py:255
  318.6 1.9 add_convert_fusion
  322.0 3.4 copy-done.1
  326.9 3.6 weight_grad.6
  332.6 5.3 %weight_grad.4 = (f32[256,128]{1,0:T(8,128)S(1)}, f32[256,128]{1,0:T(8,128)S(1)}) custom-call(s32[1]{0:T(128)} %bitcast.3.low_ref, bf16[512,8192]{1,0:T(8,128)(2,1)S(1)} %copy-done.1, bf16[8192,128]{1,0:T(8,128)(2,1)S(1)} %copy-done.10, bf16[8192,128]{1,0:T(8,128)(2,1)} %collective-permute-done.6.rest_1_, bf16[8192,128]{1,0:T(8,128)(2,1)} %collective-permute-done.11.rest_2_), custom_call_target="tpu_custom_call" | custom-call | flops 1073741824 | bytes 10485760 | tf_op jit(solution)/shard_map/weight_grad/pallas_call | solution.py:304
  338.0 33.3 %collective-permute-done.25 = f32[264,128]{1,0:T(8,128)S(1)} collective-permute-done((f32[264,128]{1,0:T(8,128)S(1)}, f32[264,128]{1,0:T(8,128)S(1)}, u32[]{:S(2)}, u32[]{:S(2)}) %collective-permute-start.25) | collective-permute-done | bytes 135200 | tf_op jit(solution)/shard_map/ppermute | solution.py:24
  371.4 3.6 weight_grad.7
  378.1 3.9 collective-permute-done.13
  382.1 1.9 collective-permute-done.28
  384.1 3.4 copy-done.2
  387.5 5.2 %weight_grad.5 = (f32[256,128]{1,0:T(8,128)S(1)}, f32[256,128]{1,0:T(8,128)S(1)}) custom-call(s32[1]{0:T(128)} %bitcast.3.low_ref, bf16[512,8192]{1,0:T(8,128)(2,1)S(1)} %copy-done.2, bf16[8192,128]{1,0:T(8,128)(2,1)S(1)} %get-tuple-element.56.rest_0_, bf16[8192,128]{1,0:T(8,128)(2,1)} %collective-permute-done.15.rest_1_, ...), custom_call_target="tpu_custom_call" | custom-call | flops 1073741824 | bytes 10485760 | tf_op jit(solution)/shard_map/weight_grad/pallas_call | solution.py:304
  395.8 4.3 %collective-permute-done.22 = f32[256,128]{1,0:T(8,128)S(1)} collective-permute-done((f32[256,128]{1,0:T(8,128)S(1)}, f32[256,128]{1,0:T(8,128)S(1)}, u32[]{:S(2)}, u32[]{:S(2)}) %collective-permute-start.22) | collective-permute-done | bytes 131104 | tf_op jit(solution)/shard_map/ppermute | solution.py:24
  (141 shorter events, 42.6 us)
Async XLA Ops:
  7.2 135.1 %reduce-scatter.3.cloned.1.call-start = ((), (), s32[]{:S(2)}) async-start(), calls=%async_computation.2 | async-start | bytes 2621440 | tf_op jit(solution)/shard_map/reduce_scatter | solution.py:354
  17.4 48.7 %collective-permute-start.1 = (bf16[128,8192]{1,0:T(8,128)(2,1)S(1)}, bf16[128,8192]{1,0:T(8,128)(2,1)}, u32[]{:S(2)}, u32[]{:S(2)}) collective-permute-start(bf16[128,8192]{1,0:T(8,128)(2,1)S(1)} %get-tuple-element.35.rest_0_), channel_id=1, source_target_pairs={{0,2},{1,3},{2,0},{3,1},{4,6},{5,7},{6,4},{7,5},{8,10},{9,11},{10,... | collective-permute-start | bytes 6291464 | tf_op jit(solution)/shard_map/ppermute | solution.py:24
  20.4 48.1 %collective-permute-start = (bf16[128,8192]{1,0:T(8,128)(2,1)S(1)}, bf16[128,8192]{1,0:T(8,128)(2,1)}, u32[]{:S(2)}, u32[]{:S(2)}) collective-permute-start(bf16[128,8192]{1,0:T(8,128)(2,1)S(1)} %get-tuple-element.35.rest_0_), channel_id=1, source_target_pairs={{0,1},{1,0},{2,3},{3,2},{4,5},{5,4},{6,7},{7,6},{8,9},{9,8},{10,11... | collective-permute-start | bytes 6291464 | tf_op jit(solution)/shard_map/ppermute | solution.py:24
  66.1 4.5 %collective-permute-start.2 = (bf16[128,8192]{1,0:T(8,128)(2,1)}, bf16[128,8192]{1,0:T(8,128)(2,1)}, u32[]{:S(2)}, u32[]{:S(2)}) collective-permute-start(bf16[128,8192]{1,0:T(8,128)(2,1)} %collective-permute-done.1.rest_2_), channel_id=1, source_target_pairs={{0,1},{1,0},{2,3},{3,2},{4,5},{5,4},{6,7},{7,6},{8,9},{9,8},{10,11... | collective-permute-start | bytes 6291464 | tf_op jit(solution)/shard_map/ppermute | solution.py:24
  94.3 98.4 %all-gather.3.cloned.1.call-start = ((), (), s32[]{:S(2)}) async-start(), calls=%async_computation.3 | async-start | bytes 2621440 | tf_op jit(solution)/shard_map/all_gather | solution.py:356
  94.4 47.9 %collective-permute-start.4 = (bf16[128,8192]{1,0:T(8,128)(2,1)S(1)}, bf16[128,8192]{1,0:T(8,128)(2,1)}, u32[]{:S(2)}, u32[]{:S(2)}) collective-permute-start(bf16[128,8192]{1,0:T(8,128)(2,1)S(1)} %copy-done.24), channel_id=1, source_target_pairs={{0,2},{1,3},{2,0},{3,1},{4,6},{5,7},{6,4},{7,5},{8,10},{9,11},{10,... | collective-permute-start | bytes 6291464 | tf_op jit(solution)/shard_map/ppermute | solution.py:24
  96.2 48.9 %collective-permute-start.3 = (bf16[128,8192]{1,0:T(8,128)(2,1)S(1)}, bf16[128,8192]{1,0:T(8,128)(2,1)}, u32[]{:S(2)}, u32[]{:S(2)}) collective-permute-start(bf16[128,8192]{1,0:T(8,128)(2,1)S(1)} %copy-done.24), channel_id=1, source_target_pairs={{0,1},{1,0},{2,3},{3,2},{4,5},{5,4},{6,7},{7,6},{8,9},{9,8},{10,11... | collective-permute-start | bytes 6291464 | tf_op jit(solution)/shard_map/ppermute | solution.py:24
  142.2 4.5 %collective-permute-start.5 = (bf16[128,8192]{1,0:T(8,128)(2,1)}, bf16[128,8192]{1,0:T(8,128)(2,1)}, u32[]{:S(2)}, u32[]{:S(2)}) collective-permute-start(bf16[128,8192]{1,0:T(8,128)(2,1)} %collective-permute-done.4.rest_2_), channel_id=1, source_target_pairs={{0,1},{1,0},{2,3},{3,2},{4,5},{5,4},{6,7},{7,6},{8,9},{9,8},{10,11... | collective-permute-start | bytes 6291464 | tf_op jit(solution)/shard_map/ppermute | solution.py:24
  145.1 92.7 %reduce-scatter.5.cloned.1.call-start = ((), (), s32[]{:S(2)}) async-start(), calls=%async_computation.4 | async-start | bytes 2621440 | tf_op jit(solution)/shard_map/reduce_scatter | solution.py:354
  192.7 93.5 %all-gather.5.cloned.1.call-start = ((), (), s32[]{:S(2)}) async-start(), calls=%async_computation.5 | async-start | bytes 2621440 | tf_op jit(solution)/shard_map/all_gather | solution.py:356
  242.5 2.0 collective-permute-start.10
  242.6 2.6 collective-permute-start.7
  243.1 2.9 collective-permute-start.8
  243.2 3.6 collective-permute-start.9
  248.7 64.0 %collective-permute-start.11 = (bf16[8192,128]{1,0:T(8,128)(2,1)}, bf16[8192,128]{1,0:T(8,128)(2,1)}, u32[]{:S(2)}, u32[]{:S(2)}) collective-permute-start(bf16[8192,128]{1,0:T(8,128)(2,1)} %add_convert_fusion.1.rest_0_), channel_id=1, source_target_pairs={{0,2},{1,3},{2,0},{3,1},{4,6},{5,7},{6,4},{7,5},{8,10},{9,11},{10,... | collective-permute-start | bytes 6291464 | tf_op jit(solution)/shard_map/ppermute | solution.py:24
  312.9 2.0 collective-permute-start.16
  313.0 2.6 collective-permute-start.17
  313.5 3.6 collective-permute-start.18
  313.6 5.1 %collective-permute-start.19 = (bf16[2048,128]{1,0:T(8,128)(2,1)S(1)}, bf16[2048,128]{1,0:T(8,128)(2,1)S(1)}, u32[]{:S(2)}, u32[]{:S(2)}) collective-permute-start(bf16[2048,128]{1,0:T(8,128)(2,1)S(1)} %get-tuple-element.67), channel_id=1, source_target_pairs={{0,1},{1,0},{2,3},{3,2},{4,5},{5,4},{6,7},{7,6},{8,9},{9,8},{10,11... | collective-permute-start | bytes 1572872 | tf_op jit(solution)/shard_map/ppermute | solution.py:24
  314.0 18.6 %collective-permute-start.6 = (bf16[8192,128]{1,0:T(8,128)(2,1)}, bf16[8192,128]{1,0:T(8,128)(2,1)}, u32[]{:S(2)}, u32[]{:S(2)}) collective-permute-start(bf16[8192,128]{1,0:T(8,128)(2,1)} %get-tuple-element.48), channel_id=1, source_target_pairs={{0,1},{1,0},{2,3},{3,2},{4,5},{5,4},{6,7},{7,6},{8,9},{9,8},{10,11... | collective-permute-start | bytes 6291464 | tf_op jit(solution)/shard_map/ppermute | solution.py:24
  314.9 69.2 %collective-permute-start.15 = (bf16[8192,128]{1,0:T(8,128)(2,1)}, bf16[8192,128]{1,0:T(8,128)(2,1)}, u32[]{:S(2)}, u32[]{:S(2)}) collective-permute-start(bf16[8192,128]{1,0:T(8,128)(2,1)} %get-tuple-element.57), channel_id=1, source_target_pairs={{0,1},{1,0},{2,3},{3,2},{4,5},{5,4},{6,7},{7,6},{8,9},{9,8},{10,11... | collective-permute-start | bytes 6291464 | tf_op jit(solution)/shard_map/ppermute | solution.py:24
  320.5 63.6 %collective-permute-start.20 = (bf16[8192,128]{1,0:T(8,128)(2,1)}, bf16[8192,128]{1,0:T(8,128)(2,1)}, u32[]{:S(2)}, u32[]{:S(2)}) collective-permute-start(bf16[8192,128]{1,0:T(8,128)(2,1)} %add_convert_fusion), channel_id=1, source_target_pairs={{0,2},{1,3},{2,0},{3,1},{4,6},{5,7},{6,4},{7,5},{8,10},{9,11},{10,... | collective-permute-start | bytes 6291464 | tf_op jit(solution)/shard_map/ppermute | solution.py:24
  331.9 39.3 %collective-permute-start.25 = (f32[264,128]{1,0:T(8,128)S(1)}, f32[264,128]{1,0:T(8,128)S(1)}, u32[]{:S(2)}, u32[]{:S(2)}) collective-permute-start(f32[264,128]{1,0:T(8,128)S(1)} %add.53), channel_id=1, source_target_pairs={{0,2},{1,3},{2,0},{3,1},{4,6},{5,7},{6,4},{7,5},{8,10},{9,11},{10,... | collective-permute-start | bytes 405512 | tf_op jit(solution)/shard_map/ppermute | solution.py:24
  337.9 37.7 %collective-permute-start.12 = (f32[256,128]{1,0:T(8,128)S(1)}, f32[256,128]{1,0:T(8,128)S(1)}, u32[]{:S(2)}, u32[]{:S(2)}) collective-permute-start(f32[256,128]{1,0:T(8,128)S(1)} %get-tuple-element.55), channel_id=1, source_target_pairs={{0,1},{1,0},{2,3},{3,2},{4,5},{5,4},{6,7},{7,6},{8,9},{9,8},{10,11... | collective-permute-start | bytes 393224 | tf_op jit(solution)/shard_map/ppermute | solution.py:24
  371.3 5.8 %collective-permute-start.26 = (f32[264,128]{1,0:T(8,128)S(1)}, f32[264,128]{1,0:T(8,128)S(1)}, u32[]{:S(2)}, u32[]{:S(2)}) collective-permute-start(f32[264,128]{1,0:T(8,128)S(1)} %add.54), channel_id=1, source_target_pairs={{0,1},{1,0},{2,3},{3,2},{4,5},{5,4},{6,7},{7,6},{8,9},{9,8},{10,11... | collective-permute-start | bytes 405512 | tf_op jit(solution)/shard_map/ppermute | solution.py:24
  375.0 2.1 collective-permute-start.27
  375.6 6.4 %collective-permute-start.13 = (f32[256,128]{1,0:T(8,128)S(1)}, f32[256,128]{1,0:T(8,128)S(1)}, u32[]{:S(2)}, u32[]{:S(2)}) collective-permute-start(f32[256,128]{1,0:T(8,128)S(1)} %add.48), channel_id=1, source_target_pairs={{0,2},{1,3},{2,0},{3,1},{4,6},{5,7},{6,4},{7,5},{8,10},{9,11},{10,... | collective-permute-start | bytes 393224 | tf_op jit(solution)/shard_map/ppermute | solution.py:24
  377.2 6.8 %collective-permute-start.28 = (f32[264,128]{1,0:T(8,128)S(1)}, f32[264,128]{1,0:T(8,128)S(1)}, u32[]{:S(2)}, u32[]{:S(2)}) collective-permute-start(f32[264,128]{1,0:T(8,128)S(1)} %add.55), channel_id=1, source_target_pairs={{0,2},{1,3},{2,0},{3,1},{4,6},{5,7},{6,4},{7,5},{8,10},{9,11},{10,... | collective-permute-start | bytes 405512 | tf_op jit(solution)/shard_map/ppermute | solution.py:24
  382.0 11.2 %collective-permute-start.14 = (f32[256,128]{1,0:T(8,128)S(1)}, f32[256,128]{1,0:T(8,128)S(1)}, u32[]{:S(2)}, u32[]{:S(2)}) collective-permute-start(f32[256,128]{1,0:T(8,128)S(1)} %add.49), channel_id=1, source_target_pairs={{0,1},{1,0},{2,3},{3,2},{4,5},{5,4},{6,7},{7,6},{8,9},{9,8},{10,11... | collective-permute-start | bytes 393224 | tf_op jit(solution)/shard_map/ppermute | solution.py:24
  384.0 9.3 %collective-permute-start.29 = (f32[264,128]{1,0:T(8,128)S(1)}, f32[264,128]{1,0:T(8,128)S(1)}, u32[]{:S(2)}, u32[]{:S(2)}) collective-permute-start(f32[264,128]{1,0:T(8,128)S(1)} %add.56), channel_id=1, source_target_pairs={{0,1},{1,0},{2,3},{3,2},{4,5},{5,4},{6,7},{7,6},{8,9},{9,8},{10,11... | collective-permute-start | bytes 405512 | tf_op jit(solution)/shard_map/ppermute | solution.py:24
  392.7 1.5 collective-permute-start.21
  394.3 5.8 %collective-permute-start.22 = (f32[256,128]{1,0:T(8,128)S(1)}, f32[256,128]{1,0:T(8,128)S(1)}, u32[]{:S(2)}, u32[]{:S(2)}) collective-permute-start(f32[256,128]{1,0:T(8,128)S(1)} %add.51), channel_id=1, source_target_pairs={{0,2},{1,3},{2,0},{3,1},{4,6},{5,7},{6,4},{7,5},{8,10},{9,11},{10,... | collective-permute-start | bytes 393224 | tf_op jit(solution)/shard_map/ppermute | solution.py:24
  (33 other events, 429.4 us)
Sparse Core Ops, SparseCore 0:
  94.4 45.3 reduce-scatter.2
  145.2 47.4 all-gather.2
  195.1 42.6 reduce-scatter.4
  241.0 45.2 all-gather.4

commit v8 on v7

--- a/solution.py
+++ b/solution.py
@@ -29,9 +29,12 @@
     return [1 << i for i in range(n.bit_length() - 1)]
 
 
-def sum_over_node(keep, send, low, n):
+def sum_near(keep, send, n):
+    return keep + swap(send, masks_of(n)[0], n)
+
+
+def sum_far(total, low, n):
     near, *far = masks_of(n)
-    total = keep + swap(send, near, n)
     for mask in far:
         total = total + swap(total, mask, n)
     other = swap(total, near, n)
@@ -272,12 +275,13 @@
     )(src, inv, nbr, grad, *after)
 
 
-def weight_grad(low, feat_t, grads, with_sum):
+def weight_grad(low, feat_t, groups, with_sum):
     width, rows = feat_t.shape
-    wide = grads[0].shape[1]
+    wide = groups[0][0].shape[1]
     step = min(2048, rows)
     tall = width + (16 if with_sum else 0)
     half = tall // 2
+    flat = [array for group in groups for array in group]
 
     def kernel(low_ref, feat_ref, *rest):
         keep_ref, send_ref, total = rest[-3:]
@@ -286,9 +290,15 @@
         def _():
             total[...] = jnp.zeros_like(total)
 
-        value = rest[0][...]
-        if len(grads) > 1:
-            value = sum(ref[...].astype(jnp.float32) for ref in rest[:-3]).astype(jnp.bfloat16)
+        at = 0
+        values = []
+        for group in groups:
+            refs = rest[at : at + len(group)]
+            at += len(group)
+            values.append(refs[0][...])
+            if len(group) > 1:
+                values[-1] = sum(ref[...].astype(jnp.float32) for ref in refs).astype(jnp.bfloat16)
+        value = jnp.concatenate(values, axis=1)
         total[:width, :] += jnp.dot(feat_ref[...], value, preferred_element_type=jnp.float32)
         if with_sum:
             total[width : width + 1, :] += jnp.sum(
@@ -301,18 +311,19 @@
             keep_ref[...] = total[pl.ds(pl.multiple_of(low * half, 8), half), :]
             send_ref[...] = total[pl.ds(pl.multiple_of((1 - low) * half, 8), half), :]
 
+    all_wide = wide * len(groups)
     return pl.pallas_call(
         kernel,
         grid=(rows // step,),
         in_specs=[SMEM, pl.BlockSpec((width, step), lambda i: (0, i))]
-        + [pl.BlockSpec((step, wide), lambda i: (i, 0))] * len(grads),
-        out_specs=[pl.BlockSpec((half, wide), lambda i: (0, 0))] * 2,
-        out_shape=[jax.ShapeDtypeStruct((half, wide), jnp.float32)] * 2,
-        scratch_shapes=[pltpu.VMEM((tall, wide), jnp.float32)],
-        compiler_params=pltpu.CompilerParams(vmem_limit_bytes=16 * MIB),
-        cost_estimate=cost(2 * width * rows * wide, 2 * rows * (width + wide)),
+        + [pl.BlockSpec((step, wide), lambda i: (i, 0))] * len(flat),
+        out_specs=[pl.BlockSpec((half, all_wide), lambda i: (0, 0))] * 2,
+        out_shape=[jax.ShapeDtypeStruct((half, all_wide), jnp.float32)] * 2,
+        scratch_shapes=[pltpu.VMEM((tall, all_wide), jnp.float32)],
+        compiler_params=pltpu.CompilerParams(vmem_limit_bytes=24 * MIB),
+        cost_estimate=cost(2 * width * rows * all_wide, 2 * rows * (width + wide * len(flat))),
         name="weight_grad",
-    )(low, feat_t, *grads)
+    )(low, feat_t, *flat)
 
 
 def on_device(n_node, n_feat, feat_t, src_blocks, nbr_rows, tile_counts, w_neigh, w_self, bias, cotangent):
@@ -355,7 +366,6 @@
         hidden, grad_pre = activate(pre, bias_row, cot_rows, hidden, c)
         pieces.append(lax.all_gather(grad_pre, "feat", axis=0, tiled=True))
 
-    grads_n, grads_s, sums = [], [], []
     after = []
     arrived = None
     sent = []
@@ -382,16 +392,17 @@
                 held = {k: [total_of(v)] if k else v for k, v in held.items()}
         arrived = held[0][-1]
         sent.append(held[0])
-        both = sum_over_node(*weight_grad(low, feat_t, [pieces[c]], True), low, n_node)
-        grads_s.append(both[:width])
-        sums.append(both[width])
-    for terms in sent:
-        grads_n.append(sum_over_node(*weight_grad(low, feat_t, terms, False), low, n_node))
+    early = [[piece] for piece in pieces] + sent[:-1]
+    early = sum_near(*weight_grad(low, feat_t, early, True), n_node)
+    last, early = lax.optimization_barrier((sent[-1], early))
+    late = sum_near(*weight_grad(low, feat_t, [last], False), n_node)
+    early = sum_far(early, low, n_node)
+    late = sum_far(late, low, n_node)
     return (
         hidden.reshape(1, share, hid),
-        jnp.concatenate(grads_n, axis=1),
-        jnp.concatenate(grads_s, axis=1),
-        jnp.concatenate(sums, axis=0),
+        jnp.concatenate([early[:width, hid:], late], axis=1),
+        early[:width, :hid],
+        early[width, :hid],
     )
 
 

time: 410 us -> 396 us (0.966)
  Pallas kernels: 125 us -> 119 us
  waiting for transfers between devices: 214 us -> 209 us
    pallas_call x4 -> x2, Pallas kernels: 17.7 us -> 12.1 us  [weight_grad(): pl.pallas_call(kernel, grid=(rows // step,), in_specs=[SMEM, pl.BlockSpec...]
    ppermute x30 -> x24, waiting for transfers between devices: 140 us -> 135 us  [swap(): return lax.ppermute(value, 'node', [(i, i ^ mask) for i in range(n)])]
    ppermute x30 -> x24, starting transfers between devices: 16.2 us -> 13.4 us  [swap(): return lax.ppermute(value, 'node', [(i, i ^ mask) for i in range(n)])]
    unnamed x61 -> x57, local copies, waits for them, and re-layouts: 28.9 us -> 28.7 us
  transfers between devices with their start and end apart: 34 -> 28, of which waited for: 21 -> 20; matrix products, arithmetic and copies ran while one was open for 2% -> 2% of each run, Pallas kernels for 23% -> 23%
where the time goes in v8:
time: 396 us
  waiting for transfers between devices  209 us (53%)
  Pallas kernels  119 us (30%)
  local copies, waits for them, and re-layouts  31.9 us (8%)
  between operations  14.1 us (4%)
  starting transfers between devices  13.8 us (3%)
  other arithmetic  7.16 us (2%)
    ppermute x24, waiting for transfers between devices, swap(): return lax.ppermute(value, 'node', [(i, i ^ mask) for i in range(n)])  135 us
    all_gather x2, waiting for transfers between devices, on_device(): pieces.append(lax.all_gather(grad_pre, 'feat', axis=0, tiled=True))  58.6 us
    pallas_call x2, Pallas kernels, spread_tiles(): pl.pallas_call(kernel, out_shape=[jax.ShapeDtypeStruct((rows, wide), jnp....  47.7 us
    pallas_call x2, Pallas kernels, mean_tiles(): pl.pallas_call(kernel, out_shape=jax.ShapeDtypeStruct((rows, wide), jnp.b...  47.2 us
    unnamed x57, local copies, waits for them, and re-layouts  28.7 us
    reduce_scatter x2, waiting for transfers between devices, on_device(): pre = lax.psum_scatter(part_pre, 'feat', scatter_dimension=0, tiled=True)  15.6 us
    ppermute x24, starting transfers between devices, swap(): return lax.ppermute(value, 'node', [(i, i ^ mask) for i in range(n)])  13.4 us
    pallas_call x2, Pallas kernels, weight_grad(): pl.pallas_call(kernel, grid=(rows // step,), in_specs=[SMEM, pl.BlockSpec...  12.1 us
  transfers between devices with their start and end apart: 28, of which 20 were waited for; matrix products, arithmetic and copies ran while one was open for 2% of the time, Pallas kernels for 23%

profile of v8, /device:TPU:0, one launch (start us, length us, event | category | flops | bytes accessed | tf_op | source)
XLA Modules:
  0.0 395.5 jit_solution(7141267475746712743)
XLA Ops:
  7.2 3.4 copy-done
  11.5 4.5 %project.2 = (bf16[128,8192]{1,0:T(8,128)(2,1)S(1)}, bf16[128,8192]{1,0:T(8,128)(2,1)S(1)}) custom-call(bf16[512,8192]{1,0:T(8,128)(2,1)S(1)} %copy-done, bf16[512,256]{1,0:T(8,128)(2,1)S(1)} %copy-done.16), custom_call_target="tpu_custom_call" | custom-call | flops 2147483648 | bytes 16777216 | tf_op jit(solution)/shard_map/project/pallas_call | solution.py:82
  17.4 3.0 collective-permute-start.1
  20.4 4.8 %project.3 = (f32[128,8192]{1,0:T(8,128)S(1)}, f32[128,8192]{1,0:T(8,128)S(1)}) custom-call(bf16[512,8192]{1,0:T(8,128)(2,1)S(1)} %copy-done, bf16[512,256]{1,0:T(8,128)(2,1)S(1)} %copy-done.17, bf16[128,8192]{1,0:T(8,128)(2,1)S(1)} %get-tuple-element.35.rest_0_), custom_call_target="tpu_custom_call" | custom-call | flops 2147483648 | bytes 16777216 | tf_op jit(solution)/shard_map/project/pallas_call | solution.py:82
  25.2 2.0 copy-done.20
  27.2 2.0 copy-done.21
  29.2 36.9 %collective-permute-done.1.rest_2_ = bf16[128,8192]{1,0:T(8,128)(2,1)} collective-permute-done((bf16[128,8192]{1,0:T(8,128)(2,1)S(1)}, bf16[128,8192]{1,0:T(8,128)(2,1)}, u32[]{:S(2)}, u32[]{:S(2)}) %collective-permute-start.1) | collective-permute-done | bytes 2097184 | tf_op jit(solution)/shard_map/ppermute | solution.py:24
  68.5 2.2 collective-permute-done.2.rest_3_
  70.6 23.6 %mean_tiles.2 = bf16[8192,128]{1,0:T(8,128)(2,1)} custom-call(s32[64,16]{1,0:T(8,128)} %fusion.2.src_ref, f32[64]{0:T(128)} %convert_divide_fusion.inv_ref, s32[64,16,128]{2,1,0:T(8,128)} %broadcast_select_fusion.nbr_ref, f32[128,8192]{1,0:T(8,128)} %copy-done.21, bf16[128,8192]{1,0:T(8,128)(2,1)} %copy-done.4, ...), custom_call_target="tpu_custom_call" | custom-call | flops 17179869184 | bytes 14680064 | tf_op jit(solution)/shard_map/mean_tiles/pallas_call | solution.py:151
  94.4 1.8 collective-permute-start.4
  96.2 46.1 %collective-permute-done.4.rest_2_ = bf16[128,8192]{1,0:T(8,128)(2,1)} collective-permute-done((bf16[128,8192]{1,0:T(8,128)(2,1)S(1)}, bf16[128,8192]{1,0:T(8,128)(2,1)}, u32[]{:S(2)}, u32[]{:S(2)}) %collective-permute-start.4) | collective-permute-done | bytes 2097184 | tf_op jit(solution)/shard_map/ppermute | solution.py:24
  143.3 1.7 activate.2
  145.1 1.6 collective-permute-done.5.rest_3_
  146.7 23.5 %mean_tiles.3 = bf16[8192,128]{1,0:T(8,128)(2,1)} custom-call(s32[64,16]{1,0:T(8,128)} %fusion.2.src_ref, f32[64]{0:T(128)} %convert_divide_fusion.inv_ref, s32[64,16,128]{2,1,0:T(8,128)} %broadcast_select_fusion.nbr_ref, f32[128,8192]{1,0:T(8,128)} %copy-done.20, bf16[128,8192]{1,0:T(8,128)(2,1)} %copy-done.22, ...), custom_call_target="tpu_custom_call" | custom-call | flops 17179869184 | bytes 14680064 | tf_op jit(solution)/shard_map/mean_tiles/pallas_call | solution.py:151
  170.3 22.5 %all-gather.3.cloned.1.call-done.grad_hbm.rest_0_ = bf16[8192,128]{1,0:T(8,128)(2,1)} async-done(((bf16[2048,128]{1,0:T(8,128)(2,1)}), bf16[8192,128]{1,0:T(8,128)(2,1)}) %all-gather.3.cloned.1.call-update) | async-done | bytes 2097168 | tf_op jit(solution)/shard_map/all_gather | solution.py:367
  195.7 23.9 %spread_tiles.2 = (bf16[8192,128]{1,0:T(8,128)(2,1)S(1)}, bf16[8192,128]{1,0:T(8,128)(2,1)}, bf16[8192,128]{1,0:T(8,128)(2,1)S(1)}, bf16[8192,128]{1,0:T(8,128)(2,1)S(1)}) custom-call(s32[64,16]{1,0:T(8,128)S(1)} %copy-done.18, f32[64]{0:T(128)S(1)} %copy-done.24, s32[64,16,128]{2,1,0:T(8,128)S(1)} %copy-done.12, bf16[8192,128]{1,0:T(8,128)(2,1)S(1)} %copy-done.5), custom_call_target="tpu_custom_call" | custom-call | flops 17179869184 | bytes 10485760 | tf_op jit(solution)/shard_map/spread_tiles/pallas_call | solution.py:258
  222.2 15.6 %reduce-scatter.5.cloned.1.call-done.pre_ref = bf16[2048,128]{1,0:T(8,128)(2,1)} async-done(((bf16[8192,128]{1,0:T(8,128)(2,1)}), bf16[2048,128]{1,0:T(8,128)(2,1)}) %reduce-scatter.5.cloned.1.call-update) | async-done | bytes 524304 | tf_op jit(solution)/shard_map/reduce_scatter | solution.py:365
  240.9 1.7 fusion.8
  246.7 2.0 add_convert_fusion.1.rest_0_
  250.2 36.1 %all-gather.5.cloned.1.call-done.grad_hbm.rest_1_ = bf16[8192,128]{1,0:T(8,128)(2,1)} async-done(((bf16[2048,128]{1,0:T(8,128)(2,1)}), bf16[8192,128]{1,0:T(8,128)(2,1)}) %all-gather.5.cloned.1.call-update) | async-done | bytes 2097168 | tf_op jit(solution)/shard_map/all_gather | solution.py:367
  286.3 1.6 copy-done.9
  288.9 23.8 %spread_tiles.3 = (bf16[8192,128]{1,0:T(8,128)(2,1)S(1)}, bf16[8192,128]{1,0:T(8,128)(2,1)}, bf16[8192,128]{1,0:T(8,128)(2,1)S(1)}, bf16[8192,128]{1,0:T(8,128)(2,1)S(1)}) custom-call(s32[64,16]{1,0:T(8,128)S(1)} %copy-done.18, f32[64]{0:T(128)S(1)} %copy-done.24, s32[64,16,128]{2,1,0:T(8,128)S(1)} %copy-done.13, bf16[8192,128]{1,0:T(8,128)(2,1)S(1)} %copy-done.9, ...), custom_call_target="tpu_custom_call" | custom-call | flops 17179869184 | bytes 10485760 | tf_op jit(solution)/shard_map/spread_tiles/pallas_call | solution.py:258
  318.6 1.9 add_convert_fusion
  322.0 3.4 copy-done.1
  325.4 1.6 copy-done.6
  326.9 1.6 copy-done.8
  330.1 7.0 %weight_grad.2 = (f32[264,384]{1,0:T(8,128)S(1)}, f32[264,384]{1,0:T(8,128)S(1)}) custom-call(s32[1]{0:T(128)} %bitcast.3.low_ref, bf16[512,8192]{1,0:T(8,128)(2,1)S(1)} %copy-done.1, bf16[8192,128]{1,0:T(8,128)(2,1)S(1)} %copy-done.6, bf16[8192,128]{1,0:T(8,128)(2,1)S(1)} %copy-done.10, bf16[8192,128]{1,0:T(8,128)(2,1)S(1)} %copy-done.8, ...), custom_call_target="tpu_custom_call" | custom-call | flops 3221225472 | bytes 18874368 | tf_op jit(solution)/shard_map/weight_grad/pallas_call | solution.py:315
  337.2 1.7 collective-permute-done.18
  339.0 29.5 %collective-permute-done.16.rest_2_ = bf16[8192,128]{1,0:T(8,128)(2,1)} collective-permute-done((bf16[8192,128]{1,0:T(8,128)(2,1)}, bf16[8192,128]{1,0:T(8,128)(2,1)}, u32[]{:S(2)}, u32[]{:S(2)}) %collective-permute-start.16) | collective-permute-done | bytes 2097184 | tf_op jit(solution)/shard_map/ppermute | solution.py:24
  369.9 5.2 %weight_grad.3 = (f32[256,128]{1,0:T(8,128)S(1)}, f32[256,128]{1,0:T(8,128)S(1)}) custom-call(s32[1]{0:T(128)} %bitcast.3.low_ref, bf16[512,8192]{1,0:T(8,128)(2,1)S(1)} %copy-done.1, bf16[8192,128]{1,0:T(8,128)(2,1)S(1)} %get-tuple-element.61.rest_0_, bf16[8192,128]{1,0:T(8,128)(2,1)} %collective-permute-done.10.rest_1_, ...), custom_call_target="tpu_custom_call" | custom-call | flops 1073741824 | bytes 14680064 | tf_op jit(solution)/shard_map/weight_grad/pallas_call | solution.py:315
  375.2 3.8 collective-permute-done.19
  380.8 4.4 %collective-permute-done.22 = f32[256,128]{1,0:T(8,128)S(1)} collective-permute-done((f32[256,128]{1,0:T(8,128)S(1)}, f32[256,128]{1,0:T(8,128)S(1)}, u32[]{:S(2)}, u32[]{:S(2)}) %collective-permute-start.22) | collective-permute-done | bytes 131104 | tf_op jit(solution)/shard_map/ppermute | solution.py:24
  (113 shorter events, 37.2 us)
Async XLA Ops:
  7.2 135.1 %reduce-scatter.3.cloned.1.call-start = ((), (), s32[]{:S(2)}) async-start(), calls=%async_computation.2 | async-start | bytes 2621440 | tf_op jit(solution)/shard_map/reduce_scatter | solution.py:365
  17.4 48.8 %copy-start.26 = (s32[64,16]{0,1:T(8,128)S(1)}, s32[64,16]{0,1:T(8,128)}, u32[]{:S(2)}) copy-start(s32[64,16]{0,1:T(8,128)} %param.9) | copy-start | bytes 12292
  17.4 48.8 %copy-start.27 = (s32[64]{0:T(128)S(1)}, s32[64]{0:T(128)}, u32[]{:S(2)}) copy-start(s32[64]{0:T(128)} %param.11) | copy-start | bytes 772
  17.4 50.1 %copy-start.25 = (s32[64,16,128]{2,1,0:T(8,128)S(1)}, s32[64,16,128]{2,1,0:T(8,128)}, u32[]{:S(2)}) copy-start(s32[64,16,128]{2,1,0:T(8,128)} %param.10) | copy-start | bytes 1572868
  17.4 48.7 %collective-permute-start.1 = (bf16[128,8192]{1,0:T(8,128)(2,1)S(1)}, bf16[128,8192]{1,0:T(8,128)(2,1)}, u32[]{:S(2)}, u32[]{:S(2)}) collective-permute-start(bf16[128,8192]{1,0:T(8,128)(2,1)S(1)} %get-tuple-element.35.rest_0_), channel_id=1, source_target_pairs={{0,2},{1,3},{2,0},{3,1},{4,6},{5,7},{6,4},{7,5},{8,10},{9,11},{10,... | collective-permute-start | bytes 6291464 | tf_op jit(solution)/shard_map/ppermute | solution.py:24
  20.4 48.1 %collective-permute-start = (bf16[128,8192]{1,0:T(8,128)(2,1)S(1)}, bf16[128,8192]{1,0:T(8,128)(2,1)}, u32[]{:S(2)}, u32[]{:S(2)}) collective-permute-start(bf16[128,8192]{1,0:T(8,128)(2,1)S(1)} %get-tuple-element.35.rest_0_), channel_id=1, source_target_pairs={{0,1},{1,0},{2,3},{3,2},{4,5},{5,4},{6,7},{7,6},{8,9},{9,8},{10,11... | collective-permute-start | bytes 6291464 | tf_op jit(solution)/shard_map/ppermute | solution.py:24
  66.1 4.5 %collective-permute-start.2 = (bf16[128,8192]{1,0:T(8,128)(2,1)}, bf16[128,8192]{1,0:T(8,128)(2,1)}, u32[]{:S(2)}, u32[]{:S(2)}) collective-permute-start(bf16[128,8192]{1,0:T(8,128)(2,1)} %collective-permute-done.1.rest_2_), channel_id=1, source_target_pairs={{0,1},{1,0},{2,3},{3,2},{4,5},{5,4},{6,7},{7,6},{8,9},{9,8},{10,11... | collective-permute-start | bytes 6291464 | tf_op jit(solution)/shard_map/ppermute | solution.py:24
  94.3 48.0 %copy-start.2 = (bf16[1,2048,256]{2,1,0:T(8,128)(2,1)S(1)}, bf16[1,2048,256]{2,1,0:T(8,128)(2,1)}, u32[]{:S(2)}) copy-start(bf16[1,2048,256]{2,1,0:T(8,128)(2,1)} %param.15) | copy-start | bytes 3145732
  94.3 98.4 %all-gather.3.cloned.1.call-start = ((), (), s32[]{:S(2)}) async-start(), calls=%async_computation.3 | async-start | bytes 2621440 | tf_op jit(solution)/shard_map/all_gather | solution.py:367
  94.4 47.9 %collective-permute-start.4 = (bf16[128,8192]{1,0:T(8,128)(2,1)S(1)}, bf16[128,8192]{1,0:T(8,128)(2,1)}, u32[]{:S(2)}, u32[]{:S(2)}) collective-permute-start(bf16[128,8192]{1,0:T(8,128)(2,1)S(1)} %copy-done.23), channel_id=1, source_target_pairs={{0,2},{1,3},{2,0},{3,1},{4,6},{5,7},{6,4},{7,5},{8,10},{9,11},{10,... | collective-permute-start | bytes 6291464 | tf_op jit(solution)/shard_map/ppermute | solution.py:24
  96.2 48.9 %collective-permute-start.3 = (bf16[128,8192]{1,0:T(8,128)(2,1)S(1)}, bf16[128,8192]{1,0:T(8,128)(2,1)}, u32[]{:S(2)}, u32[]{:S(2)}) collective-permute-start(bf16[128,8192]{1,0:T(8,128)(2,1)S(1)} %copy-done.23), channel_id=1, source_target_pairs={{0,1},{1,0},{2,3},{3,2},{4,5},{5,4},{6,7},{7,6},{8,9},{9,8},{10,11... | collective-permute-start | bytes 6291464 | tf_op jit(solution)/shard_map/ppermute | solution.py:24
  142.2 4.5 %collective-permute-start.5 = (bf16[128,8192]{1,0:T(8,128)(2,1)}, bf16[128,8192]{1,0:T(8,128)(2,1)}, u32[]{:S(2)}, u32[]{:S(2)}) collective-permute-start(bf16[128,8192]{1,0:T(8,128)(2,1)} %collective-permute-done.4.rest_2_), channel_id=1, source_target_pairs={{0,1},{1,0},{2,3},{3,2},{4,5},{5,4},{6,7},{7,6},{8,9},{9,8},{10,11... | collective-permute-start | bytes 6291464 | tf_op jit(solution)/shard_map/ppermute | solution.py:24
  145.1 92.7 %reduce-scatter.5.cloned.1.call-start = ((), (), s32[]{:S(2)}) async-start(), calls=%async_computation.4 | async-start | bytes 2621440 | tf_op jit(solution)/shard_map/reduce_scatter | solution.py:365
  192.8 93.5 %all-gather.5.cloned.1.call-start = ((), (), s32[]{:S(2)}) async-start(), calls=%async_computation.5 | async-start | bytes 2621440 | tf_op jit(solution)/shard_map/all_gather | solution.py:367
  242.5 2.0 collective-permute-start.9
  242.6 2.6 collective-permute-start.8
  243.1 2.9 collective-permute-start.7
  243.2 3.6 collective-permute-start.6
  248.7 64.0 %collective-permute-start.11 = (bf16[8192,128]{1,0:T(8,128)(2,1)}, bf16[8192,128]{1,0:T(8,128)(2,1)}, u32[]{:S(2)}, u32[]{:S(2)}) collective-permute-start(bf16[8192,128]{1,0:T(8,128)(2,1)} %add_convert_fusion.1.rest_0_), channel_id=1, source_target_pairs={{0,2},{1,3},{2,0},{3,1},{4,6},{5,7},{6,4},{7,5},{8,10},{9,11},{10,... | collective-permute-start | bytes 6291464 | tf_op jit(solution)/shard_map/ppermute | solution.py:24
  312.9 2.0 collective-permute-start.15
  313.0 2.6 collective-permute-start.14
  313.5 3.6 collective-permute-start.13
  313.5 5.1 %collective-permute-start.12 = (bf16[2048,128]{1,0:T(8,128)(2,1)S(1)}, bf16[2048,128]{1,0:T(8,128)(2,1)S(1)}, u32[]{:S(2)}, u32[]{:S(2)}) collective-permute-start(bf16[2048,128]{1,0:T(8,128)(2,1)S(1)} %get-tuple-element.66), channel_id=1, source_target_pairs={{0,1},{1,0},{2,3},{3,2},{4,5},{5,4},{6,7},{7,6},{8,9},{9,8},{10,11... | collective-permute-start | bytes 1572872 | tf_op jit(solution)/shard_map/ppermute | solution.py:24
  314.0 8.0 %collective-permute-start.17 = (bf16[8192,128]{1,0:T(8,128)(2,1)}, bf16[8192,128]{1,0:T(8,128)(2,1)}, u32[]{:S(2)}, u32[]{:S(2)}) collective-permute-start(bf16[8192,128]{1,0:T(8,128)(2,1)} %get-tuple-element.56), channel_id=1, source_target_pairs={{0,1},{1,0},{2,3},{3,2},{4,5},{5,4},{6,7},{7,6},{8,9},{9,8},{10,11... | collective-permute-start | bytes 6291464 | tf_op jit(solution)/shard_map/ppermute | solution.py:24
  314.9 24.1 %collective-permute-start.10 = (bf16[8192,128]{1,0:T(8,128)(2,1)}, bf16[8192,128]{1,0:T(8,128)(2,1)}, u32[]{:S(2)}, u32[]{:S(2)}) collective-permute-start(bf16[8192,128]{1,0:T(8,128)(2,1)} %get-tuple-element.51), channel_id=1, source_target_pairs={{0,1},{1,0},{2,3},{3,2},{4,5},{5,4},{6,7},{7,6},{8,9},{9,8},{10,11... | collective-permute-start | bytes 6291464 | tf_op jit(solution)/shard_map/ppermute | solution.py:24
  320.5 48.0 %collective-permute-start.16 = (bf16[8192,128]{1,0:T(8,128)(2,1)}, bf16[8192,128]{1,0:T(8,128)(2,1)}, u32[]{:S(2)}, u32[]{:S(2)}) collective-permute-start(bf16[8192,128]{1,0:T(8,128)(2,1)} %add_convert_fusion), channel_id=1, source_target_pairs={{0,2},{1,3},{2,0},{3,1},{4,6},{5,7},{6,4},{7,5},{8,10},{9,11},{10,... | collective-permute-start | bytes 6291464 | tf_op jit(solution)/shard_map/ppermute | solution.py:24
  337.1 1.8 collective-permute-start.18
  368.5 10.6 %collective-permute-start.19 = (f32[264,384]{1,0:T(8,128)S(1)}, f32[264,384]{1,0:T(8,128)S(1)}, u32[]{:S(2)}, u32[]{:S(2)}) collective-permute-start(f32[264,384]{1,0:T(8,128)S(1)} %add.37), channel_id=1, source_target_pairs={{0,2},{1,3},{2,0},{3,1},{4,6},{5,7},{6,4},{7,5},{8,10},{9,11},{10,... | collective-permute-start | bytes 1216520 | tf_op jit(solution)/shard_map/ppermute | solution.py:24
  375.1 4.1 %collective-permute-start.21 = (f32[256,128]{1,0:T(8,128)S(1)}, f32[256,128]{1,0:T(8,128)S(1)}, u32[]{:S(2)}, u32[]{:S(2)}) collective-permute-start(f32[256,128]{1,0:T(8,128)S(1)} %get-tuple-element.65), channel_id=1, source_target_pairs={{0,1},{1,0},{2,3},{3,2},{4,5},{5,4},{6,7},{7,6},{8,9},{9,8},{10,11... | collective-permute-start | bytes 393224 | tf_op jit(solution)/shard_map/ppermute | solution.py:24
  379.1 7.5 %collective-permute-start.20 = (f32[264,384]{1,0:T(8,128)S(1)}, f32[264,384]{1,0:T(8,128)S(1)}, u32[]{:S(2)}, u32[]{:S(2)}) collective-permute-start(f32[264,384]{1,0:T(8,128)S(1)} %add.38), channel_id=1, source_target_pairs={{0,1},{1,0},{2,3},{3,2},{4,5},{5,4},{6,7},{7,6},{8,9},{9,8},{10,11... | collective-permute-start | bytes 1216520 | tf_op jit(solution)/shard_map/ppermute | solution.py:24
  379.2 6.0 %collective-permute-start.22 = (f32[256,128]{1,0:T(8,128)S(1)}, f32[256,128]{1,0:T(8,128)S(1)}, u32[]{:S(2)}, u32[]{:S(2)}) collective-permute-start(f32[256,128]{1,0:T(8,128)S(1)} %add.39), channel_id=1, source_target_pairs={{0,2},{1,3},{2,0},{3,1},{4,6},{5,7},{6,4},{7,5},{8,10},{9,11},{10,... | collective-permute-start | bytes 393224 | tf_op jit(solution)/shard_map/ppermute | solution.py:24
  385.2 1.4 collective-permute-start.23
  (24 other events, 162.4 us)
Sparse Core Ops, SparseCore 0:
  94.5 45.3 reduce-scatter.2
  145.2 47.5 all-gather.2
  195.2 42.5 reduce-scatter.4
  241.0 45.2 all-gather.4

commit v9 on v8

--- a/solution.py
+++ b/solution.py
@@ -13,7 +13,7 @@
 HBM = pl.BlockSpec(memory_space=pl.ANY)
 VMEM = pl.BlockSpec(memory_space=pltpu.VMEM)
 SMEM = pl.BlockSpec(memory_space=pltpu.SMEM)
-PARAMS = pltpu.CompilerParams(vmem_limit_bytes=24 * MIB)
+PARAMS = pltpu.CompilerParams(vmem_limit_bytes=56 * MIB)
 
 
 def cost(flops, moved):
@@ -90,7 +90,7 @@
         out_specs=[pl.BlockSpec((wide, step), lambda i: (0, i))] * n,
         out_shape=[jax.ShapeDtypeStruct((wide, rows), dtype)] * n,
         scratch_shapes=[pltpu.VMEM((hid, width), jnp.bfloat16)],
-        compiler_params=pltpu.CompilerParams(vmem_limit_bytes=24 * MIB),
+        compiler_params=PARAMS,
         cost_estimate=cost(2 * width * rows * hid, 2 * width * rows + 4 * hid * rows),
         name="project",
     )(feat_t, weight, *after)
@@ -123,7 +123,7 @@
 
         @pl.loop(0, n_feat)
         def _(s):
-            @pl.loop(0, per_share, unroll=2)
+            @pl.loop(0, per_share, unroll=min(4, per_share))
             def _(i):
                 b = s * per_share + i
                 picked = []
@@ -160,7 +160,7 @@
             pltpu.SemaphoreType.DMA((n + 1,)),
             pltpu.SemaphoreType.DMA((n_feat,)),
         ],
-        compiler_params=pltpu.CompilerParams(vmem_limit_bytes=56 * MIB),
+        compiler_params=PARAMS,
         cost_estimate=cost(
             8 * blocks * slots * side * side * wide, 2 * n * rows * wide + 6 * rows * wide
         ),
@@ -193,7 +193,7 @@
             jax.ShapeDtypeStruct((share, wide), jnp.bfloat16),
         ],
         input_output_aliases={3: 0} if held else {},
-        compiler_params=pltpu.CompilerParams(vmem_limit_bytes=24 * MIB),
+        compiler_params=PARAMS,
         cost_estimate=cost(20 * share * wide, 8 * share * wide),
         name="activate",
     )(bias, cot, pre, *held)
@@ -220,7 +220,7 @@
 
         load.wait()
 
-        @pl.loop(0, blocks, unroll=2)
+        @pl.loop(0, blocks, unroll=min(4, blocks))
         def _(b):
             g = grad_ref[pl.ds(pl.multiple_of(b * side, side), side), :]
             scale = inv_ref[b]
@@ -267,7 +267,7 @@
             pltpu.SemaphoreType.DMA,
             pltpu.SemaphoreType.DMA((n,)),
         ],
-        compiler_params=pltpu.CompilerParams(vmem_limit_bytes=40 * MIB),
+        compiler_params=PARAMS,
         cost_estimate=cost(
             8 * blocks * slots * side * side * wide, 2 * n * rows * wide + 2 * rows * wide
         ),

time: 396 us -> 393 us (level)
  local copies, waits for them, and re-layouts: 31.9 us -> 15.4 us
  waiting for transfers between devices: 209 us -> 217 us
  Pallas kernels: 119 us -> 125 us
    unnamed x57 -> x31, local copies, waits for them, and re-layouts: 28.7 us -> 11.4 us
    pallas_call x2, Pallas kernels: 9.29 us -> 19.5 us  [project(): pl.pallas_call(kernel, grid=(rows // step,), in_specs=[pl.BlockSpec((widt...]
    pallas_call x2, Pallas kernels: 47.2 us -> 39.5 us  [mean_tiles(): pl.pallas_call(kernel, out_shape=jax.ShapeDtypeStruct((rows, wide), jnp.b...]
    all_gather x2, waiting for transfers between devices: 58.6 us -> 63.7 us  [on_device(): pieces.append(lax.all_gather(grad_pre, 'feat', axis=0, tiled=True))]
    reduce_scatter x2, waiting for transfers between devices: 15.6 us -> 20.3 us  [on_device(): pre = lax.psum_scatter(part_pre, 'feat', scatter_dimension=0, tiled=True)]
  transfers between devices with their start and end apart: 28 -> 28, of which waited for: 20 -> 20; matrix products, arithmetic and copies ran while one was open for 2% -> 2% of each run, Pallas kernels for 23% -> 24%
where the time goes in v9:
time: 393 us; the launch traced here: 392 us
  waiting for transfers between devices  217 us (55%)
  Pallas kernels  125 us (32%)
  local copies, waits for them, and re-layouts  15.4 us (4%)
  between operations  14 us (4%)
  starting transfers between devices  13.8 us (4%)
  other arithmetic  7.16 us (2%)
    ppermute x24, waiting for transfers between devices, swap(): return lax.ppermute(value, 'node', [(i, i ^ mask) for i in range(n)])  133 us
    all_gather x2, waiting for transfers between devices, on_device(): pieces.append(lax.all_gather(grad_pre, 'feat', axis=0, tiled=True))  63.7 us
    pallas_call x2, Pallas kernels, spread_tiles(): pl.pallas_call(kernel, out_shape=[jax.ShapeDtypeStruct((rows, wide), jnp....  48.9 us
    pallas_call x2, Pallas kernels, mean_tiles(): pl.pallas_call(kernel, out_shape=jax.ShapeDtypeStruct((rows, wide), jnp.b...  39.5 us
    reduce_scatter x2, waiting for transfers between devices, on_device(): pre = lax.psum_scatter(part_pre, 'feat', scatter_dimension=0, tiled=True)  20.3 us
    pallas_call x2, Pallas kernels, project(): pl.pallas_call(kernel, grid=(rows // step,), in_specs=[pl.BlockSpec((widt...  19.5 us
    ppermute x24, starting transfers between devices, swap(): return lax.ppermute(value, 'node', [(i, i ^ mask) for i in range(n)])  13.5 us
    pallas_call x2, Pallas kernels, weight_grad(): pl.pallas_call(kernel, grid=(rows // step,), in_specs=[SMEM, pl.BlockSpec...  11.8 us
  transfers between devices with their start and end apart: 28, of which 20 were waited for; matrix products, arithmetic and copies ran while one was open for 2% of the time, Pallas kernels for 24%

profile of v9, /device:TPU:0, one launch (start us, length us, event | category | flops | bytes accessed | tf_op | source)
XLA Modules:
  0.0 392.0 jit_solution(12507818035149835641)
XLA Ops:
  7.2 9.0 %project.2 = (bf16[128,8192]{1,0:T(8,128)(2,1)}, bf16[128,8192]{1,0:T(8,128)(2,1)}) custom-call(bf16[512,8192]{1,0:T(8,128)(2,1)} %feat_ref.7, bf16[512,256]{1,0:T(8,128)(2,1)} %w_ref.2), custom_call_target="tpu_custom_call" | custom-call | flops 2147483648 | bytes 16777216 | tf_op jit(solution)/shard_map/project/pallas_call | solution.py:82
  16.3 3.0 collective-permute-start.1
  19.3 10.5 %project.3 = (f32[128,8192]{1,0:T(8,128)}, f32[128,8192]{1,0:T(8,128)}) custom-call(bf16[512,8192]{1,0:T(8,128)(2,1)} %feat_ref.7, bf16[512,256]{1,0:T(8,128)(2,1)} %w_ref.3, bf16[128,8192]{1,0:T(8,128)(2,1)} %get-tuple-element.35.rest_0_), custom_call_target="tpu_custom_call" | custom-call | flops 2147483648 | bytes 16777216 | tf_op jit(solution)/shard_map/project/pallas_call | solution.py:82
  29.7 35.4 %collective-permute-done.1.rest_2_ = bf16[128,8192]{1,0:T(8,128)(2,1)S(1)} collective-permute-done((bf16[128,8192]{1,0:T(8,128)(2,1)}, bf16[128,8192]{1,0:T(8,128)(2,1)S(1)}, u32[]{:S(2)}, u32[]{:S(2)}) %collective-permute-start.1) | collective-permute-done | bytes 2097184 | tf_op jit(solution)/shard_map/ppermute | solution.py:24
  67.5 1.8 collective-permute-done.2.rest_3_
  69.4 19.7 %mean_tiles.2 = bf16[8192,128]{1,0:T(8,128)(2,1)} custom-call(s32[64,16]{1,0:T(8,128)} %fusion.2.src_ref, f32[64]{0:T(128)} %convert_divide_fusion.inv_ref, s32[64,16,128]{2,1,0:T(8,128)} %broadcast_select_fusion.nbr_ref, f32[128,8192]{1,0:T(8,128)} %get-tuple-element.37.self_hbm, bf16[128,8192]{1,0:T(8,128)(2,1)} %get-tuple-element.35.rest_0_, ...), custom_call_target="tpu_custom_call" | custom-call | flops 17179869184 | bytes 14680064 | tf_op jit(solution)/shard_map/mean_tiles/pallas_call | solution.py:151
  90.7 1.7 collective-permute-start.4
  92.5 46.0 %collective-permute-done.4.rest_2_ = bf16[128,8192]{1,0:T(8,128)(2,1)} collective-permute-done((bf16[128,8192]{1,0:T(8,128)(2,1)S(1)}, bf16[128,8192]{1,0:T(8,128)(2,1)}, u32[]{:S(2)}, u32[]{:S(2)}) %collective-permute-start.4) | collective-permute-done | bytes 2097184 | tf_op jit(solution)/shard_map/ppermute | solution.py:24
  138.5 2.5 activate.2
  141.1 1.9 collective-permute-done.5.rest_3_
  143.0 19.8 %mean_tiles.3 = bf16[8192,128]{1,0:T(8,128)(2,1)} custom-call(s32[64,16]{1,0:T(8,128)} %fusion.2.src_ref, f32[64]{0:T(128)} %convert_divide_fusion.inv_ref, s32[64,16,128]{2,1,0:T(8,128)} %broadcast_select_fusion.nbr_ref, f32[128,8192]{1,0:T(8,128)} %get-tuple-element.40.self_hbm, bf16[128,8192]{1,0:T(8,128)(2,1)} %get-tuple-element.41.rest_0_, ...), custom_call_target="tpu_custom_call" | custom-call | flops 17179869184 | bytes 14680064 | tf_op jit(solution)/shard_map/mean_tiles/pallas_call | solution.py:151
  162.8 26.0 %all-gather.3.cloned.1.call-done.grad_hbm.rest_0_ = bf16[8192,128]{1,0:T(8,128)(2,1)} async-done(((bf16[2048,128]{1,0:T(8,128)(2,1)}), bf16[8192,128]{1,0:T(8,128)(2,1)}) %all-gather.3.cloned.1.call-update) | async-done | bytes 2097168 | tf_op jit(solution)/shard_map/all_gather | solution.py:367
  189.0 24.5 %spread_tiles.2 = (bf16[8192,128]{1,0:T(8,128)(2,1)}, bf16[8192,128]{1,0:T(8,128)(2,1)}, bf16[8192,128]{1,0:T(8,128)(2,1)}, bf16[8192,128]{1,0:T(8,128)(2,1)}) custom-call(s32[64,16]{1,0:T(8,128)} %fusion.2.src_ref, f32[64]{0:T(128)} %convert_divide_fusion.inv_ref, s32[64,16,128]{2,1,0:T(8,128)} %broadcast_select_fusion.nbr_ref, ...), custom_call_target="tpu_custom_call" | custom-call | flops 17179869184 | bytes 10485760 | tf_op jit(solution)/shard_map/spread_tiles/pallas_call | solution.py:258
  213.5 20.3 %reduce-scatter.5.cloned.1.call-done.pre_ref = bf16[2048,128]{1,0:T(8,128)(2,1)} async-done(((bf16[8192,128]{1,0:T(8,128)(2,1)}), bf16[2048,128]{1,0:T(8,128)(2,1)}) %reduce-scatter.5.cloned.1.call-update) | async-done | bytes 524304 | tf_op jit(solution)/shard_map/reduce_scatter | solution.py:365
  233.8 2.5 activate.3
  240.7 1.9 add_convert_fusion.1.rest_0_
  244.0 37.7 %all-gather.5.cloned.1.call-done.grad_hbm.rest_1_ = bf16[8192,128]{1,0:T(8,128)(2,1)} async-done(((bf16[2048,128]{1,0:T(8,128)(2,1)}), bf16[8192,128]{1,0:T(8,128)(2,1)}) %all-gather.5.cloned.1.call-update) | async-done | bytes 2097168 | tf_op jit(solution)/shard_map/all_gather | solution.py:367
  281.7 24.4 %spread_tiles.3 = (bf16[8192,128]{1,0:T(8,128)(2,1)}, bf16[8192,128]{1,0:T(8,128)(2,1)}, bf16[8192,128]{1,0:T(8,128)(2,1)}, bf16[8192,128]{1,0:T(8,128)(2,1)}) custom-call(s32[64,16]{1,0:T(8,128)} %fusion.2.src_ref, f32[64]{0:T(128)} %convert_divide_fusion.inv_ref, s32[64,16,128]{2,1,0:T(8,128)} %broadcast_select_fusion.nbr_ref, ...), custom_call_target="tpu_custom_call" | custom-call | flops 17179869184 | bytes 10485760 | tf_op jit(solution)/shard_map/spread_tiles/pallas_call | solution.py:258
  306.2 2.4 fusion.7
  312.8 2.2 collective-permute-done.12
  315.1 1.9 add_convert_fusion
  318.5 3.4 copy-done
  321.8 1.6 copy-done.2
  323.4 1.6 copy-done.3
  325.0 1.6 copy-done.4
  326.6 1.6 copy-done.6
  328.2 6.9 %weight_grad.2 = (f32[264,384]{1,0:T(8,128)S(1)}, f32[264,384]{1,0:T(8,128)S(1)}) custom-call(s32[1]{0:T(128)} %bitcast.3.low_ref, bf16[512,8192]{1,0:T(8,128)(2,1)S(1)} %copy-done, bf16[8192,128]{1,0:T(8,128)(2,1)S(1)} %copy-done.2, bf16[8192,128]{1,0:T(8,128)(2,1)S(1)} %copy-done.4, bf16[8192,128]{1,0:T(8,128)(2,1)S(1)} %copy-done.3, ...), custom_call_target="tpu_custom_call" | custom-call | flops 3221225472 | bytes 18874368 | tf_op jit(solution)/shard_map/weight_grad/pallas_call | solution.py:315
  335.3 1.6 collective-permute-done.18
  337.0 28.0 %collective-permute-done.16.rest_2_ = bf16[8192,128]{1,0:T(8,128)(2,1)} collective-permute-done((bf16[8192,128]{1,0:T(8,128)(2,1)}, bf16[8192,128]{1,0:T(8,128)(2,1)}, u32[]{:S(2)}, u32[]{:S(2)}) %collective-permute-start.16) | collective-permute-done | bytes 2097184 | tf_op jit(solution)/shard_map/ppermute | solution.py:24
  366.4 4.9 %weight_grad.3 = (f32[256,128]{1,0:T(8,128)S(1)}, f32[256,128]{1,0:T(8,128)S(1)}) custom-call(s32[1]{0:T(128)} %bitcast.3.low_ref, bf16[512,8192]{1,0:T(8,128)(2,1)S(1)} %copy-done, bf16[8192,128]{1,0:T(8,128)(2,1)S(1)} %copy-done.1, bf16[8192,128]{1,0:T(8,128)(2,1)S(1)} %collective-permute-done.10.rest_1_, bf16[8192,128]{1,0:T(8,128)(2,1)} %collective-permute-done.16.rest_2_), custom_call_target="tpu_custom_call" | custom-call | flops 1073741824 | bytes 14680064 | tf_op jit(solution)/shard_map/weight_grad/pallas_call | solution.py:315
  371.4 4.2 %collective-permute-done.19 = f32[264,384]{1,0:T(8,128)S(1)} collective-permute-done((f32[264,384]{1,0:T(8,128)S(1)}, f32[264,384]{1,0:T(8,128)S(1)}, u32[]{:S(2)}, u32[]{:S(2)}) %collective-permute-start.19) | collective-permute-done | bytes 405536 | tf_op jit(solution)/shard_map/ppermute | solution.py:24
  377.3 4.4 %collective-permute-done.22 = f32[256,128]{1,0:T(8,128)S(1)} collective-permute-done((f32[256,128]{1,0:T(8,128)S(1)}, f32[256,128]{1,0:T(8,128)S(1)}, u32[]{:S(2)}, u32[]{:S(2)}) %collective-permute-start.22) | collective-permute-done | bytes 131104 | tf_op jit(solution)/shard_map/ppermute | solution.py:24
  (87 shorter events, 23.2 us)
Async XLA Ops:
  7.2 131.4 %reduce-scatter.3.cloned.1.call-start = ((), (), s32[]{:S(2)}) async-start(), calls=%async_computation.2 | async-start | bytes 2621440 | tf_op jit(solution)/shard_map/reduce_scatter | solution.py:365
  16.2 48.9 %copy-start.11 = (s32[64,16]{0,1:T(8,128)S(1)}, s32[64,16]{0,1:T(8,128)}, u32[]{:S(2)}) copy-start(s32[64,16]{0,1:T(8,128)} %param.9) | copy-start | bytes 12292
  16.3 49.0 %copy-start.12 = (s32[64]{0:T(128)S(1)}, s32[64]{0:T(128)}, u32[]{:S(2)}) copy-start(s32[64]{0:T(128)} %param.11) | copy-start | bytes 772
  16.3 50.3 %copy-start.10 = (s32[64,16,128]{2,1,0:T(8,128)S(1)}, s32[64,16,128]{2,1,0:T(8,128)}, u32[]{:S(2)}) copy-start(s32[64,16,128]{2,1,0:T(8,128)} %param.10) | copy-start | bytes 1572868
  16.3 48.8 %collective-permute-start.1 = (bf16[128,8192]{1,0:T(8,128)(2,1)}, bf16[128,8192]{1,0:T(8,128)(2,1)S(1)}, u32[]{:S(2)}, u32[]{:S(2)}) collective-permute-start(bf16[128,8192]{1,0:T(8,128)(2,1)} %get-tuple-element.35.rest_0_), channel_id=1, source_target_pairs={{0,2},{1,3},{2,0},{3,1},{4,6},{5,7},{6,4},{7,5},{8,10},{9,11},{10,... | collective-permute-start | bytes 6291464 | tf_op jit(solution)/shard_map/ppermute | solution.py:24
  19.3 48.3 %collective-permute-start = (bf16[128,8192]{1,0:T(8,128)(2,1)}, bf16[128,8192]{1,0:T(8,128)(2,1)}, u32[]{:S(2)}, u32[]{:S(2)}) collective-permute-start(bf16[128,8192]{1,0:T(8,128)(2,1)} %get-tuple-element.35.rest_0_), channel_id=1, source_target_pairs={{0,1},{1,0},{2,3},{3,2},{4,5},{5,4},{6,7},{7,6},{8,9},{9,8},{10,11... | collective-permute-start | bytes 6291464 | tf_op jit(solution)/shard_map/ppermute | solution.py:24
  65.1 4.3 %collective-permute-start.2 = (bf16[128,8192]{1,0:T(8,128)(2,1)S(1)}, bf16[128,8192]{1,0:T(8,128)(2,1)}, u32[]{:S(2)}, u32[]{:S(2)}) collective-permute-start(bf16[128,8192]{1,0:T(8,128)(2,1)S(1)} %collective-permute-done.1.rest_2_), channel_id=1, source_target_pairs={{0,1},{1,0},{2,3},{3,2},{4,5},{5,4},{6,7},{7,6},{8,9},{9,8},{10,11... | collective-permute-start | bytes 6291464 | tf_op jit(solution)/shard_map/ppermute | solution.py:24
  89.2 99.6 %all-gather.3.cloned.1.call-start = ((), (), s32[]{:S(2)}) async-start(), calls=%async_computation.3 | async-start | bytes 2621440 | tf_op jit(solution)/shard_map/all_gather | solution.py:367
  90.7 47.8 %collective-permute-start.4 = (bf16[128,8192]{1,0:T(8,128)(2,1)S(1)}, bf16[128,8192]{1,0:T(8,128)(2,1)}, u32[]{:S(2)}, u32[]{:S(2)}) collective-permute-start(bf16[128,8192]{1,0:T(8,128)(2,1)S(1)} %copy-done.13), channel_id=1, source_target_pairs={{0,2},{1,3},{2,0},{3,1},{4,6},{5,7},{6,4},{7,5},{8,10},{9,11},{10,... | collective-permute-start | bytes 6291464 | tf_op jit(solution)/shard_map/ppermute | solution.py:24
  92.5 48.6 %collective-permute-start.3 = (bf16[128,8192]{1,0:T(8,128)(2,1)S(1)}, bf16[128,8192]{1,0:T(8,128)(2,1)}, u32[]{:S(2)}, u32[]{:S(2)}) collective-permute-start(bf16[128,8192]{1,0:T(8,128)(2,1)S(1)} %copy-done.13), channel_id=1, source_target_pairs={{0,1},{1,0},{2,3},{3,2},{4,5},{5,4},{6,7},{7,6},{8,9},{9,8},{10,11... | collective-permute-start | bytes 6291464 | tf_op jit(solution)/shard_map/ppermute | solution.py:24
  138.5 4.5 %collective-permute-start.5 = (bf16[128,8192]{1,0:T(8,128)(2,1)}, bf16[128,8192]{1,0:T(8,128)(2,1)}, u32[]{:S(2)}, u32[]{:S(2)}) collective-permute-start(bf16[128,8192]{1,0:T(8,128)(2,1)} %collective-permute-done.4.rest_2_), channel_id=1, source_target_pairs={{0,1},{1,0},{2,3},{3,2},{4,5},{5,4},{6,7},{7,6},{8,9},{9,8},{10,11... | collective-permute-start | bytes 6291464 | tf_op jit(solution)/shard_map/ppermute | solution.py:24
  141.0 92.8 %reduce-scatter.5.cloned.1.call-start = ((), (), s32[]{:S(2)}) async-start(), calls=%async_computation.4 | async-start | bytes 2621440 | tf_op jit(solution)/shard_map/reduce_scatter | solution.py:365
  188.8 92.9 %all-gather.5.cloned.1.call-start = ((), (), s32[]{:S(2)}) async-start(), calls=%async_computation.5 | async-start | bytes 2621440 | tf_op jit(solution)/shard_map/all_gather | solution.py:367
  236.5 2.0 collective-permute-start.9
  236.6 2.6 collective-permute-start.8
  237.1 2.9 collective-permute-start.7
  237.1 3.6 collective-permute-start.6
  242.6 63.6 %collective-permute-start.11 = (bf16[8192,128]{1,0:T(8,128)(2,1)}, bf16[8192,128]{1,0:T(8,128)(2,1)S(1)}, u32[]{:S(2)}, u32[]{:S(2)}) collective-permute-start(bf16[8192,128]{1,0:T(8,128)(2,1)} %add_convert_fusion.1.rest_0_), channel_id=1, source_target_pairs={{0,2},{1,3},{2,0},{3,1},{4,6},{5,7},{6,4},{7,5},{8,10},{9,11},{10,... | collective-permute-start | bytes 6291464 | tf_op jit(solution)/shard_map/ppermute | solution.py:24
  308.6 2.0 collective-permute-start.15
  308.7 2.6 collective-permute-start.14
  309.2 3.6 collective-permute-start.13
  309.3 5.8 %collective-permute-start.12 = (bf16[2048,128]{1,0:T(8,128)(2,1)S(1)}, bf16[2048,128]{1,0:T(8,128)(2,1)S(1)}, u32[]{:S(2)}, u32[]{:S(2)}) collective-permute-start(bf16[2048,128]{1,0:T(8,128)(2,1)S(1)} %get-tuple-element.66), channel_id=1, source_target_pairs={{0,1},{1,0},{2,3},{3,2},{4,5},{5,4},{6,7},{7,6},{8,9},{9,8},{10,11... | collective-permute-start | bytes 1572872 | tf_op jit(solution)/shard_map/ppermute | solution.py:24
  309.7 8.7 %collective-permute-start.17 = (bf16[8192,128]{1,0:T(8,128)(2,1)}, bf16[8192,128]{1,0:T(8,128)(2,1)}, u32[]{:S(2)}, u32[]{:S(2)}) collective-permute-start(bf16[8192,128]{1,0:T(8,128)(2,1)} %get-tuple-element.56), channel_id=1, source_target_pairs={{0,1},{1,0},{2,3},{3,2},{4,5},{5,4},{6,7},{7,6},{8,9},{9,8},{10,11... | collective-permute-start | bytes 6291464 | tf_op jit(solution)/shard_map/ppermute | solution.py:24
  310.6 26.4 %collective-permute-start.10 = (bf16[8192,128]{1,0:T(8,128)(2,1)}, bf16[8192,128]{1,0:T(8,128)(2,1)S(1)}, u32[]{:S(2)}, u32[]{:S(2)}) collective-permute-start(bf16[8192,128]{1,0:T(8,128)(2,1)} %get-tuple-element.51), channel_id=1, source_target_pairs={{0,1},{1,0},{2,3},{3,2},{4,5},{5,4},{6,7},{7,6},{8,9},{9,8},{10,11... | collective-permute-start | bytes 6291464 | tf_op jit(solution)/shard_map/ppermute | solution.py:24
  317.0 48.0 %collective-permute-start.16 = (bf16[8192,128]{1,0:T(8,128)(2,1)}, bf16[8192,128]{1,0:T(8,128)(2,1)}, u32[]{:S(2)}, u32[]{:S(2)}) collective-permute-start(bf16[8192,128]{1,0:T(8,128)(2,1)} %add_convert_fusion), channel_id=1, source_target_pairs={{0,2},{1,3},{2,0},{3,1},{4,6},{5,7},{6,4},{7,5},{8,10},{9,11},{10,... | collective-permute-start | bytes 6291464 | tf_op jit(solution)/shard_map/ppermute | solution.py:24
  328.2 38.2 %copy-start.1 = (bf16[8192,128]{1,0:T(8,128)(2,1)S(1)}, bf16[8192,128]{1,0:T(8,128)(2,1)}, u32[]{:S(2)}) copy-start(bf16[8192,128]{1,0:T(8,128)(2,1)} %get-tuple-element.61.rest_0_) | copy-start | bytes 6291460
  335.1 1.8 collective-permute-start.18
  365.0 10.6 %collective-permute-start.19 = (f32[264,384]{1,0:T(8,128)S(1)}, f32[264,384]{1,0:T(8,128)S(1)}, u32[]{:S(2)}, u32[]{:S(2)}) collective-permute-start(f32[264,384]{1,0:T(8,128)S(1)} %add.37), channel_id=1, source_target_pairs={{0,2},{1,3},{2,0},{3,1},{4,6},{5,7},{6,4},{7,5},{8,10},{9,11},{10,... | collective-permute-start | bytes 1216520 | tf_op jit(solution)/shard_map/ppermute | solution.py:24
  371.3 4.4 %collective-permute-start.21 = (f32[256,128]{1,0:T(8,128)S(1)}, f32[256,128]{1,0:T(8,128)S(1)}, u32[]{:S(2)}, u32[]{:S(2)}) collective-permute-start(f32[256,128]{1,0:T(8,128)S(1)} %get-tuple-element.65), channel_id=1, source_target_pairs={{0,1},{1,0},{2,3},{3,2},{4,5},{5,4},{6,7},{7,6},{8,9},{9,8},{10,11... | collective-permute-start | bytes 393224 | tf_op jit(solution)/shard_map/ppermute | solution.py:24
  375.6 7.5 %collective-permute-start.20 = (f32[264,384]{1,0:T(8,128)S(1)}, f32[264,384]{1,0:T(8,128)S(1)}, u32[]{:S(2)}, u32[]{:S(2)}) collective-permute-start(f32[264,384]{1,0:T(8,128)S(1)} %add.38), channel_id=1, source_target_pairs={{0,1},{1,0},{2,3},{3,2},{4,5},{5,4},{6,7},{7,6},{8,9},{9,8},{10,11... | collective-permute-start | bytes 1216520 | tf_op jit(solution)/shard_map/ppermute | solution.py:24
  375.7 6.0 %collective-permute-start.22 = (f32[256,128]{1,0:T(8,128)S(1)}, f32[256,128]{1,0:T(8,128)S(1)}, u32[]{:S(2)}, u32[]{:S(2)}) collective-permute-start(f32[256,128]{1,0:T(8,128)S(1)} %add.39), channel_id=1, source_target_pairs={{0,2},{1,3},{2,0},{3,1},{4,6},{5,7},{6,4},{7,5},{8,10},{9,11},{10,... | collective-permute-start | bytes 393224 | tf_op jit(solution)/shard_map/ppermute | solution.py:24
  381.7 1.4 collective-permute-start.23
  (11 other events, 54.2 us)
Sparse Core Ops, SparseCore 0:
  89.3 45.3 reduce-scatter.2
  141.2 47.5 all-gather.2
  191.2 42.5 reduce-scatter.4
  236.4 45.2 all-gather.4

commit v10 on v9

--- a/solution.py
+++ b/solution.py
@@ -123,7 +123,7 @@
 
         @pl.loop(0, n_feat)
         def _(s):
-            @pl.loop(0, per_share, unroll=min(4, per_share))
+            @pl.loop(0, per_share, unroll=min(8, per_share))
             def _(i):
                 b = s * per_share + i
                 picked = []
@@ -220,7 +220,7 @@
 
         load.wait()
 
-        @pl.loop(0, blocks, unroll=min(4, blocks))
+        @pl.loop(0, blocks, unroll=min(2, blocks))
         def _(b):
             g = grad_ref[pl.ds(pl.multiple_of(b * side, side), side), :]
             scale = inv_ref[b]
@@ -339,8 +339,12 @@
     cot_rows = cotangent.reshape(share, hid)
     bias_row = bias[None, :]
 
-    projected = project(feat_t, w_neigh, CHUNKS, jnp.bfloat16, [])
-    own_terms = project(feat_t, w_self, CHUNKS, jnp.float32, projected[:1])
+    wide = hid // CHUNKS
+    projected = []
+    for c in range(CHUNKS):
+        columns = w_neigh[:, c * wide : (c + 1) * wide]
+        projected += project(feat_t, columns, 1, jnp.bfloat16, projected[-1:])
+    own_terms = project(feat_t, w_self, CHUNKS, jnp.float32, projected[-1:])
 
     low = jnp.reshape(jnp.bitwise_and(me, 1), (1,)).astype(jnp.int32)
     hidden = None
@@ -381,7 +385,8 @@
                     if arrived is not None and mask == 1 and k != mask:
                         theirs, arrived = lax.optimization_barrier((theirs, arrived))
                         sent[c - 1][-1] = arrived
-                    cut = rows // (NEAR_PIECES if mask == 1 and k != mask else 1)
+                    split = mask == 1 and k != mask and c < CHUNKS - 1
+                    cut = rows // (NEAR_PIECES if split else 1)
                     got = [
                         swap(theirs[at : at + cut], mask, n_node) for at in range(0, rows, cut)
                     ]

time: 393 us -> 394 us (level)
  Pallas kernels: 125 us -> 131 us
  waiting for transfers between devices: 217 us -> 211 us
    pallas_call x2 -> x3, Pallas kernels: 19.5 us -> 27 us  [project(): pl.pallas_call(kernel, grid=(rows // step,), in_specs=[pl.BlockSpec((widt...]
    ppermute x24 -> x21, waiting for transfers between devices: 133 us -> 126 us  [swap(): return lax.ppermute(value, 'node', [(i, i ^ mask) for i in range(n)])]
    unnamed x31 -> x29, local copies, waits for them, and re-layouts: 11.4 us -> 12.7 us
    ppermute x24 -> x21, starting transfers between devices: 13.5 us -> 12.5 us  [swap(): return lax.ppermute(value, 'node', [(i, i ^ mask) for i in range(n)])]
  transfers between devices with their start and end apart: 28 -> 25, of which waited for: 20 -> 17; matrix products, arithmetic and copies ran while one was open for 2% -> 2% of each run, Pallas kernels for 24% -> 26%
where the time goes in v10:
time: 394 us; the launch traced here: 393 us
  waiting for transfers between devices  211 us (54%)
  Pallas kernels  131 us (33%)
  local copies, waits for them, and re-layouts  15.9 us (4%)
  between operations  14 us (4%)
  starting transfers between devices  12.9 us (3%)
  other arithmetic  8.77 us (2%)
    ppermute x21, waiting for transfers between devices, swap(): return lax.ppermute(value, 'node', [(i, i ^ mask) for i in range(n)])  126 us
    all_gather x2, waiting for transfers between devices, on_device(): pieces.append(lax.all_gather(grad_pre, 'feat', axis=0, tiled=True))  65.4 us
    pallas_call x2, Pallas kernels, spread_tiles(): pl.pallas_call(kernel, out_shape=[jax.ShapeDtypeStruct((rows, wide), jnp....  50.8 us
    pallas_call x2, Pallas kernels, mean_tiles(): pl.pallas_call(kernel, out_shape=jax.ShapeDtypeStruct((rows, wide), jnp.b...  36 us
    pallas_call x3, Pallas kernels, project(): pl.pallas_call(kernel, grid=(rows // step,), in_specs=[pl.BlockSpec((widt...  27 us
    reduce_scatter x2, waiting for transfers between devices, on_device(): pre = lax.psum_scatter(part_pre, 'feat', scatter_dimension=0, tiled=True)  19.3 us
    unnamed x29, local copies, waits for them, and re-layouts  12.7 us
    ppermute x21, starting transfers between devices, swap(): return lax.ppermute(value, 'node', [(i, i ^ mask) for i in range(n)])  12.5 us
  transfers between devices with their start and end apart: 25, of which 17 were waited for; matrix products, arithmetic and copies ran while one was open for 2% of the time, Pallas kernels for 26%

profile of v10, /device:TPU:0, one launch (start us, length us, event | category | flops | bytes accessed | tf_op | source)
XLA Modules:
  0.0 393.3 jit_solution(7730342526760345677)
XLA Ops:
  7.2 1.7 fusion.8
  8.9 8.2 %project.3.rest_0_ = bf16[128,8192]{1,0:T(8,128)(2,1)} custom-call(bf16[512,8192]{1,0:T(8,128)(2,1)} %feat_ref.9, bf16[512,128]{1,0:T(8,128)(2,1)} %get-tuple-element.66.w_ref), custom_call_target="tpu_custom_call" | custom-call | flops 1073741824 | bytes 12582912 | tf_op jit(solution)/shard_map/project/pallas_call | solution.py:82
  17.1 2.9 collective-permute-start.1
  20.0 8.2 %project.4.rest_0_ = bf16[128,8192]{1,0:T(8,128)(2,1)} custom-call(bf16[512,8192]{1,0:T(8,128)(2,1)} %feat_ref.9, bf16[512,128]{1,0:T(8,128)(2,1)} %get-tuple-element.67.w_ref, bf16[128,8192]{1,0:T(8,128)(2,1)} %project.3.rest_0_), custom_call_target="tpu_custom_call" | custom-call | flops 1073741824 | bytes 12582912 | tf_op jit(solution)/shard_map/project/pallas_call | solution.py:82
  28.2 10.6 %project.5 = (f32[128,8192]{1,0:T(8,128)}, f32[128,8192]{1,0:T(8,128)}) custom-call(bf16[512,8192]{1,0:T(8,128)(2,1)} %feat_ref.9, bf16[512,256]{1,0:T(8,128)(2,1)} %w_ref.1, bf16[128,8192]{1,0:T(8,128)(2,1)} %project.4.rest_0_), custom_call_target="tpu_custom_call" | custom-call | flops 2147483648 | bytes 16777216 | tf_op jit(solution)/shard_map/project/pallas_call | solution.py:82
  38.8 27.1 %collective-permute-done.1.rest_2_ = bf16[128,8192]{1,0:T(8,128)(2,1)S(1)} collective-permute-done((bf16[128,8192]{1,0:T(8,128)(2,1)}, bf16[128,8192]{1,0:T(8,128)(2,1)S(1)}, u32[]{:S(2)}, u32[]{:S(2)}) %collective-permute-start.1) | collective-permute-done | bytes 2097184 | tf_op jit(solution)/shard_map/ppermute | solution.py:24
  68.3 1.8 collective-permute-done.2.rest_3_
  70.2 18.0 %mean_tiles.2 = bf16[8192,128]{1,0:T(8,128)(2,1)} custom-call(s32[64,16]{1,0:T(8,128)} %fusion.2.src_ref, f32[64]{0:T(128)} %convert_divide_fusion.inv_ref, s32[64,16,128]{2,1,0:T(8,128)} %broadcast_select_fusion.nbr_ref, f32[128,8192]{1,0:T(8,128)} %get-tuple-element.34.self_hbm, bf16[128,8192]{1,0:T(8,128)(2,1)} %project.3.rest_0_, ...), custom_call_target="tpu_custom_call" | custom-call | flops 17179869184 | bytes 14680064 | tf_op jit(solution)/shard_map/mean_tiles/pallas_call | solution.py:151
  89.8 1.8 collective-permute-start.4
  91.5 46.0 %collective-permute-done.4.rest_2_ = bf16[128,8192]{1,0:T(8,128)(2,1)} collective-permute-done((bf16[128,8192]{1,0:T(8,128)(2,1)S(1)}, bf16[128,8192]{1,0:T(8,128)(2,1)}, u32[]{:S(2)}, u32[]{:S(2)}) %collective-permute-start.4) | collective-permute-done | bytes 2097184 | tf_op jit(solution)/shard_map/ppermute | solution.py:24
  137.6 2.5 activate.2
  140.2 1.9 collective-permute-done.5.rest_3_
  142.1 18.0 %mean_tiles.3 = bf16[8192,128]{1,0:T(8,128)(2,1)} custom-call(s32[64,16]{1,0:T(8,128)} %fusion.2.src_ref, f32[64]{0:T(128)} %convert_divide_fusion.inv_ref, s32[64,16,128]{2,1,0:T(8,128)} %broadcast_select_fusion.nbr_ref, f32[128,8192]{1,0:T(8,128)} %get-tuple-element.37.self_hbm, bf16[128,8192]{1,0:T(8,128)(2,1)} %project.4.rest_0_, ...), custom_call_target="tpu_custom_call" | custom-call | flops 17179869184 | bytes 14680064 | tf_op jit(solution)/shard_map/mean_tiles/pallas_call | solution.py:151
  160.1 27.7 %all-gather.3.cloned.1.call-done.grad_hbm.rest_0_ = bf16[8192,128]{1,0:T(8,128)(2,1)} async-done(((bf16[2048,128]{1,0:T(8,128)(2,1)}), bf16[8192,128]{1,0:T(8,128)(2,1)}) %all-gather.3.cloned.1.call-update) | async-done | bytes 2097168 | tf_op jit(solution)/shard_map/all_gather | solution.py:371
  188.1 25.4 %spread_tiles.2 = (bf16[8192,128]{1,0:T(8,128)(2,1)}, bf16[8192,128]{1,0:T(8,128)(2,1)}, bf16[8192,128]{1,0:T(8,128)(2,1)}, bf16[8192,128]{1,0:T(8,128)(2,1)}) custom-call(s32[64,16]{1,0:T(8,128)} %fusion.2.src_ref, f32[64]{0:T(128)} %convert_divide_fusion.inv_ref, s32[64,16,128]{2,1,0:T(8,128)} %broadcast_select_fusion.nbr_ref, ...), custom_call_target="tpu_custom_call" | custom-call | flops 17179869184 | bytes 10485760 | tf_op jit(solution)/shard_map/spread_tiles/pallas_call | solution.py:258
  213.5 19.3 %reduce-scatter.5.cloned.1.call-done.pre_ref = bf16[2048,128]{1,0:T(8,128)(2,1)} async-done(((bf16[8192,128]{1,0:T(8,128)(2,1)}), bf16[2048,128]{1,0:T(8,128)(2,1)}) %reduce-scatter.5.cloned.1.call-update) | async-done | bytes 524304 | tf_op jit(solution)/shard_map/reduce_scatter | solution.py:369
  232.9 2.5 activate.3
  239.8 1.9 add_convert_fusion.1.rest_0_
  243.1 37.7 %all-gather.5.cloned.1.call-done.grad_hbm.rest_1_ = bf16[8192,128]{1,0:T(8,128)(2,1)} async-done(((bf16[2048,128]{1,0:T(8,128)(2,1)}), bf16[8192,128]{1,0:T(8,128)(2,1)}) %all-gather.5.cloned.1.call-update) | async-done | bytes 2097168 | tf_op jit(solution)/shard_map/all_gather | solution.py:371
  280.8 25.4 %spread_tiles.3 = (bf16[8192,128]{1,0:T(8,128)(2,1)}, bf16[8192,128]{1,0:T(8,128)(2,1)}, bf16[8192,128]{1,0:T(8,128)(2,1)}, bf16[8192,128]{1,0:T(8,128)(2,1)}) custom-call(s32[64,16]{1,0:T(8,128)} %fusion.2.src_ref, f32[64]{0:T(128)} %convert_divide_fusion.inv_ref, s32[64,16,128]{2,1,0:T(8,128)} %broadcast_select_fusion.nbr_ref, ...), custom_call_target="tpu_custom_call" | custom-call | flops 17179869184 | bytes 10485760 | tf_op jit(solution)/shard_map/spread_tiles/pallas_call | solution.py:258
  308.0 6.8 %collective-permute-done.12 = bf16[8192,128]{1,0:T(8,128)(2,1)S(1)} collective-permute-done((bf16[8192,128]{1,0:T(8,128)(2,1)}, bf16[8192,128]{1,0:T(8,128)(2,1)S(1)}, u32[]{:S(2)}, u32[]{:S(2)}) %collective-permute-start.12) | collective-permute-done | bytes 2097184 | tf_op jit(solution)/shard_map/ppermute | solution.py:24
  314.8 3.4 add_convert_fusion
  319.7 3.4 copy-done
  324.7 1.6 copy-done.3
  326.3 1.6 copy-done.4
  327.9 1.6 copy-done.6
  329.5 7.0 %weight_grad.2 = (f32[264,384]{1,0:T(8,128)S(1)}, f32[264,384]{1,0:T(8,128)S(1)}) custom-call(s32[1]{0:T(128)} %bitcast.3.low_ref, bf16[512,8192]{1,0:T(8,128)(2,1)S(1)} %copy-done, bf16[8192,128]{1,0:T(8,128)(2,1)S(1)} %copy-done.2, bf16[8192,128]{1,0:T(8,128)(2,1)S(1)} %copy-done.4, bf16[8192,128]{1,0:T(8,128)(2,1)S(1)} %copy-done.3, ...), custom_call_target="tpu_custom_call" | custom-call | flops 3221225472 | bytes 18874368 | tf_op jit(solution)/shard_map/weight_grad/pallas_call | solution.py:315
  336.6 1.7 collective-permute-done.15
  338.4 27.9 %collective-permute-done.13.rest_2_ = bf16[8192,128]{1,0:T(8,128)(2,1)} collective-permute-done((bf16[8192,128]{1,0:T(8,128)(2,1)}, bf16[8192,128]{1,0:T(8,128)(2,1)}, u32[]{:S(2)}, u32[]{:S(2)}) %collective-permute-start.13) | collective-permute-done | bytes 2097184 | tf_op jit(solution)/shard_map/ppermute | solution.py:24
  367.7 4.8 %weight_grad.3 = (f32[256,128]{1,0:T(8,128)S(1)}, f32[256,128]{1,0:T(8,128)S(1)}) custom-call(s32[1]{0:T(128)} %bitcast.3.low_ref, bf16[512,8192]{1,0:T(8,128)(2,1)S(1)} %copy-done, bf16[8192,128]{1,0:T(8,128)(2,1)S(1)} %copy-done.1, bf16[8192,128]{1,0:T(8,128)(2,1)S(1)} %collective-permute-done.10.rest_1_, bf16[8192,128]{1,0:T(8,128)(2,1)} %collective-permute-done.13.rest_2_), custom_call_target="tpu_custom_call" | custom-call | flops 1073741824 | bytes 14680064 | tf_op jit(solution)/shard_map/weight_grad/pallas_call | solution.py:315
  372.6 4.2 %collective-permute-done.16 = f32[264,384]{1,0:T(8,128)S(1)} collective-permute-done((f32[264,384]{1,0:T(8,128)S(1)}, f32[264,384]{1,0:T(8,128)S(1)}, u32[]{:S(2)}, u32[]{:S(2)}) %collective-permute-start.16) | collective-permute-done | bytes 405536 | tf_op jit(solution)/shard_map/ppermute | solution.py:24
  378.5 4.4 %collective-permute-done.19 = f32[256,128]{1,0:T(8,128)S(1)} collective-permute-done((f32[256,128]{1,0:T(8,128)S(1)}, f32[256,128]{1,0:T(8,128)S(1)}, u32[]{:S(2)}, u32[]{:S(2)}) %collective-permute-start.19) | collective-permute-done | bytes 131104 | tf_op jit(solution)/shard_map/ppermute | solution.py:24
  (80 shorter events, 22.3 us)
Async XLA Ops:
  7.2 130.4 %reduce-scatter.3.cloned.1.call-start = ((), (), s32[]{:S(2)}) async-start(), calls=%async_computation.2 | async-start | bytes 2621440 | tf_op jit(solution)/shard_map/reduce_scatter | solution.py:369
  17.1 48.8 %collective-permute-start.1 = (bf16[128,8192]{1,0:T(8,128)(2,1)}, bf16[128,8192]{1,0:T(8,128)(2,1)S(1)}, u32[]{:S(2)}, u32[]{:S(2)}) collective-permute-start(bf16[128,8192]{1,0:T(8,128)(2,1)} %project.3.rest_0_), channel_id=1, source_target_pairs={{0,2},{1,3},{2,0},{3,1},{4,6},{5,7},{6,4},{7,5},{8,10},{9,11},{10,... | collective-permute-start | bytes 6291464 | tf_op jit(solution)/shard_map/ppermute | solution.py:24
  20.0 48.3 %collective-permute-start = (bf16[128,8192]{1,0:T(8,128)(2,1)}, bf16[128,8192]{1,0:T(8,128)(2,1)}, u32[]{:S(2)}, u32[]{:S(2)}) collective-permute-start(bf16[128,8192]{1,0:T(8,128)(2,1)} %project.3.rest_0_), channel_id=1, source_target_pairs={{0,1},{1,0},{2,3},{3,2},{4,5},{5,4},{6,7},{7,6},{8,9},{9,8},{10,11... | collective-permute-start | bytes 6291464 | tf_op jit(solution)/shard_map/ppermute | solution.py:24
  28.2 37.7 %copy-start.11 = (s32[64,16]{0,1:T(8,128)S(1)}, s32[64,16]{0,1:T(8,128)}, u32[]{:S(2)}) copy-start(s32[64,16]{0,1:T(8,128)} %param.9) | copy-start | bytes 12292
  28.2 37.8 %copy-start.12 = (s32[64]{0:T(128)S(1)}, s32[64]{0:T(128)}, u32[]{:S(2)}) copy-start(s32[64]{0:T(128)} %param.11) | copy-start | bytes 772
  28.2 39.1 %copy-start.10 = (s32[64,16,128]{2,1,0:T(8,128)S(1)}, s32[64,16,128]{2,1,0:T(8,128)}, u32[]{:S(2)}) copy-start(s32[64,16,128]{2,1,0:T(8,128)} %param.10) | copy-start | bytes 1572868
  65.9 4.3 %copy-start.13 = (bf16[128,8192]{1,0:T(8,128)(2,1)}, bf16[128,8192]{1,0:T(8,128)(2,1)S(1)}, u32[]{:S(2)}) copy-start(bf16[128,8192]{1,0:T(8,128)(2,1)S(1)} %collective-permute-done.1.rest_2_) | copy-start | bytes 6291460
  65.9 4.3 %collective-permute-start.2 = (bf16[128,8192]{1,0:T(8,128)(2,1)S(1)}, bf16[128,8192]{1,0:T(8,128)(2,1)}, u32[]{:S(2)}, u32[]{:S(2)}) collective-permute-start(bf16[128,8192]{1,0:T(8,128)(2,1)S(1)} %collective-permute-done.1.rest_2_), channel_id=1, source_target_pairs={{0,1},{1,0},{2,3},{3,2},{4,5},{5,4},{6,7},{7,6},{8,9},{9,8},{10,11... | collective-permute-start | bytes 6291464 | tf_op jit(solution)/shard_map/ppermute | solution.py:24
  88.2 99.6 %all-gather.3.cloned.1.call-start = ((), (), s32[]{:S(2)}) async-start(), calls=%async_computation.3 | async-start | bytes 2621440 | tf_op jit(solution)/shard_map/all_gather | solution.py:371
  89.8 47.8 %collective-permute-start.4 = (bf16[128,8192]{1,0:T(8,128)(2,1)S(1)}, bf16[128,8192]{1,0:T(8,128)(2,1)}, u32[]{:S(2)}, u32[]{:S(2)}) collective-permute-start(bf16[128,8192]{1,0:T(8,128)(2,1)S(1)} %copy-done.7), channel_id=1, source_target_pairs={{0,2},{1,3},{2,0},{3,1},{4,6},{5,7},{6,4},{7,5},{8,10},{9,11},{10,... | collective-permute-start | bytes 6291464 | tf_op jit(solution)/shard_map/ppermute | solution.py:24
  91.5 48.6 %collective-permute-start.3 = (bf16[128,8192]{1,0:T(8,128)(2,1)S(1)}, bf16[128,8192]{1,0:T(8,128)(2,1)}, u32[]{:S(2)}, u32[]{:S(2)}) collective-permute-start(bf16[128,8192]{1,0:T(8,128)(2,1)S(1)} %copy-done.7), channel_id=1, source_target_pairs={{0,1},{1,0},{2,3},{3,2},{4,5},{5,4},{6,7},{7,6},{8,9},{9,8},{10,11... | collective-permute-start | bytes 6291464 | tf_op jit(solution)/shard_map/ppermute | solution.py:24
  137.6 4.5 %collective-permute-start.5 = (bf16[128,8192]{1,0:T(8,128)(2,1)}, bf16[128,8192]{1,0:T(8,128)(2,1)}, u32[]{:S(2)}, u32[]{:S(2)}) collective-permute-start(bf16[128,8192]{1,0:T(8,128)(2,1)} %collective-permute-done.4.rest_2_), channel_id=1, source_target_pairs={{0,1},{1,0},{2,3},{3,2},{4,5},{5,4},{6,7},{7,6},{8,9},{9,8},{10,11... | collective-permute-start | bytes 6291464 | tf_op jit(solution)/shard_map/ppermute | solution.py:24
  140.1 92.8 %reduce-scatter.5.cloned.1.call-start = ((), (), s32[]{:S(2)}) async-start(), calls=%async_computation.4 | async-start | bytes 2621440 | tf_op jit(solution)/shard_map/reduce_scatter | solution.py:369
  187.9 92.9 %all-gather.5.cloned.1.call-start = ((), (), s32[]{:S(2)}) async-start(), calls=%async_computation.5 | async-start | bytes 2621440 | tf_op jit(solution)/shard_map/all_gather | solution.py:371
  213.5 21.8 %copy-start.9 = (bf16[8192,128]{1,0:T(8,128)(2,1)S(1)}, bf16[8192,128]{1,0:T(8,128)(2,1)}, u32[]{:S(2)}) copy-start(bf16[8192,128]{1,0:T(8,128)(2,1)} %get-tuple-element.45) | copy-start | bytes 6291460
  235.4 4.4 %copy-start.8 = (bf16[8192,128]{1,0:T(8,128)(2,1)S(1)}, bf16[8192,128]{1,0:T(8,128)(2,1)}, u32[]{:S(2)}) copy-start(bf16[8192,128]{1,0:T(8,128)(2,1)} %get-tuple-element.44) | copy-start | bytes 6291460
  235.5 2.0 collective-permute-start.9
  235.6 2.6 collective-permute-start.8
  236.1 2.9 collective-permute-start.7
  236.2 3.6 collective-permute-start.6
  241.6 64.5 %collective-permute-start.11 = (bf16[8192,128]{1,0:T(8,128)(2,1)}, bf16[8192,128]{1,0:T(8,128)(2,1)S(1)}, u32[]{:S(2)}, u32[]{:S(2)}) collective-permute-start(bf16[8192,128]{1,0:T(8,128)(2,1)} %add_convert_fusion.1.rest_0_), channel_id=1, source_target_pairs={{0,2},{1,3},{2,0},{3,1},{4,6},{5,7},{6,4},{7,5},{8,10},{9,11},{10,... | collective-permute-start | bytes 6291464 | tf_op jit(solution)/shard_map/ppermute | solution.py:24
  307.5 7.3 %collective-permute-start.12 = (bf16[8192,128]{1,0:T(8,128)(2,1)}, bf16[8192,128]{1,0:T(8,128)(2,1)S(1)}, u32[]{:S(2)}, u32[]{:S(2)}) collective-permute-start(bf16[8192,128]{1,0:T(8,128)(2,1)} %get-tuple-element.50), channel_id=1, source_target_pairs={{0,1},{1,0},{2,3},{3,2},{4,5},{5,4},{6,7},{7,6},{8,9},{9,8},{10,11... | collective-permute-start | bytes 6291464 | tf_op jit(solution)/shard_map/ppermute | solution.py:24
  307.5 12.3 %collective-permute-start.14 = (bf16[8192,128]{1,0:T(8,128)(2,1)}, bf16[8192,128]{1,0:T(8,128)(2,1)}, u32[]{:S(2)}, u32[]{:S(2)}) collective-permute-start(bf16[8192,128]{1,0:T(8,128)(2,1)} %get-tuple-element.52), channel_id=1, source_target_pairs={{0,1},{1,0},{2,3},{3,2},{4,5},{5,4},{6,7},{7,6},{8,9},{9,8},{10,11... | collective-permute-start | bytes 6291464 | tf_op jit(solution)/shard_map/ppermute | solution.py:24
  308.0 30.4 %collective-permute-start.10 = (bf16[8192,128]{1,0:T(8,128)(2,1)}, bf16[8192,128]{1,0:T(8,128)(2,1)S(1)}, u32[]{:S(2)}, u32[]{:S(2)}) collective-permute-start(bf16[8192,128]{1,0:T(8,128)(2,1)} %get-tuple-element.47), channel_id=1, source_target_pairs={{0,1},{1,0},{2,3},{3,2},{4,5},{5,4},{6,7},{7,6},{8,9},{9,8},{10,11... | collective-permute-start | bytes 6291464 | tf_op jit(solution)/shard_map/ppermute | solution.py:24
  318.2 48.0 %collective-permute-start.13 = (bf16[8192,128]{1,0:T(8,128)(2,1)}, bf16[8192,128]{1,0:T(8,128)(2,1)}, u32[]{:S(2)}, u32[]{:S(2)}) collective-permute-start(bf16[8192,128]{1,0:T(8,128)(2,1)} %add_convert_fusion), channel_id=1, source_target_pairs={{0,2},{1,3},{2,0},{3,1},{4,6},{5,7},{6,4},{7,5},{8,10},{9,11},{10,... | collective-permute-start | bytes 6291464 | tf_op jit(solution)/shard_map/ppermute | solution.py:24
  329.5 38.2 %copy-start.1 = (bf16[8192,128]{1,0:T(8,128)(2,1)S(1)}, bf16[8192,128]{1,0:T(8,128)(2,1)}, u32[]{:S(2)}) copy-start(bf16[8192,128]{1,0:T(8,128)(2,1)} %get-tuple-element.57.rest_0_) | copy-start | bytes 6291460
  336.5 1.8 collective-permute-start.15
  366.2 10.6 %collective-permute-start.16 = (f32[264,384]{1,0:T(8,128)S(1)}, f32[264,384]{1,0:T(8,128)S(1)}, u32[]{:S(2)}, u32[]{:S(2)}) collective-permute-start(f32[264,384]{1,0:T(8,128)S(1)} %add.37), channel_id=1, source_target_pairs={{0,2},{1,3},{2,0},{3,1},{4,6},{5,7},{6,4},{7,5},{8,10},{9,11},{10,... | collective-permute-start | bytes 1216520 | tf_op jit(solution)/shard_map/ppermute | solution.py:24
  372.5 4.4 %collective-permute-start.18 = (f32[256,128]{1,0:T(8,128)S(1)}, f32[256,128]{1,0:T(8,128)S(1)}, u32[]{:S(2)}, u32[]{:S(2)}) collective-permute-start(f32[256,128]{1,0:T(8,128)S(1)} %get-tuple-element.61), channel_id=1, source_target_pairs={{0,1},{1,0},{2,3},{3,2},{4,5},{5,4},{6,7},{7,6},{8,9},{9,8},{10,11... | collective-permute-start | bytes 393224 | tf_op jit(solution)/shard_map/ppermute | solution.py:24
  376.9 7.5 %collective-permute-start.17 = (f32[264,384]{1,0:T(8,128)S(1)}, f32[264,384]{1,0:T(8,128)S(1)}, u32[]{:S(2)}, u32[]{:S(2)}) collective-permute-start(f32[264,384]{1,0:T(8,128)S(1)} %add.38), channel_id=1, source_target_pairs={{0,1},{1,0},{2,3},{3,2},{4,5},{5,4},{6,7},{7,6},{8,9},{9,8},{10,11... | collective-permute-start | bytes 1216520 | tf_op jit(solution)/shard_map/ppermute | solution.py:24
  377.0 6.0 %collective-permute-start.19 = (f32[256,128]{1,0:T(8,128)S(1)}, f32[256,128]{1,0:T(8,128)S(1)}, u32[]{:S(2)}, u32[]{:S(2)}) collective-permute-start(f32[256,128]{1,0:T(8,128)S(1)} %add.39), channel_id=1, source_target_pairs={{0,2},{1,3},{2,0},{3,1},{4,6},{5,7},{6,4},{7,5},{8,10},{9,11},{10,... | collective-permute-start | bytes 393224 | tf_op jit(solution)/shard_map/ppermute | solution.py:24
  383.0 1.4 collective-permute-start.20
  (7 other events, 12.7 us)
Sparse Core Ops, SparseCore 0:
  88.3 45.3 reduce-scatter.2
  140.2 47.5 all-gather.2
  190.2 42.5 reduce-scatter.4
  235.5 45.2 all-gather.4

commit v11 on v9

--- a/solution.py
+++ b/solution.py
@@ -33,11 +33,14 @@
     return keep + swap(send, masks_of(n)[0], n)
 
 
-def sum_far(total, low, n):
-    near, *far = masks_of(n)
-    for mask in far:
+def sum_far(total, n):
+    for mask in masks_of(n)[1:]:
         total = total + swap(total, mask, n)
-    other = swap(total, near, n)
+    return total
+
+
+def both_halves(total, low, n):
+    other = swap(total, masks_of(n)[0], n)
     return jnp.where(
         low[0] == 0,
         jnp.concatenate([total, other], axis=0),
@@ -123,7 +126,7 @@
 
         @pl.loop(0, n_feat)
         def _(s):
-            @pl.loop(0, per_share, unroll=min(4, per_share))
+            @pl.loop(0, per_share, unroll=min(8, per_share))
             def _(i):
                 b = s * per_share + i
                 picked = []
@@ -363,6 +366,10 @@
         if pieces:
             part_pre, pieces[-1] = lax.optimization_barrier((part_pre, pieces[-1]))
         pre = lax.psum_scatter(part_pre, "feat", scatter_dimension=0, tiled=True)
+        if c == 1:
+            first = sum_near(*weight_grad(low, feat_t, [[pieces[0]]], True), n_node)
+            pre, first = lax.optimization_barrier((pre, first))
+            first = sum_far(first, n_node)
         hidden, grad_pre = activate(pre, bias_row, cot_rows, hidden, c)
         pieces.append(lax.all_gather(grad_pre, "feat", axis=0, tiled=True))
 
@@ -390,19 +397,26 @@
             if mask == 1:
                 after = [total_of(v) for k, v in held.items() if k]
                 held = {k: [total_of(v)] if k else v for k, v in held.items()}
+                if c == 0 and CHUNKS > 1:
+                    behind = {k: v for k, v in held.items() if k}
+                    behind, first = lax.optimization_barrier((behind, first))
+                    held.update(behind)
         arrived = held[0][-1]
         sent.append(held[0])
-    early = [[piece] for piece in pieces] + sent[:-1]
+    early = [[piece] for piece in pieces[1:]] + sent[:-1]
     early = sum_near(*weight_grad(low, feat_t, early, True), n_node)
     last, early = lax.optimization_barrier((sent[-1], early))
     late = sum_near(*weight_grad(low, feat_t, [last], False), n_node)
-    early = sum_far(early, low, n_node)
-    late = sum_far(late, low, n_node)
+    early = both_halves(sum_far(early, n_node), low, n_node)
+    late = both_halves(sum_far(late, n_node), low, n_node)
+    first = both_halves(first, low, n_node)
+    rest = hid - first.shape[1]
+    grad_self = jnp.concatenate([first, early[:, :rest]], axis=1)
     return (
         hidden.reshape(1, share, hid),
-        jnp.concatenate([early[:width, hid:], late], axis=1),
-        early[:width, :hid],
-        early[width, :hid],
+        jnp.concatenate([early[:width, rest:], late], axis=1),
+        grad_self[:width],
+        grad_self[width],
     )
 
 

time: 393 us -> 383 us (0.975)
  Pallas kernels: 125 us -> 120 us
    reduce_scatter x2, waiting for transfers between devices: 20.3 us -> 11.7 us  [on_device(): pre = lax.psum_scatter(part_pre, 'feat', scatter_dimension=0, tiled=True)]
    ppermute x24 -> x27, waiting for transfers between devices: 133 us -> 137 us  [swap(): return lax.ppermute(value, 'node', [(i, i ^ mask) for i in range(n)])]
    ppermute x24 -> x27, starting transfers between devices: 13.5 us -> 14.3 us  [swap(): return lax.ppermute(value, 'node', [(i, i ^ mask) for i in range(n)])]
    pallas_call x2 -> x3, Pallas kernels: 11.8 us -> 10.9 us  [weight_grad(): pl.pallas_call(kernel, grid=(rows // step,), in_specs=[SMEM, pl.BlockSpec...]
  transfers between devices with their start and end apart: 28 -> 31, of which waited for: 20 -> 22; matrix products, arithmetic and copies ran while one was open for 2% -> 1% of each run, Pallas kernels for 24% -> 24%
where the time goes in v11:
time: 383 us; the launch traced here: 382 us
  waiting for transfers between devices  214 us (56%)
  Pallas kernels  120 us (31%)
  starting transfers between devices  14.6 us (4%)
  between operations  14.1 us (4%)
  local copies, waits for them, and re-layouts  11.7 us (3%)
  other arithmetic  7.2 us (2%)
    ppermute x27, waiting for transfers between devices, swap(): return lax.ppermute(value, 'node', [(i, i ^ mask) for i in range(n)])  137 us
    all_gather x2, waiting for transfers between devices, on_device(): pieces.append(lax.all_gather(grad_pre, 'feat', axis=0, tiled=True))  64.9 us
    pallas_call x2, Pallas kernels, spread_tiles(): pl.pallas_call(kernel, out_shape=[jax.ShapeDtypeStruct((rows, wide), jnp....  48.8 us
    pallas_call x2, Pallas kernels, mean_tiles(): pl.pallas_call(kernel, out_shape=jax.ShapeDtypeStruct((rows, wide), jnp.b...  36.1 us
    pallas_call x2, Pallas kernels, project(): pl.pallas_call(kernel, grid=(rows // step,), in_specs=[pl.BlockSpec((widt...  19.5 us
    ppermute x27, starting transfers between devices, swap(): return lax.ppermute(value, 'node', [(i, i ^ mask) for i in range(n)])  14.3 us
    reduce_scatter x2, waiting for transfers between devices, on_device(): pre = lax.psum_scatter(part_pre, 'feat', scatter_dimension=0, tiled=True)  11.7 us
    pallas_call x3, Pallas kernels, weight_grad(): pl.pallas_call(kernel, grid=(rows // step,), in_specs=[SMEM, pl.BlockSpec...  10.9 us
  transfers between devices with their start and end apart: 31, of which 22 were waited for; matrix products, arithmetic and copies ran while one was open for 1% of the time, Pallas kernels for 24%

profile of v11, /device:TPU:0, one launch (start us, length us, event | category | flops | bytes accessed | tf_op | source)
XLA Modules:
  0.0 382.0 jit_solution(7598192184129113418)
XLA Ops:
  7.2 9.0 %project.2 = (bf16[128,8192]{1,0:T(8,128)(2,1)}, bf16[128,8192]{1,0:T(8,128)(2,1)}) custom-call(bf16[512,8192]{1,0:T(8,128)(2,1)} %feat_ref.9, bf16[512,256]{1,0:T(8,128)(2,1)} %w_ref.2), custom_call_target="tpu_custom_call" | custom-call | flops 2147483648 | bytes 16777216 | tf_op jit(solution)/shard_map/project/pallas_call | solution.py:85
  16.3 3.0 collective-permute-start.1
  19.3 10.5 %project.3 = (f32[128,8192]{1,0:T(8,128)}, f32[128,8192]{1,0:T(8,128)}) custom-call(bf16[512,8192]{1,0:T(8,128)(2,1)} %feat_ref.9, bf16[512,256]{1,0:T(8,128)(2,1)} %w_ref.3, bf16[128,8192]{1,0:T(8,128)(2,1)} %get-tuple-element.41.rest_0_), custom_call_target="tpu_custom_call" | custom-call | flops 2147483648 | bytes 16777216 | tf_op jit(solution)/shard_map/project/pallas_call | solution.py:85
  29.8 35.4 %collective-permute-done.1.rest_2_ = bf16[128,8192]{1,0:T(8,128)(2,1)S(1)} collective-permute-done((bf16[128,8192]{1,0:T(8,128)(2,1)}, bf16[128,8192]{1,0:T(8,128)(2,1)S(1)}, u32[]{:S(2)}, u32[]{:S(2)}) %collective-permute-start.1) | collective-permute-done | bytes 2097184 | tf_op jit(solution)/shard_map/ppermute | solution.py:24
  67.6 1.8 collective-permute-done.2.rest_3_
  69.4 18.0 %mean_tiles.2 = bf16[8192,128]{1,0:T(8,128)(2,1)} custom-call(s32[64,16]{1,0:T(8,128)} %fusion.3.src_ref, f32[64]{0:T(128)} %convert_divide_fusion.inv_ref, s32[64,16,128]{2,1,0:T(8,128)} %broadcast_select_fusion.nbr_ref, f32[128,8192]{1,0:T(8,128)} %get-tuple-element.43.self_hbm, bf16[128,8192]{1,0:T(8,128)(2,1)} %get-tuple-element.41.rest_0_, ...), custom_call_target="tpu_custom_call" | custom-call | flops 17179869184 | bytes 14680064 | tf_op jit(solution)/shard_map/mean_tiles/pallas_call | solution.py:154
  87.5 1.5 copy-done.13
  89.0 1.8 collective-permute-start.4
  90.8 46.0 %collective-permute-done.4.rest_2_ = bf16[128,8192]{1,0:T(8,128)(2,1)} collective-permute-done((bf16[128,8192]{1,0:T(8,128)(2,1)S(1)}, bf16[128,8192]{1,0:T(8,128)(2,1)}, u32[]{:S(2)}, u32[]{:S(2)}) %collective-permute-start.4) | collective-permute-done | bytes 2097184 | tf_op jit(solution)/shard_map/ppermute | solution.py:24
  136.8 2.5 activate.2
  139.4 1.9 collective-permute-done.5.rest_3_
  141.3 18.0 %mean_tiles.3 = bf16[8192,128]{1,0:T(8,128)(2,1)} custom-call(s32[64,16]{1,0:T(8,128)} %fusion.3.src_ref, f32[64]{0:T(128)} %convert_divide_fusion.inv_ref, s32[64,16,128]{2,1,0:T(8,128)} %broadcast_select_fusion.nbr_ref, f32[128,8192]{1,0:T(8,128)} %get-tuple-element.46.self_hbm, bf16[128,8192]{1,0:T(8,128)(2,1)} %get-tuple-element.47.rest_0_, ...), custom_call_target="tpu_custom_call" | custom-call | flops 17179869184 | bytes 14680064 | tf_op jit(solution)/shard_map/mean_tiles/pallas_call | solution.py:154
  159.4 27.9 %all-gather.3.cloned.1.call-done.rest_0_.grad_hbm = bf16[8192,128]{1,0:T(8,128)(2,1)} async-done(((bf16[2048,128]{1,0:T(8,128)(2,1)}), bf16[8192,128]{1,0:T(8,128)(2,1)}) %all-gather.3.cloned.1.call-update) | async-done | bytes 2097168 | tf_op jit(solution)/shard_map/all_gather | solution.py:374
  188.9 3.4 copy-done
  192.3 3.6 weight_grad.3
  195.9 24.4 %spread_tiles.2 = (bf16[8192,128]{1,0:T(8,128)(2,1)}, bf16[8192,128]{1,0:T(8,128)(2,1)}, bf16[8192,128]{1,0:T(8,128)(2,1)}, bf16[8192,128]{1,0:T(8,128)(2,1)}) custom-call(s32[64,16]{1,0:T(8,128)} %fusion.3.src_ref, f32[64]{0:T(128)} %convert_divide_fusion.inv_ref, s32[64,16,128]{2,1,0:T(8,128)} %broadcast_select_fusion.nbr_ref, ...), custom_call_target="tpu_custom_call" | custom-call | flops 17179869184 | bytes 10485760 | tf_op jit(solution)/shard_map/spread_tiles/pallas_call | solution.py:261
  220.4 11.7 %reduce-scatter.5.cloned.1.call-done.pre_ref = bf16[2048,128]{1,0:T(8,128)(2,1)} async-done(((bf16[8192,128]{1,0:T(8,128)(2,1)}), bf16[2048,128]{1,0:T(8,128)(2,1)}) %reduce-scatter.5.cloned.1.call-update) | async-done | bytes 524304 | tf_op jit(solution)/shard_map/reduce_scatter | solution.py:368
  232.0 2.5 activate.3
  235.8 1.5 collective-permute-start.12
  238.9 1.8 add_convert_fusion.1.rest_0_
  241.4 1.5 collective-permute-start.13
  242.9 37.0 %all-gather.5.cloned.1.call-done.grad_hbm.rest_0_ = bf16[8192,128]{1,0:T(8,128)(2,1)} async-done(((bf16[2048,128]{1,0:T(8,128)(2,1)}), bf16[8192,128]{1,0:T(8,128)(2,1)}) %all-gather.5.cloned.1.call-update) | async-done | bytes 2097168 | tf_op jit(solution)/shard_map/all_gather | solution.py:374
  279.9 24.4 %spread_tiles.3 = (bf16[8192,128]{1,0:T(8,128)(2,1)}, bf16[8192,128]{1,0:T(8,128)(2,1)}, bf16[8192,128]{1,0:T(8,128)(2,1)}, bf16[8192,128]{1,0:T(8,128)(2,1)}) custom-call(s32[64,16]{1,0:T(8,128)} %fusion.3.src_ref, f32[64]{0:T(128)} %convert_divide_fusion.inv_ref, s32[64,16,128]{2,1,0:T(8,128)} %broadcast_select_fusion.nbr_ref, ...), custom_call_target="tpu_custom_call" | custom-call | flops 17179869184 | bytes 10485760 | tf_op jit(solution)/shard_map/spread_tiles/pallas_call | solution.py:261
  304.3 1.8 fusion.8
  309.6 1.5 collective-permute-done.14
  311.7 1.5 collective-permute-start.18
  313.2 3.2 collective-permute-done.19.rest_2_
  316.4 3.4 copy-done.1
  319.8 3.7 weight_grad.4
  325.2 34.3 %collective-permute-done.18.rest_2_ = bf16[8192,128]{1,0:T(8,128)(2,1)S(1)} collective-permute-done((bf16[8192,128]{1,0:T(8,128)(2,1)S(1)}, bf16[8192,128]{1,0:T(8,128)(2,1)S(1)}, u32[]{:S(2)}, u32[]{:S(2)}) %collective-permute-start.18) | collective-permute-done | bytes 2097184 | tf_op jit(solution)/shard_map/ppermute | solution.py:24
  360.9 3.7 weight_grad.5
  367.2 4.4 %collective-permute-done.24 = f32[256,128]{1,0:T(8,128)S(1)} collective-permute-done((f32[256,128]{1,0:T(8,128)S(1)}, f32[256,128]{1,0:T(8,128)S(1)}, u32[]{:S(2)}, u32[]{:S(2)}) %collective-permute-start.24) | collective-permute-done | bytes 131104 | tf_op jit(solution)/shard_map/ppermute | solution.py:24
  (98 shorter events, 21.3 us)
Async XLA Ops:
  7.2 129.7 %reduce-scatter.3.cloned.1.call-start = ((), (), s32[]{:S(2)}) async-start(), calls=%async_computation.2 | async-start | bytes 2621440 | tf_op jit(solution)/shard_map/reduce_scatter | solution.py:368
  16.3 50.3 %copy-start.9 = (s32[64,16,128]{2,1,0:T(8,128)S(1)}, s32[64,16,128]{2,1,0:T(8,128)}, u32[]{:S(2)}) copy-start(s32[64,16,128]{2,1,0:T(8,128)} %param.10) | copy-start | bytes 1572868
  16.3 48.8 %collective-permute-start.1 = (bf16[128,8192]{1,0:T(8,128)(2,1)}, bf16[128,8192]{1,0:T(8,128)(2,1)S(1)}, u32[]{:S(2)}, u32[]{:S(2)}) collective-permute-start(bf16[128,8192]{1,0:T(8,128)(2,1)} %get-tuple-element.41.rest_0_), channel_id=1, source_target_pairs={{0,2},{1,3},{2,0},{3,1},{4,6},{5,7},{6,4},{7,5},{8,10},{9,11},{10,... | collective-permute-start | bytes 6291464 | tf_op jit(solution)/shard_map/ppermute | solution.py:24
  19.3 48.3 %collective-permute-start = (bf16[128,8192]{1,0:T(8,128)(2,1)}, bf16[128,8192]{1,0:T(8,128)(2,1)}, u32[]{:S(2)}, u32[]{:S(2)}) collective-permute-start(bf16[128,8192]{1,0:T(8,128)(2,1)} %get-tuple-element.41.rest_0_), channel_id=1, source_target_pairs={{0,1},{1,0},{2,3},{3,2},{4,5},{5,4},{6,7},{7,6},{8,9},{9,8},{10,11... | collective-permute-start | bytes 6291464 | tf_op jit(solution)/shard_map/ppermute | solution.py:24
  65.1 4.3 %collective-permute-start.2 = (bf16[128,8192]{1,0:T(8,128)(2,1)S(1)}, bf16[128,8192]{1,0:T(8,128)(2,1)}, u32[]{:S(2)}, u32[]{:S(2)}) collective-permute-start(bf16[128,8192]{1,0:T(8,128)(2,1)S(1)} %collective-permute-done.1.rest_2_), channel_id=1, source_target_pairs={{0,1},{1,0},{2,3},{3,2},{4,5},{5,4},{6,7},{7,6},{8,9},{9,8},{10,11... | collective-permute-start | bytes 6291464 | tf_op jit(solution)/shard_map/ppermute | solution.py:24
  87.5 99.8 %all-gather.3.cloned.1.call-start = ((), (), s32[]{:S(2)}) async-start(), calls=%async_computation.3 | async-start | bytes 2621440 | tf_op jit(solution)/shard_map/all_gather | solution.py:374
  89.0 47.8 %collective-permute-start.4 = (bf16[128,8192]{1,0:T(8,128)(2,1)S(1)}, bf16[128,8192]{1,0:T(8,128)(2,1)}, u32[]{:S(2)}, u32[]{:S(2)}) collective-permute-start(bf16[128,8192]{1,0:T(8,128)(2,1)S(1)} %copy-done.13), channel_id=1, source_target_pairs={{0,2},{1,3},{2,0},{3,1},{4,6},{5,7},{6,4},{7,5},{8,10},{9,11},{10,... | collective-permute-start | bytes 6291464 | tf_op jit(solution)/shard_map/ppermute | solution.py:24
  90.8 48.6 %collective-permute-start.3 = (bf16[128,8192]{1,0:T(8,128)(2,1)S(1)}, bf16[128,8192]{1,0:T(8,128)(2,1)}, u32[]{:S(2)}, u32[]{:S(2)}) collective-permute-start(bf16[128,8192]{1,0:T(8,128)(2,1)S(1)} %copy-done.13), channel_id=1, source_target_pairs={{0,1},{1,0},{2,3},{3,2},{4,5},{5,4},{6,7},{7,6},{8,9},{9,8},{10,11... | collective-permute-start | bytes 6291464 | tf_op jit(solution)/shard_map/ppermute | solution.py:24
  136.8 4.5 %collective-permute-start.5 = (bf16[128,8192]{1,0:T(8,128)(2,1)}, bf16[128,8192]{1,0:T(8,128)(2,1)}, u32[]{:S(2)}, u32[]{:S(2)}) collective-permute-start(bf16[128,8192]{1,0:T(8,128)(2,1)} %collective-permute-done.4.rest_2_), channel_id=1, source_target_pairs={{0,1},{1,0},{2,3},{3,2},{4,5},{5,4},{6,7},{7,6},{8,9},{9,8},{10,11... | collective-permute-start | bytes 6291464 | tf_op jit(solution)/shard_map/ppermute | solution.py:24
  139.3 92.7 %reduce-scatter.5.cloned.1.call-start = ((), (), s32[]{:S(2)}) async-start(), calls=%async_computation.4 | async-start | bytes 2621440 | tf_op jit(solution)/shard_map/reduce_scatter | solution.py:368
  187.3 92.6 %all-gather.5.cloned.1.call-start = ((), (), s32[]{:S(2)}) async-start(), calls=%async_computation.5 | async-start | bytes 2621440 | tf_op jit(solution)/shard_map/all_gather | solution.py:374
  195.8 24.5 %collective-permute-start.6 = (f32[264,128]{1,0:T(8,128)S(1)}, f32[264,128]{1,0:T(8,128)S(1)}, u32[]{:S(2)}, u32[]{:S(2)}) collective-permute-start(f32[264,128]{1,0:T(8,128)S(1)} %get-tuple-element.52), channel_id=1, source_target_pairs={{0,1},{1,0},{2,3},{3,2},{4,5},{5,4},{6,7},{7,6},{8,9},{9,8},{10,11... | collective-permute-start | bytes 405512 | tf_op jit(solution)/shard_map/ppermute | solution.py:24
  234.7 2.6 collective-permute-start.10
  234.8 2.6 collective-permute-start.9
  235.3 2.9 collective-permute-start.8
  235.4 3.6 collective-permute-start.7
  235.8 5.6 %collective-permute-start.12 = (f32[264,128]{1,0:T(8,128)S(1)}, f32[264,128]{1,0:T(8,128)S(1)}, u32[]{:S(2)}, u32[]{:S(2)}) collective-permute-start(f32[264,128]{1,0:T(8,128)S(1)} %add.41), channel_id=1, source_target_pairs={{0,2},{1,3},{2,0},{3,1},{4,6},{5,7},{6,4},{7,5},{8,10},{9,11},{10,... | collective-permute-start | bytes 405512 | tf_op jit(solution)/shard_map/ppermute | solution.py:24
  241.4 62.9 %collective-permute-start.13 = (bf16[8192,128]{1,0:T(8,128)(2,1)}, bf16[8192,128]{1,0:T(8,128)(2,1)S(1)}, u32[]{:S(2)}, u32[]{:S(2)}) collective-permute-start(bf16[8192,128]{1,0:T(8,128)(2,1)} %add_convert_fusion.1.rest_0_), channel_id=1, source_target_pairs={{0,2},{1,3},{2,0},{3,1},{4,6},{5,7},{6,4},{7,5},{8,10},{9,11},{10,... | collective-permute-start | bytes 6291464 | tf_op jit(solution)/shard_map/ppermute | solution.py:24
  306.2 2.0 collective-permute-start.17
  306.2 2.6 collective-permute-start.16
  306.7 2.9 collective-permute-start.15
  306.8 4.3 %collective-permute-start.14 = (bf16[2048,128]{1,0:T(8,128)(2,1)S(1)}, bf16[2048,128]{1,0:T(8,128)(2,1)S(1)}, u32[]{:S(2)}, u32[]{:S(2)}) collective-permute-start(bf16[2048,128]{1,0:T(8,128)(2,1)S(1)} %get-tuple-element.78), channel_id=1, source_target_pairs={{0,1},{1,0},{2,3},{3,2},{4,5},{5,4},{6,7},{7,6},{8,9},{9,8},{10,11... | collective-permute-start | bytes 1572872 | tf_op jit(solution)/shard_map/ppermute | solution.py:24
  307.2 9.1 %collective-permute-start.19 = (bf16[8192,128]{1,0:T(8,128)(2,1)S(1)}, bf16[8192,128]{1,0:T(8,128)(2,1)S(1)}, u32[]{:S(2)}, u32[]{:S(2)}) collective-permute-start(bf16[8192,128]{1,0:T(8,128)(2,1)S(1)} %copy-done.12), channel_id=1, source_target_pairs={{0,1},{1,0},{2,3},{3,2},{4,5},{5,4},{6,7},{7,6},{8,9},{9,8},{10,11... | collective-permute-start | bytes 6291464 | tf_op jit(solution)/shard_map/ppermute | solution.py:24
  308.1 17.0 %collective-permute-start.11 = (bf16[8192,128]{1,0:T(8,128)(2,1)}, bf16[8192,128]{1,0:T(8,128)(2,1)S(1)}, u32[]{:S(2)}, u32[]{:S(2)}) collective-permute-start(bf16[8192,128]{1,0:T(8,128)(2,1)} %get-tuple-element.60), channel_id=1, source_target_pairs={{0,1},{1,0},{2,3},{3,2},{4,5},{5,4},{6,7},{7,6},{8,9},{9,8},{10,11... | collective-permute-start | bytes 6291464 | tf_op jit(solution)/shard_map/ppermute | solution.py:24
  311.7 47.7 %collective-permute-start.18 = (bf16[8192,128]{1,0:T(8,128)(2,1)S(1)}, bf16[8192,128]{1,0:T(8,128)(2,1)S(1)}, u32[]{:S(2)}, u32[]{:S(2)}) collective-permute-start(bf16[8192,128]{1,0:T(8,128)(2,1)S(1)} %add_convert_fusion), channel_id=1, source_target_pairs={{0,2},{1,3},{2,0},{3,1},{4,6},{5,7},{6,4},{7,5},{8,10},{9,11},{10,... | collective-permute-start | bytes 6291464 | tf_op jit(solution)/shard_map/ppermute | solution.py:24
  323.5 1.6 collective-permute-start.20
  359.4 7.7 %collective-permute-start.21 = (f32[264,256]{1,0:T(8,128)S(1)}, f32[264,256]{1,0:T(8,128)S(1)}, u32[]{:S(2)}, u32[]{:S(2)}) collective-permute-start(f32[264,256]{1,0:T(8,128)S(1)} %add.45), channel_id=1, source_target_pairs={{0,2},{1,3},{2,0},{3,1},{4,6},{5,7},{6,4},{7,5},{8,10},{9,11},{10,... | collective-permute-start | bytes 811016 | tf_op jit(solution)/shard_map/ppermute | solution.py:24
  364.6 1.4 collective-permute-start.23
  366.0 5.6 %collective-permute-start.24 = (f32[256,128]{1,0:T(8,128)S(1)}, f32[256,128]{1,0:T(8,128)S(1)}, u32[]{:S(2)}, u32[]{:S(2)}) collective-permute-start(f32[256,128]{1,0:T(8,128)S(1)} %add.47), channel_id=1, source_target_pairs={{0,2},{1,3},{2,0},{3,1},{4,6},{5,7},{6,4},{7,5},{8,10},{9,11},{10,... | collective-permute-start | bytes 393224 | tf_op jit(solution)/shard_map/ppermute | solution.py:24
  366.6 5.1 %collective-permute-start.26 = (f32[264,128]{1,0:T(8,128)S(1)}, f32[264,128]{1,0:T(8,128)S(1)}, u32[]{:S(2)}, u32[]{:S(2)}) collective-permute-start(f32[264,128]{1,0:T(8,128)S(1)} %add.43), channel_id=1, source_target_pairs={{0,1},{1,0},{2,3},{3,2},{4,5},{5,4},{6,7},{7,6},{8,9},{9,8},{10,11... | collective-permute-start | bytes 405512 | tf_op jit(solution)/shard_map/ppermute | solution.py:24
  367.2 5.9 %collective-permute-start.22 = (f32[264,256]{1,0:T(8,128)S(1)}, f32[264,256]{1,0:T(8,128)S(1)}, u32[]{:S(2)}, u32[]{:S(2)}) collective-permute-start(f32[264,256]{1,0:T(8,128)S(1)} %add.46), channel_id=1, source_target_pairs={{0,1},{1,0},{2,3},{3,2},{4,5},{5,4},{6,7},{7,6},{8,9},{9,8},{10,11... | collective-permute-start | bytes 811016 | tf_op jit(solution)/shard_map/ppermute | solution.py:24
  371.6 1.4 collective-permute-start.25
  (14 other events, 192.0 us)
Sparse Core Ops, SparseCore 0:
  87.6 45.3 reduce-scatter.2
  139.5 47.7 all-gather.2
  189.7 42.2 reduce-scatter.4
  234.7 45.2 all-gather.4

commit v12 on v11

--- a/solution.py
+++ b/solution.py
@@ -126,7 +126,7 @@
 
         @pl.loop(0, n_feat)
         def _(s):
-            @pl.loop(0, per_share, unroll=min(8, per_share))
+            @pl.loop(0, per_share, unroll=min(16, per_share))
             def _(i):
                 b = s * per_share + i
                 picked = []
@@ -223,7 +223,7 @@
 
         load.wait()
 
-        @pl.loop(0, blocks, unroll=min(4, blocks))
+        @pl.loop(0, blocks, unroll=min(8, blocks))
         def _(b):
             g = grad_ref[pl.ds(pl.multiple_of(b * side, side), side), :]
             scale = inv_ref[b]

time: 383 us -> 382 us (level)
  transfers between devices with their start and end apart: 31 -> 31, of which waited for: 22 -> 22; matrix products, arithmetic and copies ran while one was open for 1% -> 1% of each run, Pallas kernels for 24% -> 23%
where the time goes in v12:
time: 382 us; the launch traced here: 381 us
  waiting for transfers between devices  215 us (56%)
  Pallas kernels  118 us (31%)
  starting transfers between devices  14.6 us (4%)
  between operations  14.1 us (4%)
  local copies, waits for them, and re-layouts  11.7 us (3%)
  other arithmetic  7.2 us (2%)
    ppermute x27, waiting for transfers between devices, swap(): return lax.ppermute(value, 'node', [(i, i ^ mask) for i in range(n)])  137 us
    all_gather x2, waiting for transfers between devices, on_device(): pieces.append(lax.all_gather(grad_pre, 'feat', axis=0, tiled=True))  65.6 us
    pallas_call x2, Pallas kernels, spread_tiles(): pl.pallas_call(kernel, out_shape=[jax.ShapeDtypeStruct((rows, wide), jnp....  48 us
    pallas_call x2, Pallas kernels, mean_tiles(): pl.pallas_call(kernel, out_shape=jax.ShapeDtypeStruct((rows, wide), jnp.b...  34.3 us
    pallas_call x2, Pallas kernels, project(): pl.pallas_call(kernel, grid=(rows // step,), in_specs=[pl.BlockSpec((widt...  19.5 us
    ppermute x27, starting transfers between devices, swap(): return lax.ppermute(value, 'node', [(i, i ^ mask) for i in range(n)])  14.3 us
    reduce_scatter x2, waiting for transfers between devices, on_device(): pre = lax.psum_scatter(part_pre, 'feat', scatter_dimension=0, tiled=True)  12.3 us
    pallas_call x3, Pallas kernels, weight_grad(): pl.pallas_call(kernel, grid=(rows // step,), in_specs=[SMEM, pl.BlockSpec...  10.9 us
  transfers between devices with their start and end apart: 31, of which 22 were waited for; matrix products, arithmetic and copies ran while one was open for 1% of the time, Pallas kernels for 23%

profile of v12, /device:TPU:0, one launch (start us, length us, event | category | flops | bytes accessed | tf_op | source)
XLA Modules:
  0.0 380.8 jit_solution(16364781898989709718)
XLA Ops:
  7.2 9.0 %project.2 = (bf16[128,8192]{1,0:T(8,128)(2,1)}, bf16[128,8192]{1,0:T(8,128)(2,1)}) custom-call(bf16[512,8192]{1,0:T(8,128)(2,1)} %feat_ref.9, bf16[512,256]{1,0:T(8,128)(2,1)} %w_ref.2), custom_call_target="tpu_custom_call" | custom-call | flops 2147483648 | bytes 16777216 | tf_op jit(solution)/shard_map/project/pallas_call | solution.py:85
  16.3 3.0 collective-permute-start.1
  19.3 10.5 %project.3 = (f32[128,8192]{1,0:T(8,128)}, f32[128,8192]{1,0:T(8,128)}) custom-call(bf16[512,8192]{1,0:T(8,128)(2,1)} %feat_ref.9, bf16[512,256]{1,0:T(8,128)(2,1)} %w_ref.3, bf16[128,8192]{1,0:T(8,128)(2,1)} %get-tuple-element.41.rest_0_), custom_call_target="tpu_custom_call" | custom-call | flops 2147483648 | bytes 16777216 | tf_op jit(solution)/shard_map/project/pallas_call | solution.py:85
  29.8 35.4 %collective-permute-done.1.rest_2_ = bf16[128,8192]{1,0:T(8,128)(2,1)S(1)} collective-permute-done((bf16[128,8192]{1,0:T(8,128)(2,1)}, bf16[128,8192]{1,0:T(8,128)(2,1)S(1)}, u32[]{:S(2)}, u32[]{:S(2)}) %collective-permute-start.1) | collective-permute-done | bytes 2097184 | tf_op jit(solution)/shard_map/ppermute | solution.py:24
  67.6 1.8 collective-permute-done.2.rest_3_
  69.4 17.2 %mean_tiles.2 = bf16[8192,128]{1,0:T(8,128)(2,1)} custom-call(s32[64,16]{1,0:T(8,128)} %fusion.3.src_ref, f32[64]{0:T(128)} %convert_divide_fusion.inv_ref, s32[64,16,128]{2,1,0:T(8,128)} %broadcast_select_fusion.nbr_ref, f32[128,8192]{1,0:T(8,128)} %get-tuple-element.43.self_hbm, bf16[128,8192]{1,0:T(8,128)(2,1)} %get-tuple-element.41.rest_0_, ...), custom_call_target="tpu_custom_call" | custom-call | flops 17179869184 | bytes 14680064 | tf_op jit(solution)/shard_map/mean_tiles/pallas_call | solution.py:154
  86.7 1.5 copy-done.13
  88.2 1.8 collective-permute-start.4
  89.9 46.0 %collective-permute-done.4.rest_2_ = bf16[128,8192]{1,0:T(8,128)(2,1)} collective-permute-done((bf16[128,8192]{1,0:T(8,128)(2,1)S(1)}, bf16[128,8192]{1,0:T(8,128)(2,1)}, u32[]{:S(2)}, u32[]{:S(2)}) %collective-permute-start.4) | collective-permute-done | bytes 2097184 | tf_op jit(solution)/shard_map/ppermute | solution.py:24
  136.0 2.5 activate.2
  138.5 1.9 collective-permute-done.5.rest_3_
  140.5 17.2 %mean_tiles.3 = bf16[8192,128]{1,0:T(8,128)(2,1)} custom-call(s32[64,16]{1,0:T(8,128)} %fusion.3.src_ref, f32[64]{0:T(128)} %convert_divide_fusion.inv_ref, s32[64,16,128]{2,1,0:T(8,128)} %broadcast_select_fusion.nbr_ref, f32[128,8192]{1,0:T(8,128)} %get-tuple-element.46.self_hbm, bf16[128,8192]{1,0:T(8,128)(2,1)} %get-tuple-element.47.rest_0_, ...), custom_call_target="tpu_custom_call" | custom-call | flops 17179869184 | bytes 14680064 | tf_op jit(solution)/shard_map/mean_tiles/pallas_call | solution.py:154
  157.7 28.6 %all-gather.3.cloned.1.call-done.rest_0_.grad_hbm = bf16[8192,128]{1,0:T(8,128)(2,1)} async-done(((bf16[2048,128]{1,0:T(8,128)(2,1)}), bf16[8192,128]{1,0:T(8,128)(2,1)}) %all-gather.3.cloned.1.call-update) | async-done | bytes 2097168 | tf_op jit(solution)/shard_map/all_gather | solution.py:374
  187.8 3.4 copy-done
  191.2 3.6 weight_grad.3
  194.8 24.0 %spread_tiles.2 = (bf16[8192,128]{1,0:T(8,128)(2,1)}, bf16[8192,128]{1,0:T(8,128)(2,1)}, bf16[8192,128]{1,0:T(8,128)(2,1)}, bf16[8192,128]{1,0:T(8,128)(2,1)}) custom-call(s32[64,16]{1,0:T(8,128)} %fusion.3.src_ref, f32[64]{0:T(128)} %convert_divide_fusion.inv_ref, s32[64,16,128]{2,1,0:T(8,128)} %broadcast_select_fusion.nbr_ref, ...), custom_call_target="tpu_custom_call" | custom-call | flops 17179869184 | bytes 10485760 | tf_op jit(solution)/shard_map/spread_tiles/pallas_call | solution.py:261
  218.9 12.3 %reduce-scatter.5.cloned.1.call-done.pre_ref = bf16[2048,128]{1,0:T(8,128)(2,1)} async-done(((bf16[8192,128]{1,0:T(8,128)(2,1)}), bf16[2048,128]{1,0:T(8,128)(2,1)}) %reduce-scatter.5.cloned.1.call-update) | async-done | bytes 524304 | tf_op jit(solution)/shard_map/reduce_scatter | solution.py:368
  231.2 2.5 activate.3
  238.1 1.8 add_convert_fusion.1.rest_0_
  240.6 1.5 collective-permute-start.13
  242.1 37.0 %all-gather.5.cloned.1.call-done.grad_hbm.rest_0_ = bf16[8192,128]{1,0:T(8,128)(2,1)} async-done(((bf16[2048,128]{1,0:T(8,128)(2,1)}), bf16[8192,128]{1,0:T(8,128)(2,1)}) %all-gather.5.cloned.1.call-update) | async-done | bytes 2097168 | tf_op jit(solution)/shard_map/all_gather | solution.py:374
  279.1 23.9 %spread_tiles.3 = (bf16[8192,128]{1,0:T(8,128)(2,1)}, bf16[8192,128]{1,0:T(8,128)(2,1)}, bf16[8192,128]{1,0:T(8,128)(2,1)}, bf16[8192,128]{1,0:T(8,128)(2,1)}) custom-call(s32[64,16]{1,0:T(8,128)} %fusion.3.src_ref, f32[64]{0:T(128)} %convert_divide_fusion.inv_ref, s32[64,16,128]{2,1,0:T(8,128)} %broadcast_select_fusion.nbr_ref, ...), custom_call_target="tpu_custom_call" | custom-call | flops 17179869184 | bytes 10485760 | tf_op jit(solution)/shard_map/spread_tiles/pallas_call | solution.py:261
  303.1 1.8 fusion.8
  308.4 1.5 collective-permute-done.14
  310.5 1.5 collective-permute-start.18
  312.0 3.2 collective-permute-done.19.rest_2_
  315.2 3.4 copy-done.1
  318.6 3.7 weight_grad.4
  324.0 34.2 %collective-permute-done.18.rest_2_ = bf16[8192,128]{1,0:T(8,128)(2,1)S(1)} collective-permute-done((bf16[8192,128]{1,0:T(8,128)(2,1)S(1)}, bf16[8192,128]{1,0:T(8,128)(2,1)S(1)}, u32[]{:S(2)}, u32[]{:S(2)}) %collective-permute-start.18) | collective-permute-done | bytes 2097184 | tf_op jit(solution)/shard_map/ppermute | solution.py:24
  358.2 1.5 collective-permute-start.21
  359.7 3.7 weight_grad.5
  366.0 4.4 %collective-permute-done.24 = f32[256,128]{1,0:T(8,128)S(1)} collective-permute-done((f32[256,128]{1,0:T(8,128)S(1)}, f32[256,128]{1,0:T(8,128)S(1)}, u32[]{:S(2)}, u32[]{:S(2)}) %collective-permute-start.24) | collective-permute-done | bytes 131104 | tf_op jit(solution)/shard_map/ppermute | solution.py:24
  (98 shorter events, 21.4 us)
Async XLA Ops:
  7.2 128.8 %reduce-scatter.3.cloned.1.call-start = ((), (), s32[]{:S(2)}) async-start(), calls=%async_computation.2 | async-start | bytes 2621440 | tf_op jit(solution)/shard_map/reduce_scatter | solution.py:368
  16.3 50.3 %copy-start.9 = (s32[64,16,128]{2,1,0:T(8,128)S(1)}, s32[64,16,128]{2,1,0:T(8,128)}, u32[]{:S(2)}) copy-start(s32[64,16,128]{2,1,0:T(8,128)} %param.10) | copy-start | bytes 1572868
  16.3 48.8 %collective-permute-start.1 = (bf16[128,8192]{1,0:T(8,128)(2,1)}, bf16[128,8192]{1,0:T(8,128)(2,1)S(1)}, u32[]{:S(2)}, u32[]{:S(2)}) collective-permute-start(bf16[128,8192]{1,0:T(8,128)(2,1)} %get-tuple-element.41.rest_0_), channel_id=1, source_target_pairs={{0,2},{1,3},{2,0},{3,1},{4,6},{5,7},{6,4},{7,5},{8,10},{9,11},{10,... | collective-permute-start | bytes 6291464 | tf_op jit(solution)/shard_map/ppermute | solution.py:24
  19.3 48.3 %collective-permute-start = (bf16[128,8192]{1,0:T(8,128)(2,1)}, bf16[128,8192]{1,0:T(8,128)(2,1)}, u32[]{:S(2)}, u32[]{:S(2)}) collective-permute-start(bf16[128,8192]{1,0:T(8,128)(2,1)} %get-tuple-element.41.rest_0_), channel_id=1, source_target_pairs={{0,1},{1,0},{2,3},{3,2},{4,5},{5,4},{6,7},{7,6},{8,9},{9,8},{10,11... | collective-permute-start | bytes 6291464 | tf_op jit(solution)/shard_map/ppermute | solution.py:24
  65.1 4.3 %collective-permute-start.2 = (bf16[128,8192]{1,0:T(8,128)(2,1)S(1)}, bf16[128,8192]{1,0:T(8,128)(2,1)}, u32[]{:S(2)}, u32[]{:S(2)}) collective-permute-start(bf16[128,8192]{1,0:T(8,128)(2,1)S(1)} %collective-permute-done.1.rest_2_), channel_id=1, source_target_pairs={{0,1},{1,0},{2,3},{3,2},{4,5},{5,4},{6,7},{7,6},{8,9},{9,8},{10,11... | collective-permute-start | bytes 6291464 | tf_op jit(solution)/shard_map/ppermute | solution.py:24
  86.6 99.6 %all-gather.3.cloned.1.call-start = ((), (), s32[]{:S(2)}) async-start(), calls=%async_computation.3 | async-start | bytes 2621440 | tf_op jit(solution)/shard_map/all_gather | solution.py:374
  88.2 47.8 %collective-permute-start.4 = (bf16[128,8192]{1,0:T(8,128)(2,1)S(1)}, bf16[128,8192]{1,0:T(8,128)(2,1)}, u32[]{:S(2)}, u32[]{:S(2)}) collective-permute-start(bf16[128,8192]{1,0:T(8,128)(2,1)S(1)} %copy-done.13), channel_id=1, source_target_pairs={{0,2},{1,3},{2,0},{3,1},{4,6},{5,7},{6,4},{7,5},{8,10},{9,11},{10,... | collective-permute-start | bytes 6291464 | tf_op jit(solution)/shard_map/ppermute | solution.py:24
  89.9 48.6 %collective-permute-start.3 = (bf16[128,8192]{1,0:T(8,128)(2,1)S(1)}, bf16[128,8192]{1,0:T(8,128)(2,1)}, u32[]{:S(2)}, u32[]{:S(2)}) collective-permute-start(bf16[128,8192]{1,0:T(8,128)(2,1)S(1)} %copy-done.13), channel_id=1, source_target_pairs={{0,1},{1,0},{2,3},{3,2},{4,5},{5,4},{6,7},{7,6},{8,9},{9,8},{10,11... | collective-permute-start | bytes 6291464 | tf_op jit(solution)/shard_map/ppermute | solution.py:24
  136.0 4.5 %collective-permute-start.5 = (bf16[128,8192]{1,0:T(8,128)(2,1)}, bf16[128,8192]{1,0:T(8,128)(2,1)}, u32[]{:S(2)}, u32[]{:S(2)}) collective-permute-start(bf16[128,8192]{1,0:T(8,128)(2,1)} %collective-permute-done.4.rest_2_), channel_id=1, source_target_pairs={{0,1},{1,0},{2,3},{3,2},{4,5},{5,4},{6,7},{7,6},{8,9},{9,8},{10,11... | collective-permute-start | bytes 6291464 | tf_op jit(solution)/shard_map/ppermute | solution.py:24
  138.5 92.8 %reduce-scatter.5.cloned.1.call-start = ((), (), s32[]{:S(2)}) async-start(), calls=%async_computation.4 | async-start | bytes 2621440 | tf_op jit(solution)/shard_map/reduce_scatter | solution.py:368
  186.2 92.9 %all-gather.5.cloned.1.call-start = ((), (), s32[]{:S(2)}) async-start(), calls=%async_computation.5 | async-start | bytes 2621440 | tf_op jit(solution)/shard_map/all_gather | solution.py:374
  194.8 24.1 %collective-permute-start.6 = (f32[264,128]{1,0:T(8,128)S(1)}, f32[264,128]{1,0:T(8,128)S(1)}, u32[]{:S(2)}, u32[]{:S(2)}) collective-permute-start(f32[264,128]{1,0:T(8,128)S(1)} %get-tuple-element.52), channel_id=1, source_target_pairs={{0,1},{1,0},{2,3},{3,2},{4,5},{5,4},{6,7},{7,6},{8,9},{9,8},{10,11... | collective-permute-start | bytes 405512 | tf_op jit(solution)/shard_map/ppermute | solution.py:24
  233.9 2.6 collective-permute-start.10
  234.0 2.6 collective-permute-start.9
  234.5 2.9 collective-permute-start.8
  234.6 3.6 collective-permute-start.7
  235.0 5.6 %collective-permute-start.12 = (f32[264,128]{1,0:T(8,128)S(1)}, f32[264,128]{1,0:T(8,128)S(1)}, u32[]{:S(2)}, u32[]{:S(2)}) collective-permute-start(f32[264,128]{1,0:T(8,128)S(1)} %add.41), channel_id=1, source_target_pairs={{0,2},{1,3},{2,0},{3,1},{4,6},{5,7},{6,4},{7,5},{8,10},{9,11},{10,... | collective-permute-start | bytes 405512 | tf_op jit(solution)/shard_map/ppermute | solution.py:24
  240.6 62.5 %collective-permute-start.13 = (bf16[8192,128]{1,0:T(8,128)(2,1)}, bf16[8192,128]{1,0:T(8,128)(2,1)S(1)}, u32[]{:S(2)}, u32[]{:S(2)}) collective-permute-start(bf16[8192,128]{1,0:T(8,128)(2,1)} %add_convert_fusion.1.rest_0_), channel_id=1, source_target_pairs={{0,2},{1,3},{2,0},{3,1},{4,6},{5,7},{6,4},{7,5},{8,10},{9,11},{10,... | collective-permute-start | bytes 6291464 | tf_op jit(solution)/shard_map/ppermute | solution.py:24
  304.9 2.0 collective-permute-start.17
  305.0 2.6 collective-permute-start.16
  305.5 2.9 collective-permute-start.15
  305.6 4.3 %collective-permute-start.14 = (bf16[2048,128]{1,0:T(8,128)(2,1)S(1)}, bf16[2048,128]{1,0:T(8,128)(2,1)S(1)}, u32[]{:S(2)}, u32[]{:S(2)}) collective-permute-start(bf16[2048,128]{1,0:T(8,128)(2,1)S(1)} %get-tuple-element.78), channel_id=1, source_target_pairs={{0,1},{1,0},{2,3},{3,2},{4,5},{5,4},{6,7},{7,6},{8,9},{9,8},{10,11... | collective-permute-start | bytes 1572872 | tf_op jit(solution)/shard_map/ppermute | solution.py:24
  306.0 9.1 %collective-permute-start.19 = (bf16[8192,128]{1,0:T(8,128)(2,1)S(1)}, bf16[8192,128]{1,0:T(8,128)(2,1)S(1)}, u32[]{:S(2)}, u32[]{:S(2)}) collective-permute-start(bf16[8192,128]{1,0:T(8,128)(2,1)S(1)} %copy-done.12), channel_id=1, source_target_pairs={{0,1},{1,0},{2,3},{3,2},{4,5},{5,4},{6,7},{7,6},{8,9},{9,8},{10,11... | collective-permute-start | bytes 6291464 | tf_op jit(solution)/shard_map/ppermute | solution.py:24
  306.9 17.0 %collective-permute-start.11 = (bf16[8192,128]{1,0:T(8,128)(2,1)}, bf16[8192,128]{1,0:T(8,128)(2,1)S(1)}, u32[]{:S(2)}, u32[]{:S(2)}) collective-permute-start(bf16[8192,128]{1,0:T(8,128)(2,1)} %get-tuple-element.60), channel_id=1, source_target_pairs={{0,1},{1,0},{2,3},{3,2},{4,5},{5,4},{6,7},{7,6},{8,9},{9,8},{10,11... | collective-permute-start | bytes 6291464 | tf_op jit(solution)/shard_map/ppermute | solution.py:24
  310.5 47.7 %collective-permute-start.18 = (bf16[8192,128]{1,0:T(8,128)(2,1)S(1)}, bf16[8192,128]{1,0:T(8,128)(2,1)S(1)}, u32[]{:S(2)}, u32[]{:S(2)}) collective-permute-start(bf16[8192,128]{1,0:T(8,128)(2,1)S(1)} %add_convert_fusion), channel_id=1, source_target_pairs={{0,2},{1,3},{2,0},{3,1},{4,6},{5,7},{6,4},{7,5},{8,10},{9,11},{10,... | collective-permute-start | bytes 6291464 | tf_op jit(solution)/shard_map/ppermute | solution.py:24
  322.3 1.6 collective-permute-start.20
  358.2 7.7 %collective-permute-start.21 = (f32[264,256]{1,0:T(8,128)S(1)}, f32[264,256]{1,0:T(8,128)S(1)}, u32[]{:S(2)}, u32[]{:S(2)}) collective-permute-start(f32[264,256]{1,0:T(8,128)S(1)} %add.45), channel_id=1, source_target_pairs={{0,2},{1,3},{2,0},{3,1},{4,6},{5,7},{6,4},{7,5},{8,10},{9,11},{10,... | collective-permute-start | bytes 811016 | tf_op jit(solution)/shard_map/ppermute | solution.py:24
  363.4 1.4 collective-permute-start.23
  364.8 5.6 %collective-permute-start.24 = (f32[256,128]{1,0:T(8,128)S(1)}, f32[256,128]{1,0:T(8,128)S(1)}, u32[]{:S(2)}, u32[]{:S(2)}) collective-permute-start(f32[256,128]{1,0:T(8,128)S(1)} %add.47), channel_id=1, source_target_pairs={{0,2},{1,3},{2,0},{3,1},{4,6},{5,7},{6,4},{7,5},{8,10},{9,11},{10,... | collective-permute-start | bytes 393224 | tf_op jit(solution)/shard_map/ppermute | solution.py:24
  365.4 5.1 %collective-permute-start.26 = (f32[264,128]{1,0:T(8,128)S(1)}, f32[264,128]{1,0:T(8,128)S(1)}, u32[]{:S(2)}, u32[]{:S(2)}) collective-permute-start(f32[264,128]{1,0:T(8,128)S(1)} %add.43), channel_id=1, source_target_pairs={{0,1},{1,0},{2,3},{3,2},{4,5},{5,4},{6,7},{7,6},{8,9},{9,8},{10,11... | collective-permute-start | bytes 405512 | tf_op jit(solution)/shard_map/ppermute | solution.py:24
  365.9 5.9 %collective-permute-start.22 = (f32[264,256]{1,0:T(8,128)S(1)}, f32[264,256]{1,0:T(8,128)S(1)}, u32[]{:S(2)}, u32[]{:S(2)}) collective-permute-start(f32[264,256]{1,0:T(8,128)S(1)} %add.46), channel_id=1, source_target_pairs={{0,1},{1,0},{2,3},{3,2},{4,5},{5,4},{6,7},{7,6},{8,9},{9,8},{10,11... | collective-permute-start | bytes 811016 | tf_op jit(solution)/shard_map/ppermute | solution.py:24
  370.4 1.4 collective-permute-start.25
  (14 other events, 192.7 us)
Sparse Core Ops, SparseCore 0:
  86.7 45.3 reduce-scatter.2
  138.6 47.5 all-gather.2
  188.6 42.5 reduce-scatter.4
  233.9 45.2 all-gather.4
